TPU v7x, 256 devices: a whole 4x4x8 slice. The times are simulated.
256 devices in a mesh: row: 32 (over x, y, core), col: 8 (over z).
Axes of the slice: x: 4, y: 4, z: 8, core: 2. Of those that a mesh axis runs over, the one named last changes fastest.
Arguments:
- inputs: float32 [512, 12288], P('row', 'col'), may hold values from -600 to 600, as said below
- gain: float32 [12288], P('col'), may hold values from 0.1 to 1.9
- bias: float32 [12288], P('col'), may hold values from -3 to 3
- weight: bfloat16 [12288, 49152], P('col', 'row'), may hold values from -0.0546875 to 0.0546875
- d_act: bfloat16 [512, 49152], P('col', 'row'), may hold values from -1.5 to 1.5
Outputs:
- activated: bfloat16 [512, 49152], P('col', 'row')
- d_normed: bfloat16 [512, 12288], P('row', 'col')
- d_weight: bfloat16 [12288, 49152], P('col', 'row')
Inputs may be any that keep to these rules, and one draw needn't show every extreme that they name: `inputs`: finite values.
All inputs are finite; a program needn't handle non-finite values.
Results may differ from a plain program's by a relative error of at most 0.024.
Values may be sent and summed in bfloat16 or wider, within the bound.
No kernel may reach another device: no remote copies, remote signals or barrier semaphores. Data moves between devices by JAX's collectives and lax.ppermute only.
A program may use at most 64 MiB of HBM per device.

v0:
```python
import functools

import jax
import jax.numpy as jnp
from jax import lax
from jax.experimental import pallas as pl
from jax.experimental.pallas import tpu as pltpu
from jax.sharding import PartitionSpec as P

D = 12288
F32, BF16 = jnp.float32, jnp.bfloat16

NX, NY, NC, NZ = 4, 4, 2, 8
SHIFT = (0, 2, 3, 1)
FAR_FIRST = (4, 5, 3, 6, 2, 7, 1)
TOKENS_OWN = 16
TOKENS_Z = 64
TOKENS = 512
KERNEL_VMEM = 48 << 20


def row_pairs(dx, dy, dc):
    pairs = []
    for x in range(NX):
        for y in range(NY):
            for c in range(NC):
                source = (x * NY + y) * NC + c
                target = (((x + dx) % NX) * NY + (y + dy) % NY) * NC + (c + dc) % NC
                pairs.append((source, target))
    return pairs


def send_row(value, dx=0, dy=0, dc=0):
    return lax.ppermute(value, "row", row_pairs(dx, dy, dc))


def send_col(value, dz):
    return lax.ppermute(value, "col", [(z, (z + dz) % NZ) for z in range(NZ)])


def token_offset(core_shift, x_shift, y_shift):
    row, col = lax.axis_index("row"), lax.axis_index("col")
    x, y, c = row // (NY * NC), (row // NC) % NY, row % NC
    block = (((x + x_shift) % NX) * NY + (y + y_shift) % NY) * NC + (c + core_shift) % NC
    offset = (block * TOKENS_OWN - col * TOKENS_Z + TOKENS) % TOKENS
    return pl.multiple_of(offset, TOKENS_OWN)


def first_kernel(*refs):
    pieces, (w_ref, normed_ref), outs = refs[:8], refs[8:10], refs[10:]

    @pl.when(pl.program_id(0) == 0)
    def _():
        for core_shift in range(2):
            for iy in range(4):
                for ix in range(4):
                    offset = token_offset(core_shift, NX - SHIFT[ix], NY - SHIFT[iy])
                    normed_ref[pl.ds(offset, TOKENS_OWN), :] = pieces[core_shift * 4 + iy][
                        ix * TOKENS_OWN : (ix + 1) * TOKENS_OWN, :
                    ]

    product = jnp.dot(normed_ref[...], w_ref[...], preferred_element_type=F32)
    for k in range(NZ):
        outs[k][...] = product[k * TOKENS_Z : (k + 1) * TOKENS_Z, :].astype(outs[k].dtype)


def partial_pre(pieces, weight, tile):
    depth, width = weight.shape
    return pl.pallas_call(
        first_kernel,
        grid=(width // tile,),
        in_specs=[pl.BlockSpec(v.shape, lambda j: (0, 0)) for v in pieces]
        + [pl.BlockSpec((depth, tile), lambda j: (0, j))],
        out_specs=[pl.BlockSpec((TOKENS, depth), lambda j: (0, 0))]
        + [pl.BlockSpec((TOKENS_Z, tile), lambda j: (0, j))] * NZ,
        out_shape=[jax.ShapeDtypeStruct((TOKENS, depth), BF16)]
        + [jax.ShapeDtypeStruct((TOKENS_Z, width), BF16)] * NZ,
        compiler_params=pltpu.CompilerParams(vmem_limit_bytes=KERNEL_VMEM),
        cost_estimate=pl.CostEstimate(
            flops=2 * TOKENS * depth * width, bytes_accessed=depth * width * 2, transcendentals=0
        ),
    )(*pieces, weight)


def third_kernel(*refs):
    pieces, w_ref, slopes_ref, outs, acc = refs[:8], refs[8], refs[9], refs[10:18], refs[18]

    @pl.when(pl.program_id(0) == 0)
    def _():
        for k in range(NZ):
            slopes_ref[k * TOKENS_Z : (k + 1) * TOKENS_Z, :] = pieces[k][...]

    acc[...] = lax.dot_general(
        slopes_ref[...], w_ref[...], (((1,), (1,)), ((), ())), preferred_element_type=F32
    )
    for core_shift in range(2):
        for iy in range(4):
            for ix in range(4):
                offset = token_offset(core_shift, SHIFT[ix], SHIFT[iy])
                outs[core_shift * 4 + iy][ix * TOKENS_OWN : (ix + 1) * TOKENS_OWN, :] = acc[
                    pl.ds(offset, TOKENS_OWN), :
                ].astype(BF16)


def partial_normed(pieces, weight, tile):
    depth, width = weight.shape
    return pl.pallas_call(
        third_kernel,
        grid=(depth // tile,),
        in_specs=[pl.BlockSpec(v.shape, lambda j: (0, 0)) for v in pieces]
        + [pl.BlockSpec((tile, width), lambda j: (j, 0))],
        out_specs=[pl.BlockSpec((TOKENS, width), lambda j: (0, 0))]
        + [pl.BlockSpec((TOKENS_Z, tile), lambda j: (0, j))] * 8,
        out_shape=[jax.ShapeDtypeStruct((TOKENS, width), BF16)]
        + [jax.ShapeDtypeStruct((TOKENS_Z, depth), BF16)] * 8,
        scratch_shapes=[pltpu.VMEM((TOKENS, tile), F32)],
        compiler_params=pltpu.CompilerParams(vmem_limit_bytes=KERNEL_VMEM),
        cost_estimate=pl.CostEstimate(
            flops=2 * TOKENS * depth * width, bytes_accessed=depth * width * 2, transcendentals=0
        ),
    )(*pieces, weight)


def gelu_tanh(value):
    return jax.nn.gelu(value, approximate=True)


def add(*values):
    total = values[0].astype(F32)
    for value in values[1:]:
        total = total + value.astype(F32)
    return total


def normalize(inputs, gain, bias):
    local = inputs.shape[1]
    local_mean = jnp.sum(inputs, axis=1) / local
    centered = inputs - local_mean[:, None]
    local_square = jnp.sum(centered * centered, axis=1)
    stats = jnp.stack([local_mean, local_square])
    every = lax.all_to_all(jnp.broadcast_to(stats[None], (NZ,) + stats.shape), "col", 0, 0)
    mean = jnp.mean(every[:, 0, :], axis=0)
    offset = every[:, 0, :] - mean[None, :]
    spread = (jnp.sum(every[:, 1, :], axis=0) + local * jnp.sum(offset * offset, axis=0)) / D
    scale = lax.rsqrt(spread + 1e-05)
    moved = centered + (local_mean - mean)[:, None]
    return (moved * scale[:, None] * gain[None, :] + bias[None, :]).astype(BF16)


def per_device(inputs, gain, bias, weight, d_act):
    normed = normalize(inputs, gain, bias)

    along_x = jnp.concatenate([normed] + [send_row(normed, dx=s) for s in SHIFT[1:]])
    along_y = [along_x] + [send_row(along_x, dy=s) for s in SHIFT[1:]]
    other = [send_row(v, dc=1) for v in along_y]

    gathered, *parts = partial_pre(along_y + other, weight, 384)
    arrived = [send_col(parts[k], k) for k in FAR_FIRST]
    result, pullback = jax.vjp(gelu_tanh, add(parts[0], *arrived))
    activated = result.astype(BF16)
    slopes = pullback(d_act.astype(F32))[0].astype(BF16)
    blocks = {k: send_col(slopes, -k) for k in FAR_FIRST}
    pieces = [slopes] + [blocks[k] for k in range(1, NZ)]

    slopes_all, *parts = partial_normed(pieces, weight, 384)
    d_weight = lax.dot_general(
        gathered, slopes_all, (((0,), (0,)), ((), ())), preferred_element_type=F32
    ).astype(BF16)

    sums = [add(parts[i], send_row(parts[4 + i], dc=1)) for i in range(4)]
    arrived = [send_row(sums[i].astype(BF16), dy=SHIFT[i]) for i in range(1, 4)]
    column = add(sums[0], *arrived)
    blocks = [column[i * TOKENS_OWN : (i + 1) * TOKENS_OWN] for i in range(4)]
    arrived = [send_row(blocks[i].astype(BF16), dx=SHIFT[i]) for i in range(1, 4)]
    d_normed = add(blocks[0], *arrived).astype(BF16)
    return (activated, d_normed, d_weight)


def solution(mesh):
    return jax.shard_map(
        per_device,
        mesh=mesh,
        in_specs=(P("row", "col"), P("col"), P("col"), P("col", "row"), P("col", "row")),
        out_specs=(P("col", "row"), P("row", "col"), P("col", "row")),
        check_vma=False,
    )
```

profile of v0, /device:TPU:2, one launch (start us, length us, event | category | flops | bytes accessed | tf_op | source)
XLA Modules:
  0.0 157.4 jit_solution(10560931619951995086)
XLA Ops:
  0.6 1.0 reduce_sum.45
  1.7 1.1 multiply_reduce_fusion
  2.8 16.0 %all_to_all.5 = f32[8,2,16]{2,1,0:T(2,128)S(1)} all-to-all(f32[8,2,16]{2,1,0:T(2,128)S(1)} %broadcast_in_dim.2), channel_id=1, replica_groups=mesh['row'=32,'col'=8] {'col'}, dimensions={0} | all-to-all | bytes 2048 | tf_op jit(solution)/shard_map/all_to_all | solution.py:141
  18.8 1.0 add_convert_fusion.3
  19.8 1.6 collective-permute-start.2
  21.4 0.5 collective-permute-start.1
  22.0 2.1 %collective-permute-start = (bf16[16,1536]{1,0:T(8,128)(2,1)S(1)}, bf16[16,1536]{1,0:T(8,128)(2,1)S(1)}, u32[]{:S(2)}, u32[]{:S(2)}) collective-permute-start(bf16[16,1536]{1,0:T(8,128)(2,1)S(1)} %add_convert_fusion.3), channel_id=1, source_target_pairs={{0,128},{8,136},{16,144},{24,152},{32,160},{40,168},{48,176},{56,1... | collective-permute-start | bytes 147464 | tf_op jit(solution)/shard_map/ppermute | solution.py:34
  24.1 0.1 collective-permute-done.2
  24.2 1.3 collective-permute-done.1
  25.5 2.0 %collective-permute-done = bf16[16,1536]{1,0:T(8,128)(2,1)S(1)} collective-permute-done((bf16[16,1536]{1,0:T(8,128)(2,1)S(1)}, bf16[16,1536]{1,0:T(8,128)(2,1)S(1)}, u32[]{:S(2)}, u32[]{:S(2)}) %collective-permute-start) | collective-permute-done | bytes 49184 | tf_op jit(solution)/shard_map/ppermute | solution.py:34
  27.6 0.0 copy-start
  27.6 1.7 %collective-permute-start.5 = (bf16[64,1536]{1,0:T(8,128)(2,1)S(1)}, bf16[64,1536]{1,0:T(8,128)(2,1)S(1)}, u32[]{:S(2)}, u32[]{:S(2)}) collective-permute-start(bf16[64,1536]{1,0:T(8,128)(2,1)S(1)} %pad_maximum_fusion.refs_0_), channel_id=1, source_target_pairs={{0,16},{8,24},{16,32},{24,40},{32,48},{40,56},{48,0},{56,8},{64,80... | collective-permute-start | bytes 589832 | tf_op jit(solution)/shard_map/ppermute | solution.py:34
  29.2 1.7 %collective-permute-start.4 = (bf16[64,1536]{1,0:T(8,128)(2,1)S(1)}, bf16[64,1536]{1,0:T(8,128)(2,1)S(1)}, u32[]{:S(2)}, u32[]{:S(2)}) collective-permute-start(bf16[64,1536]{1,0:T(8,128)(2,1)S(1)} %pad_maximum_fusion.refs_0_), channel_id=1, source_target_pairs={{0,48},{8,56},{16,0},{24,8},{32,16},{40,24},{48,32},{56,40},{64,11... | collective-permute-start | bytes 589832 | tf_op jit(solution)/shard_map/ppermute | solution.py:34
  30.9 2.0 %collective-permute-start.3 = (bf16[64,1536]{1,0:T(8,128)(2,1)S(1)}, bf16[64,1536]{1,0:T(8,128)(2,1)S(1)}, u32[]{:S(2)}, u32[]{:S(2)}) collective-permute-start(bf16[64,1536]{1,0:T(8,128)(2,1)S(1)} %pad_maximum_fusion.refs_0_), channel_id=1, source_target_pairs={{0,32},{8,40},{16,48},{24,56},{32,0},{40,8},{48,16},{56,24},{64,96... | collective-permute-start | bytes 589832 | tf_op jit(solution)/shard_map/ppermute | solution.py:34
  32.9 0.0 collective-permute-start.6
  32.9 2.8 %collective-permute-done.5.refs_3_ = bf16[64,1536]{1,0:T(8,128)(2,1)S(1)} collective-permute-done((bf16[64,1536]{1,0:T(8,128)(2,1)S(1)}, bf16[64,1536]{1,0:T(8,128)(2,1)S(1)}, u32[]{:S(2)}, u32[]{:S(2)}) %collective-permute-start.5) | collective-permute-done | bytes 196640 | tf_op jit(solution)/shard_map/ppermute | solution.py:34
  35.7 0.5 collective-permute-start.8
  36.2 1.8 %collective-permute-done.3.refs_1_ = bf16[64,1536]{1,0:T(8,128)(2,1)S(1)} collective-permute-done((bf16[64,1536]{1,0:T(8,128)(2,1)S(1)}, bf16[64,1536]{1,0:T(8,128)(2,1)S(1)}, u32[]{:S(2)}, u32[]{:S(2)}) %collective-permute-start.3) | collective-permute-done | bytes 196640 | tf_op jit(solution)/shard_map/ppermute | solution.py:34
  38.1 0.0 collective-permute-done.6.refs_4_
  38.1 0.0 collective-permute-done.9.refs_7_
  38.1 0.0 collective-permute-done.8.refs_6_
  38.1 1.4 collective-permute-done.7.refs_5_
  39.5 5.9 %shard_map.76 = (bf16[512,1536]{1,0:T(8,128)(2,1)S(1)}, bf16[64,1536]{1,0:T(8,128)(2,1)S(1)}, bf16[64,1536]{1,0:T(8,128)(2,1)S(1)}, bf16[64,1536]{1,0:T(8,128)(2...) custom-call(bf16[64,1536]{1,0:T(8,128)(2,1)S(1)} %pad_maximum_fusion, ...), custom_call_target="tpu_custom_call" | custom-call | flops 2415919104 | bytes 4718592 | tf_op jit(solution)/shard_map/pallas_call | solution.py:69
  45.4 0.7 collective-permute-start.10
  46.1 4.4 %collective-permute-start.11 = (bf16[64,1536]{1,0:T(8,128)(2,1)S(1)}, bf16[64,1536]{1,0:T(8,128)(2,1)S(1)}, u32[]{:S(2)}, u32[]{:S(2)}) collective-permute-start(bf16[64,1536]{1,0:T(8,128)(2,1)S(1)} %get-tuple-element.23), channel_id=1, source_target_pairs={{0,5},{1,6},{2,7},{3,0},{4,1},{5,2},{6,3},{7,4},{8,13},{9,14},{10,... | collective-permute-start | bytes 589832 | tf_op jit(solution)/shard_map/ppermute | solution.py:38
  50.6 4.1 %collective-permute-start.13 = (bf16[64,1536]{1,0:T(8,128)(2,1)S(1)}, bf16[64,1536]{1,0:T(8,128)(2,1)S(1)}, u32[]{:S(2)}, u32[]{:S(2)}) collective-permute-start(bf16[64,1536]{1,0:T(8,128)(2,1)S(1)} %get-tuple-element.25), channel_id=1, source_target_pairs={{0,6},{1,7},{2,0},{3,1},{4,2},{5,3},{6,4},{7,5},{8,14},{9,15},{10,... | collective-permute-start | bytes 589832 | tf_op jit(solution)/shard_map/ppermute | solution.py:38
  54.7 9.6 %collective-permute-done.10 = bf16[64,1536]{1,0:T(8,128)(2,1)S(1)} collective-permute-done((bf16[64,1536]{1,0:T(8,128)(2,1)S(1)}, bf16[64,1536]{1,0:T(8,128)(2,1)S(1)}, u32[]{:S(2)}, u32[]{:S(2)}) %collective-permute-start.10) | collective-permute-done | bytes 196640 | tf_op jit(solution)/shard_map/ppermute | solution.py:38
  64.3 5.9 %collective-permute-done.11 = bf16[64,1536]{1,0:T(8,128)(2,1)S(1)} collective-permute-done((bf16[64,1536]{1,0:T(8,128)(2,1)S(1)}, bf16[64,1536]{1,0:T(8,128)(2,1)S(1)}, u32[]{:S(2)}, u32[]{:S(2)}) %collective-permute-start.11) | collective-permute-done | bytes 196640 | tf_op jit(solution)/shard_map/ppermute | solution.py:38
  70.2 4.4 %collective-permute-start.16 = (bf16[64,1536]{1,0:T(8,128)(2,1)S(1)}, bf16[64,1536]{1,0:T(8,128)(2,1)S(1)}, u32[]{:S(2)}, u32[]{:S(2)}) collective-permute-start(bf16[64,1536]{1,0:T(8,128)(2,1)S(1)} %get-tuple-element.28), channel_id=1, source_target_pairs={{0,1},{1,2},{2,3},{3,4},{4,5},{5,6},{6,7},{7,0},{8,9},{9,10},{10,1... | collective-permute-start | bytes 589832 | tf_op jit(solution)/shard_map/ppermute | solution.py:38
  74.6 5.0 %collective-permute-done.13 = bf16[64,1536]{1,0:T(8,128)(2,1)S(1)} collective-permute-done((bf16[64,1536]{1,0:T(8,128)(2,1)S(1)}, bf16[64,1536]{1,0:T(8,128)(2,1)S(1)}, u32[]{:S(2)}, u32[]{:S(2)}) %collective-permute-start.13) | collective-permute-done | bytes 196640 | tf_op jit(solution)/shard_map/ppermute | solution.py:38
  79.7 2.4 %collective-permute-done.15 = bf16[64,1536]{1,0:T(8,128)(2,1)S(1)} collective-permute-done((bf16[64,1536]{1,0:T(8,128)(2,1)S(1)}, bf16[64,1536]{1,0:T(8,128)(2,1)S(1)}, u32[]{:S(2)}, u32[]{:S(2)}) %collective-permute-start.15) | collective-permute-done | bytes 196640 | tf_op jit(solution)/shard_map/ppermute | solution.py:38
  82.0 2.1 %collective-permute-done.16 = bf16[64,1536]{1,0:T(8,128)(2,1)S(1)} collective-permute-done((bf16[64,1536]{1,0:T(8,128)(2,1)S(1)}, bf16[64,1536]{1,0:T(8,128)(2,1)S(1)}, u32[]{:S(2)}, u32[]{:S(2)}) %collective-permute-start.16) | collective-permute-done | bytes 196640 | tf_op jit(solution)/shard_map/ppermute | solution.py:38
  84.1 0.5 fusion.2
  84.6 1.2 collective-permute-start.23
  85.8 1.8 %collective-permute-start.22 = (bf16[64,1536]{1,0:T(8,128)(2,1)S(1)}, bf16[64,1536]{1,0:T(8,128)(2,1)S(1)}, u32[]{:S(2)}, u32[]{:S(2)}) collective-permute-start(bf16[64,1536]{1,0:T(8,128)(2,1)S(1)} %get-tuple-element.41.refs_0_), channel_id=1, source_target_pairs={{0,2},{1,3},{2,4},{3,5},{4,6},{5,7},{6,0},{7,1},{8,10},{9,11},{10,... | collective-permute-start | bytes 589832 | tf_op jit(solution)/shard_map/ppermute | solution.py:38
  87.6 2.3 %collective-permute-start.21 = (bf16[64,1536]{1,0:T(8,128)(2,1)S(1)}, bf16[64,1536]{1,0:T(8,128)(2,1)S(1)}, u32[]{:S(2)}, u32[]{:S(2)}) collective-permute-start(bf16[64,1536]{1,0:T(8,128)(2,1)S(1)} %get-tuple-element.41.refs_0_), channel_id=1, source_target_pairs={{0,3},{1,4},{2,5},{3,6},{4,7},{5,0},{6,1},{7,2},{8,11},{9,12},{10,... | collective-permute-start | bytes 589832 | tf_op jit(solution)/shard_map/ppermute | solution.py:38
  89.9 1.9 %collective-permute-start.20 = (bf16[64,1536]{1,0:T(8,128)(2,1)S(1)}, bf16[64,1536]{1,0:T(8,128)(2,1)S(1)}, u32[]{:S(2)}, u32[]{:S(2)}) collective-permute-start(bf16[64,1536]{1,0:T(8,128)(2,1)S(1)} %get-tuple-element.41.refs_0_), channel_id=1, source_target_pairs={{0,4},{1,5},{2,6},{3,7},{4,0},{5,1},{6,2},{7,3},{8,12},{9,13},{10,... | collective-permute-start | bytes 589832 | tf_op jit(solution)/shard_map/ppermute | solution.py:38
  91.8 2.6 %collective-permute-start.19 = (bf16[64,1536]{1,0:T(8,128)(2,1)S(1)}, bf16[64,1536]{1,0:T(8,128)(2,1)S(1)}, u32[]{:S(2)}, u32[]{:S(2)}) collective-permute-start(bf16[64,1536]{1,0:T(8,128)(2,1)S(1)} %get-tuple-element.41.refs_0_), channel_id=1, source_target_pairs={{0,5},{1,6},{2,7},{3,0},{4,1},{5,2},{6,3},{7,4},{8,13},{9,14},{10,... | collective-permute-start | bytes 589832 | tf_op jit(solution)/shard_map/ppermute | solution.py:38
  94.5 3.0 %collective-permute-done.23.refs_7_ = bf16[64,1536]{1,0:T(8,128)(2,1)S(1)} collective-permute-done((bf16[64,1536]{1,0:T(8,128)(2,1)S(1)}, bf16[64,1536]{1,0:T(8,128)(2,1)S(1)}, u32[]{:S(2)}, u32[]{:S(2)}) %collective-permute-start.23) | collective-permute-done | bytes 196640 | tf_op jit(solution)/shard_map/ppermute | solution.py:38
  97.5 0.1 collective-permute-start.18
  97.6 3.0 %collective-permute-done.22.refs_6_ = bf16[64,1536]{1,0:T(8,128)(2,1)S(1)} collective-permute-done((bf16[64,1536]{1,0:T(8,128)(2,1)S(1)}, bf16[64,1536]{1,0:T(8,128)(2,1)S(1)}, u32[]{:S(2)}, u32[]{:S(2)}) %collective-permute-start.22) | collective-permute-done | bytes 196640 | tf_op jit(solution)/shard_map/ppermute | solution.py:38
  100.6 11.9 %collective-permute-start.17 = (bf16[64,1536]{1,0:T(8,128)(2,1)S(1)}, bf16[64,1536]{1,0:T(8,128)(2,1)S(1)}, u32[]{:S(2)}, u32[]{:S(2)}) collective-permute-start(bf16[64,1536]{1,0:T(8,128)(2,1)S(1)} %get-tuple-element.41.refs_0_), channel_id=1, source_target_pairs={{0,7},{1,0},{2,1},{3,2},{4,3},{5,4},{6,5},{7,6},{8,15},{9,8},{10,9... | collective-permute-start | bytes 589832 | tf_op jit(solution)/shard_map/ppermute | solution.py:38
  112.5 6.8 %collective-permute-done.21.refs_5_ = bf16[64,1536]{1,0:T(8,128)(2,1)S(1)} collective-permute-done((bf16[64,1536]{1,0:T(8,128)(2,1)S(1)}, bf16[64,1536]{1,0:T(8,128)(2,1)S(1)}, u32[]{:S(2)}, u32[]{:S(2)}) %collective-permute-start.21) | collective-permute-done | bytes 196640 | tf_op jit(solution)/shard_map/ppermute | solution.py:38
  119.3 4.2 %collective-permute-done.18.refs_2_ = bf16[64,1536]{1,0:T(8,128)(2,1)S(1)} collective-permute-done((bf16[64,1536]{1,0:T(8,128)(2,1)S(1)}, bf16[64,1536]{1,0:T(8,128)(2,1)S(1)}, u32[]{:S(2)}, u32[]{:S(2)}) %collective-permute-start.18) | collective-permute-done | bytes 196640 | tf_op jit(solution)/shard_map/ppermute | solution.py:38
  123.5 4.1 %collective-permute-done.17.refs_1_ = bf16[64,1536]{1,0:T(8,128)(2,1)S(1)} collective-permute-done((bf16[64,1536]{1,0:T(8,128)(2,1)S(1)}, bf16[64,1536]{1,0:T(8,128)(2,1)S(1)}, u32[]{:S(2)}, u32[]{:S(2)}) %collective-permute-start.17) | collective-permute-done | bytes 196640 | tf_op jit(solution)/shard_map/ppermute | solution.py:38
  127.5 6.2 %shard_map.77 = (bf16[512,1536]{1,0:T(8,128)(2,1)S(1)}, bf16[64,1536]{1,0:T(8,128)(2,1)S(1)}, bf16[64,1536]{1,0:T(8,128)(2,1)S(1)}, bf16[64,1536]{1,0:T(8,128)(2...) custom-call(bf16[64,1536]{1,0:T(8,128)(2,1)S(1)} %get-tuple-element., ...), custom_call_target="tpu_custom_call" | custom-call | flops 2415919104 | bytes 4718592 | tf_op jit(solution)/shard_map/pallas_call | solution.py:107
  133.8 0.1 collective-permute-start.25
  133.9 0.5 collective-permute-start.24
  134.4 0.1 collective-permute-start.27
  134.5 0.4 collective-permute-start.29
  134.9 0.4 collective-permute-done.25
  135.4 2.1 %collective-permute-start.26 = (bf16[64,1536]{1,0:T(8,128)(2,1)S(1)}, bf16[64,1536]{1,0:T(8,128)(2,1)S(1)}, u32[]{:S(2)}, u32[]{:S(2)}) collective-permute-start(bf16[64,1536]{1,0:T(8,128)(2,1)S(1)} %add_convert_fusion.2), channel_id=1, source_target_pairs={{0,32},{8,40},{16,48},{24,56},{32,0},{40,8},{48,16},{56,24},{64,96... | collective-permute-start | bytes 589832 | tf_op jit(solution)/shard_map/ppermute | solution.py:34
  137.5 2.0 %collective-permute-start.28 = (bf16[64,1536]{1,0:T(8,128)(2,1)S(1)}, bf16[64,1536]{1,0:T(8,128)(2,1)S(1)}, u32[]{:S(2)}, u32[]{:S(2)}) collective-permute-start(bf16[64,1536]{1,0:T(8,128)(2,1)S(1)} %add_convert_fusion.1), channel_id=1, source_target_pairs={{0,48},{8,56},{16,0},{24,8},{32,16},{40,24},{48,32},{56,40},{64,11... | collective-permute-start | bytes 589832 | tf_op jit(solution)/shard_map/ppermute | solution.py:34
  139.6 0.2 collective-permute-start.30
  139.7 0.8 multiply_convert_fusion
  140.5 4.2 %collective-permute-done.26 = bf16[64,1536]{1,0:T(8,128)(2,1)S(1)} collective-permute-done((bf16[64,1536]{1,0:T(8,128)(2,1)S(1)}, bf16[64,1536]{1,0:T(8,128)(2,1)S(1)}, u32[]{:S(2)}, u32[]{:S(2)}) %collective-permute-start.26) | collective-permute-done | bytes 196640 | tf_op jit(solution)/shard_map/ppermute | solution.py:34
  144.7 2.6 %collective-permute-done.28 = bf16[64,1536]{1,0:T(8,128)(2,1)S(1)} collective-permute-done((bf16[64,1536]{1,0:T(8,128)(2,1)S(1)}, bf16[64,1536]{1,0:T(8,128)(2,1)S(1)}, u32[]{:S(2)}, u32[]{:S(2)}) %collective-permute-start.28) | collective-permute-done | bytes 196640 | tf_op jit(solution)/shard_map/ppermute | solution.py:34
  147.3 0.8 collective-permute-done.30
  148.1 0.1 fusion.15
  148.3 2.2 %collective-permute-start.31 = (bf16[16,1536]{1,0:T(8,128)(2,1)S(1)}, bf16[16,1536]{1,0:T(8,128)(2,1)S(1)}, u32[]{:S(2)}, u32[]{:S(2)}) collective-permute-start(bf16[16,1536]{1,0:T(8,128)(2,1)S(1)} %get-tuple-element.43), channel_id=1, source_target_pairs={{0,128},{8,136},{16,144},{24,152},{32,160},{40,168},{48,176},{56,1... | collective-permute-start | bytes 147464 | tf_op jit(solution)/shard_map/ppermute | solution.py:34
  150.5 1.1 collective-permute-start.33
  151.6 0.9 collective-permute-start.32
  152.5 4.3 %convolution_convert_fusion = bf16[1536,1536]{1,0:T(8,128)(2,1)} fusion(bf16[512,1536]{1,0:T(8,128)(2,1)S(1)} %get-tuple-element.37, bf16[512,1536]{1,0:T(8,128)(2,1)S(1)} %get-tuple-element.38), kind=kOutput, calls=%fused_computation | convolution fusion | flops 2418278400 | bytes 7864320 | tf_op jit(solution)/shard_map/dot_general | solution.py:166
  156.8 0.6 fusion.12
  (30 shorter events, 0.3 us)
Async XLA Ops:
  19.8 4.3 %collective-permute-start.2 = (bf16[16,1536]{1,0:T(8,128)(2,1)S(1)}, bf16[16,1536]{1,0:T(8,128)(2,1)S(1)}, u32[]{:S(2)}, u32[]{:S(2)}) collective-permute-start(bf16[16,1536]{1,0:T(8,128)(2,1)S(1)} %add_convert_fusion.3), channel_id=1, source_target_pairs={{0,64},{8,72},{16,80},{24,88},{32,96},{40,104},{48,112},{56,120},{... | collective-permute-start | bytes 147464 | tf_op jit(solution)/shard_map/ppermute | solution.py:34
  21.4 4.1 %collective-permute-start.1 = (bf16[16,1536]{1,0:T(8,128)(2,1)S(1)}, bf16[16,1536]{1,0:T(8,128)(2,1)S(1)}, u32[]{:S(2)}, u32[]{:S(2)}) collective-permute-start(bf16[16,1536]{1,0:T(8,128)(2,1)S(1)} %add_convert_fusion.3), channel_id=1, source_target_pairs={{0,192},{8,200},{16,208},{24,216},{32,224},{40,232},{48,240},{56,2... | collective-permute-start | bytes 147464 | tf_op jit(solution)/shard_map/ppermute | solution.py:34
  22.0 5.6 %collective-permute-start = (bf16[16,1536]{1,0:T(8,128)(2,1)S(1)}, bf16[16,1536]{1,0:T(8,128)(2,1)S(1)}, u32[]{:S(2)}, u32[]{:S(2)}) collective-permute-start(bf16[16,1536]{1,0:T(8,128)(2,1)S(1)} %add_convert_fusion.3), channel_id=1, source_target_pairs={{0,128},{8,136},{16,144},{24,152},{32,160},{40,168},{48,176},{56,1... | collective-permute-start | bytes 147464 | tf_op jit(solution)/shard_map/ppermute | solution.py:34
  27.6 56.5 %copy-start = (bf16[64,1536]{1,0:T(8,128)(2,1)S(1)}, bf16[64,1536]{1,0:T(8,128)(2,1)}, u32[]{:S(2)}) copy-start(bf16[64,1536]{1,0:T(8,128)(2,1)} %param.9) | copy-start | bytes 589828
  27.6 8.1 %collective-permute-start.5 = (bf16[64,1536]{1,0:T(8,128)(2,1)S(1)}, bf16[64,1536]{1,0:T(8,128)(2,1)S(1)}, u32[]{:S(2)}, u32[]{:S(2)}) collective-permute-start(bf16[64,1536]{1,0:T(8,128)(2,1)S(1)} %pad_maximum_fusion.refs_0_), channel_id=1, source_target_pairs={{0,16},{8,24},{16,32},{24,40},{32,48},{40,56},{48,0},{56,8},{64,80... | collective-permute-start | bytes 589832 | tf_op jit(solution)/shard_map/ppermute | solution.py:34
  29.2 6.5 %collective-permute-start.4 = (bf16[64,1536]{1,0:T(8,128)(2,1)S(1)}, bf16[64,1536]{1,0:T(8,128)(2,1)S(1)}, u32[]{:S(2)}, u32[]{:S(2)}) collective-permute-start(bf16[64,1536]{1,0:T(8,128)(2,1)S(1)} %pad_maximum_fusion.refs_0_), channel_id=1, source_target_pairs={{0,48},{8,56},{16,0},{24,8},{32,16},{40,24},{48,32},{56,40},{64,11... | collective-permute-start | bytes 589832 | tf_op jit(solution)/shard_map/ppermute | solution.py:34
  30.9 7.2 %collective-permute-start.3 = (bf16[64,1536]{1,0:T(8,128)(2,1)S(1)}, bf16[64,1536]{1,0:T(8,128)(2,1)S(1)}, u32[]{:S(2)}, u32[]{:S(2)}) collective-permute-start(bf16[64,1536]{1,0:T(8,128)(2,1)S(1)} %pad_maximum_fusion.refs_0_), channel_id=1, source_target_pairs={{0,32},{8,40},{16,48},{24,56},{32,0},{40,8},{48,16},{56,24},{64,96... | collective-permute-start | bytes 589832 | tf_op jit(solution)/shard_map/ppermute | solution.py:34
  32.9 5.2 %collective-permute-start.6 = (bf16[64,1536]{1,0:T(8,128)(2,1)S(1)}, bf16[64,1536]{1,0:T(8,128)(2,1)S(1)}, u32[]{:S(2)}, u32[]{:S(2)}) collective-permute-start(bf16[64,1536]{1,0:T(8,128)(2,1)S(1)} %pad_maximum_fusion.refs_0_), channel_id=1, source_target_pairs={{0,8},{8,0},{16,24},{24,16},{32,40},{40,32},{48,56},{56,48},{64,72... | collective-permute-start | bytes 589832 | tf_op jit(solution)/shard_map/ppermute | solution.py:34
  35.7 2.4 %collective-permute-start.9 = (bf16[64,1536]{1,0:T(8,128)(2,1)S(1)}, bf16[64,1536]{1,0:T(8,128)(2,1)S(1)}, u32[]{:S(2)}, u32[]{:S(2)}) collective-permute-start(bf16[64,1536]{1,0:T(8,128)(2,1)S(1)} %collective-permute-done.5.refs_3_), channel_id=1, source_target_pairs={{0,8},{8,0},{16,24},{24,16},{32,40},{40,32},{48,56},{56,48},{64,72... | collective-permute-start | bytes 589832 | tf_op jit(solution)/shard_map/ppermute | solution.py:34
  35.7 2.4 %collective-permute-start.8 = (bf16[64,1536]{1,0:T(8,128)(2,1)S(1)}, bf16[64,1536]{1,0:T(8,128)(2,1)S(1)}, u32[]{:S(2)}, u32[]{:S(2)}) collective-permute-start(bf16[64,1536]{1,0:T(8,128)(2,1)S(1)} %collective-permute-done.4.refs_2_), channel_id=1, source_target_pairs={{0,8},{8,0},{16,24},{24,16},{32,40},{40,32},{48,56},{56,48},{64,72... | collective-permute-start | bytes 589832 | tf_op jit(solution)/shard_map/ppermute | solution.py:34
  38.1 1.4 collective-permute-start.7
  45.4 18.9 %collective-permute-start.10 = (bf16[64,1536]{1,0:T(8,128)(2,1)S(1)}, bf16[64,1536]{1,0:T(8,128)(2,1)S(1)}, u32[]{:S(2)}, u32[]{:S(2)}) collective-permute-start(bf16[64,1536]{1,0:T(8,128)(2,1)S(1)} %get-tuple-element.22), channel_id=1, source_target_pairs={{0,4},{1,5},{2,6},{3,7},{4,0},{5,1},{6,2},{7,3},{8,12},{9,13},{10,... | collective-permute-start | bytes 589832 | tf_op jit(solution)/shard_map/ppermute | solution.py:38
  46.1 24.1 %collective-permute-start.11 = (bf16[64,1536]{1,0:T(8,128)(2,1)S(1)}, bf16[64,1536]{1,0:T(8,128)(2,1)S(1)}, u32[]{:S(2)}, u32[]{:S(2)}) collective-permute-start(bf16[64,1536]{1,0:T(8,128)(2,1)S(1)} %get-tuple-element.23), channel_id=1, source_target_pairs={{0,5},{1,6},{2,7},{3,0},{4,1},{5,2},{6,3},{7,4},{8,13},{9,14},{10,... | collective-permute-start | bytes 589832 | tf_op jit(solution)/shard_map/ppermute | solution.py:38
  50.6 24.1 %collective-permute-start.12 = (bf16[64,1536]{1,0:T(8,128)(2,1)S(1)}, bf16[64,1536]{1,0:T(8,128)(2,1)S(1)}, u32[]{:S(2)}, u32[]{:S(2)}) collective-permute-start(bf16[64,1536]{1,0:T(8,128)(2,1)S(1)} %get-tuple-element.24), channel_id=1, source_target_pairs={{0,3},{1,4},{2,5},{3,6},{4,7},{5,0},{6,1},{7,2},{8,11},{9,12},{10,... | collective-permute-start | bytes 589832 | tf_op jit(solution)/shard_map/ppermute | solution.py:38
  50.6 29.1 %collective-permute-start.13 = (bf16[64,1536]{1,0:T(8,128)(2,1)S(1)}, bf16[64,1536]{1,0:T(8,128)(2,1)S(1)}, u32[]{:S(2)}, u32[]{:S(2)}) collective-permute-start(bf16[64,1536]{1,0:T(8,128)(2,1)S(1)} %get-tuple-element.25), channel_id=1, source_target_pairs={{0,6},{1,7},{2,0},{3,1},{4,2},{5,3},{6,4},{7,5},{8,14},{9,15},{10,... | collective-permute-start | bytes 589832 | tf_op jit(solution)/shard_map/ppermute | solution.py:38
  54.7 25.0 %collective-permute-start.14 = (bf16[64,1536]{1,0:T(8,128)(2,1)S(1)}, bf16[64,1536]{1,0:T(8,128)(2,1)S(1)}, u32[]{:S(2)}, u32[]{:S(2)}) collective-permute-start(bf16[64,1536]{1,0:T(8,128)(2,1)S(1)} %get-tuple-element.26), channel_id=1, source_target_pairs={{0,2},{1,3},{2,4},{3,5},{4,6},{5,7},{6,0},{7,1},{8,10},{9,11},{10,... | collective-permute-start | bytes 589832 | tf_op jit(solution)/shard_map/ppermute | solution.py:38
  64.3 17.7 %collective-permute-start.15 = (bf16[64,1536]{1,0:T(8,128)(2,1)S(1)}, bf16[64,1536]{1,0:T(8,128)(2,1)S(1)}, u32[]{:S(2)}, u32[]{:S(2)}) collective-permute-start(bf16[64,1536]{1,0:T(8,128)(2,1)S(1)} %get-tuple-element.27), channel_id=1, source_target_pairs={{0,7},{1,0},{2,1},{3,2},{4,3},{5,4},{6,5},{7,6},{8,15},{9,8},{10,9... | collective-permute-start | bytes 589832 | tf_op jit(solution)/shard_map/ppermute | solution.py:38
  70.2 13.9 %collective-permute-start.16 = (bf16[64,1536]{1,0:T(8,128)(2,1)S(1)}, bf16[64,1536]{1,0:T(8,128)(2,1)S(1)}, u32[]{:S(2)}, u32[]{:S(2)}) collective-permute-start(bf16[64,1536]{1,0:T(8,128)(2,1)S(1)} %get-tuple-element.28), channel_id=1, source_target_pairs={{0,1},{1,2},{2,3},{3,4},{4,5},{5,6},{6,7},{7,0},{8,9},{9,10},{10,1... | collective-permute-start | bytes 589832 | tf_op jit(solution)/shard_map/ppermute | solution.py:38
  84.6 12.9 %collective-permute-start.23 = (bf16[64,1536]{1,0:T(8,128)(2,1)S(1)}, bf16[64,1536]{1,0:T(8,128)(2,1)S(1)}, u32[]{:S(2)}, u32[]{:S(2)}) collective-permute-start(bf16[64,1536]{1,0:T(8,128)(2,1)S(1)} %get-tuple-element.41.refs_0_), channel_id=1, source_target_pairs={{0,1},{1,2},{2,3},{3,4},{4,5},{5,6},{6,7},{7,0},{8,9},{9,10},{10,1... | collective-permute-start | bytes 589832 | tf_op jit(solution)/shard_map/ppermute | solution.py:38
  85.8 14.8 %collective-permute-start.22 = (bf16[64,1536]{1,0:T(8,128)(2,1)S(1)}, bf16[64,1536]{1,0:T(8,128)(2,1)S(1)}, u32[]{:S(2)}, u32[]{:S(2)}) collective-permute-start(bf16[64,1536]{1,0:T(8,128)(2,1)S(1)} %get-tuple-element.41.refs_0_), channel_id=1, source_target_pairs={{0,2},{1,3},{2,4},{3,5},{4,6},{5,7},{6,0},{7,1},{8,10},{9,11},{10,... | collective-permute-start | bytes 589832 | tf_op jit(solution)/shard_map/ppermute | solution.py:38
  87.6 31.8 %collective-permute-start.21 = (bf16[64,1536]{1,0:T(8,128)(2,1)S(1)}, bf16[64,1536]{1,0:T(8,128)(2,1)S(1)}, u32[]{:S(2)}, u32[]{:S(2)}) collective-permute-start(bf16[64,1536]{1,0:T(8,128)(2,1)S(1)} %get-tuple-element.41.refs_0_), channel_id=1, source_target_pairs={{0,3},{1,4},{2,5},{3,6},{4,7},{5,0},{6,1},{7,2},{8,11},{9,12},{10,... | collective-permute-start | bytes 589832 | tf_op jit(solution)/shard_map/ppermute | solution.py:38
  89.9 29.4 %collective-permute-start.20 = (bf16[64,1536]{1,0:T(8,128)(2,1)S(1)}, bf16[64,1536]{1,0:T(8,128)(2,1)S(1)}, u32[]{:S(2)}, u32[]{:S(2)}) collective-permute-start(bf16[64,1536]{1,0:T(8,128)(2,1)S(1)} %get-tuple-element.41.refs_0_), channel_id=1, source_target_pairs={{0,4},{1,5},{2,6},{3,7},{4,0},{5,1},{6,2},{7,3},{8,12},{9,13},{10,... | collective-permute-start | bytes 589832 | tf_op jit(solution)/shard_map/ppermute | solution.py:38
  91.8 27.5 %collective-permute-start.19 = (bf16[64,1536]{1,0:T(8,128)(2,1)S(1)}, bf16[64,1536]{1,0:T(8,128)(2,1)S(1)}, u32[]{:S(2)}, u32[]{:S(2)}) collective-permute-start(bf16[64,1536]{1,0:T(8,128)(2,1)S(1)} %get-tuple-element.41.refs_0_), channel_id=1, source_target_pairs={{0,5},{1,6},{2,7},{3,0},{4,1},{5,2},{6,3},{7,4},{8,13},{9,14},{10,... | collective-permute-start | bytes 589832 | tf_op jit(solution)/shard_map/ppermute | solution.py:38
  97.5 26.0 %collective-permute-start.18 = (bf16[64,1536]{1,0:T(8,128)(2,1)S(1)}, bf16[64,1536]{1,0:T(8,128)(2,1)S(1)}, u32[]{:S(2)}, u32[]{:S(2)}) collective-permute-start(bf16[64,1536]{1,0:T(8,128)(2,1)S(1)} %get-tuple-element.41.refs_0_), channel_id=1, source_target_pairs={{0,6},{1,7},{2,0},{3,1},{4,2},{5,3},{6,4},{7,5},{8,14},{9,15},{10,... | collective-permute-start | bytes 589832 | tf_op jit(solution)/shard_map/ppermute | solution.py:38
  100.6 27.0 %collective-permute-start.17 = (bf16[64,1536]{1,0:T(8,128)(2,1)S(1)}, bf16[64,1536]{1,0:T(8,128)(2,1)S(1)}, u32[]{:S(2)}, u32[]{:S(2)}) collective-permute-start(bf16[64,1536]{1,0:T(8,128)(2,1)S(1)} %get-tuple-element.41.refs_0_), channel_id=1, source_target_pairs={{0,7},{1,0},{2,1},{3,2},{4,3},{5,4},{6,5},{7,6},{8,15},{9,8},{10,9... | collective-permute-start | bytes 589832 | tf_op jit(solution)/shard_map/ppermute | solution.py:38
  133.8 1.5 collective-permute-start.25
  133.9 6.6 %collective-permute-start.24 = (bf16[64,1536]{1,0:T(8,128)(2,1)S(1)}, bf16[64,1536]{1,0:T(8,128)(2,1)S(1)}, u32[]{:S(2)}, u32[]{:S(2)}) collective-permute-start(bf16[64,1536]{1,0:T(8,128)(2,1)S(1)} %get-tuple-element.30), channel_id=1, source_target_pairs={{0,8},{8,0},{16,24},{24,16},{32,40},{40,32},{48,56},{56,48},{64,72... | collective-permute-start | bytes 589832 | tf_op jit(solution)/shard_map/ppermute | solution.py:34
  134.4 3.1 %collective-permute-start.27 = (bf16[64,1536]{1,0:T(8,128)(2,1)S(1)}, bf16[64,1536]{1,0:T(8,128)(2,1)S(1)}, u32[]{:S(2)}, u32[]{:S(2)}) collective-permute-start(bf16[64,1536]{1,0:T(8,128)(2,1)S(1)} %get-tuple-element.34), channel_id=1, source_target_pairs={{0,8},{8,0},{16,24},{24,16},{32,40},{40,32},{48,56},{56,48},{64,72... | collective-permute-start | bytes 589832 | tf_op jit(solution)/shard_map/ppermute | solution.py:34
  134.5 5.0 %collective-permute-start.29 = (bf16[64,1536]{1,0:T(8,128)(2,1)S(1)}, bf16[64,1536]{1,0:T(8,128)(2,1)S(1)}, u32[]{:S(2)}, u32[]{:S(2)}) collective-permute-start(bf16[64,1536]{1,0:T(8,128)(2,1)S(1)} %get-tuple-element.36), channel_id=1, source_target_pairs={{0,8},{8,0},{16,24},{24,16},{32,40},{40,32},{48,56},{56,48},{64,72... | collective-permute-start | bytes 589832 | tf_op jit(solution)/shard_map/ppermute | solution.py:34
  135.4 9.3 %collective-permute-start.26 = (bf16[64,1536]{1,0:T(8,128)(2,1)S(1)}, bf16[64,1536]{1,0:T(8,128)(2,1)S(1)}, u32[]{:S(2)}, u32[]{:S(2)}) collective-permute-start(bf16[64,1536]{1,0:T(8,128)(2,1)S(1)} %add_convert_fusion.2), channel_id=1, source_target_pairs={{0,32},{8,40},{16,48},{24,56},{32,0},{40,8},{48,16},{56,24},{64,96... | collective-permute-start | bytes 589832 | tf_op jit(solution)/shard_map/ppermute | solution.py:34
  137.5 9.8 %collective-permute-start.28 = (bf16[64,1536]{1,0:T(8,128)(2,1)S(1)}, bf16[64,1536]{1,0:T(8,128)(2,1)S(1)}, u32[]{:S(2)}, u32[]{:S(2)}) collective-permute-start(bf16[64,1536]{1,0:T(8,128)(2,1)S(1)} %add_convert_fusion.1), channel_id=1, source_target_pairs={{0,48},{8,56},{16,0},{24,8},{32,16},{40,24},{48,32},{56,40},{64,11... | collective-permute-start | bytes 589832 | tf_op jit(solution)/shard_map/ppermute | solution.py:34
  139.6 8.6 %collective-permute-start.30 = (bf16[64,1536]{1,0:T(8,128)(2,1)S(1)}, bf16[64,1536]{1,0:T(8,128)(2,1)S(1)}, u32[]{:S(2)}, u32[]{:S(2)}) collective-permute-start(bf16[64,1536]{1,0:T(8,128)(2,1)S(1)} %add_convert_fusion), channel_id=1, source_target_pairs={{0,16},{8,24},{16,32},{24,40},{32,48},{40,56},{48,0},{56,8},{64,80... | collective-permute-start | bytes 589832 | tf_op jit(solution)/shard_map/ppermute | solution.py:34
  148.3 8.5 %collective-permute-start.31 = (bf16[16,1536]{1,0:T(8,128)(2,1)S(1)}, bf16[16,1536]{1,0:T(8,128)(2,1)S(1)}, u32[]{:S(2)}, u32[]{:S(2)}) collective-permute-start(bf16[16,1536]{1,0:T(8,128)(2,1)S(1)} %get-tuple-element.43), channel_id=1, source_target_pairs={{0,128},{8,136},{16,144},{24,152},{32,160},{40,168},{48,176},{56,1... | collective-permute-start | bytes 147464 | tf_op jit(solution)/shard_map/ppermute | solution.py:34
  150.5 6.3 %collective-permute-start.33 = (bf16[16,1536]{1,0:T(8,128)(2,1)S(1)}, bf16[16,1536]{1,0:T(8,128)(2,1)S(1)}, u32[]{:S(2)}, u32[]{:S(2)}) collective-permute-start(bf16[16,1536]{1,0:T(8,128)(2,1)S(1)} %get-tuple-element.44), channel_id=1, source_target_pairs={{0,64},{8,72},{16,80},{24,88},{32,96},{40,104},{48,112},{56,120},{... | collective-permute-start | bytes 147464 | tf_op jit(solution)/shard_map/ppermute | solution.py:34
  151.6 5.2 %collective-permute-start.32 = (bf16[16,1536]{1,0:T(8,128)(2,1)S(1)}, bf16[16,1536]{1,0:T(8,128)(2,1)S(1)}, u32[]{:S(2)}, u32[]{:S(2)}) collective-permute-start(bf16[16,1536]{1,0:T(8,128)(2,1)S(1)} %get-tuple-element.45), channel_id=1, source_target_pairs={{0,192},{8,200},{16,208},{24,216},{32,224},{40,232},{48,240},{56,2... | collective-permute-start | bytes 147464 | tf_op jit(solution)/shard_map/ppermute | solution.py:34
where the time goes:
time: 159 us; the launch traced here: 157 us
  waiting for transfers between devices  63.6 us (40%)
  starting transfers between devices  55.2 us (35%)
  blocking collectives  16 us (10%)
  Pallas kernels  12.1 us (8%)
  other arithmetic  5.42 us (3%)
  matrix products  4.27 us (3%)
    ppermute x14, waiting for transfers between devices, send_col(): return lax.ppermute(value, 'col', [(z, (z + dz) % NZ) for z in range(NZ)])  46 us
    ppermute x14, starting transfers between devices, send_col(): return lax.ppermute(value, 'col', [(z, (z + dz) % NZ) for z in range(NZ)])  35.6 us
    ppermute x20, starting transfers between devices, send_row(): return lax.ppermute(value, 'row', row_pairs(dx, dy, dc))  19.6 us
    ppermute x20, waiting for transfers between devices, send_row(): return lax.ppermute(value, 'row', row_pairs(dx, dy, dc))  17.6 us
    all_to_all x1, blocking collectives, normalize(): lax.all_to_all(jnp.broadcast_to(stats[None], (NZ,) + stats.shape), 'col',...  16 us
    pallas_call x1, Pallas kernels, partial_normed(): pl.pallas_call(third_kernel, grid=(depth // tile,), in_specs=[pl.BlockSpe...  6.23 us
    pallas_call x1, Pallas kernels, partial_pre(): pl.pallas_call(first_kernel, grid=(width // tile,), in_specs=[pl.BlockSpe...  5.89 us
    dot_general x1, matrix products, per_device(): lax.dot_general(gathered, slopes_all, (((0,), (0,)), ((), ())), preferred...  4.27 us
  transfers between devices with their start and end apart: 34, of which 20 were waited for; matrix products, arithmetic and copies ran while one was open for 3% of the time, Pallas kernels for 0%

commit v1 on v0

v1 whole, which is shorter than its diff:
```python
import jax
import jax.numpy as jnp
from jax import lax
from jax.experimental import pallas as pl
from jax.experimental.pallas import tpu as pltpu
from jax.sharding import PartitionSpec as P

D = 12288
F32, BF16 = jnp.float32, jnp.bfloat16

NX, NY, NC, NZ = 4, 4, 2, 8
GATHER_SHIFT = (0, 2, 3, 1)
SUM_SHIFT = (0, 1, 3, 2)
TOKENS_OWN = 16
TOKENS_Z = 64
TOKENS = 512
HALF = TOKENS // 2
KERNEL_VMEM = 48 << 20


def pairs_of(target):
    pairs = []
    for x in range(NX):
        for y in range(NY):
            for c in range(NC):
                for z in range(NZ):
                    source = ((x * NY + y) * NC + c) * NZ + z
                    tx, ty, tc, tz = target(x, y, c, z)
                    place = ((tx % NX) * NY + ty % NY) * NC + tc % NC
                    pairs.append((source, place * NZ + tz % NZ))
    return pairs


def send(value, target):
    return lax.ppermute(value, ("row", "col"), pairs_of(target))


def send_x(value, shift):
    return send(value, lambda x, y, c, z: (x + shift, y, c, z))


def send_y(value, shift):
    return send(value, lambda x, y, c, z: (x, y + shift, c, z))


def send_plane(value, shift, x_core):
    return send(
        value,
        lambda x, y, c, z: (x + shift, y, c, z) if c == x_core else (x, y + shift, c, z),
    )


def send_core(value):
    return send(value, lambda x, y, c, z: (x, y, c + 1, z))


def send_ring(value, way):
    return send(value, lambda x, y, c, z: (x, y, c, z + way * (1 - 2 * c)))


def row_of(block):
    row, col = lax.axis_index("row"), lax.axis_index("col")
    own = TOKENS_Z // TOKENS_OWN
    place = ((block // own - col) * (1 - 2 * (row % NC)) + 1 + 2 * NZ) % NZ
    return pl.multiple_of(place * TOKENS_Z + (block % own) * TOKENS_OWN, TOKENS_OWN)


def gathered_row(core_shift, i, p):
    row = lax.axis_index("row")
    x, y, c = row // (NY * NC), (row // NC) % NY, row % NC
    x, y = (x + NX - GATHER_SHIFT[p]) % NX, (y + NY - GATHER_SHIFT[i]) % NY
    return row_of((x * NY + y) * NC + (c + core_shift) % NC)


def summed_row(core_shift, i, p):
    row = lax.axis_index("row")
    x, y, c = row // (NY * NC), (row // NC) % NY, row % NC
    core = (c + core_shift) % NC
    x = (x + jnp.where(core == 1, SUM_SHIFT[i], SUM_SHIFT[p])) % NX
    y = (y + jnp.where(core == 1, SUM_SHIFT[p], SUM_SHIFT[i])) % NY
    return row_of((x * NY + y) * NC + core)


def store_blocks(product, outs):
    for k, out in enumerate(outs):
        out[...] = product[k * TOKENS_Z : (k + 1) * TOKENS_Z, :].astype(out.dtype)


def far_kernel(*refs):
    pieces, w_ref, normed_ref, outs = refs[:8], refs[8], refs[9], refs[10:]

    @pl.when(pl.program_id(0) == 0)
    def _():
        for core_shift in range(2):
            for i in range(4):
                for p in range(4):
                    rows = pl.ds(gathered_row(core_shift, i, p), TOKENS_OWN)
                    normed_ref[rows, :] = pieces[core_shift * 4 + i][
                        p * TOKENS_OWN : (p + 1) * TOKENS_OWN, :
                    ]

    store_blocks(
        jnp.dot(normed_ref[HALF:, :], w_ref[...], preferred_element_type=F32), outs
    )


def near_kernel(normed_ref, w_ref, *outs):
    store_blocks(jnp.dot(normed_ref[...], w_ref[...], preferred_element_type=F32), outs)


def whole(shape):
    return pl.BlockSpec(shape, lambda j: (0, 0))


def settings(depth, width):
    return dict(
        compiler_params=pltpu.CompilerParams(vmem_limit_bytes=KERNEL_VMEM),
        cost_estimate=pl.CostEstimate(
            flops=TOKENS * depth * width, bytes_accessed=depth * width * 2, transcendentals=0
        ),
    )


def far_pre(pieces, weight, tile):
    depth, width = weight.shape
    return pl.pallas_call(
        far_kernel,
        grid=(width // tile,),
        in_specs=[whole(v.shape) for v in pieces] + [pl.BlockSpec((depth, tile), lambda j: (0, j))],
        out_specs=[whole((TOKENS, depth))]
        + [pl.BlockSpec((TOKENS_Z, tile), lambda j: (0, j))] * (NZ // 2),
        out_shape=[jax.ShapeDtypeStruct((TOKENS, depth), BF16)]
        + [jax.ShapeDtypeStruct((TOKENS_Z, width), BF16)] * (NZ // 2),
        **settings(depth, width),
    )(*pieces, weight)


def near_pre(normed, weight, tile):
    depth, width = weight.shape
    return pl.pallas_call(
        near_kernel,
        grid=(width // tile,),
        in_specs=[whole((HALF, depth)), pl.BlockSpec((depth, tile), lambda j: (0, j))],
        out_specs=[pl.BlockSpec((TOKENS_Z, tile), lambda j: (0, j))] * (NZ // 2),
        out_shape=[jax.ShapeDtypeStruct((TOKENS_Z, width), BF16)] * (NZ // 2),
        **settings(depth, width),
    )(normed, weight)


def transposed_dot(rows, weight):
    return lax.dot_general(rows, weight, (((1,), (1,)), ((), ())), preferred_element_type=F32)


def near_back_kernel(*refs):
    pieces, w_ref, out_ref, rows = refs[:4], refs[4], refs[5], refs[6]

    @pl.when(pl.program_id(0) == 0)
    def _():
        for k in range(4):
            rows[k * TOKENS_Z : (k + 1) * TOKENS_Z, :] = pieces[k][...]

    out_ref[...] = transposed_dot(rows[...], w_ref[...]).astype(out_ref.dtype)


def near_back(pieces, weight, tile):
    depth, width = weight.shape
    return pl.pallas_call(
        near_back_kernel,
        grid=(depth // tile,),
        in_specs=[whole(v.shape) for v in pieces] + [pl.BlockSpec((tile, width), lambda j: (j, 0))],
        out_specs=pl.BlockSpec((HALF, tile), lambda j: (0, j)),
        out_shape=jax.ShapeDtypeStruct((HALF, depth), BF16),
        scratch_shapes=[pltpu.VMEM((HALF, width), BF16)],
        **settings(depth, width),
    )(*pieces, weight)


def far_back_kernel(*refs):
    pieces, near_ref, w_ref, slopes_ref, outs, product = (
        refs[:8], refs[8], refs[9], refs[10], refs[11:19], refs[19]
    )

    @pl.when(pl.program_id(0) == 0)
    def _():
        for k in range(NZ):
            slopes_ref[k * TOKENS_Z : (k + 1) * TOKENS_Z, :] = pieces[k][...]

    product[:HALF, :] = near_ref[...].astype(F32)
    product[HALF:, :] = transposed_dot(slopes_ref[HALF:, :], w_ref[...])
    for core_shift in range(2):
        for i in range(4):
            for p in range(4):
                outs[core_shift * 4 + i][p * TOKENS_OWN : (p + 1) * TOKENS_OWN, :] = product[
                    pl.ds(summed_row(core_shift, i, p), TOKENS_OWN), :
                ].astype(BF16)


def far_back(pieces, near, weight, tile):
    depth, width = weight.shape
    return pl.pallas_call(
        far_back_kernel,
        grid=(depth // tile,),
        in_specs=[whole(v.shape) for v in pieces]
        + [pl.BlockSpec((HALF, tile), lambda j: (0, j))]
        + [pl.BlockSpec((tile, width), lambda j: (j, 0))],
        out_specs=[whole((TOKENS, width))] + [pl.BlockSpec((TOKENS_Z, tile), lambda j: (0, j))] * 8,
        out_shape=[jax.ShapeDtypeStruct((TOKENS, width), BF16)]
        + [jax.ShapeDtypeStruct((TOKENS_Z, depth), BF16)] * 8,
        scratch_shapes=[pltpu.VMEM((TOKENS, tile), F32)],
        **settings(depth, width),
    )(*pieces, near, weight)


def gelu_tanh(value):
    return jax.nn.gelu(value, approximate=True)


def add(*values):
    total = values[0].astype(F32)
    for value in values[1:]:
        total = total + value.astype(F32)
    return total


def normalize(inputs, gain, bias):
    local = inputs.shape[1]
    local_mean = jnp.sum(inputs, axis=1) / local
    centered = inputs - local_mean[:, None]
    local_square = jnp.sum(centered * centered, axis=1)
    stats = jnp.stack([local_mean, local_square])
    every = lax.all_to_all(jnp.broadcast_to(stats[None], (NZ,) + stats.shape), "col", 0, 0)
    mean = jnp.mean(every[:, 0, :], axis=0)
    offset = every[:, 0, :] - mean[None, :]
    spread = (jnp.sum(every[:, 1, :], axis=0) + local * jnp.sum(offset * offset, axis=0)) / D
    scale = lax.rsqrt(spread + 1e-05)
    moved = centered + (local_mean - mean)[:, None]
    return (moved * scale[:, None] * gain[None, :] + bias[None, :]).astype(BF16)


def reduce_chain(parts, way):
    travelling = send_ring(parts[0], way)
    for part in parts[1:]:
        travelling = send_ring(add(part, travelling).astype(BF16), way)
    return travelling


def gather_chain(own, way, count):
    got = []
    for _ in range(count):
        own = send_ring(own, way)
        got.append(own)
    return got


def per_device(inputs, gain, bias, weight, d_act):
    normed = normalize(inputs, gain, bias)

    along_x = jnp.concatenate([normed] + [send_x(normed, s) for s in GATHER_SHIFT[1:]])
    along_y = [along_x] + [send_y(along_x, s) for s in GATHER_SHIFT[1:]]
    other = [send_core(v) for v in along_y]

    gathered, *far = far_pre(along_y + other, weight, 512)
    back, own, one, two = near_pre(gathered, weight, 512)
    forward = reduce_chain([far[1], far[0], two, one], 1)
    backward = reduce_chain([far[2], far[3], back], -1)

    result, pullback = jax.vjp(gelu_tanh, add(own, forward, backward))
    activated = result.astype(BF16)
    slopes = pullback(d_act.astype(F32))[0].astype(BF16)
    behind = gather_chain(slopes, 1, 4)
    ahead = gather_chain(slopes, -1, 3)
    pieces = [behind[0], slopes] + ahead + behind[:0:-1]

    near = near_back(pieces[:4], weight, 512)
    slopes_all, *parts = far_back(pieces, near, weight, 512)
    d_weight = lax.dot_general(
        gathered, slopes_all, (((0,), (0,)), ((), ())), preferred_element_type=F32
    ).astype(BF16)

    sums = [add(parts[i], send_core(parts[4 + i])) for i in range(4)]
    arrived = [send_plane(sums[i].astype(BF16), SUM_SHIFT[i], 1) for i in range(1, 4)]
    line = add(sums[0], *arrived)
    line, d_weight = lax.optimization_barrier((line, d_weight))
    blocks = [line[i * TOKENS_OWN : (i + 1) * TOKENS_OWN] for i in range(4)]
    arrived = [send_plane(blocks[i].astype(BF16), SUM_SHIFT[i], 0) for i in range(1, 4)]
    d_normed = add(blocks[0], *arrived).astype(BF16)
    return (activated, d_normed, d_weight)


def solution(mesh):
    return jax.shard_map(
        per_device,
        mesh=mesh,
        in_specs=(P("row", "col"), P("col"), P("col"), P("col", "row"), P("col", "row")),
        out_specs=(P("col", "row"), P("row", "col"), P("col", "row")),
        check_vma=False,
    )
```

time: 159 us -> 132 us (0.83)
  waiting for transfers between devices: 63.6 us -> 44.3 us
  starting transfers between devices: 55.2 us -> 43.2 us
  Pallas kernels: 12.1 us -> 17.6 us
    ppermute x34, waiting for transfers between devices: 63.6 us -> 44.3 us  [send(): return lax.ppermute(value, ('row', 'col'), pairs_of(target))]
    ppermute x34, starting transfers between devices: 55.2 us -> 43.2 us  [send(): return lax.ppermute(value, ('row', 'col'), pairs_of(target))]
    pallas_call x2 -> x4, Pallas kernels: 12.1 us -> 17.6 us  [the longest x1 5.27 us: far_back(): pl.pallas_call(far_back_kernel, grid=(depth // tile,), in_specs=[whole(v....]
  transfers between devices with their start and end apart: 34 -> 34, of which waited for: 20 -> 23; matrix products, arithmetic and copies ran while one was open for 3% -> 4% of each run, Pallas kernels for 0% -> 6%
where the time goes in v1:
time: 132 us
  waiting for transfers between devices  44.3 us (34%)
  starting transfers between devices  43.2 us (33%)
  Pallas kernels  17.6 us (13%)
  blocking collectives  16 us (12%)
  other arithmetic  5.43 us (4%)
  matrix products  4.27 us (3%)
    ppermute x34, waiting for transfers between devices, send(): return lax.ppermute(value, ('row', 'col'), pairs_of(target))  44.3 us
    ppermute x34, starting transfers between devices, send(): return lax.ppermute(value, ('row', 'col'), pairs_of(target))  43.2 us
    all_to_all x1, blocking collectives, normalize(): lax.all_to_all(jnp.broadcast_to(stats[None], (NZ,) + stats.shape), 'col',...  16 us
    pallas_call x1, Pallas kernels, far_back(): pl.pallas_call(far_back_kernel, grid=(depth // tile,), in_specs=[whole(v....  5.27 us
    dot_general x1, matrix products, per_device(): lax.dot_general(gathered, slopes_all, (((0,), (0,)), ((), ())), preferred...  4.27 us
    pallas_call x1, Pallas kernels, far_pre(): pl.pallas_call(far_kernel, grid=(width // tile,), in_specs=[whole(v.shape...  4.25 us
    pallas_call x1, Pallas kernels, near_back(): pl.pallas_call(near_back_kernel, grid=(depth // tile,), in_specs=[whole(v...  4.1 us
    pallas_call x1, Pallas kernels, near_pre(): pl.pallas_call(near_kernel, grid=(width // tile,), in_specs=[whole((HALF,...  4.02 us
  transfers between devices with their start and end apart: 34, of which 23 were waited for; matrix products, arithmetic and copies ran while one was open for 4% of the time, Pallas kernels for 6%

profile of v1, /device:TPU:2, one launch (start us, length us, event | category | flops | bytes accessed | tf_op | source)
XLA Modules:
  0.0 131.6 jit_solution(3556303375240962787)
XLA Ops:
  0.6 1.0 reduce_sum.45
  1.7 1.1 multiply_reduce_fusion
  2.8 16.0 %all_to_all.5 = f32[8,2,16]{2,1,0:T(2,128)S(1)} all-to-all(f32[8,2,16]{2,1,0:T(2,128)S(1)} %broadcast_in_dim.2), channel_id=1, replica_groups=mesh['row'=32,'col'=8] {'col'}, dimensions={0} | all-to-all | bytes 2048 | tf_op jit(solution)/shard_map/all_to_all | solution.py:231
  18.8 1.0 add_convert_fusion.9
  19.8 1.6 %collective-permute-start.2 = (bf16[16,1536]{1,0:T(8,128)(2,1)S(1)}, bf16[16,1536]{1,0:T(8,128)(2,1)S(1)}, u32[]{:S(2)}, u32[]{:S(2)}) collective-permute-start(bf16[16,1536]{1,0:T(8,128)(2,1)S(1)} %add_convert_fusion.9), channel_id=1, source_target_pairs={{0,64},{1,65},{2,66},{3,67},{4,68},{5,69},{6,70},{7,71},{8,72},{9,... | collective-permute-start | bytes 147464 | tf_op jit(solution)/shard_map/ppermute | solution.py:35
  21.4 0.5 collective-permute-start.1
  22.0 2.1 %collective-permute-start = (bf16[16,1536]{1,0:T(8,128)(2,1)S(1)}, bf16[16,1536]{1,0:T(8,128)(2,1)S(1)}, u32[]{:S(2)}, u32[]{:S(2)}) collective-permute-start(bf16[16,1536]{1,0:T(8,128)(2,1)S(1)} %add_convert_fusion.9), channel_id=1, source_target_pairs={{0,128},{1,129},{2,130},{3,131},{4,132},{5,133},{6,134},{7,135},{8... | collective-permute-start | bytes 147464 | tf_op jit(solution)/shard_map/ppermute | solution.py:35
  24.1 0.1 collective-permute-done.2
  24.2 1.3 %collective-permute-done.1 = bf16[16,1536]{1,0:T(8,128)(2,1)S(1)} collective-permute-done((bf16[16,1536]{1,0:T(8,128)(2,1)S(1)}, bf16[16,1536]{1,0:T(8,128)(2,1)S(1)}, u32[]{:S(2)}, u32[]{:S(2)}) %collective-permute-start.1) | collective-permute-done | bytes 49184 | tf_op jit(solution)/shard_map/ppermute | solution.py:35
  25.5 2.0 %collective-permute-done = bf16[16,1536]{1,0:T(8,128)(2,1)S(1)} collective-permute-done((bf16[16,1536]{1,0:T(8,128)(2,1)S(1)}, bf16[16,1536]{1,0:T(8,128)(2,1)S(1)}, u32[]{:S(2)}, u32[]{:S(2)}) %collective-permute-start) | collective-permute-done | bytes 49184 | tf_op jit(solution)/shard_map/ppermute | solution.py:35
  27.6 1.7 %collective-permute-start.5 = (bf16[64,1536]{1,0:T(8,128)(2,1)S(1)}, bf16[64,1536]{1,0:T(8,128)(2,1)S(1)}, u32[]{:S(2)}, u32[]{:S(2)}) collective-permute-start(bf16[64,1536]{1,0:T(8,128)(2,1)S(1)} %pad_maximum_fusion.refs_0_), channel_id=1, source_target_pairs={{0,16},{1,17},{2,18},{3,19},{4,20},{5,21},{6,22},{7,23},{8,24},{9,... | collective-permute-start | bytes 589832 | tf_op jit(solution)/shard_map/ppermute | solution.py:35
  29.2 1.7 %collective-permute-start.4 = (bf16[64,1536]{1,0:T(8,128)(2,1)S(1)}, bf16[64,1536]{1,0:T(8,128)(2,1)S(1)}, u32[]{:S(2)}, u32[]{:S(2)}) collective-permute-start(bf16[64,1536]{1,0:T(8,128)(2,1)S(1)} %pad_maximum_fusion.refs_0_), channel_id=1, source_target_pairs={{0,48},{1,49},{2,50},{3,51},{4,52},{5,53},{6,54},{7,55},{8,56},{9,... | collective-permute-start | bytes 589832 | tf_op jit(solution)/shard_map/ppermute | solution.py:35
  30.9 2.0 %collective-permute-start.3 = (bf16[64,1536]{1,0:T(8,128)(2,1)S(1)}, bf16[64,1536]{1,0:T(8,128)(2,1)S(1)}, u32[]{:S(2)}, u32[]{:S(2)}) collective-permute-start(bf16[64,1536]{1,0:T(8,128)(2,1)S(1)} %pad_maximum_fusion.refs_0_), channel_id=1, source_target_pairs={{0,32},{1,33},{2,34},{3,35},{4,36},{5,37},{6,38},{7,39},{8,40},{9,... | collective-permute-start | bytes 589832 | tf_op jit(solution)/shard_map/ppermute | solution.py:35
  32.9 2.8 %collective-permute-done.5.refs_3_ = bf16[64,1536]{1,0:T(8,128)(2,1)S(1)} collective-permute-done((bf16[64,1536]{1,0:T(8,128)(2,1)S(1)}, bf16[64,1536]{1,0:T(8,128)(2,1)S(1)}, u32[]{:S(2)}, u32[]{:S(2)}) %collective-permute-start.5) | collective-permute-done | bytes 196640 | tf_op jit(solution)/shard_map/ppermute | solution.py:35
  35.7 0.0 collective-permute-start.9
  35.7 0.0 collective-permute-done.4.refs_2_
  35.7 0.5 collective-permute-start.8
  36.2 1.8 %collective-permute-done.3.refs_1_ = bf16[64,1536]{1,0:T(8,128)(2,1)S(1)} collective-permute-done((bf16[64,1536]{1,0:T(8,128)(2,1)S(1)}, bf16[64,1536]{1,0:T(8,128)(2,1)S(1)}, u32[]{:S(2)}, u32[]{:S(2)}) %collective-permute-start.3) | collective-permute-done | bytes 196640 | tf_op jit(solution)/shard_map/ppermute | solution.py:35
  38.1 1.4 %collective-permute-done.7.refs_5_ = bf16[64,1536]{1,0:T(8,128)(2,1)S(1)} collective-permute-done((bf16[64,1536]{1,0:T(8,128)(2,1)S(1)}, bf16[64,1536]{1,0:T(8,128)(2,1)S(1)}, u32[]{:S(2)}, u32[]{:S(2)}) %collective-permute-start.7) | collective-permute-done | bytes 196640 | tf_op jit(solution)/shard_map/ppermute | solution.py:35
  39.5 4.2 %shard_map.76 = (bf16[512,1536]{1,0:T(8,128)(2,1)S(1)}, bf16[64,1536]{1,0:T(8,128)(2,1)S(1)}, bf16[64,1536]{1,0:T(8,128)(2,1)S(1)}, bf16[64,1536]{1,0:T(8,128)(2,1)S(1)}, bf16[64,1536]{1,0:T(8,128)(2,1)S(1)}) custom-call(bf16[64,1536]{1,0:T(8,128)(2,1)S(1)} %pad_maximum_fusion.refs_0_, bf16[64,1536]{1,0:T(8,128)(2,1)S(1)} %collective-permute-done.3.refs_1_, ...), custom_call_target="tpu_custom_call" | custom-call | flops 1207959552 | bytes 4718592 | tf_op jit(solution)/shard_map/pallas_call | solution.py:126
  43.8 0.7 collective-permute-start.10
  44.4 2.7 %collective-permute-start.14 = (bf16[64,1536]{1,0:T(8,128)(2,1)S(1)}, bf16[64,1536]{1,0:T(8,128)(2,1)S(1)}, u32[]{:S(2)}, u32[]{:S(2)}) collective-permute-start(bf16[64,1536]{1,0:T(8,128)(2,1)S(1)} %get-tuple-element.31), channel_id=1, source_target_pairs={{0,7},{1,0},{2,1},{3,2},{4,3},{5,4},{6,5},{7,6},{8,9},{9,10},{10,1... | collective-permute-start | bytes 589832 | tf_op jit(solution)/shard_map/ppermute | solution.py:35
  47.1 4.0 %shard_map.77 = (bf16[64,1536]{1,0:T(8,128)(2,1)S(1)}, bf16[64,1536]{1,0:T(8,128)(2,1)S(1)}, bf16[64,1536]{1,0:T(8,128)(2,1)S(1)}, bf16[64,1536]{1,0:T(8,128)(2,1)S(1)}) custom-call(bf16[512,1536]{1,0:T(8,128)(2,1)S(1)} %get-tuple-element.23.normed_ref, bf16[1536,1536]{1,0:T(8,128)(2,1)} %refs_9_.1), custom_call_target="tpu_custom_call" | custom-call | flops 1207959552 | bytes 4718592 | tf_op jit(solution)/shard_map/pallas_call | solution.py:140
  51.1 0.0 copy-start
  51.1 1.2 collective-permute-done.10
  52.3 0.1 collective-permute-start.11
  52.5 3.3 %collective-permute-start.15 = (bf16[64,1536]{1,0:T(8,128)(2,1)S(1)}, bf16[64,1536]{1,0:T(8,128)(2,1)S(1)}, u32[]{:S(2)}, u32[]{:S(2)}) collective-permute-start(bf16[64,1536]{1,0:T(8,128)(2,1)S(1)} %add_convert_fusion.4), channel_id=1, source_target_pairs={{0,7},{1,0},{2,1},{3,2},{4,3},{5,4},{6,5},{7,6},{8,9},{9,10},{10,1... | collective-permute-start | bytes 589832 | tf_op jit(solution)/shard_map/ppermute | solution.py:35
  55.8 4.3 %collective-permute-done.11 = bf16[64,1536]{1,0:T(8,128)(2,1)S(1)} collective-permute-done((bf16[64,1536]{1,0:T(8,128)(2,1)S(1)}, bf16[64,1536]{1,0:T(8,128)(2,1)S(1)}, u32[]{:S(2)}, u32[]{:S(2)}) %collective-permute-start.11) | collective-permute-done | bytes 196640 | tf_op jit(solution)/shard_map/ppermute | solution.py:35
  60.1 0.1 collective-permute-start.12
  60.2 0.4 collective-permute-done.15
  60.7 3.9 %collective-permute-start.16 = (bf16[64,1536]{1,0:T(8,128)(2,1)S(1)}, bf16[64,1536]{1,0:T(8,128)(2,1)S(1)}, u32[]{:S(2)}, u32[]{:S(2)}) collective-permute-start(bf16[64,1536]{1,0:T(8,128)(2,1)S(1)} %add_convert_fusion.3), channel_id=1, source_target_pairs={{0,7},{1,0},{2,1},{3,2},{4,3},{5,4},{6,5},{7,6},{8,9},{9,10},{10,1... | collective-permute-start | bytes 589832 | tf_op jit(solution)/shard_map/ppermute | solution.py:35
  64.6 2.5 %collective-permute-done.12 = bf16[64,1536]{1,0:T(8,128)(2,1)S(1)} collective-permute-done((bf16[64,1536]{1,0:T(8,128)(2,1)S(1)}, bf16[64,1536]{1,0:T(8,128)(2,1)S(1)}, u32[]{:S(2)}, u32[]{:S(2)}) %collective-permute-start.12) | collective-permute-done | bytes 196640 | tf_op jit(solution)/shard_map/ppermute | solution.py:35
  67.2 0.1 collective-permute-start.13
  67.3 1.7 %collective-permute-done.16 = bf16[64,1536]{1,0:T(8,128)(2,1)S(1)} collective-permute-done((bf16[64,1536]{1,0:T(8,128)(2,1)S(1)}, bf16[64,1536]{1,0:T(8,128)(2,1)S(1)}, u32[]{:S(2)}, u32[]{:S(2)}) %collective-permute-start.16) | collective-permute-done | bytes 196640 | tf_op jit(solution)/shard_map/ppermute | solution.py:35
  69.0 5.1 %collective-permute-done.13 = bf16[64,1536]{1,0:T(8,128)(2,1)S(1)} collective-permute-done((bf16[64,1536]{1,0:T(8,128)(2,1)S(1)}, bf16[64,1536]{1,0:T(8,128)(2,1)S(1)}, u32[]{:S(2)}, u32[]{:S(2)}) %collective-permute-start.13) | collective-permute-done | bytes 196640 | tf_op jit(solution)/shard_map/ppermute | solution.py:35
  74.2 1.0 fusion.2
  75.2 3.2 %collective-permute-start.18 = (bf16[64,1536]{1,0:T(8,128)(2,1)S(1)}, bf16[64,1536]{1,0:T(8,128)(2,1)S(1)}, u32[]{:S(2)}, u32[]{:S(2)}) collective-permute-start(bf16[64,1536]{1,0:T(8,128)(2,1)S(1)} %get-tuple-element.43.refs_1_), channel_id=1, source_target_pairs={{0,7},{1,0},{2,1},{3,2},{4,3},{5,4},{6,5},{7,6},{8,9},{9,10},{10,1... | collective-permute-start | bytes 589832 | tf_op jit(solution)/shard_map/ppermute | solution.py:35
  78.4 3.6 %collective-permute-done.17.refs_0_ = bf16[64,1536]{1,0:T(8,128)(2,1)S(1)} collective-permute-done((bf16[64,1536]{1,0:T(8,128)(2,1)S(1)}, bf16[64,1536]{1,0:T(8,128)(2,1)S(1)}, u32[]{:S(2)}, u32[]{:S(2)}) %collective-permute-start.17) | collective-permute-done | bytes 196640 | tf_op jit(solution)/shard_map/ppermute | solution.py:35
  82.1 1.0 collective-permute-done.18.refs_2_
  83.1 3.7 %collective-permute-start.19 = (bf16[64,1536]{1,0:T(8,128)(2,1)S(1)}, bf16[64,1536]{1,0:T(8,128)(2,1)S(1)}, u32[]{:S(2)}, u32[]{:S(2)}) collective-permute-start(bf16[64,1536]{1,0:T(8,128)(2,1)S(1)} %collective-permute-done.18.refs_2_), channel_id=1, source_target_pairs={{0,7},{1,0},{2,1},{3,2},{4,3},{5,4},{6,5},{7,6},{8,9},{9,10},{10,1... | collective-permute-start | bytes 589832 | tf_op jit(solution)/shard_map/ppermute | solution.py:35
  86.8 2.2 %collective-permute-done.21.refs_7_ = bf16[64,1536]{1,0:T(8,128)(2,1)S(1)} collective-permute-done((bf16[64,1536]{1,0:T(8,128)(2,1)S(1)}, bf16[64,1536]{1,0:T(8,128)(2,1)S(1)}, u32[]{:S(2)}, u32[]{:S(2)}) %collective-permute-start.21) | collective-permute-done | bytes 196640 | tf_op jit(solution)/shard_map/ppermute | solution.py:35
  89.0 1.6 %collective-permute-done.19.refs_3_ = bf16[64,1536]{1,0:T(8,128)(2,1)S(1)} collective-permute-done((bf16[64,1536]{1,0:T(8,128)(2,1)S(1)}, bf16[64,1536]{1,0:T(8,128)(2,1)S(1)}, u32[]{:S(2)}, u32[]{:S(2)}) %collective-permute-start.19) | collective-permute-done | bytes 196640 | tf_op jit(solution)/shard_map/ppermute | solution.py:35
  90.6 3.7 %collective-permute-start.20 = (bf16[64,1536]{1,0:T(8,128)(2,1)S(1)}, bf16[64,1536]{1,0:T(8,128)(2,1)S(1)}, u32[]{:S(2)}, u32[]{:S(2)}) collective-permute-start(bf16[64,1536]{1,0:T(8,128)(2,1)S(1)} %collective-permute-done.19.refs_3_), channel_id=1, source_target_pairs={{0,7},{1,0},{2,1},{3,2},{4,3},{5,4},{6,5},{7,6},{8,9},{9,10},{10,1... | collective-permute-start | bytes 589832 | tf_op jit(solution)/shard_map/ppermute | solution.py:35
  94.3 1.6 %collective-permute-done.22.refs_6_ = bf16[64,1536]{1,0:T(8,128)(2,1)S(1)} collective-permute-done((bf16[64,1536]{1,0:T(8,128)(2,1)S(1)}, bf16[64,1536]{1,0:T(8,128)(2,1)S(1)}, u32[]{:S(2)}, u32[]{:S(2)}) %collective-permute-start.22) | collective-permute-done | bytes 196640 | tf_op jit(solution)/shard_map/ppermute | solution.py:35
  95.9 4.1 %shard_map.78.refs_8_ = bf16[256,1536]{1,0:T(8,128)(2,1)S(1)} custom-call(bf16[64,1536]{1,0:T(8,128)(2,1)S(1)} %collective-permute-done.17.refs_0_, bf16[64,1536]{1,0:T(8,128)(2,1)S(1)} %get-tuple-element.43.refs_1_, bf16[64,1536]{1,0:T(8,128)(2,1)S(1)} %collective-permute-done.18.refs_2_, bf16[64,1536]{1,0:T(8,128)(2,1)S(1)} %collective-permute-done.19.refs_3_, ...), custom_call_target="tpu_custom_call" | custom-call | flops 1207959552 | bytes 4718592 | tf_op jit(solution)/shard_map/pallas_call | solution.py:167
  100.0 2.8 %collective-permute-done.23.refs_5_ = bf16[64,1536]{1,0:T(8,128)(2,1)S(1)} collective-permute-done((bf16[64,1536]{1,0:T(8,128)(2,1)S(1)}, bf16[64,1536]{1,0:T(8,128)(2,1)S(1)}, u32[]{:S(2)}, u32[]{:S(2)}) %collective-permute-start.23) | collective-permute-done | bytes 196640 | tf_op jit(solution)/shard_map/ppermute | solution.py:35
  102.7 5.3 %shard_map.79 = (bf16[512,1536]{1,0:T(8,128)(2,1)S(1)}, bf16[64,1536]{1,0:T(8,128)(2,1)S(1)}, bf16[64,1536]{1,0:T(8,128)(2,1)S(1)}, bf16[64,1536]{1,0:T(8,128)(2...) custom-call(bf16[64,1536]{1,0:T(8,128)(2,1)S(1)} %collective-permute, ...), custom_call_target="tpu_custom_call" | custom-call | flops 1207959552 | bytes 4718592 | tf_op jit(solution)/shard_map/pallas_call | solution.py:200
  108.0 0.1 collective-permute-start.25
  108.1 0.5 collective-permute-start.24
  108.6 0.1 collective-permute-start.27
  108.7 0.4 collective-permute-start.29
  109.1 0.4 collective-permute-done.25
  109.6 1.3 collective-permute-start.26
  110.9 2.3 %collective-permute-start.28 = (bf16[64,1536]{1,0:T(8,128)(2,1)S(1)}, bf16[64,1536]{1,0:T(8,128)(2,1)S(1)}, u32[]{:S(2)}, u32[]{:S(2)}) collective-permute-start(bf16[64,1536]{1,0:T(8,128)(2,1)S(1)} %add_convert_fusion.1), channel_id=1, source_target_pairs={{0,48},{1,49},{2,50},{3,51},{4,52},{5,53},{6,54},{7,55},{8,200},{9... | collective-permute-start | bytes 589832 | tf_op jit(solution)/shard_map/ppermute | solution.py:35
  113.3 0.8 collective-permute-start.30
  114.1 4.3 %convolution_convert_fusion = bf16[1536,1536]{1,0:T(8,128)(2,1)} fusion(bf16[512,1536]{1,0:T(8,128)(2,1)S(1)} %get-tuple-element.23.normed_ref, bf16[512,1536]{1,0:T(8,128)(2,1)S(1)} %get-tuple-element.40), kind=kOutput, calls=%fused_computation | convolution fusion | flops 2418278400 | bytes 7864320 | tf_op jit(solution)/shard_map/dot_general | solution.py:276
  118.4 0.2 collective-permute-done.28
  118.6 2.0 %collective-permute-done.30 = bf16[64,1536]{1,0:T(8,128)(2,1)S(1)} collective-permute-done((bf16[64,1536]{1,0:T(8,128)(2,1)S(1)}, bf16[64,1536]{1,0:T(8,128)(2,1)S(1)}, u32[]{:S(2)}, u32[]{:S(2)}) %collective-permute-start.30) | collective-permute-done | bytes 196640 | tf_op jit(solution)/shard_map/ppermute | solution.py:35
  120.6 0.1 convert_add_fusion
  120.7 1.6 %collective-permute-start.31 = (bf16[16,1536]{1,0:T(8,128)(2,1)S(1)}, bf16[16,1536]{1,0:T(8,128)(2,1)S(1)}, u32[]{:S(2)}, u32[]{:S(2)}) collective-permute-start(bf16[16,1536]{1,0:T(8,128)(2,1)S(1)} %get-tuple-element.45), channel_id=1, source_target_pairs={{0,64},{1,65},{2,66},{3,67},{4,68},{5,69},{6,70},{7,71},{8,24},{9,... | collective-permute-start | bytes 147464 | tf_op jit(solution)/shard_map/ppermute | solution.py:35
  122.3 4.6 %collective-permute-start.33 = (bf16[16,1536]{1,0:T(8,128)(2,1)S(1)}, bf16[16,1536]{1,0:T(8,128)(2,1)S(1)}, u32[]{:S(2)}, u32[]{:S(2)}) collective-permute-start(bf16[16,1536]{1,0:T(8,128)(2,1)S(1)} %get-tuple-element.46), channel_id=1, source_target_pairs={{0,128},{1,129},{2,130},{3,131},{4,132},{5,133},{6,134},{7,135},{8... | collective-permute-start | bytes 147464 | tf_op jit(solution)/shard_map/ppermute | solution.py:35
  126.9 2.1 %collective-permute-done.33 = bf16[16,1536]{1,0:T(8,128)(2,1)S(1)} collective-permute-done((bf16[16,1536]{1,0:T(8,128)(2,1)S(1)}, bf16[16,1536]{1,0:T(8,128)(2,1)S(1)}, u32[]{:S(2)}, u32[]{:S(2)}) %collective-permute-start.33) | collective-permute-done | bytes 49184 | tf_op jit(solution)/shard_map/ppermute | solution.py:35
  129.0 2.0 %collective-permute-done.32 = bf16[16,1536]{1,0:T(8,128)(2,1)S(1)} collective-permute-done((bf16[16,1536]{1,0:T(8,128)(2,1)S(1)}, bf16[16,1536]{1,0:T(8,128)(2,1)S(1)}, u32[]{:S(2)}, u32[]{:S(2)}) %collective-permute-start.32) | collective-permute-done | bytes 49184 | tf_op jit(solution)/shard_map/ppermute | solution.py:35
  131.0 0.6 add_convert_fusion.8
  (37 shorter events, 0.6 us)
Async XLA Ops:
  19.8 4.3 %collective-permute-start.2 = (bf16[16,1536]{1,0:T(8,128)(2,1)S(1)}, bf16[16,1536]{1,0:T(8,128)(2,1)S(1)}, u32[]{:S(2)}, u32[]{:S(2)}) collective-permute-start(bf16[16,1536]{1,0:T(8,128)(2,1)S(1)} %add_convert_fusion.9), channel_id=1, source_target_pairs={{0,64},{1,65},{2,66},{3,67},{4,68},{5,69},{6,70},{7,71},{8,72},{9,... | collective-permute-start | bytes 147464 | tf_op jit(solution)/shard_map/ppermute | solution.py:35
  21.4 4.1 %collective-permute-start.1 = (bf16[16,1536]{1,0:T(8,128)(2,1)S(1)}, bf16[16,1536]{1,0:T(8,128)(2,1)S(1)}, u32[]{:S(2)}, u32[]{:S(2)}) collective-permute-start(bf16[16,1536]{1,0:T(8,128)(2,1)S(1)} %add_convert_fusion.9), channel_id=1, source_target_pairs={{0,192},{1,193},{2,194},{3,195},{4,196},{5,197},{6,198},{7,199},{8... | collective-permute-start | bytes 147464 | tf_op jit(solution)/shard_map/ppermute | solution.py:35
  22.0 5.6 %collective-permute-start = (bf16[16,1536]{1,0:T(8,128)(2,1)S(1)}, bf16[16,1536]{1,0:T(8,128)(2,1)S(1)}, u32[]{:S(2)}, u32[]{:S(2)}) collective-permute-start(bf16[16,1536]{1,0:T(8,128)(2,1)S(1)} %add_convert_fusion.9), channel_id=1, source_target_pairs={{0,128},{1,129},{2,130},{3,131},{4,132},{5,133},{6,134},{7,135},{8... | collective-permute-start | bytes 147464 | tf_op jit(solution)/shard_map/ppermute | solution.py:35
  27.6 8.1 %collective-permute-start.5 = (bf16[64,1536]{1,0:T(8,128)(2,1)S(1)}, bf16[64,1536]{1,0:T(8,128)(2,1)S(1)}, u32[]{:S(2)}, u32[]{:S(2)}) collective-permute-start(bf16[64,1536]{1,0:T(8,128)(2,1)S(1)} %pad_maximum_fusion.refs_0_), channel_id=1, source_target_pairs={{0,16},{1,17},{2,18},{3,19},{4,20},{5,21},{6,22},{7,23},{8,24},{9,... | collective-permute-start | bytes 589832 | tf_op jit(solution)/shard_map/ppermute | solution.py:35
  29.2 6.5 %collective-permute-start.4 = (bf16[64,1536]{1,0:T(8,128)(2,1)S(1)}, bf16[64,1536]{1,0:T(8,128)(2,1)S(1)}, u32[]{:S(2)}, u32[]{:S(2)}) collective-permute-start(bf16[64,1536]{1,0:T(8,128)(2,1)S(1)} %pad_maximum_fusion.refs_0_), channel_id=1, source_target_pairs={{0,48},{1,49},{2,50},{3,51},{4,52},{5,53},{6,54},{7,55},{8,56},{9,... | collective-permute-start | bytes 589832 | tf_op jit(solution)/shard_map/ppermute | solution.py:35
  30.9 7.2 %collective-permute-start.3 = (bf16[64,1536]{1,0:T(8,128)(2,1)S(1)}, bf16[64,1536]{1,0:T(8,128)(2,1)S(1)}, u32[]{:S(2)}, u32[]{:S(2)}) collective-permute-start(bf16[64,1536]{1,0:T(8,128)(2,1)S(1)} %pad_maximum_fusion.refs_0_), channel_id=1, source_target_pairs={{0,32},{1,33},{2,34},{3,35},{4,36},{5,37},{6,38},{7,39},{8,40},{9,... | collective-permute-start | bytes 589832 | tf_op jit(solution)/shard_map/ppermute | solution.py:35
  32.9 5.2 %collective-permute-start.6 = (bf16[64,1536]{1,0:T(8,128)(2,1)S(1)}, bf16[64,1536]{1,0:T(8,128)(2,1)S(1)}, u32[]{:S(2)}, u32[]{:S(2)}) collective-permute-start(bf16[64,1536]{1,0:T(8,128)(2,1)S(1)} %pad_maximum_fusion.refs_0_), channel_id=1, source_target_pairs={{0,8},{1,9},{2,10},{3,11},{4,12},{5,13},{6,14},{7,15},{8,0},{9,1},... | collective-permute-start | bytes 589832 | tf_op jit(solution)/shard_map/ppermute | solution.py:35
  35.7 2.4 %collective-permute-start.9 = (bf16[64,1536]{1,0:T(8,128)(2,1)S(1)}, bf16[64,1536]{1,0:T(8,128)(2,1)S(1)}, u32[]{:S(2)}, u32[]{:S(2)}) collective-permute-start(bf16[64,1536]{1,0:T(8,128)(2,1)S(1)} %collective-permute-done.5.refs_3_), channel_id=1, source_target_pairs={{0,8},{1,9},{2,10},{3,11},{4,12},{5,13},{6,14},{7,15},{8,0},{9,1},... | collective-permute-start | bytes 589832 | tf_op jit(solution)/shard_map/ppermute | solution.py:35
  35.7 2.4 %collective-permute-start.8 = (bf16[64,1536]{1,0:T(8,128)(2,1)S(1)}, bf16[64,1536]{1,0:T(8,128)(2,1)S(1)}, u32[]{:S(2)}, u32[]{:S(2)}) collective-permute-start(bf16[64,1536]{1,0:T(8,128)(2,1)S(1)} %collective-permute-done.4.refs_2_), channel_id=1, source_target_pairs={{0,8},{1,9},{2,10},{3,11},{4,12},{5,13},{6,14},{7,15},{8,0},{9,1},... | collective-permute-start | bytes 589832 | tf_op jit(solution)/shard_map/ppermute | solution.py:35
  38.1 1.4 %collective-permute-start.7 = (bf16[64,1536]{1,0:T(8,128)(2,1)S(1)}, bf16[64,1536]{1,0:T(8,128)(2,1)S(1)}, u32[]{:S(2)}, u32[]{:S(2)}) collective-permute-start(bf16[64,1536]{1,0:T(8,128)(2,1)S(1)} %collective-permute-done.3.refs_1_), channel_id=1, source_target_pairs={{0,8},{1,9},{2,10},{3,11},{4,12},{5,13},{6,14},{7,15},{8,0},{9,1},... | collective-permute-start | bytes 589832 | tf_op jit(solution)/shard_map/ppermute | solution.py:35
  43.8 8.5 %collective-permute-start.10 = (bf16[64,1536]{1,0:T(8,128)(2,1)S(1)}, bf16[64,1536]{1,0:T(8,128)(2,1)S(1)}, u32[]{:S(2)}, u32[]{:S(2)}) collective-permute-start(bf16[64,1536]{1,0:T(8,128)(2,1)S(1)} %get-tuple-element.28), channel_id=1, source_target_pairs={{0,1},{1,2},{2,3},{3,4},{4,5},{5,6},{6,7},{7,0},{8,15},{9,8},{10,9... | collective-permute-start | bytes 589832 | tf_op jit(solution)/shard_map/ppermute | solution.py:35
  44.4 8.0 %collective-permute-start.14 = (bf16[64,1536]{1,0:T(8,128)(2,1)S(1)}, bf16[64,1536]{1,0:T(8,128)(2,1)S(1)}, u32[]{:S(2)}, u32[]{:S(2)}) collective-permute-start(bf16[64,1536]{1,0:T(8,128)(2,1)S(1)} %get-tuple-element.31), channel_id=1, source_target_pairs={{0,7},{1,0},{2,1},{3,2},{4,3},{5,4},{6,5},{7,6},{8,9},{9,10},{10,1... | collective-permute-start | bytes 589832 | tf_op jit(solution)/shard_map/ppermute | solution.py:35
  51.1 23.1 %copy-start = (bf16[64,1536]{1,0:T(8,128)(2,1)S(1)}, bf16[64,1536]{1,0:T(8,128)(2,1)}, u32[]{:S(2)}) copy-start(bf16[64,1536]{1,0:T(8,128)(2,1)} %param.9) | copy-start | bytes 589828
  52.3 7.7 %collective-permute-start.11 = (bf16[64,1536]{1,0:T(8,128)(2,1)S(1)}, bf16[64,1536]{1,0:T(8,128)(2,1)S(1)}, u32[]{:S(2)}, u32[]{:S(2)}) collective-permute-start(bf16[64,1536]{1,0:T(8,128)(2,1)S(1)} %add_convert_fusion.7), channel_id=1, source_target_pairs={{0,1},{1,2},{2,3},{3,4},{4,5},{5,6},{6,7},{7,0},{8,15},{9,8},{10,9... | collective-permute-start | bytes 589832 | tf_op jit(solution)/shard_map/ppermute | solution.py:35
  52.5 8.1 %collective-permute-start.15 = (bf16[64,1536]{1,0:T(8,128)(2,1)S(1)}, bf16[64,1536]{1,0:T(8,128)(2,1)S(1)}, u32[]{:S(2)}, u32[]{:S(2)}) collective-permute-start(bf16[64,1536]{1,0:T(8,128)(2,1)S(1)} %add_convert_fusion.4), channel_id=1, source_target_pairs={{0,7},{1,0},{2,1},{3,2},{4,3},{5,4},{6,5},{7,6},{8,9},{9,10},{10,1... | collective-permute-start | bytes 589832 | tf_op jit(solution)/shard_map/ppermute | solution.py:35
  60.1 7.0 %collective-permute-start.12 = (bf16[64,1536]{1,0:T(8,128)(2,1)S(1)}, bf16[64,1536]{1,0:T(8,128)(2,1)S(1)}, u32[]{:S(2)}, u32[]{:S(2)}) collective-permute-start(bf16[64,1536]{1,0:T(8,128)(2,1)S(1)} %add_convert_fusion.6), channel_id=1, source_target_pairs={{0,1},{1,2},{2,3},{3,4},{4,5},{5,6},{6,7},{7,0},{8,15},{9,8},{10,9... | collective-permute-start | bytes 589832 | tf_op jit(solution)/shard_map/ppermute | solution.py:35
  60.7 8.4 %collective-permute-start.16 = (bf16[64,1536]{1,0:T(8,128)(2,1)S(1)}, bf16[64,1536]{1,0:T(8,128)(2,1)S(1)}, u32[]{:S(2)}, u32[]{:S(2)}) collective-permute-start(bf16[64,1536]{1,0:T(8,128)(2,1)S(1)} %add_convert_fusion.3), channel_id=1, source_target_pairs={{0,7},{1,0},{2,1},{3,2},{4,3},{5,4},{6,5},{7,6},{8,9},{9,10},{10,1... | collective-permute-start | bytes 589832 | tf_op jit(solution)/shard_map/ppermute | solution.py:35
  67.2 7.0 %collective-permute-start.13 = (bf16[64,1536]{1,0:T(8,128)(2,1)S(1)}, bf16[64,1536]{1,0:T(8,128)(2,1)S(1)}, u32[]{:S(2)}, u32[]{:S(2)}) collective-permute-start(bf16[64,1536]{1,0:T(8,128)(2,1)S(1)} %add_convert_fusion.5), channel_id=1, source_target_pairs={{0,1},{1,2},{2,3},{3,4},{4,5},{5,6},{6,7},{7,0},{8,15},{9,8},{10,9... | collective-permute-start | bytes 589832 | tf_op jit(solution)/shard_map/ppermute | solution.py:35
  75.2 6.9 %collective-permute-start.17 = (bf16[64,1536]{1,0:T(8,128)(2,1)S(1)}, bf16[64,1536]{1,0:T(8,128)(2,1)S(1)}, u32[]{:S(2)}, u32[]{:S(2)}) collective-permute-start(bf16[64,1536]{1,0:T(8,128)(2,1)S(1)} %get-tuple-element.43.refs_1_), channel_id=1, source_target_pairs={{0,1},{1,2},{2,3},{3,4},{4,5},{5,6},{6,7},{7,0},{8,15},{9,8},{10,9... | collective-permute-start | bytes 589832 | tf_op jit(solution)/shard_map/ppermute | solution.py:35
  75.2 7.9 %collective-permute-start.18 = (bf16[64,1536]{1,0:T(8,128)(2,1)S(1)}, bf16[64,1536]{1,0:T(8,128)(2,1)S(1)}, u32[]{:S(2)}, u32[]{:S(2)}) collective-permute-start(bf16[64,1536]{1,0:T(8,128)(2,1)S(1)} %get-tuple-element.43.refs_1_), channel_id=1, source_target_pairs={{0,7},{1,0},{2,1},{3,2},{4,3},{5,4},{6,5},{7,6},{8,9},{9,10},{10,1... | collective-permute-start | bytes 589832 | tf_op jit(solution)/shard_map/ppermute | solution.py:35
  82.1 6.9 %collective-permute-start.21 = (bf16[64,1536]{1,0:T(8,128)(2,1)S(1)}, bf16[64,1536]{1,0:T(8,128)(2,1)S(1)}, u32[]{:S(2)}, u32[]{:S(2)}) collective-permute-start(bf16[64,1536]{1,0:T(8,128)(2,1)S(1)} %collective-permute-done.17.refs_0_), channel_id=1, source_target_pairs={{0,1},{1,2},{2,3},{3,4},{4,5},{5,6},{6,7},{7,0},{8,15},{9,8},{10,9... | collective-permute-start | bytes 589832 | tf_op jit(solution)/shard_map/ppermute | solution.py:35
  83.1 7.5 %collective-permute-start.19 = (bf16[64,1536]{1,0:T(8,128)(2,1)S(1)}, bf16[64,1536]{1,0:T(8,128)(2,1)S(1)}, u32[]{:S(2)}, u32[]{:S(2)}) collective-permute-start(bf16[64,1536]{1,0:T(8,128)(2,1)S(1)} %collective-permute-done.18.refs_2_), channel_id=1, source_target_pairs={{0,7},{1,0},{2,1},{3,2},{4,3},{5,4},{6,5},{7,6},{8,9},{9,10},{10,1... | collective-permute-start | bytes 589832 | tf_op jit(solution)/shard_map/ppermute | solution.py:35
  89.0 6.9 %collective-permute-start.22 = (bf16[64,1536]{1,0:T(8,128)(2,1)S(1)}, bf16[64,1536]{1,0:T(8,128)(2,1)S(1)}, u32[]{:S(2)}, u32[]{:S(2)}) collective-permute-start(bf16[64,1536]{1,0:T(8,128)(2,1)S(1)} %collective-permute-done.21.refs_7_), channel_id=1, source_target_pairs={{0,1},{1,2},{2,3},{3,4},{4,5},{5,6},{6,7},{7,0},{8,15},{9,8},{10,9... | collective-permute-start | bytes 589832 | tf_op jit(solution)/shard_map/ppermute | solution.py:35
  90.6 9.4 %collective-permute-start.20 = (bf16[64,1536]{1,0:T(8,128)(2,1)S(1)}, bf16[64,1536]{1,0:T(8,128)(2,1)S(1)}, u32[]{:S(2)}, u32[]{:S(2)}) collective-permute-start(bf16[64,1536]{1,0:T(8,128)(2,1)S(1)} %collective-permute-done.19.refs_3_), channel_id=1, source_target_pairs={{0,7},{1,0},{2,1},{3,2},{4,3},{5,4},{6,5},{7,6},{8,9},{9,10},{10,1... | collective-permute-start | bytes 589832 | tf_op jit(solution)/shard_map/ppermute | solution.py:35
  95.9 6.9 %collective-permute-start.23 = (bf16[64,1536]{1,0:T(8,128)(2,1)S(1)}, bf16[64,1536]{1,0:T(8,128)(2,1)S(1)}, u32[]{:S(2)}, u32[]{:S(2)}) collective-permute-start(bf16[64,1536]{1,0:T(8,128)(2,1)S(1)} %collective-permute-done.22.refs_6_), channel_id=1, source_target_pairs={{0,1},{1,2},{2,3},{3,4},{4,5},{5,6},{6,7},{7,0},{8,15},{9,8},{10,9... | collective-permute-start | bytes 589832 | tf_op jit(solution)/shard_map/ppermute | solution.py:35
  108.0 1.5 %collective-permute-start.25 = (bf16[64,1536]{1,0:T(8,128)(2,1)S(1)}, bf16[64,1536]{1,0:T(8,128)(2,1)S(1)}, u32[]{:S(2)}, u32[]{:S(2)}) collective-permute-start(bf16[64,1536]{1,0:T(8,128)(2,1)S(1)} %get-tuple-element.35), channel_id=1, source_target_pairs={{0,8},{1,9},{2,10},{3,11},{4,12},{5,13},{6,14},{7,15},{8,0},{9,1},... | collective-permute-start | bytes 589832 | tf_op jit(solution)/shard_map/ppermute | solution.py:35
  108.1 10.3 %collective-permute-start.24 = (bf16[64,1536]{1,0:T(8,128)(2,1)S(1)}, bf16[64,1536]{1,0:T(8,128)(2,1)S(1)}, u32[]{:S(2)}, u32[]{:S(2)}) collective-permute-start(bf16[64,1536]{1,0:T(8,128)(2,1)S(1)} %get-tuple-element.33), channel_id=1, source_target_pairs={{0,8},{1,9},{2,10},{3,11},{4,12},{5,13},{6,14},{7,15},{8,0},{9,1},... | collective-permute-start | bytes 589832 | tf_op jit(solution)/shard_map/ppermute | solution.py:35
  108.6 2.3 %collective-permute-start.27 = (bf16[64,1536]{1,0:T(8,128)(2,1)S(1)}, bf16[64,1536]{1,0:T(8,128)(2,1)S(1)}, u32[]{:S(2)}, u32[]{:S(2)}) collective-permute-start(bf16[64,1536]{1,0:T(8,128)(2,1)S(1)} %get-tuple-element.37), channel_id=1, source_target_pairs={{0,8},{1,9},{2,10},{3,11},{4,12},{5,13},{6,14},{7,15},{8,0},{9,1},... | collective-permute-start | bytes 589832 | tf_op jit(solution)/shard_map/ppermute | solution.py:35
  108.7 4.6 %collective-permute-start.29 = (bf16[64,1536]{1,0:T(8,128)(2,1)S(1)}, bf16[64,1536]{1,0:T(8,128)(2,1)S(1)}, u32[]{:S(2)}, u32[]{:S(2)}) collective-permute-start(bf16[64,1536]{1,0:T(8,128)(2,1)S(1)} %get-tuple-element.39), channel_id=1, source_target_pairs={{0,8},{1,9},{2,10},{3,11},{4,12},{5,13},{6,14},{7,15},{8,0},{9,1},... | collective-permute-start | bytes 589832 | tf_op jit(solution)/shard_map/ppermute | solution.py:35
  109.6 8.8 %collective-permute-start.26 = (bf16[64,1536]{1,0:T(8,128)(2,1)S(1)}, bf16[64,1536]{1,0:T(8,128)(2,1)S(1)}, u32[]{:S(2)}, u32[]{:S(2)}) collective-permute-start(bf16[64,1536]{1,0:T(8,128)(2,1)S(1)} %add_convert_fusion.2), channel_id=1, source_target_pairs={{0,16},{1,17},{2,18},{3,19},{4,20},{5,21},{6,22},{7,23},{8,72},{9,... | collective-permute-start | bytes 589832 | tf_op jit(solution)/shard_map/ppermute | solution.py:35
  110.9 7.7 %collective-permute-start.28 = (bf16[64,1536]{1,0:T(8,128)(2,1)S(1)}, bf16[64,1536]{1,0:T(8,128)(2,1)S(1)}, u32[]{:S(2)}, u32[]{:S(2)}) collective-permute-start(bf16[64,1536]{1,0:T(8,128)(2,1)S(1)} %add_convert_fusion.1), channel_id=1, source_target_pairs={{0,48},{1,49},{2,50},{3,51},{4,52},{5,53},{6,54},{7,55},{8,200},{9... | collective-permute-start | bytes 589832 | tf_op jit(solution)/shard_map/ppermute | solution.py:35
  113.3 7.3 %collective-permute-start.30 = (bf16[64,1536]{1,0:T(8,128)(2,1)S(1)}, bf16[64,1536]{1,0:T(8,128)(2,1)S(1)}, u32[]{:S(2)}, u32[]{:S(2)}) collective-permute-start(bf16[64,1536]{1,0:T(8,128)(2,1)S(1)} %add_convert_fusion), channel_id=1, source_target_pairs={{0,32},{1,33},{2,34},{3,35},{4,36},{5,37},{6,38},{7,39},{8,136},{9... | collective-permute-start | bytes 589832 | tf_op jit(solution)/shard_map/ppermute | solution.py:35
  120.7 6.1 %collective-permute-start.31 = (bf16[16,1536]{1,0:T(8,128)(2,1)S(1)}, bf16[16,1536]{1,0:T(8,128)(2,1)S(1)}, u32[]{:S(2)}, u32[]{:S(2)}) collective-permute-start(bf16[16,1536]{1,0:T(8,128)(2,1)S(1)} %get-tuple-element.45), channel_id=1, source_target_pairs={{0,64},{1,65},{2,66},{3,67},{4,68},{5,69},{6,70},{7,71},{8,24},{9,... | collective-permute-start | bytes 147464 | tf_op jit(solution)/shard_map/ppermute | solution.py:35
  122.3 6.6 %collective-permute-start.33 = (bf16[16,1536]{1,0:T(8,128)(2,1)S(1)}, bf16[16,1536]{1,0:T(8,128)(2,1)S(1)}, u32[]{:S(2)}, u32[]{:S(2)}) collective-permute-start(bf16[16,1536]{1,0:T(8,128)(2,1)S(1)} %get-tuple-element.46), channel_id=1, source_target_pairs={{0,128},{1,129},{2,130},{3,131},{4,132},{5,133},{6,134},{7,135},{8... | collective-permute-start | bytes 147464 | tf_op jit(solution)/shard_map/ppermute | solution.py:35
  126.9 4.1 %collective-permute-start.32 = (bf16[16,1536]{1,0:T(8,128)(2,1)S(1)}, bf16[16,1536]{1,0:T(8,128)(2,1)S(1)}, u32[]{:S(2)}, u32[]{:S(2)}) collective-permute-start(bf16[16,1536]{1,0:T(8,128)(2,1)S(1)} %get-tuple-element.47), channel_id=1, source_target_pairs={{0,192},{1,193},{2,194},{3,195},{4,196},{5,197},{6,198},{7,199},{8... | collective-permute-start | bytes 147464 | tf_op jit(solution)/shard_map/ppermute | solution.py:35

commit v2 on v1

v2 whole, which is shorter than its diff:
```python
import jax
import jax.numpy as jnp
from jax import lax
from jax.experimental import pallas as pl
from jax.experimental.pallas import tpu as pltpu
from jax.sharding import PartitionSpec as P

D = 12288
F32, BF16 = jnp.float32, jnp.bfloat16

NX, NY, NC, NZ = 4, 4, 2, 8
GATHER_SHIFT = (0, 2, 3, 1)
SUM_SHIFT = (0, 1, 3, 2)
TOKENS_OWN = 16
TOKENS_Z = 64
TOKENS = 512
HALF = TOKENS // 2


def pairs_of(target):
    pairs = []
    for x in range(NX):
        for y in range(NY):
            for c in range(NC):
                for z in range(NZ):
                    source = ((x * NY + y) * NC + c) * NZ + z
                    tx, ty, tc, tz = target(x, y, c, z)
                    place = ((tx % NX) * NY + ty % NY) * NC + tc % NC
                    pairs.append((source, place * NZ + tz % NZ))
    return pairs


def send(value, target):
    return lax.ppermute(value, ("row", "col"), pairs_of(target))


def send_x(value, shift):
    return send(value, lambda x, y, c, z: (x + shift, y, c, z))


def send_y(value, shift):
    return send(value, lambda x, y, c, z: (x, y + shift, c, z))


def send_plane(value, shift, x_core):
    return send(
        value,
        lambda x, y, c, z: (x + shift, y, c, z) if c == x_core else (x, y + shift, c, z),
    )


def send_core(value):
    return send(value, lambda x, y, c, z: (x, y, c + 1, z))


def send_ring(value, way):
    return send(value, lambda x, y, c, z: (x, y, c, z + way * (1 - 2 * ((z + c) % 2))))


def row_of(block):
    row, col = lax.axis_index("row"), lax.axis_index("col")
    own = TOKENS_Z // TOKENS_OWN
    place = ((block // own - col) * (1 - 2 * ((row + col) % 2)) + 1 + 2 * NZ) % NZ
    return pl.multiple_of(place * TOKENS_Z + (block % own) * TOKENS_OWN, TOKENS_OWN)


def gathered_row(core_shift, i, p):
    row = lax.axis_index("row")
    x, y, c = row // (NY * NC), (row // NC) % NY, row % NC
    x, y = (x + NX - GATHER_SHIFT[p]) % NX, (y + NY - GATHER_SHIFT[i]) % NY
    return row_of((x * NY + y) * NC + (c + core_shift) % NC)


def summed_row(core_shift, i, p):
    row = lax.axis_index("row")
    x, y, c = row // (NY * NC), (row // NC) % NY, row % NC
    core = (c + core_shift) % NC
    x = (x + jnp.where(core == 1, SUM_SHIFT[i], SUM_SHIFT[p])) % NX
    y = (y + jnp.where(core == 1, SUM_SHIFT[p], SUM_SHIFT[i])) % NY
    return row_of((x * NY + y) * NC + core)


WHOLE = pl.BlockSpec(memory_space=pltpu.VMEM)
TILE = 512


def settings(weight, limit):
    depth, width = weight.shape
    return dict(
        compiler_params=pltpu.CompilerParams(vmem_limit_bytes=limit << 20),
        cost_estimate=pl.CostEstimate(
            flops=TOKENS * depth * width, bytes_accessed=depth * width * 2, transcendentals=0
        ),
    )


def stage_kernel(w_ref, out_ref, sem):
    copy = pltpu.make_async_copy(w_ref, out_ref, sem)
    copy.start()
    copy.wait()


def stage(weight):
    return pl.pallas_call(
        stage_kernel,
        in_specs=[pl.BlockSpec(memory_space=pl.ANY)],
        out_specs=WHOLE,
        out_shape=jax.ShapeDtypeStruct(weight.shape, weight.dtype),
        scratch_shapes=[pltpu.SemaphoreType.DMA],
        **settings(weight, 48),
    )(weight)


def multiply(rows, w_ref, outs):
    for start in range(0, w_ref.shape[1], TILE):
        columns = slice(start, start + TILE)
        product = jnp.dot(rows, w_ref[:, columns], preferred_element_type=F32)
        for k, out in enumerate(outs):
            out[:, columns] = product[k * TOKENS_Z : (k + 1) * TOKENS_Z, :].astype(out.dtype)


def far_kernel(*refs):
    pieces, w_ref, normed_ref, outs = refs[:8], refs[8], refs[9], refs[10:]
    for core_shift in range(2):
        for i in range(4):
            for p in range(4):
                rows = pl.ds(gathered_row(core_shift, i, p), TOKENS_OWN)
                normed_ref[rows, :] = pieces[core_shift * 4 + i][
                    p * TOKENS_OWN : (p + 1) * TOKENS_OWN, :
                ]
    multiply(normed_ref[HALF:, :], w_ref, outs)


def near_kernel(normed_ref, w_ref, *outs):
    multiply(normed_ref[:HALF, :], w_ref, outs)


def far_pre(pieces, weight):
    depth, width = weight.shape
    return pl.pallas_call(
        far_kernel,
        in_specs=[WHOLE] * 9,
        out_specs=[WHOLE] * 5,
        out_shape=[jax.ShapeDtypeStruct((TOKENS, depth), BF16)]
        + [jax.ShapeDtypeStruct((TOKENS_Z, width), BF16)] * 4,
        **settings(weight, 16),
    )(*pieces, weight)


def near_pre(normed, weight):
    return pl.pallas_call(
        near_kernel,
        in_specs=[WHOLE] * 2,
        out_specs=[WHOLE] * 4,
        out_shape=[jax.ShapeDtypeStruct((TOKENS_Z, weight.shape[1]), BF16)] * 4,
        **settings(weight, 16),
    )(normed, weight)


def transposed_dot(rows, weight):
    return lax.dot_general(rows, weight, (((1,), (1,)), ((), ())), preferred_element_type=F32)


def near_back_kernel(*refs):
    pieces, w_ref, out_ref = refs[:4], refs[4], refs[5]
    rows = jnp.concatenate([piece[...] for piece in pieces], axis=0)
    for start in range(0, w_ref.shape[0], TILE):
        part = slice(start, start + TILE)
        out_ref[:, part] = transposed_dot(rows, w_ref[part, :]).astype(out_ref.dtype)


def near_back(pieces, weight):
    return pl.pallas_call(
        near_back_kernel,
        in_specs=[WHOLE] * 5,
        out_specs=WHOLE,
        out_shape=jax.ShapeDtypeStruct((HALF, weight.shape[0]), BF16),
        **settings(weight, 16),
    )(*pieces, weight)


def far_back_kernel(*refs):
    pieces, near_ref, w_ref, slopes_ref, outs, product = (
        refs[:8], refs[8], refs[9], refs[10], refs[11:19], refs[19]
    )
    for k in range(NZ):
        slopes_ref[k * TOKENS_Z : (k + 1) * TOKENS_Z, :] = pieces[k][...]
    product[:HALF, :] = near_ref[...].astype(F32)
    rows = slopes_ref[HALF:, :]
    for start in range(0, w_ref.shape[0], TILE):
        part = slice(start, start + TILE)
        product[HALF:, part] = transposed_dot(rows, w_ref[part, :])
    for core_shift in (1, 0):
        for i in range(4):
            for p in range(4):
                outs[core_shift * 4 + i][p * TOKENS_OWN : (p + 1) * TOKENS_OWN, :] = product[
                    pl.ds(summed_row(core_shift, i, p), TOKENS_OWN), :
                ].astype(BF16)


def far_back(pieces, near, weight):
    depth, width = weight.shape
    return pl.pallas_call(
        far_back_kernel,
        in_specs=[WHOLE] * 10,
        out_specs=[WHOLE] * 9,
        out_shape=[jax.ShapeDtypeStruct((TOKENS, width), BF16)]
        + [jax.ShapeDtypeStruct((TOKENS_Z, depth), BF16)] * 8,
        scratch_shapes=[pltpu.VMEM((TOKENS, depth), F32)],
        **settings(weight, 16),
    )(*pieces, near, weight)


def gelu_tanh(value):
    return jax.nn.gelu(value, approximate=True)


def add(*values):
    total = values[0].astype(F32)
    for value in values[1:]:
        total = total + value.astype(F32)
    return total


def normalize(inputs, gain, bias):
    local = inputs.shape[1]
    local_mean = jnp.sum(inputs, axis=1) / local
    centered = inputs - local_mean[:, None]
    local_square = jnp.sum(centered * centered, axis=1)
    stats = jnp.stack([local_mean, local_square])
    every = lax.all_to_all(jnp.broadcast_to(stats[None], (NZ,) + stats.shape), "col", 0, 0)
    mean = jnp.mean(every[:, 0, :], axis=0)
    offset = every[:, 0, :] - mean[None, :]
    spread = (jnp.sum(every[:, 1, :], axis=0) + local * jnp.sum(offset * offset, axis=0)) / D
    scale = lax.rsqrt(spread + 1e-05)
    moved = centered + (local_mean - mean)[:, None]
    return (moved * scale[:, None] * gain[None, :] + bias[None, :]).astype(BF16)


def reduce_chain(parts):
    travelling = send_ring(parts[0], 1)
    for step, part in enumerate(parts[1:]):
        travelling = send_ring(add(part, travelling).astype(BF16), 2 * (step % 2) - 1)
    return travelling


def gather_chain(own, way, count):
    got = []
    for _ in range(count):
        own = send_ring(own, way)
        way = -way
        got.append(own)
    return got


def per_device(inputs, gain, bias, weight, d_act):
    normed = normalize(inputs, gain, bias)

    along_x = jnp.concatenate([normed] + [send_x(normed, s) for s in GATHER_SHIFT[1:]])
    along_y = [along_x] + [send_y(along_x, s) for s in GATHER_SHIFT[1:]]
    weight, _ = lax.optimization_barrier((weight, along_x))
    along_y[3], weight = lax.optimization_barrier((along_y[3], stage(weight)))
    other = [send_core(v) for v in along_y]

    gathered, *far = far_pre(along_y + other, weight)
    back, own, one, two = near_pre(gathered, weight)
    longer = reduce_chain([far[1], far[2], two, back])
    shorter = reduce_chain([far[0], far[3], one])

    pre = add(own, longer, shorter)
    slopes = jax.vjp(gelu_tanh, pre)[1](d_act.astype(F32))[0].astype(BF16)
    block_1, block_6, block_3, block_4 = gather_chain(slopes, 1, 4)
    block_7, block_2, block_5 = gather_chain(slopes, -1, 3)
    pieces = [block_7, slopes, block_1, block_2, block_3, block_4, block_5, block_6]
    pre, _ = lax.optimization_barrier((pre, block_1))
    activated = gelu_tanh(pre).astype(BF16)

    near = near_back(pieces[:4], weight)
    slopes_all, *parts = far_back(pieces, near, weight)
    d_weight = lax.dot_general(
        gathered, slopes_all, (((0,), (0,)), ((), ())), preferred_element_type=F32
    ).astype(BF16)

    sums = [add(parts[i], send_core(parts[4 + i])) for i in range(4)]
    arrived = [send_plane(sums[i].astype(BF16), SUM_SHIFT[i], 1) for i in range(1, 4)]
    line = add(sums[0], *arrived)
    line, d_weight = lax.optimization_barrier((line, d_weight))
    blocks = [line[i * TOKENS_OWN : (i + 1) * TOKENS_OWN] for i in range(4)]
    arrived = [send_plane(blocks[i].astype(BF16), SUM_SHIFT[i], 0) for i in range(1, 4)]
    d_normed = add(blocks[0], *arrived).astype(BF16)
    return (activated, d_normed, d_weight)


def solution(mesh):
    return jax.shard_map(
        per_device,
        mesh=mesh,
        in_specs=(P("row", "col"), P("col"), P("col"), P("col", "row"), P("col", "row")),
        out_specs=(P("col", "row"), P("row", "col"), P("col", "row")),
        check_vma=False,
    )
```

time: 132 us -> 120 us (0.909)
  starting transfers between devices: 43.2 us -> 30.1 us
  waiting for transfers between devices: 44.3 us -> 53.7 us
  Pallas kernels: 17.6 us -> 8.91 us
    ppermute x34, starting transfers between devices: 43.2 us -> 30.1 us  [send(): return lax.ppermute(value, ('row', 'col'), pairs_of(target))]
    ppermute x34, waiting for transfers between devices: 44.3 us -> 53.7 us  [send(): return lax.ppermute(value, ('row', 'col'), pairs_of(target))]
    pallas_call x4 -> x5, Pallas kernels: 17.6 us -> 8.91 us  [the longest x1 2.34 us: stage(): pl.pallas_call(stage_kernel, in_specs=[pl.BlockSpec(memory_space=pl.ANY)]...]
  transfers between devices with their start and end apart: 34 -> 34, of which waited for: 23 -> 22; matrix products, arithmetic and copies ran while one was open for 4% -> 5% of each run, Pallas kernels for 6% -> 4%
where the time goes in v2:
time: 120 us; the launch traced here: 119 us
  waiting for transfers between devices  53.7 us (45%)
  starting transfers between devices  30.1 us (25%)
  blocking collectives  16 us (13%)
  Pallas kernels  8.91 us (7%)
  other arithmetic  5.54 us (5%)
  matrix products  4.27 us (4%)
    ppermute x34, waiting for transfers between devices, send(): return lax.ppermute(value, ('row', 'col'), pairs_of(target))  53.7 us
    ppermute x34, starting transfers between devices, send(): return lax.ppermute(value, ('row', 'col'), pairs_of(target))  30.1 us
    all_to_all x1, blocking collectives, normalize(): lax.all_to_all(jnp.broadcast_to(stats[None], (NZ,) + stats.shape), 'col',...  16 us
    dot_general x1, matrix products, per_device(): lax.dot_general(gathered, slopes_all, (((0,), (0,)), ((), ())), preferred...  4.27 us
  transfers between devices with their start and end apart: 34, of which 22 were waited for; matrix products, arithmetic and copies ran while one was open for 5% of the time, Pallas kernels for 4%

profile of v2, /device:TPU:2, one launch (start us, length us, event | category | flops | bytes accessed | tf_op | source)
XLA Modules:
  0.0 119.3 jit_solution(9371772118047539711)
XLA Ops:
  0.6 1.0 reduce_sum.45
  1.7 1.1 multiply_reduce_fusion
  2.8 16.0 %all_to_all.5 = f32[8,2,16]{2,1,0:T(2,128)S(1)} all-to-all(f32[8,2,16]{2,1,0:T(2,128)S(1)} %broadcast_in_dim.2), channel_id=1, replica_groups=mesh['row'=32,'col'=8] {'col'}, dimensions={0} | all-to-all | bytes 2048 | tf_op jit(solution)/shard_map/all_to_all | solution.py:231
  18.8 1.0 add_convert_fusion.9
  19.8 1.6 %collective-permute-start.2 = (bf16[16,1536]{1,0:T(8,128)(2,1)S(1)}, bf16[16,1536]{1,0:T(8,128)(2,1)S(1)}, u32[]{:S(2)}, u32[]{:S(2)}) collective-permute-start(bf16[16,1536]{1,0:T(8,128)(2,1)S(1)} %add_convert_fusion.9), channel_id=1, source_target_pairs={{0,64},{1,65},{2,66},{3,67},{4,68},{5,69},{6,70},{7,71},{8,72},{9,... | collective-permute-start | bytes 147464 | tf_op jit(solution)/shard_map/ppermute | solution.py:34
  21.4 0.5 collective-permute-start.1
  22.0 2.1 %collective-permute-start = (bf16[16,1536]{1,0:T(8,128)(2,1)S(1)}, bf16[16,1536]{1,0:T(8,128)(2,1)S(1)}, u32[]{:S(2)}, u32[]{:S(2)}) collective-permute-start(bf16[16,1536]{1,0:T(8,128)(2,1)S(1)} %add_convert_fusion.9), channel_id=1, source_target_pairs={{0,128},{1,129},{2,130},{3,131},{4,132},{5,133},{6,134},{7,135},{8... | collective-permute-start | bytes 147464 | tf_op jit(solution)/shard_map/ppermute | solution.py:34
  24.1 0.1 collective-permute-done.2
  24.2 1.3 %collective-permute-done.1 = bf16[16,1536]{1,0:T(8,128)(2,1)S(1)} collective-permute-done((bf16[16,1536]{1,0:T(8,128)(2,1)S(1)}, bf16[16,1536]{1,0:T(8,128)(2,1)S(1)}, u32[]{:S(2)}, u32[]{:S(2)}) %collective-permute-start.1) | collective-permute-done | bytes 49184 | tf_op jit(solution)/shard_map/ppermute | solution.py:34
  25.5 2.0 %collective-permute-done = bf16[16,1536]{1,0:T(8,128)(2,1)S(1)} collective-permute-done((bf16[16,1536]{1,0:T(8,128)(2,1)S(1)}, bf16[16,1536]{1,0:T(8,128)(2,1)S(1)}, u32[]{:S(2)}, u32[]{:S(2)}) %collective-permute-start) | collective-permute-done | bytes 49184 | tf_op jit(solution)/shard_map/ppermute | solution.py:34
  27.6 1.7 %collective-permute-start.5 = (bf16[64,1536]{1,0:T(8,128)(2,1)S(1)}, bf16[64,1536]{1,0:T(8,128)(2,1)S(1)}, u32[]{:S(2)}, u32[]{:S(2)}) collective-permute-start(bf16[64,1536]{1,0:T(8,128)(2,1)S(1)} %pad_maximum_fusion.refs_0_), channel_id=1, source_target_pairs={{0,16},{1,17},{2,18},{3,19},{4,20},{5,21},{6,22},{7,23},{8,24},{9,... | collective-permute-start | bytes 589832 | tf_op jit(solution)/shard_map/ppermute | solution.py:34
  29.2 1.7 %collective-permute-start.4 = (bf16[64,1536]{1,0:T(8,128)(2,1)S(1)}, bf16[64,1536]{1,0:T(8,128)(2,1)S(1)}, u32[]{:S(2)}, u32[]{:S(2)}) collective-permute-start(bf16[64,1536]{1,0:T(8,128)(2,1)S(1)} %pad_maximum_fusion.refs_0_), channel_id=1, source_target_pairs={{0,48},{1,49},{2,50},{3,51},{4,52},{5,53},{6,54},{7,55},{8,56},{9,... | collective-permute-start | bytes 589832 | tf_op jit(solution)/shard_map/ppermute | solution.py:34
  30.9 2.0 %collective-permute-start.3 = (bf16[64,1536]{1,0:T(8,128)(2,1)S(1)}, bf16[64,1536]{1,0:T(8,128)(2,1)S(1)}, u32[]{:S(2)}, u32[]{:S(2)}) collective-permute-start(bf16[64,1536]{1,0:T(8,128)(2,1)S(1)} %pad_maximum_fusion.refs_0_), channel_id=1, source_target_pairs={{0,32},{1,33},{2,34},{3,35},{4,36},{5,37},{6,38},{7,39},{8,40},{9,... | collective-permute-start | bytes 589832 | tf_op jit(solution)/shard_map/ppermute | solution.py:34
  32.9 2.3 %shard_map.76.refs_8_.w_ref.refs_4_.refs_9_ = bf16[1536,1536]{1,0:T(8,128)(2,1)S(1)} custom-call(bf16[1536,1536]{1,0:T(8,128)(2,1)} %w_ref), custom_call_target="tpu_custom_call" | custom-call | flops 1207959552 | bytes 4718592 | tf_op jit(solution)/shard_map/pallas_call | solution.py:104
  35.2 0.5 collective-permute-done.5.refs_3_
  35.7 0.1 collective-permute-start.8
  35.8 2.2 %collective-permute-done.3.refs_1_ = bf16[64,1536]{1,0:T(8,128)(2,1)S(1)} collective-permute-done((bf16[64,1536]{1,0:T(8,128)(2,1)S(1)}, bf16[64,1536]{1,0:T(8,128)(2,1)S(1)}, u32[]{:S(2)}, u32[]{:S(2)}) %collective-permute-start.3) | collective-permute-done | bytes 196640 | tf_op jit(solution)/shard_map/ppermute | solution.py:34
  38.1 0.5 collective-permute-start.9
  38.6 0.9 collective-permute-done.7.refs_5_
  39.5 0.3 collective-permute-done.9.refs_7_
  39.8 1.7 %shard_map.77 = (bf16[512,1536]{1,0:T(8,128)(2,1)S(1)}, bf16[64,1536]{1,0:T(8,128)(2,1)S(1)}, bf16[64,1536]{1,0:T(8,128)(2,1)S(1)}, bf16[64,1536]{1,0:T(8,128)(2,1)S(1)}, bf16[64,1536]{1,0:T(8,128)(2,1)S(1)}) custom-call(bf16[64,1536]{1,0:T(8,128)(2,1)S(1)} %pad_maximum_fusion.refs_0_, bf16[64,1536]{1,0:T(8,128)(2,1)S(1)} %collective-permute-done.3.refs_1_, ...), custom_call_target="tpu_custom_call" | custom-call | flops 1207959552 | bytes 4718592 | tf_op jit(solution)/shard_map/pallas_call | solution.py:140
  41.5 0.7 collective-permute-start.10
  42.2 1.4 %collective-permute-start.14 = (bf16[64,1536]{1,0:T(8,128)(2,1)S(1)}, bf16[64,1536]{1,0:T(8,128)(2,1)S(1)}, u32[]{:S(2)}, u32[]{:S(2)}) collective-permute-start(bf16[64,1536]{1,0:T(8,128)(2,1)S(1)} %get-tuple-element.38), channel_id=1, source_target_pairs={{0,1},{1,0},{2,3},{3,2},{4,5},{5,4},{6,7},{7,6},{8,15},{9,10},{10,... | collective-permute-start | bytes 589832 | tf_op jit(solution)/shard_map/ppermute | solution.py:34
  43.6 1.4 %shard_map.78 = (bf16[64,1536]{1,0:T(8,128)(2,1)S(1)}, bf16[64,1536]{1,0:T(8,128)(2,1)S(1)}, bf16[64,1536]{1,0:T(8,128)(2,1)S(1)}, bf16[64,1536]{1,0:T(8,128)(2,1)S(1)}) custom-call(bf16[512,1536]{1,0:T(8,128)(2,1)S(1)} %get-tuple-element.30.normed_ref, bf16[1536,1536]{1,0:T(8,128)(2,1)S(1)} %shard_map.76.refs_8_.w_ref.refs_4_.refs_9_), custom_call_target="tpu_custom_call" | custom-call | flops 1207959552 | bytes 4718592 | tf_op jit(solution)/shard_map/pallas_call | solution.py:151
  45.0 2.2 %collective-permute-done.10 = bf16[64,1536]{1,0:T(8,128)(2,1)S(1)} collective-permute-done((bf16[64,1536]{1,0:T(8,128)(2,1)S(1)}, bf16[64,1536]{1,0:T(8,128)(2,1)S(1)}, u32[]{:S(2)}, u32[]{:S(2)}) %collective-permute-start.10) | collective-permute-done | bytes 196640 | tf_op jit(solution)/shard_map/ppermute | solution.py:34
  47.3 0.7 collective-permute-start.11
  48.0 1.4 %collective-permute-done.14 = bf16[64,1536]{1,0:T(8,128)(2,1)S(1)} collective-permute-done((bf16[64,1536]{1,0:T(8,128)(2,1)S(1)}, bf16[64,1536]{1,0:T(8,128)(2,1)S(1)}, u32[]{:S(2)}, u32[]{:S(2)}) %collective-permute-start.14) | collective-permute-done | bytes 196640 | tf_op jit(solution)/shard_map/ppermute | solution.py:34
  49.4 1.4 %collective-permute-start.15 = (bf16[64,1536]{1,0:T(8,128)(2,1)S(1)}, bf16[64,1536]{1,0:T(8,128)(2,1)S(1)}, u32[]{:S(2)}, u32[]{:S(2)}) collective-permute-start(bf16[64,1536]{1,0:T(8,128)(2,1)S(1)} %add_convert_fusion.4), channel_id=1, source_target_pairs={{0,7},{1,2},{2,1},{3,4},{4,3},{5,6},{6,5},{7,0},{8,9},{9,8},{10,11... | collective-permute-start | bytes 589832 | tf_op jit(solution)/shard_map/ppermute | solution.py:34
  50.8 3.5 %collective-permute-done.11 = bf16[64,1536]{1,0:T(8,128)(2,1)S(1)} collective-permute-done((bf16[64,1536]{1,0:T(8,128)(2,1)S(1)}, bf16[64,1536]{1,0:T(8,128)(2,1)S(1)}, u32[]{:S(2)}, u32[]{:S(2)}) %collective-permute-start.11) | collective-permute-done | bytes 196640 | tf_op jit(solution)/shard_map/ppermute | solution.py:34
  54.3 0.1 collective-permute-start.12
  54.5 2.0 %collective-permute-done.15 = bf16[64,1536]{1,0:T(8,128)(2,1)S(1)} collective-permute-done((bf16[64,1536]{1,0:T(8,128)(2,1)S(1)}, bf16[64,1536]{1,0:T(8,128)(2,1)S(1)}, u32[]{:S(2)}, u32[]{:S(2)}) %collective-permute-start.15) | collective-permute-done | bytes 196640 | tf_op jit(solution)/shard_map/ppermute | solution.py:34
  56.5 0.3 collective-permute-start.16
  56.8 3.3 %collective-permute-done.12 = bf16[64,1536]{1,0:T(8,128)(2,1)S(1)} collective-permute-done((bf16[64,1536]{1,0:T(8,128)(2,1)S(1)}, bf16[64,1536]{1,0:T(8,128)(2,1)S(1)}, u32[]{:S(2)}, u32[]{:S(2)}) %collective-permute-start.12) | collective-permute-done | bytes 196640 | tf_op jit(solution)/shard_map/ppermute | solution.py:34
  60.2 0.7 collective-permute-start.13
  60.8 2.9 %collective-permute-done.16 = bf16[64,1536]{1,0:T(8,128)(2,1)S(1)} collective-permute-done((bf16[64,1536]{1,0:T(8,128)(2,1)S(1)}, bf16[64,1536]{1,0:T(8,128)(2,1)S(1)}, u32[]{:S(2)}, u32[]{:S(2)}) %collective-permute-start.16) | collective-permute-done | bytes 196640 | tf_op jit(solution)/shard_map/ppermute | solution.py:34
  63.7 3.4 %collective-permute-done.13 = bf16[64,1536]{1,0:T(8,128)(2,1)S(1)} collective-permute-done((bf16[64,1536]{1,0:T(8,128)(2,1)S(1)}, bf16[64,1536]{1,0:T(8,128)(2,1)S(1)}, u32[]{:S(2)}, u32[]{:S(2)}) %collective-permute-start.13) | collective-permute-done | bytes 196640 | tf_op jit(solution)/shard_map/ppermute | solution.py:34
  67.1 0.3 fusion.2
  67.6 0.6 collective-permute-start.18
  68.2 5.5 %collective-permute-done.17.refs_2_ = bf16[64,1536]{1,0:T(8,128)(2,1)S(1)} collective-permute-done((bf16[64,1536]{1,0:T(8,128)(2,1)S(1)}, bf16[64,1536]{1,0:T(8,128)(2,1)S(1)}, u32[]{:S(2)}, u32[]{:S(2)}) %collective-permute-start.17) | collective-permute-done | bytes 196640 | tf_op jit(solution)/shard_map/ppermute | solution.py:34
  73.7 0.8 collective-permute-start.20
  74.5 1.1 collective-permute-start.19
  75.6 6.5 %collective-permute-done.20.refs_7_ = bf16[64,1536]{1,0:T(8,128)(2,1)S(1)} collective-permute-done((bf16[64,1536]{1,0:T(8,128)(2,1)S(1)}, bf16[64,1536]{1,0:T(8,128)(2,1)S(1)}, u32[]{:S(2)}, u32[]{:S(2)}) %collective-permute-start.20) | collective-permute-done | bytes 196640 | tf_op jit(solution)/shard_map/ppermute | solution.py:34
  82.1 1.6 %collective-permute-start.23 = (bf16[64,1536]{1,0:T(8,128)(2,1)S(1)}, bf16[64,1536]{1,0:T(8,128)(2,1)S(1)}, u32[]{:S(2)}, u32[]{:S(2)}) collective-permute-start(bf16[64,1536]{1,0:T(8,128)(2,1)S(1)} %collective-permute-done.19.refs_3_), channel_id=1, source_target_pairs={{0,7},{1,2},{2,1},{3,4},{4,3},{5,6},{6,5},{7,0},{8,9},{9,8},{10,11... | collective-permute-start | bytes 589832 | tf_op jit(solution)/shard_map/ppermute | solution.py:34
  83.7 5.6 %collective-permute-done.21.refs_4_ = bf16[64,1536]{1,0:T(8,128)(2,1)S(1)} collective-permute-done((bf16[64,1536]{1,0:T(8,128)(2,1)S(1)}, bf16[64,1536]{1,0:T(8,128)(2,1)S(1)}, u32[]{:S(2)}, u32[]{:S(2)}) %collective-permute-start.21) | collective-permute-done | bytes 196640 | tf_op jit(solution)/shard_map/ppermute | solution.py:34
  89.3 1.4 %shard_map.79.refs_8_ = bf16[256,1536]{1,0:T(8,128)(2,1)S(1)} custom-call(bf16[64,1536]{1,0:T(8,128)(2,1)S(1)} %collective-permute-done.18.refs_0_, bf16[64,1536]{1,0:T(8,128)(2,1)S(1)} %get-tuple-element.51.refs_1_, bf16[64,1536]{1,0:T(8,128)(2,1)S(1)} %collective-permute-done.17.refs_2_, bf16[64,1536]{1,0:T(8,128)(2,1)S(1)} %collective-permute-done.19.refs_3_, ...), custom_call_target="tpu_custom_call" | custom-call | flops 1207959552 | bytes 4718592 | tf_op jit(solution)/shard_map/pallas_call | solution.py:173
  90.8 5.4 %collective-permute-done.22.refs_5_ = bf16[64,1536]{1,0:T(8,128)(2,1)S(1)} collective-permute-done((bf16[64,1536]{1,0:T(8,128)(2,1)S(1)}, bf16[64,1536]{1,0:T(8,128)(2,1)S(1)}, u32[]{:S(2)}, u32[]{:S(2)}) %collective-permute-start.22) | collective-permute-done | bytes 196640 | tf_op jit(solution)/shard_map/ppermute | solution.py:34
  96.2 2.0 %shard_map.80 = (bf16[512,1536]{1,0:T(8,128)(2,1)S(1)}, bf16[64,1536]{1,0:T(8,128)(2,1)S(1)}, bf16[64,1536]{1,0:T(8,128)(2,1)S(1)}, bf16[64,1536]{1,0:T(8,128)(2...) custom-call(bf16[64,1536]{1,0:T(8,128)(2,1)S(1)} %collective-permute, ...), custom_call_target="tpu_custom_call" | custom-call | flops 1207959552 | bytes 4718592 | tf_op jit(solution)/shard_map/pallas_call | solution.py:203
  98.4 0.5 collective-permute-start.24
  98.9 0.1 collective-permute-start.27
  99.0 0.4 collective-permute-start.29
  99.4 0.4 collective-permute-done.25
  99.8 1.4 %collective-permute-start.26 = (bf16[64,1536]{1,0:T(8,128)(2,1)S(1)}, bf16[64,1536]{1,0:T(8,128)(2,1)S(1)}, u32[]{:S(2)}, u32[]{:S(2)}) collective-permute-start(bf16[64,1536]{1,0:T(8,128)(2,1)S(1)} %add_convert_fusion.2), channel_id=1, source_target_pairs={{0,16},{1,17},{2,18},{3,19},{4,20},{5,21},{6,22},{7,23},{8,72},{9,... | collective-permute-start | bytes 589832 | tf_op jit(solution)/shard_map/ppermute | solution.py:34
  101.3 2.0 %collective-permute-start.28 = (bf16[64,1536]{1,0:T(8,128)(2,1)S(1)}, bf16[64,1536]{1,0:T(8,128)(2,1)S(1)}, u32[]{:S(2)}, u32[]{:S(2)}) collective-permute-start(bf16[64,1536]{1,0:T(8,128)(2,1)S(1)} %add_convert_fusion.1), channel_id=1, source_target_pairs={{0,48},{1,49},{2,50},{3,51},{4,52},{5,53},{6,54},{7,55},{8,200},{9... | collective-permute-start | bytes 589832 | tf_op jit(solution)/shard_map/ppermute | solution.py:34
  103.3 1.1 collective-permute-start.30
  104.5 4.3 %convolution_convert_fusion = bf16[1536,1536]{1,0:T(8,128)(2,1)} fusion(bf16[512,1536]{1,0:T(8,128)(2,1)S(1)} %get-tuple-element.30.normed_ref, bf16[512,1536]{1,0:T(8,128)(2,1)S(1)} %get-tuple-element.48), kind=kOutput, calls=%fused_computation | convolution fusion | flops 2418278400 | bytes 7864320 | tf_op jit(solution)/shard_map/dot_general | solution.py:280
  108.8 2.1 %collective-permute-done.30 = bf16[64,1536]{1,0:T(8,128)(2,1)S(1)} collective-permute-done((bf16[64,1536]{1,0:T(8,128)(2,1)S(1)}, bf16[64,1536]{1,0:T(8,128)(2,1)S(1)}, u32[]{:S(2)}, u32[]{:S(2)}) %collective-permute-start.30) | collective-permute-done | bytes 196640 | tf_op jit(solution)/shard_map/ppermute | solution.py:34
  110.8 0.1 convert_add_fusion
  111.0 1.6 %collective-permute-start.31 = (bf16[16,1536]{1,0:T(8,128)(2,1)S(1)}, bf16[16,1536]{1,0:T(8,128)(2,1)S(1)}, u32[]{:S(2)}, u32[]{:S(2)}) collective-permute-start(bf16[16,1536]{1,0:T(8,128)(2,1)S(1)} %get-tuple-element.53), channel_id=1, source_target_pairs={{0,64},{1,65},{2,66},{3,67},{4,68},{5,69},{6,70},{7,71},{8,24},{9,... | collective-permute-start | bytes 147464 | tf_op jit(solution)/shard_map/ppermute | solution.py:34
  112.6 1.9 %collective-permute-start.33 = (bf16[16,1536]{1,0:T(8,128)(2,1)S(1)}, bf16[16,1536]{1,0:T(8,128)(2,1)S(1)}, u32[]{:S(2)}, u32[]{:S(2)}) collective-permute-start(bf16[16,1536]{1,0:T(8,128)(2,1)S(1)} %get-tuple-element.54), channel_id=1, source_target_pairs={{0,128},{1,129},{2,130},{3,131},{4,132},{5,133},{6,134},{7,135},{8... | collective-permute-start | bytes 147464 | tf_op jit(solution)/shard_map/ppermute | solution.py:34
  114.5 1.3 %collective-permute-start.32 = (bf16[16,1536]{1,0:T(8,128)(2,1)S(1)}, bf16[16,1536]{1,0:T(8,128)(2,1)S(1)}, u32[]{:S(2)}, u32[]{:S(2)}) collective-permute-start(bf16[16,1536]{1,0:T(8,128)(2,1)S(1)} %get-tuple-element.55), channel_id=1, source_target_pairs={{0,192},{1,193},{2,194},{3,195},{4,196},{5,197},{6,198},{7,199},{8... | collective-permute-start | bytes 147464 | tf_op jit(solution)/shard_map/ppermute | solution.py:34
  115.8 0.8 fusion.17
  116.6 1.5 %collective-permute-done.33 = bf16[16,1536]{1,0:T(8,128)(2,1)S(1)} collective-permute-done((bf16[16,1536]{1,0:T(8,128)(2,1)S(1)}, bf16[16,1536]{1,0:T(8,128)(2,1)S(1)}, u32[]{:S(2)}, u32[]{:S(2)}) %collective-permute-start.33) | collective-permute-done | bytes 49184 | tf_op jit(solution)/shard_map/ppermute | solution.py:34
  118.2 0.5 collective-permute-done.32
  118.7 0.6 add_convert_fusion.8
  (39 shorter events, 0.8 us)
Async XLA Ops:
  19.8 4.3 %collective-permute-start.2 = (bf16[16,1536]{1,0:T(8,128)(2,1)S(1)}, bf16[16,1536]{1,0:T(8,128)(2,1)S(1)}, u32[]{:S(2)}, u32[]{:S(2)}) collective-permute-start(bf16[16,1536]{1,0:T(8,128)(2,1)S(1)} %add_convert_fusion.9), channel_id=1, source_target_pairs={{0,64},{1,65},{2,66},{3,67},{4,68},{5,69},{6,70},{7,71},{8,72},{9,... | collective-permute-start | bytes 147464 | tf_op jit(solution)/shard_map/ppermute | solution.py:34
  21.4 4.1 %collective-permute-start.1 = (bf16[16,1536]{1,0:T(8,128)(2,1)S(1)}, bf16[16,1536]{1,0:T(8,128)(2,1)S(1)}, u32[]{:S(2)}, u32[]{:S(2)}) collective-permute-start(bf16[16,1536]{1,0:T(8,128)(2,1)S(1)} %add_convert_fusion.9), channel_id=1, source_target_pairs={{0,192},{1,193},{2,194},{3,195},{4,196},{5,197},{6,198},{7,199},{8... | collective-permute-start | bytes 147464 | tf_op jit(solution)/shard_map/ppermute | solution.py:34
  22.0 5.6 %collective-permute-start = (bf16[16,1536]{1,0:T(8,128)(2,1)S(1)}, bf16[16,1536]{1,0:T(8,128)(2,1)S(1)}, u32[]{:S(2)}, u32[]{:S(2)}) collective-permute-start(bf16[16,1536]{1,0:T(8,128)(2,1)S(1)} %add_convert_fusion.9), channel_id=1, source_target_pairs={{0,128},{1,129},{2,130},{3,131},{4,132},{5,133},{6,134},{7,135},{8... | collective-permute-start | bytes 147464 | tf_op jit(solution)/shard_map/ppermute | solution.py:34
  27.6 8.1 %collective-permute-start.5 = (bf16[64,1536]{1,0:T(8,128)(2,1)S(1)}, bf16[64,1536]{1,0:T(8,128)(2,1)S(1)}, u32[]{:S(2)}, u32[]{:S(2)}) collective-permute-start(bf16[64,1536]{1,0:T(8,128)(2,1)S(1)} %pad_maximum_fusion.refs_0_), channel_id=1, source_target_pairs={{0,16},{1,17},{2,18},{3,19},{4,20},{5,21},{6,22},{7,23},{8,24},{9,... | collective-permute-start | bytes 589832 | tf_op jit(solution)/shard_map/ppermute | solution.py:34
  29.2 6.5 %collective-permute-start.4 = (bf16[64,1536]{1,0:T(8,128)(2,1)S(1)}, bf16[64,1536]{1,0:T(8,128)(2,1)S(1)}, u32[]{:S(2)}, u32[]{:S(2)}) collective-permute-start(bf16[64,1536]{1,0:T(8,128)(2,1)S(1)} %pad_maximum_fusion.refs_0_), channel_id=1, source_target_pairs={{0,48},{1,49},{2,50},{3,51},{4,52},{5,53},{6,54},{7,55},{8,56},{9,... | collective-permute-start | bytes 589832 | tf_op jit(solution)/shard_map/ppermute | solution.py:34
  30.9 7.2 %collective-permute-start.3 = (bf16[64,1536]{1,0:T(8,128)(2,1)S(1)}, bf16[64,1536]{1,0:T(8,128)(2,1)S(1)}, u32[]{:S(2)}, u32[]{:S(2)}) collective-permute-start(bf16[64,1536]{1,0:T(8,128)(2,1)S(1)} %pad_maximum_fusion.refs_0_), channel_id=1, source_target_pairs={{0,32},{1,33},{2,34},{3,35},{4,36},{5,37},{6,38},{7,39},{8,40},{9,... | collective-permute-start | bytes 589832 | tf_op jit(solution)/shard_map/ppermute | solution.py:34
  32.9 5.7 %collective-permute-start.6 = (bf16[64,1536]{1,0:T(8,128)(2,1)S(1)}, bf16[64,1536]{1,0:T(8,128)(2,1)S(1)}, u32[]{:S(2)}, u32[]{:S(2)}) collective-permute-start(bf16[64,1536]{1,0:T(8,128)(2,1)S(1)} %pad_maximum_fusion.refs_0_), channel_id=1, source_target_pairs={{0,8},{1,9},{2,10},{3,11},{4,12},{5,13},{6,14},{7,15},{8,0},{9,1},... | collective-permute-start | bytes 589832 | tf_op jit(solution)/shard_map/ppermute | solution.py:34
  35.7 2.9 %collective-permute-start.8 = (bf16[64,1536]{1,0:T(8,128)(2,1)S(1)}, bf16[64,1536]{1,0:T(8,128)(2,1)S(1)}, u32[]{:S(2)}, u32[]{:S(2)}) collective-permute-start(bf16[64,1536]{1,0:T(8,128)(2,1)S(1)} %collective-permute-done.4.refs_2_), channel_id=1, source_target_pairs={{0,8},{1,9},{2,10},{3,11},{4,12},{5,13},{6,14},{7,15},{8,0},{9,1},... | collective-permute-start | bytes 589832 | tf_op jit(solution)/shard_map/ppermute | solution.py:34
  38.1 1.4 %collective-permute-start.7 = (bf16[64,1536]{1,0:T(8,128)(2,1)S(1)}, bf16[64,1536]{1,0:T(8,128)(2,1)S(1)}, u32[]{:S(2)}, u32[]{:S(2)}) collective-permute-start(bf16[64,1536]{1,0:T(8,128)(2,1)S(1)} %collective-permute-done.3.refs_1_), channel_id=1, source_target_pairs={{0,8},{1,9},{2,10},{3,11},{4,12},{5,13},{6,14},{7,15},{8,0},{9,1},... | collective-permute-start | bytes 589832 | tf_op jit(solution)/shard_map/ppermute | solution.py:34
  38.1 1.7 %collective-permute-start.9 = (bf16[64,1536]{1,0:T(8,128)(2,1)S(1)}, bf16[64,1536]{1,0:T(8,128)(2,1)S(1)}, u32[]{:S(2)}, u32[]{:S(2)}) collective-permute-start(bf16[64,1536]{1,0:T(8,128)(2,1)S(1)} %collective-permute-done.5.refs_3_), channel_id=1, source_target_pairs={{0,8},{1,9},{2,10},{3,11},{4,12},{5,13},{6,14},{7,15},{8,0},{9,1},... | collective-permute-start | bytes 589832 | tf_op jit(solution)/shard_map/ppermute | solution.py:34
  41.5 5.8 %collective-permute-start.10 = (bf16[64,1536]{1,0:T(8,128)(2,1)S(1)}, bf16[64,1536]{1,0:T(8,128)(2,1)S(1)}, u32[]{:S(2)}, u32[]{:S(2)}) collective-permute-start(bf16[64,1536]{1,0:T(8,128)(2,1)S(1)} %get-tuple-element.35), channel_id=1, source_target_pairs={{0,1},{1,0},{2,3},{3,2},{4,5},{5,4},{6,7},{7,6},{8,15},{9,10},{10,... | collective-permute-start | bytes 589832 | tf_op jit(solution)/shard_map/ppermute | solution.py:34
  42.2 7.2 %collective-permute-start.14 = (bf16[64,1536]{1,0:T(8,128)(2,1)S(1)}, bf16[64,1536]{1,0:T(8,128)(2,1)S(1)}, u32[]{:S(2)}, u32[]{:S(2)}) collective-permute-start(bf16[64,1536]{1,0:T(8,128)(2,1)S(1)} %get-tuple-element.38), channel_id=1, source_target_pairs={{0,1},{1,0},{2,3},{3,2},{4,5},{5,4},{6,7},{7,6},{8,15},{9,10},{10,... | collective-permute-start | bytes 589832 | tf_op jit(solution)/shard_map/ppermute | solution.py:34
  45.0 22.1 %copy-start = (bf16[64,1536]{1,0:T(8,128)(2,1)S(1)}, bf16[64,1536]{1,0:T(8,128)(2,1)}, u32[]{:S(2)}) copy-start(bf16[64,1536]{1,0:T(8,128)(2,1)} %param.9) | copy-start | bytes 589828
  47.3 7.0 %collective-permute-start.11 = (bf16[64,1536]{1,0:T(8,128)(2,1)S(1)}, bf16[64,1536]{1,0:T(8,128)(2,1)S(1)}, u32[]{:S(2)}, u32[]{:S(2)}) collective-permute-start(bf16[64,1536]{1,0:T(8,128)(2,1)S(1)} %add_convert_fusion.7), channel_id=1, source_target_pairs={{0,7},{1,2},{2,1},{3,4},{4,3},{5,6},{6,5},{7,0},{8,9},{9,8},{10,11... | collective-permute-start | bytes 589832 | tf_op jit(solution)/shard_map/ppermute | solution.py:34
  49.4 7.0 %collective-permute-start.15 = (bf16[64,1536]{1,0:T(8,128)(2,1)S(1)}, bf16[64,1536]{1,0:T(8,128)(2,1)S(1)}, u32[]{:S(2)}, u32[]{:S(2)}) collective-permute-start(bf16[64,1536]{1,0:T(8,128)(2,1)S(1)} %add_convert_fusion.4), channel_id=1, source_target_pairs={{0,7},{1,2},{2,1},{3,4},{4,3},{5,6},{6,5},{7,0},{8,9},{9,8},{10,11... | collective-permute-start | bytes 589832 | tf_op jit(solution)/shard_map/ppermute | solution.py:34
  54.3 5.8 %collective-permute-start.12 = (bf16[64,1536]{1,0:T(8,128)(2,1)S(1)}, bf16[64,1536]{1,0:T(8,128)(2,1)S(1)}, u32[]{:S(2)}, u32[]{:S(2)}) collective-permute-start(bf16[64,1536]{1,0:T(8,128)(2,1)S(1)} %add_convert_fusion.6), channel_id=1, source_target_pairs={{0,1},{1,0},{2,3},{3,2},{4,5},{5,4},{6,7},{7,6},{8,15},{9,10},{10,... | collective-permute-start | bytes 589832 | tf_op jit(solution)/shard_map/ppermute | solution.py:34
  56.5 7.2 %collective-permute-start.16 = (bf16[64,1536]{1,0:T(8,128)(2,1)S(1)}, bf16[64,1536]{1,0:T(8,128)(2,1)S(1)}, u32[]{:S(2)}, u32[]{:S(2)}) collective-permute-start(bf16[64,1536]{1,0:T(8,128)(2,1)S(1)} %add_convert_fusion.3), channel_id=1, source_target_pairs={{0,1},{1,0},{2,3},{3,2},{4,5},{5,4},{6,7},{7,6},{8,15},{9,10},{10,... | collective-permute-start | bytes 589832 | tf_op jit(solution)/shard_map/ppermute | solution.py:34
  60.2 7.0 %collective-permute-start.13 = (bf16[64,1536]{1,0:T(8,128)(2,1)S(1)}, bf16[64,1536]{1,0:T(8,128)(2,1)S(1)}, u32[]{:S(2)}, u32[]{:S(2)}) collective-permute-start(bf16[64,1536]{1,0:T(8,128)(2,1)S(1)} %add_convert_fusion.5), channel_id=1, source_target_pairs={{0,7},{1,2},{2,1},{3,4},{4,3},{5,6},{6,5},{7,0},{8,9},{9,8},{10,11... | collective-permute-start | bytes 589832 | tf_op jit(solution)/shard_map/ppermute | solution.py:34
  67.5 6.2 %collective-permute-start.17 = (bf16[64,1536]{1,0:T(8,128)(2,1)S(1)}, bf16[64,1536]{1,0:T(8,128)(2,1)S(1)}, u32[]{:S(2)}, u32[]{:S(2)}) collective-permute-start(bf16[64,1536]{1,0:T(8,128)(2,1)S(1)} %get-tuple-element.51.refs_1_), channel_id=1, source_target_pairs={{0,1},{1,0},{2,3},{3,2},{4,5},{5,4},{6,7},{7,6},{8,15},{9,10},{10,... | collective-permute-start | bytes 589832 | tf_op jit(solution)/shard_map/ppermute | solution.py:34
  67.6 7.0 %collective-permute-start.18 = (bf16[64,1536]{1,0:T(8,128)(2,1)S(1)}, bf16[64,1536]{1,0:T(8,128)(2,1)S(1)}, u32[]{:S(2)}, u32[]{:S(2)}) collective-permute-start(bf16[64,1536]{1,0:T(8,128)(2,1)S(1)} %get-tuple-element.51.refs_1_), channel_id=1, source_target_pairs={{0,7},{1,2},{2,1},{3,4},{4,3},{5,6},{6,5},{7,0},{8,9},{9,8},{10,11... | collective-permute-start | bytes 589832 | tf_op jit(solution)/shard_map/ppermute | solution.py:34
  73.7 8.4 %collective-permute-start.20 = (bf16[64,1536]{1,0:T(8,128)(2,1)S(1)}, bf16[64,1536]{1,0:T(8,128)(2,1)S(1)}, u32[]{:S(2)}, u32[]{:S(2)}) collective-permute-start(bf16[64,1536]{1,0:T(8,128)(2,1)S(1)} %collective-permute-done.17.refs_2_), channel_id=1, source_target_pairs={{0,7},{1,2},{2,1},{3,4},{4,3},{5,6},{6,5},{7,0},{8,9},{9,8},{10,11... | collective-permute-start | bytes 589832 | tf_op jit(solution)/shard_map/ppermute | solution.py:34
  74.5 7.5 %collective-permute-start.19 = (bf16[64,1536]{1,0:T(8,128)(2,1)S(1)}, bf16[64,1536]{1,0:T(8,128)(2,1)S(1)}, u32[]{:S(2)}, u32[]{:S(2)}) collective-permute-start(bf16[64,1536]{1,0:T(8,128)(2,1)S(1)} %collective-permute-done.18.refs_0_), channel_id=1, source_target_pairs={{0,1},{1,0},{2,3},{3,2},{4,5},{5,4},{6,7},{7,6},{8,15},{9,10},{10,... | collective-permute-start | bytes 589832 | tf_op jit(solution)/shard_map/ppermute | solution.py:34
  82.1 7.3 %collective-permute-start.21 = (bf16[64,1536]{1,0:T(8,128)(2,1)S(1)}, bf16[64,1536]{1,0:T(8,128)(2,1)S(1)}, u32[]{:S(2)}, u32[]{:S(2)}) collective-permute-start(bf16[64,1536]{1,0:T(8,128)(2,1)S(1)} %collective-permute-done.20.refs_7_), channel_id=1, source_target_pairs={{0,1},{1,0},{2,3},{3,2},{4,5},{5,4},{6,7},{7,6},{8,15},{9,10},{10,... | collective-permute-start | bytes 589832 | tf_op jit(solution)/shard_map/ppermute | solution.py:34
  82.1 8.7 %collective-permute-start.23 = (bf16[64,1536]{1,0:T(8,128)(2,1)S(1)}, bf16[64,1536]{1,0:T(8,128)(2,1)S(1)}, u32[]{:S(2)}, u32[]{:S(2)}) collective-permute-start(bf16[64,1536]{1,0:T(8,128)(2,1)S(1)} %collective-permute-done.19.refs_3_), channel_id=1, source_target_pairs={{0,7},{1,2},{2,1},{3,4},{4,3},{5,6},{6,5},{7,0},{8,9},{9,8},{10,11... | collective-permute-start | bytes 589832 | tf_op jit(solution)/shard_map/ppermute | solution.py:34
  89.3 6.9 %collective-permute-start.22 = (bf16[64,1536]{1,0:T(8,128)(2,1)S(1)}, bf16[64,1536]{1,0:T(8,128)(2,1)S(1)}, u32[]{:S(2)}, u32[]{:S(2)}) collective-permute-start(bf16[64,1536]{1,0:T(8,128)(2,1)S(1)} %collective-permute-done.21.refs_4_), channel_id=1, source_target_pairs={{0,7},{1,2},{2,1},{3,4},{4,3},{5,6},{6,5},{7,0},{8,9},{9,8},{10,11... | collective-permute-start | bytes 589832 | tf_op jit(solution)/shard_map/ppermute | solution.py:34
  98.3 1.5 %collective-permute-start.25 = (bf16[64,1536]{1,0:T(8,128)(2,1)S(1)}, bf16[64,1536]{1,0:T(8,128)(2,1)S(1)}, u32[]{:S(2)}, u32[]{:S(2)}) collective-permute-start(bf16[64,1536]{1,0:T(8,128)(2,1)S(1)} %get-tuple-element.43), channel_id=1, source_target_pairs={{0,8},{1,9},{2,10},{3,11},{4,12},{5,13},{6,14},{7,15},{8,0},{9,1},... | collective-permute-start | bytes 589832 | tf_op jit(solution)/shard_map/ppermute | solution.py:34
  98.4 10.4 %collective-permute-start.24 = (bf16[64,1536]{1,0:T(8,128)(2,1)S(1)}, bf16[64,1536]{1,0:T(8,128)(2,1)S(1)}, u32[]{:S(2)}, u32[]{:S(2)}) collective-permute-start(bf16[64,1536]{1,0:T(8,128)(2,1)S(1)} %get-tuple-element.41), channel_id=1, source_target_pairs={{0,8},{1,9},{2,10},{3,11},{4,12},{5,13},{6,14},{7,15},{8,0},{9,1},... | collective-permute-start | bytes 589832 | tf_op jit(solution)/shard_map/ppermute | solution.py:34
  98.9 2.4 %collective-permute-start.27 = (bf16[64,1536]{1,0:T(8,128)(2,1)S(1)}, bf16[64,1536]{1,0:T(8,128)(2,1)S(1)}, u32[]{:S(2)}, u32[]{:S(2)}) collective-permute-start(bf16[64,1536]{1,0:T(8,128)(2,1)S(1)} %get-tuple-element.45), channel_id=1, source_target_pairs={{0,8},{1,9},{2,10},{3,11},{4,12},{5,13},{6,14},{7,15},{8,0},{9,1},... | collective-permute-start | bytes 589832 | tf_op jit(solution)/shard_map/ppermute | solution.py:34
  99.0 4.3 %collective-permute-start.29 = (bf16[64,1536]{1,0:T(8,128)(2,1)S(1)}, bf16[64,1536]{1,0:T(8,128)(2,1)S(1)}, u32[]{:S(2)}, u32[]{:S(2)}) collective-permute-start(bf16[64,1536]{1,0:T(8,128)(2,1)S(1)} %get-tuple-element.47), channel_id=1, source_target_pairs={{0,8},{1,9},{2,10},{3,11},{4,12},{5,13},{6,14},{7,15},{8,0},{9,1},... | collective-permute-start | bytes 589832 | tf_op jit(solution)/shard_map/ppermute | solution.py:34
  99.8 8.9 %collective-permute-start.26 = (bf16[64,1536]{1,0:T(8,128)(2,1)S(1)}, bf16[64,1536]{1,0:T(8,128)(2,1)S(1)}, u32[]{:S(2)}, u32[]{:S(2)}) collective-permute-start(bf16[64,1536]{1,0:T(8,128)(2,1)S(1)} %add_convert_fusion.2), channel_id=1, source_target_pairs={{0,16},{1,17},{2,18},{3,19},{4,20},{5,21},{6,22},{7,23},{8,72},{9,... | collective-permute-start | bytes 589832 | tf_op jit(solution)/shard_map/ppermute | solution.py:34
  101.3 7.5 %collective-permute-start.28 = (bf16[64,1536]{1,0:T(8,128)(2,1)S(1)}, bf16[64,1536]{1,0:T(8,128)(2,1)S(1)}, u32[]{:S(2)}, u32[]{:S(2)}) collective-permute-start(bf16[64,1536]{1,0:T(8,128)(2,1)S(1)} %add_convert_fusion.1), channel_id=1, source_target_pairs={{0,48},{1,49},{2,50},{3,51},{4,52},{5,53},{6,54},{7,55},{8,200},{9... | collective-permute-start | bytes 589832 | tf_op jit(solution)/shard_map/ppermute | solution.py:34
  103.3 7.5 %collective-permute-start.30 = (bf16[64,1536]{1,0:T(8,128)(2,1)S(1)}, bf16[64,1536]{1,0:T(8,128)(2,1)S(1)}, u32[]{:S(2)}, u32[]{:S(2)}) collective-permute-start(bf16[64,1536]{1,0:T(8,128)(2,1)S(1)} %add_convert_fusion), channel_id=1, source_target_pairs={{0,32},{1,33},{2,34},{3,35},{4,36},{5,37},{6,38},{7,39},{8,136},{9... | collective-permute-start | bytes 589832 | tf_op jit(solution)/shard_map/ppermute | solution.py:34
  111.0 5.6 %collective-permute-start.31 = (bf16[16,1536]{1,0:T(8,128)(2,1)S(1)}, bf16[16,1536]{1,0:T(8,128)(2,1)S(1)}, u32[]{:S(2)}, u32[]{:S(2)}) collective-permute-start(bf16[16,1536]{1,0:T(8,128)(2,1)S(1)} %get-tuple-element.53), channel_id=1, source_target_pairs={{0,64},{1,65},{2,66},{3,67},{4,68},{5,69},{6,70},{7,71},{8,24},{9,... | collective-permute-start | bytes 147464 | tf_op jit(solution)/shard_map/ppermute | solution.py:34
  112.6 5.6 %collective-permute-start.33 = (bf16[16,1536]{1,0:T(8,128)(2,1)S(1)}, bf16[16,1536]{1,0:T(8,128)(2,1)S(1)}, u32[]{:S(2)}, u32[]{:S(2)}) collective-permute-start(bf16[16,1536]{1,0:T(8,128)(2,1)S(1)} %get-tuple-element.54), channel_id=1, source_target_pairs={{0,128},{1,129},{2,130},{3,131},{4,132},{5,133},{6,134},{7,135},{8... | collective-permute-start | bytes 147464 | tf_op jit(solution)/shard_map/ppermute | solution.py:34
  114.5 4.2 %collective-permute-start.32 = (bf16[16,1536]{1,0:T(8,128)(2,1)S(1)}, bf16[16,1536]{1,0:T(8,128)(2,1)S(1)}, u32[]{:S(2)}, u32[]{:S(2)}) collective-permute-start(bf16[16,1536]{1,0:T(8,128)(2,1)S(1)} %get-tuple-element.55), channel_id=1, source_target_pairs={{0,192},{1,193},{2,194},{3,195},{4,196},{5,197},{6,198},{7,199},{8... | collective-permute-start | bytes 147464 | tf_op jit(solution)/shard_map/ppermute | solution.py:34

commit v3 on v2

--- a/solution.py
+++ b/solution.py
@@ -53,8 +53,8 @@
     return send(value, lambda x, y, c, z: (x, y, c + 1, z))
 
 
-def send_ring(value, way):
-    return send(value, lambda x, y, c, z: (x, y, c, z + way * (1 - 2 * ((z + c) % 2))))
+def send_ring(value, way, hops=1):
+    return send(value, lambda x, y, c, z: (x, y, c, z + way * hops * (1 - 2 * ((z + c) % 2))))
 
 
 def row_of(block):
@@ -222,12 +222,30 @@
     return total
 
 
+def center_kernel(inputs_ref, centered_ref, mean_ref, square_ref):
+    rows = inputs_ref[...]
+    mean = jnp.sum(rows, axis=1, keepdims=True) / rows.shape[1]
+    centered = rows - mean
+    centered_ref[...] = centered
+    mean_ref[...] = mean
+    square_ref[...] = jnp.sum(centered * centered, axis=1, keepdims=True)
+
+
+def center(inputs):
+    column = jax.ShapeDtypeStruct((inputs.shape[0], 1), F32)
+    return pl.pallas_call(
+        center_kernel,
+        in_specs=[WHOLE],
+        out_specs=[WHOLE] * 3,
+        out_shape=[jax.ShapeDtypeStruct(inputs.shape, F32), column, column],
+    )(inputs)
+
+
 def normalize(inputs, gain, bias):
     local = inputs.shape[1]
-    local_mean = jnp.sum(inputs, axis=1) / local
-    centered = inputs - local_mean[:, None]
-    local_square = jnp.sum(centered * centered, axis=1)
-    stats = jnp.stack([local_mean, local_square])
+    centered, local_mean, local_square = center(inputs)
+    local_mean = local_mean[:, 0]
+    stats = jnp.stack([local_mean, local_square[:, 0]])
     every = lax.all_to_all(jnp.broadcast_to(stats[None], (NZ,) + stats.shape), "col", 0, 0)
     mean = jnp.mean(every[:, 0, :], axis=0)
     offset = every[:, 0, :] - mean[None, :]
@@ -237,22 +255,6 @@
     return (moved * scale[:, None] * gain[None, :] + bias[None, :]).astype(BF16)
 
 
-def reduce_chain(parts):
-    travelling = send_ring(parts[0], 1)
-    for step, part in enumerate(parts[1:]):
-        travelling = send_ring(add(part, travelling).astype(BF16), 2 * (step % 2) - 1)
-    return travelling
-
-
-def gather_chain(own, way, count):
-    got = []
-    for _ in range(count):
-        own = send_ring(own, way)
-        way = -way
-        got.append(own)
-    return got
-
-
 def per_device(inputs, gain, bias, weight, d_act):
     normed = normalize(inputs, gain, bias)
 
@@ -264,13 +266,23 @@
 
     gathered, *far = far_pre(along_y + other, weight)
     back, own, one, two = near_pre(gathered, weight)
-    longer = reduce_chain([far[1], far[2], two, back])
-    shorter = reduce_chain([far[0], far[3], one])
-
-    pre = add(own, longer, shorter)
+    four = send_ring(far[1], 1, 2)
+    three = send_ring(far[0], 1)
+    five = send_ring(far[2], -1)
+    two = send_ring(add(two, four, five).astype(BF16), 1)
+    six = send_ring(add(far[3], three).astype(BF16), -1)
+    back = send_ring(add(back, two).astype(BF16), -1)
+    one = send_ring(add(one, six).astype(BF16), 1)
+
+    pre = add(own, back, one)
     slopes = jax.vjp(gelu_tanh, pre)[1](d_act.astype(F32))[0].astype(BF16)
-    block_1, block_6, block_3, block_4 = gather_chain(slopes, 1, 4)
-    block_7, block_2, block_5 = gather_chain(slopes, -1, 3)
+    block_1 = send_ring(slopes, 1)
+    block_7 = send_ring(slopes, -1)
+    block_6 = send_ring(block_1, -1)
+    block_2 = send_ring(block_7, 1)
+    block_4 = send_ring(block_2, -1, 2)
+    block_3 = send_ring(block_6, 1)
+    block_5 = send_ring(block_2, -1)
     pieces = [block_7, slopes, block_1, block_2, block_3, block_4, block_5, block_6]
     pre, _ = lax.optimization_barrier((pre, block_1))
     activated = gelu_tanh(pre).astype(BF16)

time: 120 us -> 121 us (level)
  waiting for transfers between devices: 53.7 us -> 46.3 us
  starting transfers between devices: 30.1 us -> 36.7 us
  Pallas kernels: 8.91 us -> 10.6 us
    ppermute x34, waiting for transfers between devices: 53.7 us -> 46.3 us  [send(): return lax.ppermute(value, ('row', 'col'), pairs_of(target))]
    ppermute x34, starting transfers between devices: 30.1 us -> 36.7 us  [send(): return lax.ppermute(value, ('row', 'col'), pairs_of(target))]
    reduce_sum x2 -> x0, other arithmetic: 2.11 us -> none  [the longest x1 1.09 us: normalize(): local_square = jnp.sum(centered * centered, axis=1)]
    pallas_call x0 -> x1, Pallas kernels: none -> 1.67 us  [center(): pl.pallas_call(center_kernel, in_specs=[WHOLE], out_specs=[WHOLE] * 3, ou...]
    pallas_call x0 -> x2, other arithmetic: none -> 1.63 us  [center(): pl.pallas_call(center_kernel, in_specs=[WHOLE], out_specs=[WHOLE] * 3, ou...]
  transfers between devices with their start and end apart: 34 -> 34, of which waited for: 22 -> 20; matrix products, arithmetic and copies ran while one was open for 5% -> 5% of each run, Pallas kernels for 4% -> 4%
where the time goes in v3:
time: 121 us
  waiting for transfers between devices  46.3 us (38%)
  starting transfers between devices  36.7 us (30%)
  blocking collectives  16 us (13%)
  Pallas kernels  10.6 us (9%)
  other arithmetic  5.84 us (5%)
  matrix products  4.27 us (4%)
    ppermute x34, waiting for transfers between devices, send(): return lax.ppermute(value, ('row', 'col'), pairs_of(target))  46.3 us
    ppermute x34, starting transfers between devices, send(): return lax.ppermute(value, ('row', 'col'), pairs_of(target))  36.7 us
    all_to_all x1, blocking collectives, normalize(): lax.all_to_all(jnp.broadcast_to(stats[None], (NZ,) + stats.shape), 'col',...  16 us
    dot_general x1, matrix products, per_device(): lax.dot_general(gathered, slopes_all, (((0,), (0,)), ((), ())), preferred...  4.27 us
  transfers between devices with their start and end apart: 34, of which 20 were waited for; matrix products, arithmetic and copies ran while one was open for 5% of the time, Pallas kernels for 4%

profile of v3, /device:TPU:2, one launch (start us, length us, event | category | flops | bytes accessed | tf_op | source)
XLA Modules:
  0.0 120.6 jit_solution(6684631513964816565)
XLA Ops:
  0.6 1.7 %shard_map.76 = (f32[16,1536]{1,0:T(8,128)}, f32[16,1]{1,0:T(8,128)}, f32[16,1]{1,0:T(8,128)}) custom-call(f32[16,1536]{1,0:T(8,128)} %inputs_ref.1), custom_call_target="tpu_custom_call" | custom-call | tf_op jit(solution)/shard_map/pallas_call | solution.py:236
  2.3 0.8 reduce.3
  3.1 0.8 reduce.2
  3.9 16.0 %all_to_all.5 = f32[8,2,16]{2,1,0:T(2,128)S(1)} all-to-all(f32[8,2,16]{2,1,0:T(2,128)S(1)} %broadcast_in_dim.2), channel_id=1, replica_groups=mesh['row'=32,'col'=8] {'col'}, dimensions={0} | all-to-all | bytes 2048 | tf_op jit(solution)/shard_map/all_to_all | solution.py:249
  20.1 0.8 subtract_reduce_fusion
  20.9 1.0 add_convert_fusion.8
  21.9 1.6 %collective-permute-start.2 = (bf16[16,1536]{1,0:T(8,128)(2,1)S(1)}, bf16[16,1536]{1,0:T(8,128)(2,1)S(1)}, u32[]{:S(2)}, u32[]{:S(2)}) collective-permute-start(bf16[16,1536]{1,0:T(8,128)(2,1)S(1)} %add_convert_fusion.8), channel_id=1, source_target_pairs={{0,64},{1,65},{2,66},{3,67},{4,68},{5,69},{6,70},{7,71},{8,72},{9,... | collective-permute-start | bytes 147464 | tf_op jit(solution)/shard_map/ppermute | solution.py:34
  23.5 0.5 collective-permute-start.1
  24.0 2.1 %collective-permute-start = (bf16[16,1536]{1,0:T(8,128)(2,1)S(1)}, bf16[16,1536]{1,0:T(8,128)(2,1)S(1)}, u32[]{:S(2)}, u32[]{:S(2)}) collective-permute-start(bf16[16,1536]{1,0:T(8,128)(2,1)S(1)} %add_convert_fusion.8), channel_id=1, source_target_pairs={{0,128},{1,129},{2,130},{3,131},{4,132},{5,133},{6,134},{7,135},{8... | collective-permute-start | bytes 147464 | tf_op jit(solution)/shard_map/ppermute | solution.py:34
  26.2 0.1 collective-permute-done.2
  26.3 1.3 %collective-permute-done.1 = bf16[16,1536]{1,0:T(8,128)(2,1)S(1)} collective-permute-done((bf16[16,1536]{1,0:T(8,128)(2,1)S(1)}, bf16[16,1536]{1,0:T(8,128)(2,1)S(1)}, u32[]{:S(2)}, u32[]{:S(2)}) %collective-permute-start.1) | collective-permute-done | bytes 49184 | tf_op jit(solution)/shard_map/ppermute | solution.py:34
  27.6 2.0 %collective-permute-done = bf16[16,1536]{1,0:T(8,128)(2,1)S(1)} collective-permute-done((bf16[16,1536]{1,0:T(8,128)(2,1)S(1)}, bf16[16,1536]{1,0:T(8,128)(2,1)S(1)}, u32[]{:S(2)}, u32[]{:S(2)}) %collective-permute-start) | collective-permute-done | bytes 49184 | tf_op jit(solution)/shard_map/ppermute | solution.py:34
  29.6 1.7 %collective-permute-start.5 = (bf16[64,1536]{1,0:T(8,128)(2,1)S(1)}, bf16[64,1536]{1,0:T(8,128)(2,1)S(1)}, u32[]{:S(2)}, u32[]{:S(2)}) collective-permute-start(bf16[64,1536]{1,0:T(8,128)(2,1)S(1)} %pad_maximum_fusion.refs_0_), channel_id=1, source_target_pairs={{0,16},{1,17},{2,18},{3,19},{4,20},{5,21},{6,22},{7,23},{8,24},{9,... | collective-permute-start | bytes 589832 | tf_op jit(solution)/shard_map/ppermute | solution.py:34
  31.3 1.7 %collective-permute-start.4 = (bf16[64,1536]{1,0:T(8,128)(2,1)S(1)}, bf16[64,1536]{1,0:T(8,128)(2,1)S(1)}, u32[]{:S(2)}, u32[]{:S(2)}) collective-permute-start(bf16[64,1536]{1,0:T(8,128)(2,1)S(1)} %pad_maximum_fusion.refs_0_), channel_id=1, source_target_pairs={{0,48},{1,49},{2,50},{3,51},{4,52},{5,53},{6,54},{7,55},{8,56},{9,... | collective-permute-start | bytes 589832 | tf_op jit(solution)/shard_map/ppermute | solution.py:34
  33.0 2.0 %collective-permute-start.3 = (bf16[64,1536]{1,0:T(8,128)(2,1)S(1)}, bf16[64,1536]{1,0:T(8,128)(2,1)S(1)}, u32[]{:S(2)}, u32[]{:S(2)}) collective-permute-start(bf16[64,1536]{1,0:T(8,128)(2,1)S(1)} %pad_maximum_fusion.refs_0_), channel_id=1, source_target_pairs={{0,32},{1,33},{2,34},{3,35},{4,36},{5,37},{6,38},{7,39},{8,40},{9,... | collective-permute-start | bytes 589832 | tf_op jit(solution)/shard_map/ppermute | solution.py:34
  34.9 2.3 %shard_map.77.refs_8_.w_ref.refs_4_.refs_9_ = bf16[1536,1536]{1,0:T(8,128)(2,1)S(1)} custom-call(bf16[1536,1536]{1,0:T(8,128)(2,1)} %w_ref), custom_call_target="tpu_custom_call" | custom-call | flops 1207959552 | bytes 4718592 | tf_op jit(solution)/shard_map/pallas_call | solution.py:104
  37.3 0.5 collective-permute-done.5.refs_3_
  37.8 0.1 collective-permute-start.8
  37.9 2.2 %collective-permute-done.3.refs_1_ = bf16[64,1536]{1,0:T(8,128)(2,1)S(1)} collective-permute-done((bf16[64,1536]{1,0:T(8,128)(2,1)S(1)}, bf16[64,1536]{1,0:T(8,128)(2,1)S(1)}, u32[]{:S(2)}, u32[]{:S(2)}) %collective-permute-start.3) | collective-permute-done | bytes 196640 | tf_op jit(solution)/shard_map/ppermute | solution.py:34
  40.1 0.5 collective-permute-start.9
  40.7 0.9 collective-permute-done.7.refs_5_
  41.6 0.3 collective-permute-done.9.refs_7_
  41.9 1.7 %shard_map.78 = (bf16[512,1536]{1,0:T(8,128)(2,1)S(1)}, bf16[64,1536]{1,0:T(8,128)(2,1)S(1)}, bf16[64,1536]{1,0:T(8,128)(2,1)S(1)}, bf16[64,1536]{1,0:T(8,128)(2,1)S(1)}, bf16[64,1536]{1,0:T(8,128)(2,1)S(1)}) custom-call(bf16[64,1536]{1,0:T(8,128)(2,1)S(1)} %pad_maximum_fusion.refs_0_, bf16[64,1536]{1,0:T(8,128)(2,1)S(1)} %collective-permute-done.3.refs_1_, ...), custom_call_target="tpu_custom_call" | custom-call | flops 1207959552 | bytes 4718592 | tf_op jit(solution)/shard_map/pallas_call | solution.py:140
  43.6 0.6 collective-permute-start.10
  44.2 0.6 collective-permute-start.11
  44.8 0.9 collective-permute-start.14
  45.7 1.4 %shard_map.79 = (bf16[64,1536]{1,0:T(8,128)(2,1)S(1)}, bf16[64,1536]{1,0:T(8,128)(2,1)S(1)}, bf16[64,1536]{1,0:T(8,128)(2,1)S(1)}, bf16[64,1536]{1,0:T(8,128)(2,1)S(1)}) custom-call(bf16[512,1536]{1,0:T(8,128)(2,1)S(1)} %get-tuple-element.36.normed_ref, bf16[1536,1536]{1,0:T(8,128)(2,1)S(1)} %shard_map.77.refs_8_.w_ref.refs_4_.refs_9_), custom_call_target="tpu_custom_call" | custom-call | flops 1207959552 | bytes 4718592 | tf_op jit(solution)/shard_map/pallas_call | solution.py:151
  47.1 7.2 %collective-permute-done.10 = bf16[64,1536]{1,0:T(8,128)(2,1)S(1)} collective-permute-done((bf16[64,1536]{1,0:T(8,128)(2,1)S(1)}, bf16[64,1536]{1,0:T(8,128)(2,1)S(1)}, u32[]{:S(2)}, u32[]{:S(2)}) %collective-permute-start.10) | collective-permute-done | bytes 196640 | tf_op jit(solution)/shard_map/ppermute | solution.py:34
  54.3 1.1 collective-permute-done.11
  55.6 1.7 %collective-permute-start.15 = (bf16[64,1536]{1,0:T(8,128)(2,1)S(1)}, bf16[64,1536]{1,0:T(8,128)(2,1)S(1)}, u32[]{:S(2)}, u32[]{:S(2)}) collective-permute-start(bf16[64,1536]{1,0:T(8,128)(2,1)S(1)} %add_convert_fusion.4), channel_id=1, source_target_pairs={{0,7},{1,2},{2,1},{3,4},{4,3},{5,6},{6,5},{7,0},{8,9},{9,8},{10,11... | collective-permute-start | bytes 589832 | tf_op jit(solution)/shard_map/ppermute | solution.py:34
  57.3 5.9 %collective-permute-done.12 = bf16[64,1536]{1,0:T(8,128)(2,1)S(1)} collective-permute-done((bf16[64,1536]{1,0:T(8,128)(2,1)S(1)}, bf16[64,1536]{1,0:T(8,128)(2,1)S(1)}, u32[]{:S(2)}, u32[]{:S(2)}) %collective-permute-start.12) | collective-permute-done | bytes 196640 | tf_op jit(solution)/shard_map/ppermute | solution.py:34
  63.3 0.5 collective-permute-start.13
  63.9 0.3 collective-permute-start.16
  64.2 6.7 %collective-permute-done.13 = bf16[64,1536]{1,0:T(8,128)(2,1)S(1)} collective-permute-done((bf16[64,1536]{1,0:T(8,128)(2,1)S(1)}, bf16[64,1536]{1,0:T(8,128)(2,1)S(1)}, u32[]{:S(2)}, u32[]{:S(2)}) %collective-permute-start.13) | collective-permute-done | bytes 196640 | tf_op jit(solution)/shard_map/ppermute | solution.py:34
  70.9 0.3 fusion.2
  71.2 1.8 %collective-permute-start.18 = (bf16[64,1536]{1,0:T(8,128)(2,1)S(1)}, bf16[64,1536]{1,0:T(8,128)(2,1)S(1)}, u32[]{:S(2)}, u32[]{:S(2)}) collective-permute-start(bf16[64,1536]{1,0:T(8,128)(2,1)S(1)} %get-tuple-element.57.refs_1_), channel_id=1, source_target_pairs={{0,7},{1,2},{2,1},{3,4},{4,3},{5,6},{6,5},{7,0},{8,9},{9,8},{10,11... | collective-permute-start | bytes 589832 | tf_op jit(solution)/shard_map/ppermute | solution.py:34
  73.0 5.3 %collective-permute-done.18.refs_0_ = bf16[64,1536]{1,0:T(8,128)(2,1)S(1)} collective-permute-done((bf16[64,1536]{1,0:T(8,128)(2,1)S(1)}, bf16[64,1536]{1,0:T(8,128)(2,1)S(1)}, u32[]{:S(2)}, u32[]{:S(2)}) %collective-permute-start.18) | collective-permute-done | bytes 196640 | tf_op jit(solution)/shard_map/ppermute | solution.py:34
  78.4 0.3 collective-permute-done.17.refs_2_
  78.7 2.2 %collective-permute-start.20 = (bf16[64,1536]{1,0:T(8,128)(2,1)S(1)}, bf16[64,1536]{1,0:T(8,128)(2,1)S(1)}, u32[]{:S(2)}, u32[]{:S(2)}) collective-permute-start(bf16[64,1536]{1,0:T(8,128)(2,1)S(1)} %collective-permute-done.17.refs_2_), channel_id=1, source_target_pairs={{0,7},{1,2},{2,1},{3,4},{4,3},{5,6},{6,5},{7,0},{8,9},{9,8},{10,11... | collective-permute-start | bytes 589832 | tf_op jit(solution)/shard_map/ppermute | solution.py:34
  80.9 4.3 %collective-permute-done.19.refs_3_ = bf16[64,1536]{1,0:T(8,128)(2,1)S(1)} collective-permute-done((bf16[64,1536]{1,0:T(8,128)(2,1)S(1)}, bf16[64,1536]{1,0:T(8,128)(2,1)S(1)}, u32[]{:S(2)}, u32[]{:S(2)}) %collective-permute-start.19) | collective-permute-done | bytes 196640 | tf_op jit(solution)/shard_map/ppermute | solution.py:34
  85.2 3.5 %collective-permute-start.23 = (bf16[64,1536]{1,0:T(8,128)(2,1)S(1)}, bf16[64,1536]{1,0:T(8,128)(2,1)S(1)}, u32[]{:S(2)}, u32[]{:S(2)}) collective-permute-start(bf16[64,1536]{1,0:T(8,128)(2,1)S(1)} %collective-permute-done.19.refs_3_), channel_id=1, source_target_pairs={{0,7},{1,2},{2,1},{3,4},{4,3},{5,6},{6,5},{7,0},{8,9},{9,8},{10,11... | collective-permute-start | bytes 589832 | tf_op jit(solution)/shard_map/ppermute | solution.py:34
  88.7 1.8 %collective-permute-start.22 = (bf16[64,1536]{1,0:T(8,128)(2,1)S(1)}, bf16[64,1536]{1,0:T(8,128)(2,1)S(1)}, u32[]{:S(2)}, u32[]{:S(2)}) collective-permute-start(bf16[64,1536]{1,0:T(8,128)(2,1)S(1)} %collective-permute-done.19.refs_3_), channel_id=1, source_target_pairs={{0,6},{1,3},{2,0},{3,5},{4,2},{5,7},{6,4},{7,1},{8,10},{9,15},{10,... | collective-permute-start | bytes 589832 | tf_op jit(solution)/shard_map/ppermute | solution.py:34
  90.5 2.1 %collective-permute-start.21 = (bf16[64,1536]{1,0:T(8,128)(2,1)S(1)}, bf16[64,1536]{1,0:T(8,128)(2,1)S(1)}, u32[]{:S(2)}, u32[]{:S(2)}) collective-permute-start(bf16[64,1536]{1,0:T(8,128)(2,1)S(1)} %collective-permute-done.20.refs_7_), channel_id=1, source_target_pairs={{0,1},{1,0},{2,3},{3,2},{4,5},{5,4},{6,7},{7,6},{8,15},{9,10},{10,... | collective-permute-start | bytes 589832 | tf_op jit(solution)/shard_map/ppermute | solution.py:34
  92.5 1.4 %shard_map.80.refs_8_ = bf16[256,1536]{1,0:T(8,128)(2,1)S(1)} custom-call(bf16[64,1536]{1,0:T(8,128)(2,1)S(1)} %collective-permute-done.18.refs_0_, bf16[64,1536]{1,0:T(8,128)(2,1)S(1)} %get-tuple-element.57.refs_1_, bf16[64,1536]{1,0:T(8,128)(2,1)S(1)} %collective-permute-done.17.refs_2_, bf16[64,1536]{1,0:T(8,128)(2,1)S(1)} %collective-permute-done.19.refs_3_, ...), custom_call_target="tpu_custom_call" | custom-call | flops 1207959552 | bytes 4718592 | tf_op jit(solution)/shard_map/pallas_call | solution.py:173
  94.0 1.4 %collective-permute-done.22.refs_5_ = bf16[64,1536]{1,0:T(8,128)(2,1)S(1)} collective-permute-done((bf16[64,1536]{1,0:T(8,128)(2,1)S(1)}, bf16[64,1536]{1,0:T(8,128)(2,1)S(1)}, u32[]{:S(2)}, u32[]{:S(2)}) %collective-permute-start.22) | collective-permute-done | bytes 196640 | tf_op jit(solution)/shard_map/ppermute | solution.py:34
  95.4 2.0 %collective-permute-done.21.refs_4_ = bf16[64,1536]{1,0:T(8,128)(2,1)S(1)} collective-permute-done((bf16[64,1536]{1,0:T(8,128)(2,1)S(1)}, bf16[64,1536]{1,0:T(8,128)(2,1)S(1)}, u32[]{:S(2)}, u32[]{:S(2)}) %collective-permute-start.21) | collective-permute-done | bytes 196640 | tf_op jit(solution)/shard_map/ppermute | solution.py:34
  97.4 2.0 %shard_map.81 = (bf16[512,1536]{1,0:T(8,128)(2,1)S(1)}, bf16[64,1536]{1,0:T(8,128)(2,1)S(1)}, bf16[64,1536]{1,0:T(8,128)(2,1)S(1)}, bf16[64,1536]{1,0:T(8,128)(2...) custom-call(bf16[64,1536]{1,0:T(8,128)(2,1)S(1)} %collective-permute, ...), custom_call_target="tpu_custom_call" | custom-call | flops 1207959552 | bytes 4718592 | tf_op jit(solution)/shard_map/pallas_call | solution.py:203
  99.5 0.5 collective-permute-start.24
  100.0 0.1 collective-permute-start.27
  100.1 0.4 collective-permute-start.29
  100.5 0.4 collective-permute-done.25
  101.0 1.3 %collective-permute-start.26 = (bf16[64,1536]{1,0:T(8,128)(2,1)S(1)}, bf16[64,1536]{1,0:T(8,128)(2,1)S(1)}, u32[]{:S(2)}, u32[]{:S(2)}) collective-permute-start(bf16[64,1536]{1,0:T(8,128)(2,1)S(1)} %add_convert_fusion.2), channel_id=1, source_target_pairs={{0,16},{1,17},{2,18},{3,19},{4,20},{5,21},{6,22},{7,23},{8,72},{9,... | collective-permute-start | bytes 589832 | tf_op jit(solution)/shard_map/ppermute | solution.py:34
  102.3 2.1 %collective-permute-start.28 = (bf16[64,1536]{1,0:T(8,128)(2,1)S(1)}, bf16[64,1536]{1,0:T(8,128)(2,1)S(1)}, u32[]{:S(2)}, u32[]{:S(2)}) collective-permute-start(bf16[64,1536]{1,0:T(8,128)(2,1)S(1)} %add_convert_fusion.1), channel_id=1, source_target_pairs={{0,48},{1,49},{2,50},{3,51},{4,52},{5,53},{6,54},{7,55},{8,200},{9... | collective-permute-start | bytes 589832 | tf_op jit(solution)/shard_map/ppermute | solution.py:34
  104.5 1.0 collective-permute-start.30
  105.5 4.3 %convolution_convert_fusion = bf16[1536,1536]{1,0:T(8,128)(2,1)} fusion(bf16[512,1536]{1,0:T(8,128)(2,1)S(1)} %get-tuple-element.36.normed_ref, bf16[512,1536]{1,0:T(8,128)(2,1)S(1)} %get-tuple-element.54), kind=kOutput, calls=%fused_computation | convolution fusion | flops 2418278400 | bytes 7864320 | tf_op jit(solution)/shard_map/dot_general | solution.py:292
  109.8 2.2 %collective-permute-done.30 = bf16[64,1536]{1,0:T(8,128)(2,1)S(1)} collective-permute-done((bf16[64,1536]{1,0:T(8,128)(2,1)S(1)}, bf16[64,1536]{1,0:T(8,128)(2,1)S(1)}, u32[]{:S(2)}, u32[]{:S(2)}) %collective-permute-start.30) | collective-permute-done | bytes 196640 | tf_op jit(solution)/shard_map/ppermute | solution.py:34
  112.0 0.1 convert_add_fusion
  112.2 1.6 %collective-permute-start.31 = (bf16[16,1536]{1,0:T(8,128)(2,1)S(1)}, bf16[16,1536]{1,0:T(8,128)(2,1)S(1)}, u32[]{:S(2)}, u32[]{:S(2)}) collective-permute-start(bf16[16,1536]{1,0:T(8,128)(2,1)S(1)} %get-tuple-element.59), channel_id=1, source_target_pairs={{0,64},{1,65},{2,66},{3,67},{4,68},{5,69},{6,70},{7,71},{8,24},{9,... | collective-permute-start | bytes 147464 | tf_op jit(solution)/shard_map/ppermute | solution.py:34
  113.7 2.1 %collective-permute-start.33 = (bf16[16,1536]{1,0:T(8,128)(2,1)S(1)}, bf16[16,1536]{1,0:T(8,128)(2,1)S(1)}, u32[]{:S(2)}, u32[]{:S(2)}) collective-permute-start(bf16[16,1536]{1,0:T(8,128)(2,1)S(1)} %get-tuple-element.60), channel_id=1, source_target_pairs={{0,128},{1,129},{2,130},{3,131},{4,132},{5,133},{6,134},{7,135},{8... | collective-permute-start | bytes 147464 | tf_op jit(solution)/shard_map/ppermute | solution.py:34
  115.9 1.1 collective-permute-start.32
  117.0 0.8 fusion.17
  117.8 1.5 %collective-permute-done.33 = bf16[16,1536]{1,0:T(8,128)(2,1)S(1)} collective-permute-done((bf16[16,1536]{1,0:T(8,128)(2,1)S(1)}, bf16[16,1536]{1,0:T(8,128)(2,1)S(1)}, u32[]{:S(2)}, u32[]{:S(2)}) %collective-permute-start.33) | collective-permute-done | bytes 49184 | tf_op jit(solution)/shard_map/ppermute | solution.py:34
  119.3 0.6 collective-permute-done.32
  119.9 0.6 add_convert_fusion.7
  (40 shorter events, 0.9 us)
Async XLA Ops:
  21.9 4.3 %collective-permute-start.2 = (bf16[16,1536]{1,0:T(8,128)(2,1)S(1)}, bf16[16,1536]{1,0:T(8,128)(2,1)S(1)}, u32[]{:S(2)}, u32[]{:S(2)}) collective-permute-start(bf16[16,1536]{1,0:T(8,128)(2,1)S(1)} %add_convert_fusion.8), channel_id=1, source_target_pairs={{0,64},{1,65},{2,66},{3,67},{4,68},{5,69},{6,70},{7,71},{8,72},{9,... | collective-permute-start | bytes 147464 | tf_op jit(solution)/shard_map/ppermute | solution.py:34
  23.5 4.1 %collective-permute-start.1 = (bf16[16,1536]{1,0:T(8,128)(2,1)S(1)}, bf16[16,1536]{1,0:T(8,128)(2,1)S(1)}, u32[]{:S(2)}, u32[]{:S(2)}) collective-permute-start(bf16[16,1536]{1,0:T(8,128)(2,1)S(1)} %add_convert_fusion.8), channel_id=1, source_target_pairs={{0,192},{1,193},{2,194},{3,195},{4,196},{5,197},{6,198},{7,199},{8... | collective-permute-start | bytes 147464 | tf_op jit(solution)/shard_map/ppermute | solution.py:34
  24.0 5.6 %collective-permute-start = (bf16[16,1536]{1,0:T(8,128)(2,1)S(1)}, bf16[16,1536]{1,0:T(8,128)(2,1)S(1)}, u32[]{:S(2)}, u32[]{:S(2)}) collective-permute-start(bf16[16,1536]{1,0:T(8,128)(2,1)S(1)} %add_convert_fusion.8), channel_id=1, source_target_pairs={{0,128},{1,129},{2,130},{3,131},{4,132},{5,133},{6,134},{7,135},{8... | collective-permute-start | bytes 147464 | tf_op jit(solution)/shard_map/ppermute | solution.py:34
  29.6 8.1 %collective-permute-start.5 = (bf16[64,1536]{1,0:T(8,128)(2,1)S(1)}, bf16[64,1536]{1,0:T(8,128)(2,1)S(1)}, u32[]{:S(2)}, u32[]{:S(2)}) collective-permute-start(bf16[64,1536]{1,0:T(8,128)(2,1)S(1)} %pad_maximum_fusion.refs_0_), channel_id=1, source_target_pairs={{0,16},{1,17},{2,18},{3,19},{4,20},{5,21},{6,22},{7,23},{8,24},{9,... | collective-permute-start | bytes 589832 | tf_op jit(solution)/shard_map/ppermute | solution.py:34
  31.3 6.5 %collective-permute-start.4 = (bf16[64,1536]{1,0:T(8,128)(2,1)S(1)}, bf16[64,1536]{1,0:T(8,128)(2,1)S(1)}, u32[]{:S(2)}, u32[]{:S(2)}) collective-permute-start(bf16[64,1536]{1,0:T(8,128)(2,1)S(1)} %pad_maximum_fusion.refs_0_), channel_id=1, source_target_pairs={{0,48},{1,49},{2,50},{3,51},{4,52},{5,53},{6,54},{7,55},{8,56},{9,... | collective-permute-start | bytes 589832 | tf_op jit(solution)/shard_map/ppermute | solution.py:34
  33.0 7.2 %collective-permute-start.3 = (bf16[64,1536]{1,0:T(8,128)(2,1)S(1)}, bf16[64,1536]{1,0:T(8,128)(2,1)S(1)}, u32[]{:S(2)}, u32[]{:S(2)}) collective-permute-start(bf16[64,1536]{1,0:T(8,128)(2,1)S(1)} %pad_maximum_fusion.refs_0_), channel_id=1, source_target_pairs={{0,32},{1,33},{2,34},{3,35},{4,36},{5,37},{6,38},{7,39},{8,40},{9,... | collective-permute-start | bytes 589832 | tf_op jit(solution)/shard_map/ppermute | solution.py:34
  34.9 5.7 %collective-permute-start.6 = (bf16[64,1536]{1,0:T(8,128)(2,1)S(1)}, bf16[64,1536]{1,0:T(8,128)(2,1)S(1)}, u32[]{:S(2)}, u32[]{:S(2)}) collective-permute-start(bf16[64,1536]{1,0:T(8,128)(2,1)S(1)} %pad_maximum_fusion.refs_0_), channel_id=1, source_target_pairs={{0,8},{1,9},{2,10},{3,11},{4,12},{5,13},{6,14},{7,15},{8,0},{9,1},... | collective-permute-start | bytes 589832 | tf_op jit(solution)/shard_map/ppermute | solution.py:34
  37.8 2.9 %collective-permute-start.8 = (bf16[64,1536]{1,0:T(8,128)(2,1)S(1)}, bf16[64,1536]{1,0:T(8,128)(2,1)S(1)}, u32[]{:S(2)}, u32[]{:S(2)}) collective-permute-start(bf16[64,1536]{1,0:T(8,128)(2,1)S(1)} %collective-permute-done.4.refs_2_), channel_id=1, source_target_pairs={{0,8},{1,9},{2,10},{3,11},{4,12},{5,13},{6,14},{7,15},{8,0},{9,1},... | collective-permute-start | bytes 589832 | tf_op jit(solution)/shard_map/ppermute | solution.py:34
  40.1 1.4 %collective-permute-start.7 = (bf16[64,1536]{1,0:T(8,128)(2,1)S(1)}, bf16[64,1536]{1,0:T(8,128)(2,1)S(1)}, u32[]{:S(2)}, u32[]{:S(2)}) collective-permute-start(bf16[64,1536]{1,0:T(8,128)(2,1)S(1)} %collective-permute-done.3.refs_1_), channel_id=1, source_target_pairs={{0,8},{1,9},{2,10},{3,11},{4,12},{5,13},{6,14},{7,15},{8,0},{9,1},... | collective-permute-start | bytes 589832 | tf_op jit(solution)/shard_map/ppermute | solution.py:34
  40.1 1.7 %collective-permute-start.9 = (bf16[64,1536]{1,0:T(8,128)(2,1)S(1)}, bf16[64,1536]{1,0:T(8,128)(2,1)S(1)}, u32[]{:S(2)}, u32[]{:S(2)}) collective-permute-start(bf16[64,1536]{1,0:T(8,128)(2,1)S(1)} %collective-permute-done.5.refs_3_), channel_id=1, source_target_pairs={{0,8},{1,9},{2,10},{3,11},{4,12},{5,13},{6,14},{7,15},{8,0},{9,1},... | collective-permute-start | bytes 589832 | tf_op jit(solution)/shard_map/ppermute | solution.py:34
  43.6 10.7 %collective-permute-start.10 = (bf16[64,1536]{1,0:T(8,128)(2,1)S(1)}, bf16[64,1536]{1,0:T(8,128)(2,1)S(1)}, u32[]{:S(2)}, u32[]{:S(2)}) collective-permute-start(bf16[64,1536]{1,0:T(8,128)(2,1)S(1)} %get-tuple-element.40), channel_id=1, source_target_pairs={{0,2},{1,7},{2,4},{3,1},{4,6},{5,3},{6,0},{7,5},{8,14},{9,11},{10,... | collective-permute-start | bytes 589832 | tf_op jit(solution)/shard_map/ppermute | solution.py:34
  44.2 11.1 %collective-permute-start.11 = (bf16[64,1536]{1,0:T(8,128)(2,1)S(1)}, bf16[64,1536]{1,0:T(8,128)(2,1)S(1)}, u32[]{:S(2)}, u32[]{:S(2)}) collective-permute-start(bf16[64,1536]{1,0:T(8,128)(2,1)S(1)} %get-tuple-element.41), channel_id=1, source_target_pairs={{0,7},{1,2},{2,1},{3,4},{4,3},{5,6},{6,5},{7,0},{8,9},{9,8},{10,11... | collective-permute-start | bytes 589832 | tf_op jit(solution)/shard_map/ppermute | solution.py:34
  44.8 10.7 %collective-permute-start.14 = (bf16[64,1536]{1,0:T(8,128)(2,1)S(1)}, bf16[64,1536]{1,0:T(8,128)(2,1)S(1)}, u32[]{:S(2)}, u32[]{:S(2)}) collective-permute-start(bf16[64,1536]{1,0:T(8,128)(2,1)S(1)} %get-tuple-element.44), channel_id=1, source_target_pairs={{0,1},{1,0},{2,3},{3,2},{4,5},{5,4},{6,7},{7,6},{8,15},{9,10},{10,... | collective-permute-start | bytes 589832 | tf_op jit(solution)/shard_map/ppermute | solution.py:34
  47.1 23.8 %copy-start = (bf16[64,1536]{1,0:T(8,128)(2,1)S(1)}, bf16[64,1536]{1,0:T(8,128)(2,1)}, u32[]{:S(2)}) copy-start(bf16[64,1536]{1,0:T(8,128)(2,1)} %param.9) | copy-start | bytes 589828
  55.4 7.8 %collective-permute-start.12 = (bf16[64,1536]{1,0:T(8,128)(2,1)S(1)}, bf16[64,1536]{1,0:T(8,128)(2,1)S(1)}, u32[]{:S(2)}, u32[]{:S(2)}) collective-permute-start(bf16[64,1536]{1,0:T(8,128)(2,1)S(1)} %add_convert_fusion.6), channel_id=1, source_target_pairs={{0,1},{1,0},{2,3},{3,2},{4,5},{5,4},{6,7},{7,6},{8,15},{9,10},{10,... | collective-permute-start | bytes 589832 | tf_op jit(solution)/shard_map/ppermute | solution.py:34
  55.6 8.2 %collective-permute-start.15 = (bf16[64,1536]{1,0:T(8,128)(2,1)S(1)}, bf16[64,1536]{1,0:T(8,128)(2,1)S(1)}, u32[]{:S(2)}, u32[]{:S(2)}) collective-permute-start(bf16[64,1536]{1,0:T(8,128)(2,1)S(1)} %add_convert_fusion.4), channel_id=1, source_target_pairs={{0,7},{1,2},{2,1},{3,4},{4,3},{5,6},{6,5},{7,0},{8,9},{9,8},{10,11... | collective-permute-start | bytes 589832 | tf_op jit(solution)/shard_map/ppermute | solution.py:34
  63.3 7.6 %collective-permute-start.13 = (bf16[64,1536]{1,0:T(8,128)(2,1)S(1)}, bf16[64,1536]{1,0:T(8,128)(2,1)S(1)}, u32[]{:S(2)}, u32[]{:S(2)}) collective-permute-start(bf16[64,1536]{1,0:T(8,128)(2,1)S(1)} %add_convert_fusion.5), channel_id=1, source_target_pairs={{0,7},{1,2},{2,1},{3,4},{4,3},{5,6},{6,5},{7,0},{8,9},{9,8},{10,11... | collective-permute-start | bytes 589832 | tf_op jit(solution)/shard_map/ppermute | solution.py:34
  63.9 7.0 %collective-permute-start.16 = (bf16[64,1536]{1,0:T(8,128)(2,1)S(1)}, bf16[64,1536]{1,0:T(8,128)(2,1)S(1)}, u32[]{:S(2)}, u32[]{:S(2)}) collective-permute-start(bf16[64,1536]{1,0:T(8,128)(2,1)S(1)} %add_convert_fusion.3), channel_id=1, source_target_pairs={{0,1},{1,0},{2,3},{3,2},{4,5},{5,4},{6,7},{7,6},{8,15},{9,10},{10,... | collective-permute-start | bytes 589832 | tf_op jit(solution)/shard_map/ppermute | solution.py:34
  71.2 7.1 %collective-permute-start.18 = (bf16[64,1536]{1,0:T(8,128)(2,1)S(1)}, bf16[64,1536]{1,0:T(8,128)(2,1)S(1)}, u32[]{:S(2)}, u32[]{:S(2)}) collective-permute-start(bf16[64,1536]{1,0:T(8,128)(2,1)S(1)} %get-tuple-element.57.refs_1_), channel_id=1, source_target_pairs={{0,7},{1,2},{2,1},{3,4},{4,3},{5,6},{6,5},{7,0},{8,9},{9,8},{10,11... | collective-permute-start | bytes 589832 | tf_op jit(solution)/shard_map/ppermute | solution.py:34
  73.0 5.7 %collective-permute-start.17 = (bf16[64,1536]{1,0:T(8,128)(2,1)S(1)}, bf16[64,1536]{1,0:T(8,128)(2,1)S(1)}, u32[]{:S(2)}, u32[]{:S(2)}) collective-permute-start(bf16[64,1536]{1,0:T(8,128)(2,1)S(1)} %get-tuple-element.57.refs_1_), channel_id=1, source_target_pairs={{0,1},{1,0},{2,3},{3,2},{4,5},{5,4},{6,7},{7,6},{8,15},{9,10},{10,... | collective-permute-start | bytes 589832 | tf_op jit(solution)/shard_map/ppermute | solution.py:34
  78.3 6.9 %collective-permute-start.19 = (bf16[64,1536]{1,0:T(8,128)(2,1)S(1)}, bf16[64,1536]{1,0:T(8,128)(2,1)S(1)}, u32[]{:S(2)}, u32[]{:S(2)}) collective-permute-start(bf16[64,1536]{1,0:T(8,128)(2,1)S(1)} %collective-permute-done.18.refs_0_), channel_id=1, source_target_pairs={{0,1},{1,0},{2,3},{3,2},{4,5},{5,4},{6,7},{7,6},{8,15},{9,10},{10,... | collective-permute-start | bytes 589832 | tf_op jit(solution)/shard_map/ppermute | solution.py:34
  78.7 11.8 %collective-permute-start.20 = (bf16[64,1536]{1,0:T(8,128)(2,1)S(1)}, bf16[64,1536]{1,0:T(8,128)(2,1)S(1)}, u32[]{:S(2)}, u32[]{:S(2)}) collective-permute-start(bf16[64,1536]{1,0:T(8,128)(2,1)S(1)} %collective-permute-done.17.refs_2_), channel_id=1, source_target_pairs={{0,7},{1,2},{2,1},{3,4},{4,3},{5,6},{6,5},{7,0},{8,9},{9,8},{10,11... | collective-permute-start | bytes 589832 | tf_op jit(solution)/shard_map/ppermute | solution.py:34
  85.2 8.7 %collective-permute-start.23 = (bf16[64,1536]{1,0:T(8,128)(2,1)S(1)}, bf16[64,1536]{1,0:T(8,128)(2,1)S(1)}, u32[]{:S(2)}, u32[]{:S(2)}) collective-permute-start(bf16[64,1536]{1,0:T(8,128)(2,1)S(1)} %collective-permute-done.19.refs_3_), channel_id=1, source_target_pairs={{0,7},{1,2},{2,1},{3,4},{4,3},{5,6},{6,5},{7,0},{8,9},{9,8},{10,11... | collective-permute-start | bytes 589832 | tf_op jit(solution)/shard_map/ppermute | solution.py:34
  88.7 6.7 %collective-permute-start.22 = (bf16[64,1536]{1,0:T(8,128)(2,1)S(1)}, bf16[64,1536]{1,0:T(8,128)(2,1)S(1)}, u32[]{:S(2)}, u32[]{:S(2)}) collective-permute-start(bf16[64,1536]{1,0:T(8,128)(2,1)S(1)} %collective-permute-done.19.refs_3_), channel_id=1, source_target_pairs={{0,6},{1,3},{2,0},{3,5},{4,2},{5,7},{6,4},{7,1},{8,10},{9,15},{10,... | collective-permute-start | bytes 589832 | tf_op jit(solution)/shard_map/ppermute | solution.py:34
  90.5 6.9 %collective-permute-start.21 = (bf16[64,1536]{1,0:T(8,128)(2,1)S(1)}, bf16[64,1536]{1,0:T(8,128)(2,1)S(1)}, u32[]{:S(2)}, u32[]{:S(2)}) collective-permute-start(bf16[64,1536]{1,0:T(8,128)(2,1)S(1)} %collective-permute-done.20.refs_7_), channel_id=1, source_target_pairs={{0,1},{1,0},{2,3},{3,2},{4,5},{5,4},{6,7},{7,6},{8,15},{9,10},{10,... | collective-permute-start | bytes 589832 | tf_op jit(solution)/shard_map/ppermute | solution.py:34
  99.4 1.5 %collective-permute-start.25 = (bf16[64,1536]{1,0:T(8,128)(2,1)S(1)}, bf16[64,1536]{1,0:T(8,128)(2,1)S(1)}, u32[]{:S(2)}, u32[]{:S(2)}) collective-permute-start(bf16[64,1536]{1,0:T(8,128)(2,1)S(1)} %get-tuple-element.49), channel_id=1, source_target_pairs={{0,8},{1,9},{2,10},{3,11},{4,12},{5,13},{6,14},{7,15},{8,0},{9,1},... | collective-permute-start | bytes 589832 | tf_op jit(solution)/shard_map/ppermute | solution.py:34
  99.5 10.3 %collective-permute-start.24 = (bf16[64,1536]{1,0:T(8,128)(2,1)S(1)}, bf16[64,1536]{1,0:T(8,128)(2,1)S(1)}, u32[]{:S(2)}, u32[]{:S(2)}) collective-permute-start(bf16[64,1536]{1,0:T(8,128)(2,1)S(1)} %get-tuple-element.47), channel_id=1, source_target_pairs={{0,8},{1,9},{2,10},{3,11},{4,12},{5,13},{6,14},{7,15},{8,0},{9,1},... | collective-permute-start | bytes 589832 | tf_op jit(solution)/shard_map/ppermute | solution.py:34
  100.0 2.2 %collective-permute-start.27 = (bf16[64,1536]{1,0:T(8,128)(2,1)S(1)}, bf16[64,1536]{1,0:T(8,128)(2,1)S(1)}, u32[]{:S(2)}, u32[]{:S(2)}) collective-permute-start(bf16[64,1536]{1,0:T(8,128)(2,1)S(1)} %get-tuple-element.51), channel_id=1, source_target_pairs={{0,8},{1,9},{2,10},{3,11},{4,12},{5,13},{6,14},{7,15},{8,0},{9,1},... | collective-permute-start | bytes 589832 | tf_op jit(solution)/shard_map/ppermute | solution.py:34
  100.1 4.3 %collective-permute-start.29 = (bf16[64,1536]{1,0:T(8,128)(2,1)S(1)}, bf16[64,1536]{1,0:T(8,128)(2,1)S(1)}, u32[]{:S(2)}, u32[]{:S(2)}) collective-permute-start(bf16[64,1536]{1,0:T(8,128)(2,1)S(1)} %get-tuple-element.53), channel_id=1, source_target_pairs={{0,8},{1,9},{2,10},{3,11},{4,12},{5,13},{6,14},{7,15},{8,0},{9,1},... | collective-permute-start | bytes 589832 | tf_op jit(solution)/shard_map/ppermute | solution.py:34
  101.0 8.8 %collective-permute-start.26 = (bf16[64,1536]{1,0:T(8,128)(2,1)S(1)}, bf16[64,1536]{1,0:T(8,128)(2,1)S(1)}, u32[]{:S(2)}, u32[]{:S(2)}) collective-permute-start(bf16[64,1536]{1,0:T(8,128)(2,1)S(1)} %add_convert_fusion.2), channel_id=1, source_target_pairs={{0,16},{1,17},{2,18},{3,19},{4,20},{5,21},{6,22},{7,23},{8,72},{9,... | collective-permute-start | bytes 589832 | tf_op jit(solution)/shard_map/ppermute | solution.py:34
  102.3 7.5 %collective-permute-start.28 = (bf16[64,1536]{1,0:T(8,128)(2,1)S(1)}, bf16[64,1536]{1,0:T(8,128)(2,1)S(1)}, u32[]{:S(2)}, u32[]{:S(2)}) collective-permute-start(bf16[64,1536]{1,0:T(8,128)(2,1)S(1)} %add_convert_fusion.1), channel_id=1, source_target_pairs={{0,48},{1,49},{2,50},{3,51},{4,52},{5,53},{6,54},{7,55},{8,200},{9... | collective-permute-start | bytes 589832 | tf_op jit(solution)/shard_map/ppermute | solution.py:34
  104.5 7.5 %collective-permute-start.30 = (bf16[64,1536]{1,0:T(8,128)(2,1)S(1)}, bf16[64,1536]{1,0:T(8,128)(2,1)S(1)}, u32[]{:S(2)}, u32[]{:S(2)}) collective-permute-start(bf16[64,1536]{1,0:T(8,128)(2,1)S(1)} %add_convert_fusion), channel_id=1, source_target_pairs={{0,32},{1,33},{2,34},{3,35},{4,36},{5,37},{6,38},{7,39},{8,136},{9... | collective-permute-start | bytes 589832 | tf_op jit(solution)/shard_map/ppermute | solution.py:34
  112.2 5.6 %collective-permute-start.31 = (bf16[16,1536]{1,0:T(8,128)(2,1)S(1)}, bf16[16,1536]{1,0:T(8,128)(2,1)S(1)}, u32[]{:S(2)}, u32[]{:S(2)}) collective-permute-start(bf16[16,1536]{1,0:T(8,128)(2,1)S(1)} %get-tuple-element.59), channel_id=1, source_target_pairs={{0,64},{1,65},{2,66},{3,67},{4,68},{5,69},{6,70},{7,71},{8,24},{9,... | collective-permute-start | bytes 147464 | tf_op jit(solution)/shard_map/ppermute | solution.py:34
  113.7 5.6 %collective-permute-start.33 = (bf16[16,1536]{1,0:T(8,128)(2,1)S(1)}, bf16[16,1536]{1,0:T(8,128)(2,1)S(1)}, u32[]{:S(2)}, u32[]{:S(2)}) collective-permute-start(bf16[16,1536]{1,0:T(8,128)(2,1)S(1)} %get-tuple-element.60), channel_id=1, source_target_pairs={{0,128},{1,129},{2,130},{3,131},{4,132},{5,133},{6,134},{7,135},{8... | collective-permute-start | bytes 147464 | tf_op jit(solution)/shard_map/ppermute | solution.py:34
  115.9 4.1 %collective-permute-start.32 = (bf16[16,1536]{1,0:T(8,128)(2,1)S(1)}, bf16[16,1536]{1,0:T(8,128)(2,1)S(1)}, u32[]{:S(2)}, u32[]{:S(2)}) collective-permute-start(bf16[16,1536]{1,0:T(8,128)(2,1)S(1)} %get-tuple-element.61), channel_id=1, source_target_pairs={{0,192},{1,193},{2,194},{3,195},{4,196},{5,197},{6,198},{7,199},{8... | collective-permute-start | bytes 147464 | tf_op jit(solution)/shard_map/ppermute | solution.py:34

commit v4 on v2

--- a/solution.py
+++ b/solution.py
@@ -9,8 +9,7 @@
 F32, BF16 = jnp.float32, jnp.bfloat16
 
 NX, NY, NC, NZ = 4, 4, 2, 8
-GATHER_SHIFT = (0, 2, 3, 1)
-SUM_SHIFT = (0, 1, 3, 2)
+GATHER_X, GATHER_Y, SUM = (0, 1, 3, 2), (0, 2, 3, 1), (0, 1, 3, 2)
 TOKENS_OWN = 16
 TOKENS_Z = 64
 TOKENS = 512
@@ -34,19 +33,16 @@
     return lax.ppermute(value, ("row", "col"), pairs_of(target))
 
 
-def send_x(value, shift):
-    return send(value, lambda x, y, c, z: (x + shift, y, c, z))
-
-
-def send_y(value, shift):
-    return send(value, lambda x, y, c, z: (x, y + shift, c, z))
-
-
-def send_plane(value, shift, x_core):
-    return send(
-        value,
-        lambda x, y, c, z: (x + shift, y, c, z) if c == x_core else (x, y + shift, c, z),
-    )
+def send_x(value, k):
+    return send(value, lambda x, y, c, z: (x ^ k, y, c, z))
+
+
+def send_y(value, k):
+    return send(value, lambda x, y, c, z: (x, y ^ k, c, z))
+
+
+def send_plane(value, k, x_core):
+    return send(value, lambda x, y, c, z: (x ^ k, y, c, z) if c == x_core else (x, y ^ k, c, z))
 
 
 def send_core(value):
@@ -67,7 +63,7 @@
 def gathered_row(core_shift, i, p):
     row = lax.axis_index("row")
     x, y, c = row // (NY * NC), (row // NC) % NY, row % NC
-    x, y = (x + NX - GATHER_SHIFT[p]) % NX, (y + NY - GATHER_SHIFT[i]) % NY
+    x, y = x ^ GATHER_X[p], y ^ GATHER_Y[i]
     return row_of((x * NY + y) * NC + (c + core_shift) % NC)
 
 
@@ -75,8 +71,8 @@
     row = lax.axis_index("row")
     x, y, c = row // (NY * NC), (row // NC) % NY, row % NC
     core = (c + core_shift) % NC
-    x = (x + jnp.where(core == 1, SUM_SHIFT[i], SUM_SHIFT[p])) % NX
-    y = (y + jnp.where(core == 1, SUM_SHIFT[p], SUM_SHIFT[i])) % NY
+    x = x ^ jnp.where(core == 1, SUM[i], SUM[p])
+    y = y ^ jnp.where(core == 1, SUM[p], SUM[i])
     return row_of((x * NY + y) * NC + core)
 
 
@@ -112,11 +108,14 @@
 
 
 def multiply(rows, w_ref, outs):
-    for start in range(0, w_ref.shape[1], TILE):
-        columns = slice(start, start + TILE)
-        product = jnp.dot(rows, w_ref[:, columns], preferred_element_type=F32)
-        for k, out in enumerate(outs):
-            out[:, columns] = product[k * TOKENS_Z : (k + 1) * TOKENS_Z, :].astype(out.dtype)
+    half = w_ref.shape[1] // 2
+    blocks = len(outs) // 2
+    for h in range(2):
+        product = jnp.dot(
+            rows, w_ref[:, h * half : (h + 1) * half], preferred_element_type=F32
+        ).astype(BF16)
+        for k in range(blocks):
+            outs[h * blocks + k][...] = product[k * TOKENS_Z : (k + 1) * TOKENS_Z, :]
 
 
 def far_kernel(*refs):
@@ -140,9 +139,9 @@
     return pl.pallas_call(
         far_kernel,
         in_specs=[WHOLE] * 9,
-        out_specs=[WHOLE] * 5,
+        out_specs=[WHOLE] * 9,
         out_shape=[jax.ShapeDtypeStruct((TOKENS, depth), BF16)]
-        + [jax.ShapeDtypeStruct((TOKENS_Z, width), BF16)] * 4,
+        + [jax.ShapeDtypeStruct((TOKENS_Z, width // 2), BF16)] * 8,
         **settings(weight, 16),
     )(*pieces, weight)
 
@@ -151,8 +150,8 @@
     return pl.pallas_call(
         near_kernel,
         in_specs=[WHOLE] * 2,
-        out_specs=[WHOLE] * 4,
-        out_shape=[jax.ShapeDtypeStruct((TOKENS_Z, weight.shape[1]), BF16)] * 4,
+        out_specs=[WHOLE] * 8,
+        out_shape=[jax.ShapeDtypeStruct((TOKENS_Z, weight.shape[1] // 2), BF16)] * 8,
         **settings(weight, 16),
     )(normed, weight)
 
@@ -161,9 +160,19 @@
     return lax.dot_general(rows, weight, (((1,), (1,)), ((), ())), preferred_element_type=F32)
 
 
+def fill(rows_ref, pieces, blocks):
+    half = rows_ref.shape[1] // 2
+    for h in range(2):
+        for k in range(blocks):
+            rows_ref[
+                k * TOKENS_Z : (k + 1) * TOKENS_Z, h * half : (h + 1) * half
+            ] = pieces[h * blocks + k][...]
+
+
 def near_back_kernel(*refs):
-    pieces, w_ref, out_ref = refs[:4], refs[4], refs[5]
-    rows = jnp.concatenate([piece[...] for piece in pieces], axis=0)
+    pieces, w_ref, out_ref, rows_ref = refs[:8], refs[8], refs[9], refs[10]
+    fill(rows_ref, pieces, 4)
+    rows = rows_ref[...]
     for start in range(0, w_ref.shape[0], TILE):
         part = slice(start, start + TILE)
         out_ref[:, part] = transposed_dot(rows, w_ref[part, :]).astype(out_ref.dtype)
@@ -172,19 +181,19 @@
 def near_back(pieces, weight):
     return pl.pallas_call(
         near_back_kernel,
-        in_specs=[WHOLE] * 5,
+        in_specs=[WHOLE] * 9,
         out_specs=WHOLE,
         out_shape=jax.ShapeDtypeStruct((HALF, weight.shape[0]), BF16),
+        scratch_shapes=[pltpu.VMEM((HALF, weight.shape[1]), BF16)],
         **settings(weight, 16),
     )(*pieces, weight)
 
 
 def far_back_kernel(*refs):
     pieces, near_ref, w_ref, slopes_ref, outs, product = (
-        refs[:8], refs[8], refs[9], refs[10], refs[11:19], refs[19]
+        refs[:16], refs[16], refs[17], refs[18], refs[19:27], refs[27]
     )
-    for k in range(NZ):
-        slopes_ref[k * TOKENS_Z : (k + 1) * TOKENS_Z, :] = pieces[k][...]
+    fill(slopes_ref, pieces, NZ)
     product[:HALF, :] = near_ref[...].astype(F32)
     rows = slopes_ref[HALF:, :]
     for start in range(0, w_ref.shape[0], TILE):
@@ -202,7 +211,7 @@
     depth, width = weight.shape
     return pl.pallas_call(
         far_back_kernel,
-        in_specs=[WHOLE] * 10,
+        in_specs=[WHOLE] * 18,
         out_specs=[WHOLE] * 9,
         out_shape=[jax.ShapeDtypeStruct((TOKENS, width), BF16)]
         + [jax.ShapeDtypeStruct((TOKENS_Z, depth), BF16)] * 8,
@@ -256,37 +265,43 @@
 def per_device(inputs, gain, bias, weight, d_act):
     normed = normalize(inputs, gain, bias)
 
-    along_x = jnp.concatenate([normed] + [send_x(normed, s) for s in GATHER_SHIFT[1:]])
-    along_y = [along_x] + [send_y(along_x, s) for s in GATHER_SHIFT[1:]]
+    along_x = jnp.concatenate([normed] + [send_x(normed, s) for s in GATHER_X[1:]])
+    along_y = [along_x] + [send_y(along_x, s) for s in GATHER_Y[1:]]
     weight, _ = lax.optimization_barrier((weight, along_x))
     along_y[3], weight = lax.optimization_barrier((along_y[3], stage(weight)))
     other = [send_core(v) for v in along_y]
 
     gathered, *far = far_pre(along_y + other, weight)
-    back, own, one, two = near_pre(gathered, weight)
-    longer = reduce_chain([far[1], far[2], two, back])
-    shorter = reduce_chain([far[0], far[3], one])
-
-    pre = add(own, longer, shorter)
-    slopes = jax.vjp(gelu_tanh, pre)[1](d_act.astype(F32))[0].astype(BF16)
-    block_1, block_6, block_3, block_4 = gather_chain(slopes, 1, 4)
-    block_7, block_2, block_5 = gather_chain(slopes, -1, 3)
-    pieces = [block_7, slopes, block_1, block_2, block_3, block_4, block_5, block_6]
-    pre, _ = lax.optimization_barrier((pre, block_1))
-    activated = gelu_tanh(pre).astype(BF16)
-
-    near = near_back(pieces[:4], weight)
+    near = near_pre(gathered, weight)
+    half = weight.shape[1] // 2
+    d_halves = lax.optimization_barrier((d_act[:, :half], d_act[:, half:]))
+    pres, pieces, nearest = [], [], []
+    for h in range(2):
+        three, four, five, six = far[4 * h : 4 * h + 4]
+        back, own, one, two = near[4 * h : 4 * h + 4]
+        longer = reduce_chain([four, five, two, back])
+        shorter = reduce_chain([three, six, one])
+        pre = add(own, longer, shorter)
+        slopes = jax.vjp(gelu_tanh, pre)[1](d_halves[h].astype(F32))[0].astype(BF16)
+        block_1, block_6, block_3, block_4 = gather_chain(slopes, 1, 4)
+        block_7, block_2, block_5 = gather_chain(slopes, -1, 3)
+        nearest += [block_7, slopes, block_1, block_2]
+        pieces += [block_7, slopes, block_1, block_2, block_3, block_4, block_5, block_6]
+        pres.append(lax.optimization_barrier((pre, block_1))[0])
+    activated = jnp.concatenate([gelu_tanh(pre).astype(BF16) for pre in pres], axis=1)
+
+    near = near_back(nearest, weight)
     slopes_all, *parts = far_back(pieces, near, weight)
     d_weight = lax.dot_general(
         gathered, slopes_all, (((0,), (0,)), ((), ())), preferred_element_type=F32
     ).astype(BF16)
 
     sums = [add(parts[i], send_core(parts[4 + i])) for i in range(4)]
-    arrived = [send_plane(sums[i].astype(BF16), SUM_SHIFT[i], 1) for i in range(1, 4)]
+    arrived = [send_plane(sums[i].astype(BF16), SUM[i], 1) for i in range(1, 4)]
     line = add(sums[0], *arrived)
     line, d_weight = lax.optimization_barrier((line, d_weight))
     blocks = [line[i * TOKENS_OWN : (i + 1) * TOKENS_OWN] for i in range(4)]
-    arrived = [send_plane(blocks[i].astype(BF16), SUM_SHIFT[i], 0) for i in range(1, 4)]
+    arrived = [send_plane(blocks[i].astype(BF16), SUM[i], 0) for i in range(1, 4)]
     d_normed = add(blocks[0], *arrived).astype(BF16)
     return (activated, d_normed, d_weight)
 

time: 120 us -> 117 us (0.975)
  waiting for transfers between devices: 53.7 us -> 24.5 us
  starting transfers between devices: 30.1 us -> 55.4 us
    ppermute x34 -> x48, waiting for transfers between devices: 53.7 us -> 24.5 us  [send(): return lax.ppermute(value, ('row', 'col'), pairs_of(target))]
    ppermute x34 -> x48, starting transfers between devices: 30.1 us -> 55.4 us  [send(): return lax.ppermute(value, ('row', 'col'), pairs_of(target))]
  transfers between devices with their start and end apart: 34 -> 48, of which waited for: 22 -> 20; matrix products, arithmetic and copies ran while one was open for 5% -> 5% of each run, Pallas kernels for 4% -> 4%
where the time goes in v4:
time: 117 us; the launch traced here: 115 us
  starting transfers between devices  55.4 us (47%)
  waiting for transfers between devices  24.5 us (21%)
  blocking collectives  16 us (14%)
  Pallas kernels  8.75 us (7%)
  other arithmetic  5.59 us (5%)
  matrix products  4.27 us (4%)
    ppermute x48, starting transfers between devices, send(): return lax.ppermute(value, ('row', 'col'), pairs_of(target))  55.4 us
    ppermute x48, waiting for transfers between devices, send(): return lax.ppermute(value, ('row', 'col'), pairs_of(target))  24.5 us
    all_to_all x1, blocking collectives, normalize(): lax.all_to_all(jnp.broadcast_to(stats[None], (NZ,) + stats.shape), 'col',...  16 us
    dot_general x1, matrix products, per_device(): lax.dot_general(gathered, slopes_all, (((0,), (0,)), ((), ())), preferred...  4.27 us
    pallas_call x1, Pallas kernels, stage(): pl.pallas_call(stage_kernel, in_specs=[pl.BlockSpec(memory_space=pl.ANY)]...  2.34 us
  transfers between devices with their start and end apart: 48, of which 20 were waited for; matrix products, arithmetic and copies ran while one was open for 5% of the time, Pallas kernels for 4%

profile of v4, /device:TPU:2, one launch (start us, length us, event | category | flops | bytes accessed | tf_op | source)
XLA Modules:
  0.0 115.5 jit_solution(7758471454029158914)
XLA Ops:
  0.6 1.0 reduce_sum.45
  1.7 1.1 multiply_reduce_fusion
  2.8 16.0 %all_to_all.5 = f32[8,2,16]{2,1,0:T(2,128)S(1)} all-to-all(f32[8,2,16]{2,1,0:T(2,128)S(1)} %broadcast_in_dim.2), channel_id=1, replica_groups=mesh['row'=32,'col'=8] {'col'}, dimensions={0} | all-to-all | bytes 2048 | tf_op jit(solution)/shard_map/all_to_all | solution.py:240
  18.8 1.0 add_convert_fusion.14
  19.8 2.2 %collective-permute-start.2 = (bf16[16,1536]{1,0:T(8,128)(2,1)S(1)}, bf16[16,1536]{1,0:T(8,128)(2,1)S(1)}, u32[]{:S(2)}, u32[]{:S(2)}) collective-permute-start(bf16[16,1536]{1,0:T(8,128)(2,1)S(1)} %add_convert_fusion.14), channel_id=1, source_target_pairs={{0,128},{1,129},{2,130},{3,131},{4,132},{5,133},{6,134},{7,135},{8... | collective-permute-start | bytes 147464 | tf_op jit(solution)/shard_map/ppermute | solution.py:33
  22.1 2.6 %collective-permute-start = (bf16[16,1536]{1,0:T(8,128)(2,1)S(1)}, bf16[16,1536]{1,0:T(8,128)(2,1)S(1)}, u32[]{:S(2)}, u32[]{:S(2)}) collective-permute-start(bf16[16,1536]{1,0:T(8,128)(2,1)S(1)} %add_convert_fusion.14), channel_id=1, source_target_pairs={{0,64},{1,65},{2,66},{3,67},{4,68},{5,69},{6,70},{7,71},{8,72},{9,... | collective-permute-start | bytes 147464 | tf_op jit(solution)/shard_map/ppermute | solution.py:33
  24.6 0.9 collective-permute-done.2
  25.5 0.6 collective-permute-done.1
  26.7 1.7 %collective-permute-start.5 = (bf16[64,1536]{1,0:T(8,128)(2,1)S(1)}, bf16[64,1536]{1,0:T(8,128)(2,1)S(1)}, u32[]{:S(2)}, u32[]{:S(2)}) collective-permute-start(bf16[64,1536]{1,0:T(8,128)(2,1)S(1)} %pad_maximum_fusion.refs_0_), channel_id=1, source_target_pairs={{0,16},{1,17},{2,18},{3,19},{4,20},{5,21},{6,22},{7,23},{8,24},{9,... | collective-permute-start | bytes 589832 | tf_op jit(solution)/shard_map/ppermute | solution.py:33
  28.4 2.2 %collective-permute-start.4 = (bf16[64,1536]{1,0:T(8,128)(2,1)S(1)}, bf16[64,1536]{1,0:T(8,128)(2,1)S(1)}, u32[]{:S(2)}, u32[]{:S(2)}) collective-permute-start(bf16[64,1536]{1,0:T(8,128)(2,1)S(1)} %pad_maximum_fusion.refs_0_), channel_id=1, source_target_pairs={{0,48},{1,49},{2,50},{3,51},{4,52},{5,53},{6,54},{7,55},{8,56},{9,... | collective-permute-start | bytes 589832 | tf_op jit(solution)/shard_map/ppermute | solution.py:33
  30.6 0.7 collective-permute-start.3
  31.3 2.3 %shard_map.76.refs_8_.w_ref.refs_17_ = bf16[1536,1536]{1,0:T(8,128)(2,1)S(1)} custom-call(bf16[1536,1536]{1,0:T(8,128)(2,1)} %w_ref), custom_call_target="tpu_custom_call" | custom-call | flops 1207959552 | bytes 4718592 | tf_op jit(solution)/shard_map/pallas_call | solution.py:100
  34.3 1.7 %collective-permute-done.4.refs_2_ = bf16[64,1536]{1,0:T(8,128)(2,1)S(1)} collective-permute-done((bf16[64,1536]{1,0:T(8,128)(2,1)S(1)}, bf16[64,1536]{1,0:T(8,128)(2,1)S(1)}, u32[]{:S(2)}, u32[]{:S(2)}) %collective-permute-start.4) | collective-permute-done | bytes 196640 | tf_op jit(solution)/shard_map/ppermute | solution.py:33
  36.0 1.8 %collective-permute-done.3.refs_1_ = bf16[64,1536]{1,0:T(8,128)(2,1)S(1)} collective-permute-done((bf16[64,1536]{1,0:T(8,128)(2,1)S(1)}, bf16[64,1536]{1,0:T(8,128)(2,1)S(1)}, u32[]{:S(2)}, u32[]{:S(2)}) %collective-permute-start.3) | collective-permute-done | bytes 196640 | tf_op jit(solution)/shard_map/ppermute | solution.py:33
  37.8 1.4 %collective-permute-done.7.refs_5_ = bf16[64,1536]{1,0:T(8,128)(2,1)S(1)} collective-permute-done((bf16[64,1536]{1,0:T(8,128)(2,1)S(1)}, bf16[64,1536]{1,0:T(8,128)(2,1)S(1)}, u32[]{:S(2)}, u32[]{:S(2)}) %collective-permute-start.7) | collective-permute-done | bytes 196640 | tf_op jit(solution)/shard_map/ppermute | solution.py:33
  39.2 1.7 %shard_map.77 = (bf16[512,1536]{1,0:T(8,128)(2,1)S(1)}, bf16[64,768]{1,0:T(8,128)(2,1)S(1)}, bf16[64,768]{1,0:T(8,128)(2,1)S(1)}, bf16[64,768]{1,0:T(8,128)(2,1)...) custom-call(bf16[64,1536]{1,0:T(8,128)(2,1)S(1)} %pad_maximum_fusion, ...), custom_call_target="tpu_custom_call" | custom-call | flops 1207959552 | bytes 4718592 | tf_op jit(solution)/shard_map/pallas_call | solution.py:139
  40.9 0.7 collective-permute-start.10
  41.6 1.4 %collective-permute-start.14 = (bf16[64,768]{1,0:T(8,128)(2,1)S(1)}, bf16[64,768]{1,0:T(8,128)(2,1)S(1)}, u32[]{:S(2)}, u32[]{:S(2)}) collective-permute-start(bf16[64,768]{1,0:T(8,128)(2,1)S(1)} %get-tuple-element.49), channel_id=1, source_target_pairs={{0,1},{1,0},{2,3},{3,2},{4,5},{5,4},{6,7},{7,6},{8,15},{9,10},{10,... | collective-permute-start | bytes 294920 | tf_op jit(solution)/shard_map/ppermute | solution.py:33
  43.0 0.6 collective-permute-start.18
  43.6 1.4 %collective-permute-start.22 = (bf16[64,768]{1,0:T(8,128)(2,1)S(1)}, bf16[64,768]{1,0:T(8,128)(2,1)S(1)}, u32[]{:S(2)}, u32[]{:S(2)}) collective-permute-start(bf16[64,768]{1,0:T(8,128)(2,1)S(1)} %get-tuple-element.59), channel_id=1, source_target_pairs={{0,1},{1,0},{2,3},{3,2},{4,5},{5,4},{6,7},{7,6},{8,15},{9,10},{10,... | collective-permute-start | bytes 294920 | tf_op jit(solution)/shard_map/ppermute | solution.py:33
  45.1 1.4 %shard_map.78 = (bf16[64,768]{1,0:T(8,128)(2,1)S(1)}, bf16[64,768]{1,0:T(8,128)(2,1)S(1)}, bf16[64,768]{1,0:T(8,128)(2,1)S(1)}, bf16[64,768]{1,0:T(8,128)(2,1)S(...) custom-call(bf16[512,1536]{1,0:T(8,128)(2,1)S(1)} %get-tuple-element, ...), custom_call_target="tpu_custom_call" | custom-call | flops 1207959552 | bytes 4718592 | tf_op jit(solution)/shard_map/pallas_call | solution.py:150
  46.5 0.7 collective-permute-start.11
  47.2 2.7 %collective-permute-start.15 = (bf16[64,768]{1,0:T(8,128)(2,1)S(1)}, bf16[64,768]{1,0:T(8,128)(2,1)S(1)}, u32[]{:S(2)}, u32[]{:S(2)}) collective-permute-start(bf16[64,768]{1,0:T(8,128)(2,1)S(1)} %add_convert_fusion.9), channel_id=1, source_target_pairs={{0,7},{1,2},{2,1},{3,4},{4,3},{5,6},{6,5},{7,0},{8,9},{9,8},{10,11... | collective-permute-start | bytes 294920 | tf_op jit(solution)/shard_map/ppermute | solution.py:33
  50.0 0.7 collective-permute-start.19
  50.7 2.9 %collective-permute-start.23 = (bf16[64,768]{1,0:T(8,128)(2,1)S(1)}, bf16[64,768]{1,0:T(8,128)(2,1)S(1)}, u32[]{:S(2)}, u32[]{:S(2)}) collective-permute-start(bf16[64,768]{1,0:T(8,128)(2,1)S(1)} %add_convert_fusion.4), channel_id=1, source_target_pairs={{0,7},{1,2},{2,1},{3,4},{4,3},{5,6},{6,5},{7,0},{8,9},{9,8},{10,11... | collective-permute-start | bytes 294920 | tf_op jit(solution)/shard_map/ppermute | solution.py:33
  53.8 2.1 %collective-permute-start.16 = (bf16[64,768]{1,0:T(8,128)(2,1)S(1)}, bf16[64,768]{1,0:T(8,128)(2,1)S(1)}, u32[]{:S(2)}, u32[]{:S(2)}) collective-permute-start(bf16[64,768]{1,0:T(8,128)(2,1)S(1)} %add_convert_fusion.8), channel_id=1, source_target_pairs={{0,1},{1,0},{2,3},{3,2},{4,5},{5,4},{6,7},{7,6},{8,15},{9,10},{10,... | collective-permute-start | bytes 294920 | tf_op jit(solution)/shard_map/ppermute | solution.py:33
  56.2 2.0 %collective-permute-done.23 = bf16[64,768]{1,0:T(8,128)(2,1)S(1)} collective-permute-done((bf16[64,768]{1,0:T(8,128)(2,1)S(1)}, bf16[64,768]{1,0:T(8,128)(2,1)S(1)}, u32[]{:S(2)}, u32[]{:S(2)}) %collective-permute-start.23) | collective-permute-done | bytes 98336 | tf_op jit(solution)/shard_map/ppermute | solution.py:33
  58.4 2.0 %collective-permute-start.13 = (bf16[64,768]{1,0:T(8,128)(2,1)S(1)}, bf16[64,768]{1,0:T(8,128)(2,1)S(1)}, u32[]{:S(2)}, u32[]{:S(2)}) collective-permute-start(bf16[64,768]{1,0:T(8,128)(2,1)S(1)} %add_convert_fusion.10), channel_id=1, source_target_pairs={{0,7},{1,2},{2,1},{3,4},{4,3},{5,6},{6,5},{7,0},{8,9},{9,8},{10,11... | collective-permute-start | bytes 294920 | tf_op jit(solution)/shard_map/ppermute | solution.py:33
  60.4 0.6 collective-permute-done.20
  61.1 1.5 %collective-permute-start.21 = (bf16[64,768]{1,0:T(8,128)(2,1)S(1)}, bf16[64,768]{1,0:T(8,128)(2,1)S(1)}, u32[]{:S(2)}, u32[]{:S(2)}) collective-permute-start(bf16[64,768]{1,0:T(8,128)(2,1)S(1)} %add_convert_fusion.5), channel_id=1, source_target_pairs={{0,7},{1,2},{2,1},{3,4},{4,3},{5,6},{6,5},{7,0},{8,9},{9,8},{10,11... | collective-permute-start | bytes 294920 | tf_op jit(solution)/shard_map/ppermute | solution.py:33
  62.6 1.7 %collective-permute-done.13 = bf16[64,768]{1,0:T(8,128)(2,1)S(1)} collective-permute-done((bf16[64,768]{1,0:T(8,128)(2,1)S(1)}, bf16[64,768]{1,0:T(8,128)(2,1)S(1)}, u32[]{:S(2)}, u32[]{:S(2)}) %collective-permute-start.13) | collective-permute-done | bytes 98336 | tf_op jit(solution)/shard_map/ppermute | solution.py:33
  64.5 0.9 collective-permute-start.17
  65.3 2.5 %collective-permute-done.21 = bf16[64,768]{1,0:T(8,128)(2,1)S(1)} collective-permute-done((bf16[64,768]{1,0:T(8,128)(2,1)S(1)}, bf16[64,768]{1,0:T(8,128)(2,1)S(1)}, u32[]{:S(2)}, u32[]{:S(2)}) %collective-permute-start.21) | collective-permute-done | bytes 98336 | tf_op jit(solution)/shard_map/ppermute | solution.py:33
  68.1 1.7 %collective-permute-start.26 = (bf16[64,768]{1,0:T(8,128)(2,1)S(1)}, bf16[64,768]{1,0:T(8,128)(2,1)S(1)}, u32[]{:S(2)}, u32[]{:S(2)}) collective-permute-start(bf16[64,768]{1,0:T(8,128)(2,1)S(1)} %get-tuple-element.73.refs_1_), channel_id=1, source_target_pairs={{0,7},{1,2},{2,1},{3,4},{4,3},{5,6},{6,5},{7,0},{8,9},{9,8},{10,11... | collective-permute-start | bytes 294920 | tf_op jit(solution)/shard_map/ppermute | solution.py:33
  69.8 1.6 %collective-permute-start.32 = (bf16[64,768]{1,0:T(8,128)(2,1)S(1)}, bf16[64,768]{1,0:T(8,128)(2,1)S(1)}, u32[]{:S(2)}, u32[]{:S(2)}) collective-permute-start(bf16[64,768]{1,0:T(8,128)(2,1)S(1)} %get-tuple-element.75.refs_5_.refs_9_), channel_id=1, source_target_pairs={{0,7},{1,2},{2,1},{3,4},{4,3},{5,6},{6,5},{7,0},{8,9},{9,8},{10,11... | collective-permute-start | bytes 294920 | tf_op jit(solution)/shard_map/ppermute | solution.py:33
  71.5 1.6 %collective-permute-start.28 = (bf16[64,768]{1,0:T(8,128)(2,1)S(1)}, bf16[64,768]{1,0:T(8,128)(2,1)S(1)}, u32[]{:S(2)}, u32[]{:S(2)}) collective-permute-start(bf16[64,768]{1,0:T(8,128)(2,1)S(1)} %collective-permute-done.17.refs_2_), channel_id=1, source_target_pairs={{0,7},{1,2},{2,1},{3,4},{4,3},{5,6},{6,5},{7,0},{8,9},{9,8},{10,11... | collective-permute-start | bytes 294920 | tf_op jit(solution)/shard_map/ppermute | solution.py:33
  73.1 0.8 collective-permute-done.25.refs_6_.refs_10_
  73.9 1.2 %collective-permute-start.34 = (bf16[64,768]{1,0:T(8,128)(2,1)S(1)}, bf16[64,768]{1,0:T(8,128)(2,1)S(1)}, u32[]{:S(2)}, u32[]{:S(2)}) collective-permute-start(bf16[64,768]{1,0:T(8,128)(2,1)S(1)} %collective-permute-done.25.refs_6_.refs_10_), channel_id=1, source_target_pairs={{0,7},{1,2},{2,1},{3,4},{4,3},{5,6},{6,5},{7,0},{8,9},{9,8},{10,11... | collective-permute-start | bytes 294920 | tf_op jit(solution)/shard_map/ppermute | solution.py:33
  75.0 0.8 collective-permute-start.27
  75.8 0.9 collective-permute-done.32.refs_4_.refs_8_
  76.7 1.3 %collective-permute-start.33 = (bf16[64,768]{1,0:T(8,128)(2,1)S(1)}, bf16[64,768]{1,0:T(8,128)(2,1)S(1)}, u32[]{:S(2)}, u32[]{:S(2)}) collective-permute-start(bf16[64,768]{1,0:T(8,128)(2,1)S(1)} %collective-permute-done.32.refs_4_.refs_8_), channel_id=1, source_target_pairs={{0,1},{1,0},{2,3},{3,2},{4,5},{5,4},{6,7},{7,6},{8,15},{9,10},{10,... | collective-permute-start | bytes 294920 | tf_op jit(solution)/shard_map/ppermute | solution.py:33
  77.9 0.9 collective-permute-done.28.refs_7_
  78.8 1.3 %collective-permute-start.29 = (bf16[64,768]{1,0:T(8,128)(2,1)S(1)}, bf16[64,768]{1,0:T(8,128)(2,1)S(1)}, u32[]{:S(2)}, u32[]{:S(2)}) collective-permute-start(bf16[64,768]{1,0:T(8,128)(2,1)S(1)} %collective-permute-done.28.refs_7_), channel_id=1, source_target_pairs={{0,1},{1,0},{2,3},{3,2},{4,5},{5,4},{6,7},{7,6},{8,15},{9,10},{10,... | collective-permute-start | bytes 294920 | tf_op jit(solution)/shard_map/ppermute | solution.py:33
  80.0 0.9 collective-permute-done.34.refs_15_
  80.9 1.2 %collective-permute-start.35 = (bf16[64,768]{1,0:T(8,128)(2,1)S(1)}, bf16[64,768]{1,0:T(8,128)(2,1)S(1)}, u32[]{:S(2)}, u32[]{:S(2)}) collective-permute-start(bf16[64,768]{1,0:T(8,128)(2,1)S(1)} %collective-permute-done.34.refs_15_), channel_id=1, source_target_pairs={{0,1},{1,0},{2,3},{3,2},{4,5},{5,4},{6,7},{7,6},{8,15},{9,10},{10,... | collective-permute-start | bytes 294920 | tf_op jit(solution)/shard_map/ppermute | solution.py:33
  82.1 0.8 collective-permute-start.31
  83.0 2.4 %collective-permute-start.37 = (bf16[64,768]{1,0:T(8,128)(2,1)S(1)}, bf16[64,768]{1,0:T(8,128)(2,1)S(1)}, u32[]{:S(2)}, u32[]{:S(2)}) collective-permute-start(bf16[64,768]{1,0:T(8,128)(2,1)S(1)} %collective-permute-done.33.refs_7_.refs_11_), channel_id=1, source_target_pairs={{0,7},{1,2},{2,1},{3,4},{4,3},{5,6},{6,5},{7,0},{8,9},{9,8},{10,11... | collective-permute-start | bytes 294920 | tf_op jit(solution)/shard_map/ppermute | solution.py:33
  85.4 1.6 %collective-permute-start.30 = (bf16[64,768]{1,0:T(8,128)(2,1)S(1)}, bf16[64,768]{1,0:T(8,128)(2,1)S(1)}, u32[]{:S(2)}, u32[]{:S(2)}) collective-permute-start(bf16[64,768]{1,0:T(8,128)(2,1)S(1)} %collective-permute-done.29.refs_4_), channel_id=1, source_target_pairs={{0,7},{1,2},{2,1},{3,4},{4,3},{5,6},{6,5},{7,0},{8,9},{9,8},{10,11... | collective-permute-start | bytes 294920 | tf_op jit(solution)/shard_map/ppermute | solution.py:33
  87.0 2.0 %collective-permute-start.36 = (bf16[64,768]{1,0:T(8,128)(2,1)S(1)}, bf16[64,768]{1,0:T(8,128)(2,1)S(1)}, u32[]{:S(2)}, u32[]{:S(2)}) collective-permute-start(bf16[64,768]{1,0:T(8,128)(2,1)S(1)} %collective-permute-done.35.refs_12_), channel_id=1, source_target_pairs={{0,7},{1,2},{2,1},{3,4},{4,3},{5,6},{6,5},{7,0},{8,9},{9,8},{10,11... | collective-permute-start | bytes 294920 | tf_op jit(solution)/shard_map/ppermute | solution.py:33
  89.0 1.4 %shard_map.79.refs_16_ = bf16[256,1536]{1,0:T(8,128)(2,1)S(1)} custom-call(bf16[64,768]{1,0:T(8,128)(2,1)S(1)} %collective-permute-done.26.refs_0_, bf16[64,768]{1,0:T(8,128)(2,1)S(1)} %get-tuple-element.73.refs_1_, bf16[64,768]{1,0:T(8,128)(2,1)S(1)} %collective-permute-done.17.refs_2_, bf16[64,768]{1,0:T(8,128)(2,1)S(1)} %collective-permute-done.27.refs_3_, ...), custom_call_target="tpu_custom_call" | custom-call | flops 1207959552 | bytes 4718592 | tf_op jit(solution)/shard_map/pallas_call | solution.py:182
  90.4 0.8 collective-permute-done.30.refs_5_
  91.2 1.6 %collective-permute-done.36.refs_13_ = bf16[64,768]{1,0:T(8,128)(2,1)S(1)} collective-permute-done((bf16[64,768]{1,0:T(8,128)(2,1)S(1)}, bf16[64,768]{1,0:T(8,128)(2,1)S(1)}, u32[]{:S(2)}, u32[]{:S(2)}) %collective-permute-start.36) | collective-permute-done | bytes 98336 | tf_op jit(solution)/shard_map/ppermute | solution.py:33
  92.8 1.9 %shard_map.80 = (bf16[512,1536]{1,0:T(8,128)(2,1)S(1)}, bf16[64,1536]{1,0:T(8,128)(2,1)S(1)}, bf16[64,1536]{1,0:T(8,128)(2,1)S(1)}, bf16[64,1536]{1,0:T(8,128)(2...) custom-call(bf16[64,768]{1,0:T(8,128)(2,1)S(1)} %collective-permute-, ...), custom_call_target="tpu_custom_call" | custom-call | flops 1207959552 | bytes 4718592 | tf_op jit(solution)/shard_map/pallas_call | solution.py:212
  95.0 0.6 collective-permute-start.38
  96.3 0.8 collective-permute-start.40
  97.1 1.6 %collective-permute-start.42 = (bf16[64,1536]{1,0:T(8,128)(2,1)S(1)}, bf16[64,1536]{1,0:T(8,128)(2,1)S(1)}, u32[]{:S(2)}, u32[]{:S(2)}) collective-permute-start(bf16[64,1536]{1,0:T(8,128)(2,1)S(1)} %add_convert_fusion.1), channel_id=1, source_target_pairs={{0,48},{1,49},{2,50},{3,51},{4,52},{5,53},{6,54},{7,55},{8,200},{9... | collective-permute-start | bytes 589832 | tf_op jit(solution)/shard_map/ppermute | solution.py:33
  98.7 2.0 %collective-permute-start.44 = (bf16[64,1536]{1,0:T(8,128)(2,1)S(1)}, bf16[64,1536]{1,0:T(8,128)(2,1)S(1)}, u32[]{:S(2)}, u32[]{:S(2)}) collective-permute-start(bf16[64,1536]{1,0:T(8,128)(2,1)S(1)} %add_convert_fusion), channel_id=1, source_target_pairs={{0,32},{1,33},{2,34},{3,35},{4,36},{5,37},{6,38},{7,39},{8,136},{9... | collective-permute-start | bytes 589832 | tf_op jit(solution)/shard_map/ppermute | solution.py:33
  100.8 4.3 %convolution_convert_fusion = bf16[1536,1536]{1,0:T(8,128)(2,1)} fusion(bf16[512,1536]{1,0:T(8,128)(2,1)S(1)} %get-tuple-element.41.normed_ref, bf16[512,1536]{1,0:T(8,128)(2,1)S(1)} %get-tuple-element.70), kind=kOutput, calls=%fused_computation | convolution fusion | flops 2418278400 | bytes 7864320 | tf_op jit(solution)/shard_map/dot_general | solution.py:295
  105.1 1.2 %collective-permute-done.42 = bf16[64,1536]{1,0:T(8,128)(2,1)S(1)} collective-permute-done((bf16[64,1536]{1,0:T(8,128)(2,1)S(1)}, bf16[64,1536]{1,0:T(8,128)(2,1)S(1)}, u32[]{:S(2)}, u32[]{:S(2)}) %collective-permute-start.42) | collective-permute-done | bytes 196640 | tf_op jit(solution)/shard_map/ppermute | solution.py:33
  106.4 2.8 %collective-permute-start.45 = (bf16[16,1536]{1,0:T(8,128)(2,1)S(1)}, bf16[16,1536]{1,0:T(8,128)(2,1)S(1)}, u32[]{:S(2)}, u32[]{:S(2)}) collective-permute-start(bf16[16,1536]{1,0:T(8,128)(2,1)S(1)} %get-tuple-element.77), channel_id=1, source_target_pairs={{0,64},{1,65},{2,66},{3,67},{4,68},{5,69},{6,70},{7,71},{8,24},{9,... | collective-permute-start | bytes 147464 | tf_op jit(solution)/shard_map/ppermute | solution.py:33
  109.8 1.0 collective-permute-start.46
  110.8 0.7 pad_maximum_fusion.1
  111.5 3.3 %collective-permute-done.47 = bf16[16,1536]{1,0:T(8,128)(2,1)S(1)} collective-permute-done((bf16[16,1536]{1,0:T(8,128)(2,1)S(1)}, bf16[16,1536]{1,0:T(8,128)(2,1)S(1)}, u32[]{:S(2)}, u32[]{:S(2)}) %collective-permute-start.47) | collective-permute-done | bytes 49184 | tf_op jit(solution)/shard_map/ppermute | solution.py:33
  114.8 0.6 add_convert_fusion.13
  (75 shorter events, 4.4 us)
Async XLA Ops:
  19.8 5.7 %collective-permute-start.2 = (bf16[16,1536]{1,0:T(8,128)(2,1)S(1)}, bf16[16,1536]{1,0:T(8,128)(2,1)S(1)}, u32[]{:S(2)}, u32[]{:S(2)}) collective-permute-start(bf16[16,1536]{1,0:T(8,128)(2,1)S(1)} %add_convert_fusion.14), channel_id=1, source_target_pairs={{0,128},{1,129},{2,130},{3,131},{4,132},{5,133},{6,134},{7,135},{8... | collective-permute-start | bytes 147464 | tf_op jit(solution)/shard_map/ppermute | solution.py:33
  22.1 4.1 %collective-permute-start.1 = (bf16[16,1536]{1,0:T(8,128)(2,1)S(1)}, bf16[16,1536]{1,0:T(8,128)(2,1)S(1)}, u32[]{:S(2)}, u32[]{:S(2)}) collective-permute-start(bf16[16,1536]{1,0:T(8,128)(2,1)S(1)} %add_convert_fusion.14), channel_id=1, source_target_pairs={{0,192},{1,193},{2,194},{3,195},{4,196},{5,197},{6,198},{7,199},{8... | collective-permute-start | bytes 147464 | tf_op jit(solution)/shard_map/ppermute | solution.py:33
  22.1 4.6 %collective-permute-start = (bf16[16,1536]{1,0:T(8,128)(2,1)S(1)}, bf16[16,1536]{1,0:T(8,128)(2,1)S(1)}, u32[]{:S(2)}, u32[]{:S(2)}) collective-permute-start(bf16[16,1536]{1,0:T(8,128)(2,1)S(1)} %add_convert_fusion.14), channel_id=1, source_target_pairs={{0,64},{1,65},{2,66},{3,67},{4,68},{5,69},{6,70},{7,71},{8,72},{9,... | collective-permute-start | bytes 147464 | tf_op jit(solution)/shard_map/ppermute | solution.py:33
  26.7 11.0 %copy-start = (bf16[64,1536]{1,0:T(8,128)(2,1)S(1)}, bf16[64,1536]{1,0:T(8,128)(2,1)}, u32[]{:S(2)}) copy-start(bf16[64,1536]{1,0:T(8,128)(2,1)} %param.9) | copy-start | bytes 589828
  26.7 7.0 %collective-permute-start.5 = (bf16[64,1536]{1,0:T(8,128)(2,1)S(1)}, bf16[64,1536]{1,0:T(8,128)(2,1)S(1)}, u32[]{:S(2)}, u32[]{:S(2)}) collective-permute-start(bf16[64,1536]{1,0:T(8,128)(2,1)S(1)} %pad_maximum_fusion.refs_0_), channel_id=1, source_target_pairs={{0,16},{1,17},{2,18},{3,19},{4,20},{5,21},{6,22},{7,23},{8,24},{9,... | collective-permute-start | bytes 589832 | tf_op jit(solution)/shard_map/ppermute | solution.py:33
  28.4 7.6 %collective-permute-start.4 = (bf16[64,1536]{1,0:T(8,128)(2,1)S(1)}, bf16[64,1536]{1,0:T(8,128)(2,1)S(1)}, u32[]{:S(2)}, u32[]{:S(2)}) collective-permute-start(bf16[64,1536]{1,0:T(8,128)(2,1)S(1)} %pad_maximum_fusion.refs_0_), channel_id=1, source_target_pairs={{0,48},{1,49},{2,50},{3,51},{4,52},{5,53},{6,54},{7,55},{8,56},{9,... | collective-permute-start | bytes 589832 | tf_op jit(solution)/shard_map/ppermute | solution.py:33
  30.6 7.2 %collective-permute-start.3 = (bf16[64,1536]{1,0:T(8,128)(2,1)S(1)}, bf16[64,1536]{1,0:T(8,128)(2,1)S(1)}, u32[]{:S(2)}, u32[]{:S(2)}) collective-permute-start(bf16[64,1536]{1,0:T(8,128)(2,1)S(1)} %pad_maximum_fusion.refs_0_), channel_id=1, source_target_pairs={{0,32},{1,33},{2,34},{3,35},{4,36},{5,37},{6,38},{7,39},{8,40},{9,... | collective-permute-start | bytes 589832 | tf_op jit(solution)/shard_map/ppermute | solution.py:33
  31.3 6.5 %collective-permute-start.6 = (bf16[64,1536]{1,0:T(8,128)(2,1)S(1)}, bf16[64,1536]{1,0:T(8,128)(2,1)S(1)}, u32[]{:S(2)}, u32[]{:S(2)}) collective-permute-start(bf16[64,1536]{1,0:T(8,128)(2,1)S(1)} %pad_maximum_fusion.refs_0_), channel_id=1, source_target_pairs={{0,8},{1,9},{2,10},{3,11},{4,12},{5,13},{6,14},{7,15},{8,0},{9,1},... | collective-permute-start | bytes 589832 | tf_op jit(solution)/shard_map/ppermute | solution.py:33
  33.7 5.5 %collective-permute-start.9 = (bf16[64,1536]{1,0:T(8,128)(2,1)S(1)}, bf16[64,1536]{1,0:T(8,128)(2,1)S(1)}, u32[]{:S(2)}, u32[]{:S(2)}) collective-permute-start(bf16[64,1536]{1,0:T(8,128)(2,1)S(1)} %collective-permute-done.5.refs_3_), channel_id=1, source_target_pairs={{0,8},{1,9},{2,10},{3,11},{4,12},{5,13},{6,14},{7,15},{8,0},{9,1},... | collective-permute-start | bytes 589832 | tf_op jit(solution)/shard_map/ppermute | solution.py:33
  36.0 1.8 %collective-permute-start.8 = (bf16[64,1536]{1,0:T(8,128)(2,1)S(1)}, bf16[64,1536]{1,0:T(8,128)(2,1)S(1)}, u32[]{:S(2)}, u32[]{:S(2)}) collective-permute-start(bf16[64,1536]{1,0:T(8,128)(2,1)S(1)} %collective-permute-done.4.refs_2_), channel_id=1, source_target_pairs={{0,8},{1,9},{2,10},{3,11},{4,12},{5,13},{6,14},{7,15},{8,0},{9,1},... | collective-permute-start | bytes 589832 | tf_op jit(solution)/shard_map/ppermute | solution.py:33
  37.8 1.4 %collective-permute-start.7 = (bf16[64,1536]{1,0:T(8,128)(2,1)S(1)}, bf16[64,1536]{1,0:T(8,128)(2,1)S(1)}, u32[]{:S(2)}, u32[]{:S(2)}) collective-permute-start(bf16[64,1536]{1,0:T(8,128)(2,1)S(1)} %collective-permute-done.3.refs_1_), channel_id=1, source_target_pairs={{0,8},{1,9},{2,10},{3,11},{4,12},{5,13},{6,14},{7,15},{8,0},{9,1},... | collective-permute-start | bytes 589832 | tf_op jit(solution)/shard_map/ppermute | solution.py:33
  40.9 5.5 %collective-permute-start.10 = (bf16[64,768]{1,0:T(8,128)(2,1)S(1)}, bf16[64,768]{1,0:T(8,128)(2,1)S(1)}, u32[]{:S(2)}, u32[]{:S(2)}) collective-permute-start(bf16[64,768]{1,0:T(8,128)(2,1)S(1)} %get-tuple-element.46), channel_id=1, source_target_pairs={{0,1},{1,0},{2,3},{3,2},{4,5},{5,4},{6,7},{7,6},{8,15},{9,10},{10,... | collective-permute-start | bytes 294920 | tf_op jit(solution)/shard_map/ppermute | solution.py:33
  41.6 5.6 %collective-permute-start.14 = (bf16[64,768]{1,0:T(8,128)(2,1)S(1)}, bf16[64,768]{1,0:T(8,128)(2,1)S(1)}, u32[]{:S(2)}, u32[]{:S(2)}) collective-permute-start(bf16[64,768]{1,0:T(8,128)(2,1)S(1)} %get-tuple-element.49), channel_id=1, source_target_pairs={{0,1},{1,0},{2,3},{3,2},{4,5},{5,4},{6,7},{7,6},{8,15},{9,10},{10,... | collective-permute-start | bytes 294920 | tf_op jit(solution)/shard_map/ppermute | solution.py:33
  43.0 6.9 %collective-permute-start.18 = (bf16[64,768]{1,0:T(8,128)(2,1)S(1)}, bf16[64,768]{1,0:T(8,128)(2,1)S(1)}, u32[]{:S(2)}, u32[]{:S(2)}) collective-permute-start(bf16[64,768]{1,0:T(8,128)(2,1)S(1)} %get-tuple-element.56), channel_id=1, source_target_pairs={{0,1},{1,0},{2,3},{3,2},{4,5},{5,4},{6,7},{7,6},{8,15},{9,10},{10,... | collective-permute-start | bytes 294920 | tf_op jit(solution)/shard_map/ppermute | solution.py:33
  43.6 7.0 %collective-permute-start.22 = (bf16[64,768]{1,0:T(8,128)(2,1)S(1)}, bf16[64,768]{1,0:T(8,128)(2,1)S(1)}, u32[]{:S(2)}, u32[]{:S(2)}) collective-permute-start(bf16[64,768]{1,0:T(8,128)(2,1)S(1)} %get-tuple-element.59), channel_id=1, source_target_pairs={{0,1},{1,0},{2,3},{3,2},{4,5},{5,4},{6,7},{7,6},{8,15},{9,10},{10,... | collective-permute-start | bytes 294920 | tf_op jit(solution)/shard_map/ppermute | solution.py:33
  46.5 7.1 %collective-permute-start.11 = (bf16[64,768]{1,0:T(8,128)(2,1)S(1)}, bf16[64,768]{1,0:T(8,128)(2,1)S(1)}, u32[]{:S(2)}, u32[]{:S(2)}) collective-permute-start(bf16[64,768]{1,0:T(8,128)(2,1)S(1)} %add_convert_fusion.12), channel_id=1, source_target_pairs={{0,7},{1,2},{2,1},{3,4},{4,3},{5,6},{6,5},{7,0},{8,9},{9,8},{10,11... | collective-permute-start | bytes 294920 | tf_op jit(solution)/shard_map/ppermute | solution.py:33
  47.2 6.5 %collective-permute-start.15 = (bf16[64,768]{1,0:T(8,128)(2,1)S(1)}, bf16[64,768]{1,0:T(8,128)(2,1)S(1)}, u32[]{:S(2)}, u32[]{:S(2)}) collective-permute-start(bf16[64,768]{1,0:T(8,128)(2,1)S(1)} %add_convert_fusion.9), channel_id=1, source_target_pairs={{0,7},{1,2},{2,1},{3,4},{4,3},{5,6},{6,5},{7,0},{8,9},{9,8},{10,11... | collective-permute-start | bytes 294920 | tf_op jit(solution)/shard_map/ppermute | solution.py:33
  50.0 6.1 %collective-permute-start.19 = (bf16[64,768]{1,0:T(8,128)(2,1)S(1)}, bf16[64,768]{1,0:T(8,128)(2,1)S(1)}, u32[]{:S(2)}, u32[]{:S(2)}) collective-permute-start(bf16[64,768]{1,0:T(8,128)(2,1)S(1)} %add_convert_fusion.7), channel_id=1, source_target_pairs={{0,7},{1,2},{2,1},{3,4},{4,3},{5,6},{6,5},{7,0},{8,9},{9,8},{10,11... | collective-permute-start | bytes 294920 | tf_op jit(solution)/shard_map/ppermute | solution.py:33
  50.7 7.5 %collective-permute-start.23 = (bf16[64,768]{1,0:T(8,128)(2,1)S(1)}, bf16[64,768]{1,0:T(8,128)(2,1)S(1)}, u32[]{:S(2)}, u32[]{:S(2)}) collective-permute-start(bf16[64,768]{1,0:T(8,128)(2,1)S(1)} %add_convert_fusion.4), channel_id=1, source_target_pairs={{0,7},{1,2},{2,1},{3,4},{4,3},{5,6},{6,5},{7,0},{8,9},{9,8},{10,11... | collective-permute-start | bytes 294920 | tf_op jit(solution)/shard_map/ppermute | solution.py:33
  53.6 4.7 %collective-permute-start.12 = (bf16[64,768]{1,0:T(8,128)(2,1)S(1)}, bf16[64,768]{1,0:T(8,128)(2,1)S(1)}, u32[]{:S(2)}, u32[]{:S(2)}) collective-permute-start(bf16[64,768]{1,0:T(8,128)(2,1)S(1)} %add_convert_fusion.11), channel_id=1, source_target_pairs={{0,1},{1,0},{2,3},{3,2},{4,5},{5,4},{6,7},{7,6},{8,15},{9,10},{10,... | collective-permute-start | bytes 294920 | tf_op jit(solution)/shard_map/ppermute | solution.py:33
  53.8 8.8 %collective-permute-start.16 = (bf16[64,768]{1,0:T(8,128)(2,1)S(1)}, bf16[64,768]{1,0:T(8,128)(2,1)S(1)}, u32[]{:S(2)}, u32[]{:S(2)}) collective-permute-start(bf16[64,768]{1,0:T(8,128)(2,1)S(1)} %add_convert_fusion.8), channel_id=1, source_target_pairs={{0,1},{1,0},{2,3},{3,2},{4,5},{5,4},{6,7},{7,6},{8,15},{9,10},{10,... | collective-permute-start | bytes 294920 | tf_op jit(solution)/shard_map/ppermute | solution.py:33
  56.1 4.9 %collective-permute-start.20 = (bf16[64,768]{1,0:T(8,128)(2,1)S(1)}, bf16[64,768]{1,0:T(8,128)(2,1)S(1)}, u32[]{:S(2)}, u32[]{:S(2)}) collective-permute-start(bf16[64,768]{1,0:T(8,128)(2,1)S(1)} %add_convert_fusion.6), channel_id=1, source_target_pairs={{0,1},{1,0},{2,3},{3,2},{4,5},{5,4},{6,7},{7,6},{8,15},{9,10},{10,... | collective-permute-start | bytes 294920 | tf_op jit(solution)/shard_map/ppermute | solution.py:33
  58.2 7.1 %collective-permute-start.24 = (bf16[64,768]{1,0:T(8,128)(2,1)S(1)}, bf16[64,768]{1,0:T(8,128)(2,1)S(1)}, u32[]{:S(2)}, u32[]{:S(2)}) collective-permute-start(bf16[64,768]{1,0:T(8,128)(2,1)S(1)} %add_convert_fusion.3), channel_id=1, source_target_pairs={{0,1},{1,0},{2,3},{3,2},{4,5},{5,4},{6,7},{7,6},{8,15},{9,10},{10,... | collective-permute-start | bytes 294920 | tf_op jit(solution)/shard_map/ppermute | solution.py:33
  58.4 5.9 %collective-permute-start.13 = (bf16[64,768]{1,0:T(8,128)(2,1)S(1)}, bf16[64,768]{1,0:T(8,128)(2,1)S(1)}, u32[]{:S(2)}, u32[]{:S(2)}) collective-permute-start(bf16[64,768]{1,0:T(8,128)(2,1)S(1)} %add_convert_fusion.10), channel_id=1, source_target_pairs={{0,7},{1,2},{2,1},{3,4},{4,3},{5,6},{6,5},{7,0},{8,9},{9,8},{10,11... | collective-permute-start | bytes 294920 | tf_op jit(solution)/shard_map/ppermute | solution.py:33
  61.1 6.8 %collective-permute-start.21 = (bf16[64,768]{1,0:T(8,128)(2,1)S(1)}, bf16[64,768]{1,0:T(8,128)(2,1)S(1)}, u32[]{:S(2)}, u32[]{:S(2)}) collective-permute-start(bf16[64,768]{1,0:T(8,128)(2,1)S(1)} %add_convert_fusion.5), channel_id=1, source_target_pairs={{0,7},{1,2},{2,1},{3,4},{4,3},{5,6},{6,5},{7,0},{8,9},{9,8},{10,11... | collective-permute-start | bytes 294920 | tf_op jit(solution)/shard_map/ppermute | solution.py:33
  64.5 7.0 %collective-permute-start.17 = (bf16[64,768]{1,0:T(8,128)(2,1)S(1)}, bf16[64,768]{1,0:T(8,128)(2,1)S(1)}, u32[]{:S(2)}, u32[]{:S(2)}) collective-permute-start(bf16[64,768]{1,0:T(8,128)(2,1)S(1)} %get-tuple-element.73.refs_1_), channel_id=1, source_target_pairs={{0,1},{1,0},{2,3},{3,2},{4,5},{5,4},{6,7},{7,6},{8,15},{9,10},{10,... | collective-permute-start | bytes 294920 | tf_op jit(solution)/shard_map/ppermute | solution.py:33
  68.0 5.8 %collective-permute-start.25 = (bf16[64,768]{1,0:T(8,128)(2,1)S(1)}, bf16[64,768]{1,0:T(8,128)(2,1)S(1)}, u32[]{:S(2)}, u32[]{:S(2)}) collective-permute-start(bf16[64,768]{1,0:T(8,128)(2,1)S(1)} %get-tuple-element.75.refs_5_.refs_9_), channel_id=1, source_target_pairs={{0,1},{1,0},{2,3},{3,2},{4,5},{5,4},{6,7},{7,6},{8,15},{9,10},{10,... | collective-permute-start | bytes 294920 | tf_op jit(solution)/shard_map/ppermute | solution.py:33
  68.1 6.9 %collective-permute-start.26 = (bf16[64,768]{1,0:T(8,128)(2,1)S(1)}, bf16[64,768]{1,0:T(8,128)(2,1)S(1)}, u32[]{:S(2)}, u32[]{:S(2)}) collective-permute-start(bf16[64,768]{1,0:T(8,128)(2,1)S(1)} %get-tuple-element.73.refs_1_), channel_id=1, source_target_pairs={{0,7},{1,2},{2,1},{3,4},{4,3},{5,6},{6,5},{7,0},{8,9},{9,8},{10,11... | collective-permute-start | bytes 294920 | tf_op jit(solution)/shard_map/ppermute | solution.py:33
  69.8 6.8 %collective-permute-start.32 = (bf16[64,768]{1,0:T(8,128)(2,1)S(1)}, bf16[64,768]{1,0:T(8,128)(2,1)S(1)}, u32[]{:S(2)}, u32[]{:S(2)}) collective-permute-start(bf16[64,768]{1,0:T(8,128)(2,1)S(1)} %get-tuple-element.75.refs_5_.refs_9_), channel_id=1, source_target_pairs={{0,7},{1,2},{2,1},{3,4},{4,3},{5,6},{6,5},{7,0},{8,9},{9,8},{10,11... | collective-permute-start | bytes 294920 | tf_op jit(solution)/shard_map/ppermute | solution.py:33
  71.5 7.3 %collective-permute-start.28 = (bf16[64,768]{1,0:T(8,128)(2,1)S(1)}, bf16[64,768]{1,0:T(8,128)(2,1)S(1)}, u32[]{:S(2)}, u32[]{:S(2)}) collective-permute-start(bf16[64,768]{1,0:T(8,128)(2,1)S(1)} %collective-permute-done.17.refs_2_), channel_id=1, source_target_pairs={{0,7},{1,2},{2,1},{3,4},{4,3},{5,6},{6,5},{7,0},{8,9},{9,8},{10,11... | collective-permute-start | bytes 294920 | tf_op jit(solution)/shard_map/ppermute | solution.py:33
  73.9 7.0 %collective-permute-start.34 = (bf16[64,768]{1,0:T(8,128)(2,1)S(1)}, bf16[64,768]{1,0:T(8,128)(2,1)S(1)}, u32[]{:S(2)}, u32[]{:S(2)}) collective-permute-start(bf16[64,768]{1,0:T(8,128)(2,1)S(1)} %collective-permute-done.25.refs_6_.refs_10_), channel_id=1, source_target_pairs={{0,7},{1,2},{2,1},{3,4},{4,3},{5,6},{6,5},{7,0},{8,9},{9,8},{10,11... | collective-permute-start | bytes 294920 | tf_op jit(solution)/shard_map/ppermute | solution.py:33
  75.0 7.1 %collective-permute-start.27 = (bf16[64,768]{1,0:T(8,128)(2,1)S(1)}, bf16[64,768]{1,0:T(8,128)(2,1)S(1)}, u32[]{:S(2)}, u32[]{:S(2)}) collective-permute-start(bf16[64,768]{1,0:T(8,128)(2,1)S(1)} %collective-permute-done.26.refs_0_), channel_id=1, source_target_pairs={{0,1},{1,0},{2,3},{3,2},{4,5},{5,4},{6,7},{7,6},{8,15},{9,10},{10,... | collective-permute-start | bytes 294920 | tf_op jit(solution)/shard_map/ppermute | solution.py:33
  76.7 6.3 %collective-permute-start.33 = (bf16[64,768]{1,0:T(8,128)(2,1)S(1)}, bf16[64,768]{1,0:T(8,128)(2,1)S(1)}, u32[]{:S(2)}, u32[]{:S(2)}) collective-permute-start(bf16[64,768]{1,0:T(8,128)(2,1)S(1)} %collective-permute-done.32.refs_4_.refs_8_), channel_id=1, source_target_pairs={{0,1},{1,0},{2,3},{3,2},{4,5},{5,4},{6,7},{7,6},{8,15},{9,10},{10,... | collective-permute-start | bytes 294920 | tf_op jit(solution)/shard_map/ppermute | solution.py:33
  78.8 6.6 %collective-permute-start.29 = (bf16[64,768]{1,0:T(8,128)(2,1)S(1)}, bf16[64,768]{1,0:T(8,128)(2,1)S(1)}, u32[]{:S(2)}, u32[]{:S(2)}) collective-permute-start(bf16[64,768]{1,0:T(8,128)(2,1)S(1)} %collective-permute-done.28.refs_7_), channel_id=1, source_target_pairs={{0,1},{1,0},{2,3},{3,2},{4,5},{5,4},{6,7},{7,6},{8,15},{9,10},{10,... | collective-permute-start | bytes 294920 | tf_op jit(solution)/shard_map/ppermute | solution.py:33
  80.9 6.1 %collective-permute-start.35 = (bf16[64,768]{1,0:T(8,128)(2,1)S(1)}, bf16[64,768]{1,0:T(8,128)(2,1)S(1)}, u32[]{:S(2)}, u32[]{:S(2)}) collective-permute-start(bf16[64,768]{1,0:T(8,128)(2,1)S(1)} %collective-permute-done.34.refs_15_), channel_id=1, source_target_pairs={{0,1},{1,0},{2,3},{3,2},{4,5},{5,4},{6,7},{7,6},{8,15},{9,10},{10,... | collective-permute-start | bytes 294920 | tf_op jit(solution)/shard_map/ppermute | solution.py:33
  82.1 8.3 %collective-permute-start.31 = (bf16[64,768]{1,0:T(8,128)(2,1)S(1)}, bf16[64,768]{1,0:T(8,128)(2,1)S(1)}, u32[]{:S(2)}, u32[]{:S(2)}) collective-permute-start(bf16[64,768]{1,0:T(8,128)(2,1)S(1)} %collective-permute-done.27.refs_3_), channel_id=1, source_target_pairs={{0,7},{1,2},{2,1},{3,4},{4,3},{5,6},{6,5},{7,0},{8,9},{9,8},{10,11... | collective-permute-start | bytes 294920 | tf_op jit(solution)/shard_map/ppermute | solution.py:33
  83.0 7.5 %collective-permute-start.37 = (bf16[64,768]{1,0:T(8,128)(2,1)S(1)}, bf16[64,768]{1,0:T(8,128)(2,1)S(1)}, u32[]{:S(2)}, u32[]{:S(2)}) collective-permute-start(bf16[64,768]{1,0:T(8,128)(2,1)S(1)} %collective-permute-done.33.refs_7_.refs_11_), channel_id=1, source_target_pairs={{0,7},{1,2},{2,1},{3,4},{4,3},{5,6},{6,5},{7,0},{8,9},{9,8},{10,11... | collective-permute-start | bytes 294920 | tf_op jit(solution)/shard_map/ppermute | solution.py:33
  85.4 5.8 %collective-permute-start.30 = (bf16[64,768]{1,0:T(8,128)(2,1)S(1)}, bf16[64,768]{1,0:T(8,128)(2,1)S(1)}, u32[]{:S(2)}, u32[]{:S(2)}) collective-permute-start(bf16[64,768]{1,0:T(8,128)(2,1)S(1)} %collective-permute-done.29.refs_4_), channel_id=1, source_target_pairs={{0,7},{1,2},{2,1},{3,4},{4,3},{5,6},{6,5},{7,0},{8,9},{9,8},{10,11... | collective-permute-start | bytes 294920 | tf_op jit(solution)/shard_map/ppermute | solution.py:33
  87.0 5.8 %collective-permute-start.36 = (bf16[64,768]{1,0:T(8,128)(2,1)S(1)}, bf16[64,768]{1,0:T(8,128)(2,1)S(1)}, u32[]{:S(2)}, u32[]{:S(2)}) collective-permute-start(bf16[64,768]{1,0:T(8,128)(2,1)S(1)} %collective-permute-done.35.refs_12_), channel_id=1, source_target_pairs={{0,7},{1,2},{2,1},{3,4},{4,3},{5,6},{6,5},{7,0},{8,9},{9,8},{10,11... | collective-permute-start | bytes 294920 | tf_op jit(solution)/shard_map/ppermute | solution.py:33
  94.7 1.5 %collective-permute-start.39 = (bf16[64,1536]{1,0:T(8,128)(2,1)S(1)}, bf16[64,1536]{1,0:T(8,128)(2,1)S(1)}, u32[]{:S(2)}, u32[]{:S(2)}) collective-permute-start(bf16[64,1536]{1,0:T(8,128)(2,1)S(1)} %get-tuple-element.65), channel_id=1, source_target_pairs={{0,8},{1,9},{2,10},{3,11},{4,12},{5,13},{6,14},{7,15},{8,0},{9,1},... | collective-permute-start | bytes 589832 | tf_op jit(solution)/shard_map/ppermute | solution.py:33
  95.0 10.1 %collective-permute-start.38 = (bf16[64,1536]{1,0:T(8,128)(2,1)S(1)}, bf16[64,1536]{1,0:T(8,128)(2,1)S(1)}, u32[]{:S(2)}, u32[]{:S(2)}) collective-permute-start(bf16[64,1536]{1,0:T(8,128)(2,1)S(1)} %get-tuple-element.63), channel_id=1, source_target_pairs={{0,8},{1,9},{2,10},{3,11},{4,12},{5,13},{6,14},{7,15},{8,0},{9,1},... | collective-permute-start | bytes 589832 | tf_op jit(solution)/shard_map/ppermute | solution.py:33
  95.5 1.5 %collective-permute-start.41 = (bf16[64,1536]{1,0:T(8,128)(2,1)S(1)}, bf16[64,1536]{1,0:T(8,128)(2,1)S(1)}, u32[]{:S(2)}, u32[]{:S(2)}) collective-permute-start(bf16[64,1536]{1,0:T(8,128)(2,1)S(1)} %get-tuple-element.67), channel_id=1, source_target_pairs={{0,8},{1,9},{2,10},{3,11},{4,12},{5,13},{6,14},{7,15},{8,0},{9,1},... | collective-permute-start | bytes 589832 | tf_op jit(solution)/shard_map/ppermute | solution.py:33
  95.7 3.0 %collective-permute-start.43 = (bf16[64,1536]{1,0:T(8,128)(2,1)S(1)}, bf16[64,1536]{1,0:T(8,128)(2,1)S(1)}, u32[]{:S(2)}, u32[]{:S(2)}) collective-permute-start(bf16[64,1536]{1,0:T(8,128)(2,1)S(1)} %get-tuple-element.69), channel_id=1, source_target_pairs={{0,8},{1,9},{2,10},{3,11},{4,12},{5,13},{6,14},{7,15},{8,0},{9,1},... | collective-permute-start | bytes 589832 | tf_op jit(solution)/shard_map/ppermute | solution.py:33
  96.3 8.7 %collective-permute-start.40 = (bf16[64,1536]{1,0:T(8,128)(2,1)S(1)}, bf16[64,1536]{1,0:T(8,128)(2,1)S(1)}, u32[]{:S(2)}, u32[]{:S(2)}) collective-permute-start(bf16[64,1536]{1,0:T(8,128)(2,1)S(1)} %add_convert_fusion.2), channel_id=1, source_target_pairs={{0,16},{1,17},{2,18},{3,19},{4,20},{5,21},{6,22},{7,23},{8,72},{9,... | collective-permute-start | bytes 589832 | tf_op jit(solution)/shard_map/ppermute | solution.py:33
  97.1 9.1 %collective-permute-start.42 = (bf16[64,1536]{1,0:T(8,128)(2,1)S(1)}, bf16[64,1536]{1,0:T(8,128)(2,1)S(1)}, u32[]{:S(2)}, u32[]{:S(2)}) collective-permute-start(bf16[64,1536]{1,0:T(8,128)(2,1)S(1)} %add_convert_fusion.1), channel_id=1, source_target_pairs={{0,48},{1,49},{2,50},{3,51},{4,52},{5,53},{6,54},{7,55},{8,200},{9... | collective-permute-start | bytes 589832 | tf_op jit(solution)/shard_map/ppermute | solution.py:33
  98.7 7.5 %collective-permute-start.44 = (bf16[64,1536]{1,0:T(8,128)(2,1)S(1)}, bf16[64,1536]{1,0:T(8,128)(2,1)S(1)}, u32[]{:S(2)}, u32[]{:S(2)}) collective-permute-start(bf16[64,1536]{1,0:T(8,128)(2,1)S(1)} %add_convert_fusion), channel_id=1, source_target_pairs={{0,32},{1,33},{2,34},{3,35},{4,36},{5,37},{6,38},{7,39},{8,136},{9... | collective-permute-start | bytes 589832 | tf_op jit(solution)/shard_map/ppermute | solution.py:33
  106.4 5.1 %collective-permute-start.45 = (bf16[16,1536]{1,0:T(8,128)(2,1)S(1)}, bf16[16,1536]{1,0:T(8,128)(2,1)S(1)}, u32[]{:S(2)}, u32[]{:S(2)}) collective-permute-start(bf16[16,1536]{1,0:T(8,128)(2,1)S(1)} %get-tuple-element.77), channel_id=1, source_target_pairs={{0,64},{1,65},{2,66},{3,67},{4,68},{5,69},{6,70},{7,71},{8,24},{9,... | collective-permute-start | bytes 147464 | tf_op jit(solution)/shard_map/ppermute | solution.py:33
  109.2 5.6 %collective-permute-start.47 = (bf16[16,1536]{1,0:T(8,128)(2,1)S(1)}, bf16[16,1536]{1,0:T(8,128)(2,1)S(1)}, u32[]{:S(2)}, u32[]{:S(2)}) collective-permute-start(bf16[16,1536]{1,0:T(8,128)(2,1)S(1)} %get-tuple-element.78), channel_id=1, source_target_pairs={{0,128},{1,129},{2,130},{3,131},{4,132},{5,133},{6,134},{7,135},{8... | collective-permute-start | bytes 147464 | tf_op jit(solution)/shard_map/ppermute | solution.py:33
  109.8 5.0 %collective-permute-start.46 = (bf16[16,1536]{1,0:T(8,128)(2,1)S(1)}, bf16[16,1536]{1,0:T(8,128)(2,1)S(1)}, u32[]{:S(2)}, u32[]{:S(2)}) collective-permute-start(bf16[16,1536]{1,0:T(8,128)(2,1)S(1)} %get-tuple-element.79), channel_id=1, source_target_pairs={{0,192},{1,193},{2,194},{3,195},{4,196},{5,197},{6,198},{7,199},{8... | collective-permute-start | bytes 147464 | tf_op jit(solution)/shard_map/ppermute | solution.py:33

commit v5 on v4

--- a/solution.py
+++ b/solution.py
@@ -9,7 +9,7 @@
 F32, BF16 = jnp.float32, jnp.bfloat16
 
 NX, NY, NC, NZ = 4, 4, 2, 8
-GATHER_X, GATHER_Y, SUM = (0, 1, 3, 2), (0, 2, 3, 1), (0, 1, 3, 2)
+GATHER_X, GATHER_Y, SUM_FIRST, SUM_LAST = (0, 1, 3, 2), (0, 2, 3, 1), (0, 1, 3, 2), (0, 3, 1, 2)
 TOKENS_OWN = 16
 TOKENS_Z = 64
 TOKENS = 512
@@ -37,8 +37,8 @@
     return send(value, lambda x, y, c, z: (x ^ k, y, c, z))
 
 
-def send_y(value, k):
-    return send(value, lambda x, y, c, z: (x, y ^ k, c, z))
+def send_y(value, shift):
+    return send(value, lambda x, y, c, z: (x, y + shift, c, z))
 
 
 def send_plane(value, k, x_core):
@@ -63,7 +63,7 @@
 def gathered_row(core_shift, i, p):
     row = lax.axis_index("row")
     x, y, c = row // (NY * NC), (row // NC) % NY, row % NC
-    x, y = x ^ GATHER_X[p], y ^ GATHER_Y[i]
+    x, y = x ^ GATHER_X[p], (y + NY - GATHER_Y[i]) % NY
     return row_of((x * NY + y) * NC + (c + core_shift) % NC)
 
 
@@ -71,8 +71,8 @@
     row = lax.axis_index("row")
     x, y, c = row // (NY * NC), (row // NC) % NY, row % NC
     core = (c + core_shift) % NC
-    x = x ^ jnp.where(core == 1, SUM[i], SUM[p])
-    y = y ^ jnp.where(core == 1, SUM[p], SUM[i])
+    x = x ^ jnp.where(core == 1, SUM_FIRST[i], SUM_LAST[p])
+    y = y ^ jnp.where(core == 1, SUM_LAST[p], SUM_FIRST[i])
     return row_of((x * NY + y) * NC + core)
 
 
@@ -109,13 +109,32 @@
 
 def multiply(rows, w_ref, outs):
     half = w_ref.shape[1] // 2
-    blocks = len(outs) // 2
     for h in range(2):
-        product = jnp.dot(
-            rows, w_ref[:, h * half : (h + 1) * half], preferred_element_type=F32
-        ).astype(BF16)
-        for k in range(blocks):
-            outs[h * blocks + k][...] = product[k * TOKENS_Z : (k + 1) * TOKENS_Z, :]
+        columns = slice(h * half, (h + 1) * half)
+        product = jnp.dot(rows, w_ref[:, columns], preferred_element_type=F32).astype(BF16)
+        for k, out in enumerate(outs):
+            block = product[k * TOKENS_Z : (k + 1) * TOKENS_Z, :]
+            if len(out) == 2:
+                out[h][...] = block
+            else:
+                out[0][:, columns] = block
+
+
+def halves_of(cut, refs):
+    refs = list(refs)
+    return [[refs.pop(0) for _ in range(1 + flag)] for flag in cut]
+
+
+def shapes_of(cut, width):
+    return [
+        jax.ShapeDtypeStruct((TOKENS_Z, width // (1 + flag)), BF16)
+        for flag in cut
+        for _ in range(1 + flag)
+    ]
+
+
+SUM_CUT = (1, 0, 0, 1, 0, 1, 1, 0)
+GATHER_CUT = (0, 0, 1, 0, 1, 1, 0, 1)
 
 
 def far_kernel(*refs):
@@ -127,11 +146,11 @@
                 normed_ref[rows, :] = pieces[core_shift * 4 + i][
                     p * TOKENS_OWN : (p + 1) * TOKENS_OWN, :
                 ]
-    multiply(normed_ref[HALF:, :], w_ref, outs)
+    multiply(normed_ref[HALF:, :], w_ref, halves_of(SUM_CUT[4:], outs))
 
 
 def near_kernel(normed_ref, w_ref, *outs):
-    multiply(normed_ref[:HALF, :], w_ref, outs)
+    multiply(normed_ref[:HALF, :], w_ref, halves_of(SUM_CUT[:4], outs))
 
 
 def far_pre(pieces, weight):
@@ -139,9 +158,8 @@
     return pl.pallas_call(
         far_kernel,
         in_specs=[WHOLE] * 9,
-        out_specs=[WHOLE] * 9,
-        out_shape=[jax.ShapeDtypeStruct((TOKENS, depth), BF16)]
-        + [jax.ShapeDtypeStruct((TOKENS_Z, width // 2), BF16)] * 8,
+        out_specs=[WHOLE] * (5 + sum(SUM_CUT[4:])),
+        out_shape=[jax.ShapeDtypeStruct((TOKENS, depth), BF16)] + shapes_of(SUM_CUT[4:], width),
         **settings(weight, 16),
     )(*pieces, weight)
 
@@ -150,8 +168,8 @@
     return pl.pallas_call(
         near_kernel,
         in_specs=[WHOLE] * 2,
-        out_specs=[WHOLE] * 8,
-        out_shape=[jax.ShapeDtypeStruct((TOKENS_Z, weight.shape[1] // 2), BF16)] * 8,
+        out_specs=[WHOLE] * (4 + sum(SUM_CUT[:4])),
+        out_shape=shapes_of(SUM_CUT[:4], weight.shape[1]),
         **settings(weight, 16),
     )(normed, weight)
 
@@ -160,18 +178,20 @@
     return lax.dot_general(rows, weight, (((1,), (1,)), ((), ())), preferred_element_type=F32)
 
 
-def fill(rows_ref, pieces, blocks):
+def fill(rows_ref, blocks):
     half = rows_ref.shape[1] // 2
-    for h in range(2):
-        for k in range(blocks):
-            rows_ref[
-                k * TOKENS_Z : (k + 1) * TOKENS_Z, h * half : (h + 1) * half
-            ] = pieces[h * blocks + k][...]
+    for k, block in enumerate(blocks):
+        rows = slice(k * TOKENS_Z, (k + 1) * TOKENS_Z)
+        if len(block) == 2:
+            rows_ref[rows, :half] = block[0][...]
+            rows_ref[rows, half:] = block[1][...]
+        else:
+            rows_ref[rows, :] = block[0][...]
 
 
 def near_back_kernel(*refs):
-    pieces, w_ref, out_ref, rows_ref = refs[:8], refs[8], refs[9], refs[10]
-    fill(rows_ref, pieces, 4)
+    *pieces, w_ref, out_ref, rows_ref = refs
+    fill(rows_ref, halves_of(GATHER_CUT[:4], pieces))
     rows = rows_ref[...]
     for start in range(0, w_ref.shape[0], TILE):
         part = slice(start, start + TILE)
@@ -181,7 +201,7 @@
 def near_back(pieces, weight):
     return pl.pallas_call(
         near_back_kernel,
-        in_specs=[WHOLE] * 9,
+        in_specs=[WHOLE] * (len(pieces) + 1),
         out_specs=WHOLE,
         out_shape=jax.ShapeDtypeStruct((HALF, weight.shape[0]), BF16),
         scratch_shapes=[pltpu.VMEM((HALF, weight.shape[1]), BF16)],
@@ -190,10 +210,9 @@
 
 
 def far_back_kernel(*refs):
-    pieces, near_ref, w_ref, slopes_ref, outs, product = (
-        refs[:16], refs[16], refs[17], refs[18], refs[19:27], refs[27]
-    )
-    fill(slopes_ref, pieces, NZ)
+    *pieces, near_ref, w_ref, slopes_ref = refs[:-9]
+    outs, product = refs[-9:-1], refs[-1]
+    fill(slopes_ref, halves_of(GATHER_CUT, pieces))
     product[:HALF, :] = near_ref[...].astype(F32)
     rows = slopes_ref[HALF:, :]
     for start in range(0, w_ref.shape[0], TILE):
@@ -211,7 +230,7 @@
     depth, width = weight.shape
     return pl.pallas_call(
         far_back_kernel,
-        in_specs=[WHOLE] * 18,
+        in_specs=[WHOLE] * (len(pieces) + 2),
         out_specs=[WHOLE] * 9,
         out_shape=[jax.ShapeDtypeStruct((TOKENS, width), BF16)]
         + [jax.ShapeDtypeStruct((TOKENS_Z, depth), BF16)] * 8,
@@ -272,23 +291,21 @@
     other = [send_core(v) for v in along_y]
 
     gathered, *far = far_pre(along_y + other, weight)
-    near = near_pre(gathered, weight)
+    three, four, five, six = halves_of(SUM_CUT[4:], far)
+    back, own, one, two = halves_of(SUM_CUT[:4], near_pre(gathered, weight))
+    longer = [reduce_chain([four[h], five[h], two[h], back[h]]) for h in range(2)]
+    shorter = reduce_chain([three[0], six[0], one[0]])
+    pre = add(own[0], jnp.concatenate(longer, axis=1), shorter)
+    slopes = jax.vjp(gelu_tanh, pre)[1](d_act.astype(F32))[0].astype(BF16)
+
     half = weight.shape[1] // 2
-    d_halves = lax.optimization_barrier((d_act[:, :half], d_act[:, half:]))
-    pres, pieces, nearest = [], [], []
-    for h in range(2):
-        three, four, five, six = far[4 * h : 4 * h + 4]
-        back, own, one, two = near[4 * h : 4 * h + 4]
-        longer = reduce_chain([four, five, two, back])
-        shorter = reduce_chain([three, six, one])
-        pre = add(own, longer, shorter)
-        slopes = jax.vjp(gelu_tanh, pre)[1](d_halves[h].astype(F32))[0].astype(BF16)
-        block_1, block_6, block_3, block_4 = gather_chain(slopes, 1, 4)
-        block_7, block_2, block_5 = gather_chain(slopes, -1, 3)
-        nearest += [block_7, slopes, block_1, block_2]
-        pieces += [block_7, slopes, block_1, block_2, block_3, block_4, block_5, block_6]
-        pres.append(lax.optimization_barrier((pre, block_1))[0])
-    activated = jnp.concatenate([gelu_tanh(pre).astype(BF16) for pre in pres], axis=1)
+    longer = [gather_chain(slopes[:, h * half : (h + 1) * half], 1, 4) for h in range(2)]
+    block_1, block_6, block_3, block_4 = ([chain[i] for chain in longer] for i in range(4))
+    block_7, block_2, block_5 = ([v] for v in gather_chain(slopes, -1, 3))
+    nearest = block_7 + [slopes] + block_1 + block_2
+    pieces = nearest + block_3 + block_4 + block_5 + block_6
+    pre, _ = lax.optimization_barrier((pre, block_4[0]))
+    activated = gelu_tanh(pre).astype(BF16)
 
     near = near_back(nearest, weight)
     slopes_all, *parts = far_back(pieces, near, weight)
@@ -297,11 +314,11 @@
     ).astype(BF16)
 
     sums = [add(parts[i], send_core(parts[4 + i])) for i in range(4)]
-    arrived = [send_plane(sums[i].astype(BF16), SUM[i], 1) for i in range(1, 4)]
+    arrived = [send_plane(sums[i].astype(BF16), SUM_FIRST[i], 1) for i in range(1, 4)]
     line = add(sums[0], *arrived)
     line, d_weight = lax.optimization_barrier((line, d_weight))
     blocks = [line[i * TOKENS_OWN : (i + 1) * TOKENS_OWN] for i in range(4)]
-    arrived = [send_plane(blocks[i].astype(BF16), SUM[i], 0) for i in range(1, 4)]
+    arrived = [send_plane(blocks[i].astype(BF16), SUM_LAST[i], 0) for i in range(1, 4)]
     d_normed = add(blocks[0], *arrived).astype(BF16)
     return (activated, d_normed, d_weight)
 

time: 117 us -> 117 us (level)
  waiting for transfers between devices: 24.5 us -> 35.6 us
  starting transfers between devices: 55.4 us -> 45.4 us
    ppermute x48 -> x42, waiting for transfers between devices: 24.5 us -> 35.6 us  [send(): return lax.ppermute(value, ('row', 'col'), pairs_of(target))]
    ppermute x48 -> x42, starting transfers between devices: 55.4 us -> 45.4 us  [send(): return lax.ppermute(value, ('row', 'col'), pairs_of(target))]
  transfers between devices with their start and end apart: 48 -> 42, of which waited for: 20 -> 25; matrix products, arithmetic and copies ran while one was open for 5% -> 5% of each run, Pallas kernels for 4% -> 4%
where the time goes in v5:
time: 117 us; the launch traced here: 116 us
  starting transfers between devices  45.4 us (39%)
  waiting for transfers between devices  35.6 us (30%)
  blocking collectives  16 us (14%)
  Pallas kernels  8.77 us (7%)
  other arithmetic  5.55 us (5%)
  matrix products  4.27 us (4%)
    ppermute x42, starting transfers between devices, send(): return lax.ppermute(value, ('row', 'col'), pairs_of(target))  45.4 us
    ppermute x42, waiting for transfers between devices, send(): return lax.ppermute(value, ('row', 'col'), pairs_of(target))  35.6 us
    all_to_all x1, blocking collectives, normalize(): lax.all_to_all(jnp.broadcast_to(stats[None], (NZ,) + stats.shape), 'col',...  16 us
    dot_general x1, matrix products, per_device(): lax.dot_general(gathered, slopes_all, (((0,), (0,)), ((), ())), preferred...  4.27 us
    pallas_call x1, Pallas kernels, stage(): pl.pallas_call(stage_kernel, in_specs=[pl.BlockSpec(memory_space=pl.ANY)]...  2.34 us
  transfers between devices with their start and end apart: 42, of which 25 were waited for; matrix products, arithmetic and copies ran while one was open for 5% of the time, Pallas kernels for 4%

profile of v5, /device:TPU:2, one launch (start us, length us, event | category | flops | bytes accessed | tf_op | source)
XLA Modules:
  0.0 116.5 jit_solution(2855071946947860578)
XLA Ops:
  0.6 1.0 reduce_sum.45
  1.7 1.1 multiply_reduce_fusion
  2.8 16.0 %all_to_all.5 = f32[8,2,16]{2,1,0:T(2,128)S(1)} all-to-all(f32[8,2,16]{2,1,0:T(2,128)S(1)} %broadcast_in_dim.2), channel_id=1, replica_groups=mesh['row'=32,'col'=8] {'col'}, dimensions={0} | all-to-all | bytes 2048 | tf_op jit(solution)/shard_map/all_to_all | solution.py:259
  18.8 1.0 add_convert_fusion.12
  19.8 2.2 %collective-permute-start.2 = (bf16[16,1536]{1,0:T(8,128)(2,1)S(1)}, bf16[16,1536]{1,0:T(8,128)(2,1)S(1)}, u32[]{:S(2)}, u32[]{:S(2)}) collective-permute-start(bf16[16,1536]{1,0:T(8,128)(2,1)S(1)} %add_convert_fusion.12), channel_id=1, source_target_pairs={{0,128},{1,129},{2,130},{3,131},{4,132},{5,133},{6,134},{7,135},{8... | collective-permute-start | bytes 147464 | tf_op jit(solution)/shard_map/ppermute | solution.py:33
  22.1 2.6 %collective-permute-start = (bf16[16,1536]{1,0:T(8,128)(2,1)S(1)}, bf16[16,1536]{1,0:T(8,128)(2,1)S(1)}, u32[]{:S(2)}, u32[]{:S(2)}) collective-permute-start(bf16[16,1536]{1,0:T(8,128)(2,1)S(1)} %add_convert_fusion.12), channel_id=1, source_target_pairs={{0,64},{1,65},{2,66},{3,67},{4,68},{5,69},{6,70},{7,71},{8,72},{9,... | collective-permute-start | bytes 147464 | tf_op jit(solution)/shard_map/ppermute | solution.py:33
  24.6 0.9 collective-permute-done.2
  25.5 0.6 collective-permute-done.1
  26.2 0.6 collective-permute-done
  26.7 1.7 %collective-permute-start.5 = (bf16[64,1536]{1,0:T(8,128)(2,1)S(1)}, bf16[64,1536]{1,0:T(8,128)(2,1)S(1)}, u32[]{:S(2)}, u32[]{:S(2)}) collective-permute-start(bf16[64,1536]{1,0:T(8,128)(2,1)S(1)} %pad_maximum_fusion.refs_0_), channel_id=1, source_target_pairs={{0,16},{1,17},{2,18},{3,19},{4,20},{5,21},{6,22},{7,23},{8,24},{9,... | collective-permute-start | bytes 589832 | tf_op jit(solution)/shard_map/ppermute | solution.py:33
  28.4 1.7 %collective-permute-start.4 = (bf16[64,1536]{1,0:T(8,128)(2,1)S(1)}, bf16[64,1536]{1,0:T(8,128)(2,1)S(1)}, u32[]{:S(2)}, u32[]{:S(2)}) collective-permute-start(bf16[64,1536]{1,0:T(8,128)(2,1)S(1)} %pad_maximum_fusion.refs_0_), channel_id=1, source_target_pairs={{0,48},{1,49},{2,50},{3,51},{4,52},{5,53},{6,54},{7,55},{8,56},{9,... | collective-permute-start | bytes 589832 | tf_op jit(solution)/shard_map/ppermute | solution.py:33
  30.0 2.0 %collective-permute-start.3 = (bf16[64,1536]{1,0:T(8,128)(2,1)S(1)}, bf16[64,1536]{1,0:T(8,128)(2,1)S(1)}, u32[]{:S(2)}, u32[]{:S(2)}) collective-permute-start(bf16[64,1536]{1,0:T(8,128)(2,1)S(1)} %pad_maximum_fusion.refs_0_), channel_id=1, source_target_pairs={{0,32},{1,33},{2,34},{3,35},{4,36},{5,37},{6,38},{7,39},{8,40},{9,... | collective-permute-start | bytes 589832 | tf_op jit(solution)/shard_map/ppermute | solution.py:33
  32.0 2.3 %shard_map.76.refs_8_.w_ref.refs_5_.refs_13_ = bf16[1536,1536]{1,0:T(8,128)(2,1)S(1)} custom-call(bf16[1536,1536]{1,0:T(8,128)(2,1)} %w_ref), custom_call_target="tpu_custom_call" | custom-call | flops 1207959552 | bytes 4718592 | tf_op jit(solution)/shard_map/pallas_call | solution.py:100
  34.4 0.8 collective-permute-done.5.refs_3_
  35.1 2.1 %collective-permute-done.3.refs_1_ = bf16[64,1536]{1,0:T(8,128)(2,1)S(1)} collective-permute-done((bf16[64,1536]{1,0:T(8,128)(2,1)S(1)}, bf16[64,1536]{1,0:T(8,128)(2,1)S(1)}, u32[]{:S(2)}, u32[]{:S(2)}) %collective-permute-start.3) | collective-permute-done | bytes 196640 | tf_op jit(solution)/shard_map/ppermute | solution.py:33
  37.2 0.5 collective-permute-start.9
  37.8 0.9 collective-permute-done.7.refs_5_
  39.0 1.7 %shard_map.77 = (bf16[512,1536]{1,0:T(8,128)(2,1)S(1)}, bf16[64,1536]{1,0:T(8,128)(2,1)S(1)}, bf16[64,768]{1,0:T(8,128)(2,1)S(1)}, bf16[64,768]{1,0:T(8,128)(2,1...) custom-call(bf16[64,1536]{1,0:T(8,128)(2,1)S(1)} %pad_maximum_fusion.refs_0_, ...), custom_call_target="tpu_custom_call" | custom-call | flops 1207959552 | bytes 4718592 | tf_op jit(solution)/shard_map/pallas_call | solution.py:158
  40.7 0.7 collective-permute-start.10
  41.4 1.4 %collective-permute-start.14 = (bf16[64,768]{1,0:T(8,128)(2,1)S(1)}, bf16[64,768]{1,0:T(8,128)(2,1)S(1)}, u32[]{:S(2)}, u32[]{:S(2)}) collective-permute-start(bf16[64,768]{1,0:T(8,128)(2,1)S(1)} %get-tuple-element.43), channel_id=1, source_target_pairs={{0,1},{1,0},{2,3},{3,2},{4,5},{5,4},{6,7},{7,6},{8,15},{9,10},{10,... | collective-permute-start | bytes 294920 | tf_op jit(solution)/shard_map/ppermute | solution.py:33
  42.8 0.6 collective-permute-start.18
  43.4 1.4 %shard_map.78 = (bf16[64,768]{1,0:T(8,128)(2,1)S(1)}, bf16[64,768]{1,0:T(8,128)(2,1)S(1)}, bf16[64,1536]{1,0:T(8,128)(2,1)S(1)}, bf16[64,1536]{1,0:T(8,128)(2,1)...) custom-call(bf16[512,1536]{1,0:T(8,128)(2,1)S(1)} %get-tuple-element.34.normed_ref, ...), custom_call_target="tpu_custom_call" | custom-call | flops 1207959552 | bytes 4718592 | tf_op jit(solution)/shard_map/pallas_call | solution.py:168
  44.8 0.6 collective-permute-done.10
  45.4 0.9 collective-permute-start.11
  46.5 2.4 %collective-permute-start.15 = (bf16[64,768]{1,0:T(8,128)(2,1)S(1)}, bf16[64,768]{1,0:T(8,128)(2,1)S(1)}, u32[]{:S(2)}, u32[]{:S(2)}) collective-permute-start(bf16[64,768]{1,0:T(8,128)(2,1)S(1)} %add_convert_fusion.7), channel_id=1, source_target_pairs={{0,7},{1,2},{2,1},{3,4},{4,3},{5,6},{6,5},{7,0},{8,9},{9,8},{10,11... | collective-permute-start | bytes 294920 | tf_op jit(solution)/shard_map/ppermute | solution.py:33
  48.9 1.0 collective-permute-start.19
  50.0 1.4 %collective-permute-done.11 = bf16[64,768]{1,0:T(8,128)(2,1)S(1)} collective-permute-done((bf16[64,768]{1,0:T(8,128)(2,1)S(1)}, bf16[64,768]{1,0:T(8,128)(2,1)S(1)}, u32[]{:S(2)}, u32[]{:S(2)}) %collective-permute-start.11) | collective-permute-done | bytes 98336 | tf_op jit(solution)/shard_map/ppermute | solution.py:33
  51.7 0.7 collective-permute-done.15
  52.4 1.4 %collective-permute-start.16 = (bf16[64,768]{1,0:T(8,128)(2,1)S(1)}, bf16[64,768]{1,0:T(8,128)(2,1)S(1)}, u32[]{:S(2)}, u32[]{:S(2)}) collective-permute-start(bf16[64,768]{1,0:T(8,128)(2,1)S(1)} %add_convert_fusion.6), channel_id=1, source_target_pairs={{0,1},{1,0},{2,3},{3,2},{4,5},{5,4},{6,7},{7,6},{8,15},{9,10},{10,... | collective-permute-start | bytes 294920 | tf_op jit(solution)/shard_map/ppermute | solution.py:33
  53.8 2.5 %collective-permute-done.12 = bf16[64,768]{1,0:T(8,128)(2,1)S(1)} collective-permute-done((bf16[64,768]{1,0:T(8,128)(2,1)S(1)}, bf16[64,768]{1,0:T(8,128)(2,1)S(1)}, u32[]{:S(2)}, u32[]{:S(2)}) %collective-permute-start.12) | collective-permute-done | bytes 98336 | tf_op jit(solution)/shard_map/ppermute | solution.py:33
  56.3 1.0 collective-permute-start.13
  57.3 0.5 collective-permute-done.19
  57.8 0.4 collective-permute-start.20
  58.2 1.7 %collective-permute-start.17 = (bf16[64,768]{1,0:T(8,128)(2,1)S(1)}, bf16[64,768]{1,0:T(8,128)(2,1)S(1)}, u32[]{:S(2)}, u32[]{:S(2)}) collective-permute-start(bf16[64,768]{1,0:T(8,128)(2,1)S(1)} %add_convert_fusion.5), channel_id=1, source_target_pairs={{0,7},{1,2},{2,1},{3,4},{4,3},{5,6},{6,5},{7,0},{8,9},{9,8},{10,11... | collective-permute-start | bytes 294920 | tf_op jit(solution)/shard_map/ppermute | solution.py:33
  59.9 3.3 %collective-permute-done.13 = bf16[64,768]{1,0:T(8,128)(2,1)S(1)} collective-permute-done((bf16[64,768]{1,0:T(8,128)(2,1)S(1)}, bf16[64,768]{1,0:T(8,128)(2,1)S(1)}, u32[]{:S(2)}, u32[]{:S(2)}) %collective-permute-start.13) | collective-permute-done | bytes 98336 | tf_op jit(solution)/shard_map/ppermute | solution.py:33
  63.3 1.2 %collective-permute-done.17 = bf16[64,768]{1,0:T(8,128)(2,1)S(1)} collective-permute-done((bf16[64,768]{1,0:T(8,128)(2,1)S(1)}, bf16[64,768]{1,0:T(8,128)(2,1)S(1)}, u32[]{:S(2)}, u32[]{:S(2)}) %collective-permute-start.17) | collective-permute-done | bytes 98336 | tf_op jit(solution)/shard_map/ppermute | solution.py:33
  64.8 1.7 %collective-permute-start.25 = (bf16[64,1536]{1,0:T(8,128)(2,1)S(1)}, bf16[64,1536]{1,0:T(8,128)(2,1)S(1)}, u32[]{:S(2)}, u32[]{:S(2)}) collective-permute-start(bf16[64,1536]{1,0:T(8,128)(2,1)S(1)} %get-tuple-element.59.refs_1_), channel_id=1, source_target_pairs={{0,7},{1,2},{2,1},{3,4},{4,3},{5,6},{6,5},{7,0},{8,9},{9,8},{10,11... | collective-permute-start | bytes 589832 | tf_op jit(solution)/shard_map/ppermute | solution.py:33
  66.6 2.0 %collective-permute-start.21 = (bf16[64,768]{1,0:T(8,128)(2,1)S(1)}, bf16[64,768]{1,0:T(8,128)(2,1)S(1)}, u32[]{:S(2)}, u32[]{:S(2)}) collective-permute-start(bf16[64,768]{1,0:T(8,128)(2,1)S(1)} %get-tuple-element.65), channel_id=1, source_target_pairs={{0,1},{1,0},{2,3},{3,2},{4,5},{5,4},{6,7},{7,6},{8,15},{9,10},{10,... | collective-permute-start | bytes 294920 | tf_op jit(solution)/shard_map/ppermute | solution.py:33
  68.6 4.0 %collective-permute-done.25.refs_0_ = bf16[64,1536]{1,0:T(8,128)(2,1)S(1)} collective-permute-done((bf16[64,1536]{1,0:T(8,128)(2,1)S(1)}, bf16[64,1536]{1,0:T(8,128)(2,1)S(1)}, u32[]{:S(2)}, u32[]{:S(2)}) %collective-permute-start.25) | collective-permute-done | bytes 196640 | tf_op jit(solution)/shard_map/ppermute | solution.py:33
  72.9 1.8 %collective-permute-start.28 = (bf16[64,768]{1,0:T(8,128)(2,1)S(1)}, bf16[64,768]{1,0:T(8,128)(2,1)S(1)}, u32[]{:S(2)}, u32[]{:S(2)}) collective-permute-start(bf16[64,768]{1,0:T(8,128)(2,1)S(1)} %collective-permute-done.26.refs_3_), channel_id=1, source_target_pairs={{0,7},{1,2},{2,1},{3,4},{4,3},{5,6},{6,5},{7,0},{8,9},{9,8},{10,11... | collective-permute-start | bytes 294920 | tf_op jit(solution)/shard_map/ppermute | solution.py:33
  74.7 1.5 %collective-permute-start.22 = (bf16[64,768]{1,0:T(8,128)(2,1)S(1)}, bf16[64,768]{1,0:T(8,128)(2,1)S(1)}, u32[]{:S(2)}, u32[]{:S(2)}) collective-permute-start(bf16[64,768]{1,0:T(8,128)(2,1)S(1)} %collective-permute-done.21.refs_2_), channel_id=1, source_target_pairs={{0,7},{1,2},{2,1},{3,4},{4,3},{5,6},{6,5},{7,0},{8,9},{9,8},{10,11... | collective-permute-start | bytes 294920 | tf_op jit(solution)/shard_map/ppermute | solution.py:33
  76.1 3.6 %collective-permute-done.28.refs_11_ = bf16[64,768]{1,0:T(8,128)(2,1)S(1)} collective-permute-done((bf16[64,768]{1,0:T(8,128)(2,1)S(1)}, bf16[64,768]{1,0:T(8,128)(2,1)S(1)}, u32[]{:S(2)}, u32[]{:S(2)}) %collective-permute-start.28) | collective-permute-done | bytes 98336 | tf_op jit(solution)/shard_map/ppermute | solution.py:33
  79.9 1.5 %collective-permute-done.22.refs_10_ = bf16[64,768]{1,0:T(8,128)(2,1)S(1)} collective-permute-done((bf16[64,768]{1,0:T(8,128)(2,1)S(1)}, bf16[64,768]{1,0:T(8,128)(2,1)S(1)}, u32[]{:S(2)}, u32[]{:S(2)}) %collective-permute-start.22) | collective-permute-done | bytes 98336 | tf_op jit(solution)/shard_map/ppermute | solution.py:33
  81.7 1.8 %collective-permute-start.31 = (bf16[64,1536]{1,0:T(8,128)(2,1)S(1)}, bf16[64,1536]{1,0:T(8,128)(2,1)S(1)}, u32[]{:S(2)}, u32[]{:S(2)}) collective-permute-start(bf16[64,1536]{1,0:T(8,128)(2,1)S(1)} %collective-permute-done.27.refs_4_), channel_id=1, source_target_pairs={{0,7},{1,2},{2,1},{3,4},{4,3},{5,6},{6,5},{7,0},{8,9},{9,8},{10,11... | collective-permute-start | bytes 589832 | tf_op jit(solution)/shard_map/ppermute | solution.py:33
  83.5 1.3 %collective-permute-done.29.refs_6_ = bf16[64,768]{1,0:T(8,128)(2,1)S(1)} collective-permute-done((bf16[64,768]{1,0:T(8,128)(2,1)S(1)}, bf16[64,768]{1,0:T(8,128)(2,1)S(1)}, u32[]{:S(2)}, u32[]{:S(2)}) %collective-permute-start.29) | collective-permute-done | bytes 98336 | tf_op jit(solution)/shard_map/ppermute | solution.py:33
  84.8 2.2 %collective-permute-start.30 = (bf16[64,768]{1,0:T(8,128)(2,1)S(1)}, bf16[64,768]{1,0:T(8,128)(2,1)S(1)}, u32[]{:S(2)}, u32[]{:S(2)}) collective-permute-start(bf16[64,768]{1,0:T(8,128)(2,1)S(1)} %collective-permute-done.29.refs_6_), channel_id=1, source_target_pairs={{0,7},{1,2},{2,1},{3,4},{4,3},{5,6},{6,5},{7,0},{8,9},{9,8},{10,11... | collective-permute-start | bytes 294920 | tf_op jit(solution)/shard_map/ppermute | solution.py:33
  87.1 1.1 collective-permute-start.24
  88.2 1.4 %shard_map.79.refs_12_ = bf16[256,1536]{1,0:T(8,128)(2,1)S(1)} custom-call(bf16[64,1536]{1,0:T(8,128)(2,1)S(1)} %collective-permute-done.25.refs_0_, bf16[64,1536]{1,0:T(8,128)(2,1)S(1)} %get-tuple-element.59.refs_1_, bf16[64,768]{1,0:T(8,128)(2,1)S(1)} %collective-permute-done.21.refs_2_, bf16[64,768]{1,0:T(8,128)(2,1)S(1)} %collective-permute-done.26.refs_3_, ...), custom_call_target="tpu_custom_call" | custom-call | flops 1207959552 | bytes 4718592 | tf_op jit(solution)/shard_map/pallas_call | solution.py:202
  89.6 1.0 collective-permute-done.30.refs_8_
  90.7 2.2 %collective-permute-done.24.refs_7_ = bf16[64,768]{1,0:T(8,128)(2,1)S(1)} collective-permute-done((bf16[64,768]{1,0:T(8,128)(2,1)S(1)}, bf16[64,768]{1,0:T(8,128)(2,1)S(1)}, u32[]{:S(2)}, u32[]{:S(2)}) %collective-permute-start.24) | collective-permute-done | bytes 98336 | tf_op jit(solution)/shard_map/ppermute | solution.py:33
  92.9 1.9 %shard_map.80 = (bf16[512,1536]{1,0:T(8,128)(2,1)S(1)}, bf16[64,1536]{1,0:T(8,128)(2,1)S(1)}, bf16[64,1536]{1,0:T(8,128)(2,1)S(1)}, bf16[64,1536]{1,0:T(8,128)(2...) custom-call(bf16[64,1536]{1,0:T(8,128)(2,1)S(1)} %collective-permute, ...), custom_call_target="tpu_custom_call" | custom-call | flops 1207959552 | bytes 4718592 | tf_op jit(solution)/shard_map/pallas_call | solution.py:231
  94.9 0.5 collective-permute-start.32
  95.9 0.4 collective-permute-done.33
  96.4 1.3 %collective-permute-start.34 = (bf16[64,1536]{1,0:T(8,128)(2,1)S(1)}, bf16[64,1536]{1,0:T(8,128)(2,1)S(1)}, u32[]{:S(2)}, u32[]{:S(2)}) collective-permute-start(bf16[64,1536]{1,0:T(8,128)(2,1)S(1)} %add_convert_fusion.2), channel_id=1, source_target_pairs={{0,16},{1,17},{2,18},{3,19},{4,20},{5,21},{6,22},{7,23},{8,72},{9,... | collective-permute-start | bytes 589832 | tf_op jit(solution)/shard_map/ppermute | solution.py:33
  97.8 1.4 %collective-permute-start.36 = (bf16[64,1536]{1,0:T(8,128)(2,1)S(1)}, bf16[64,1536]{1,0:T(8,128)(2,1)S(1)}, u32[]{:S(2)}, u32[]{:S(2)}) collective-permute-start(bf16[64,1536]{1,0:T(8,128)(2,1)S(1)} %add_convert_fusion.1), channel_id=1, source_target_pairs={{0,48},{1,49},{2,50},{3,51},{4,52},{5,53},{6,54},{7,55},{8,200},{9... | collective-permute-start | bytes 589832 | tf_op jit(solution)/shard_map/ppermute | solution.py:33
  99.2 1.6 %collective-permute-start.38 = (bf16[64,1536]{1,0:T(8,128)(2,1)S(1)}, bf16[64,1536]{1,0:T(8,128)(2,1)S(1)}, u32[]{:S(2)}, u32[]{:S(2)}) collective-permute-start(bf16[64,1536]{1,0:T(8,128)(2,1)S(1)} %add_convert_fusion), channel_id=1, source_target_pairs={{0,32},{1,33},{2,34},{3,35},{4,36},{5,37},{6,38},{7,39},{8,136},{9... | collective-permute-start | bytes 589832 | tf_op jit(solution)/shard_map/ppermute | solution.py:33
  100.9 4.3 %convolution_convert_fusion = bf16[1536,1536]{1,0:T(8,128)(2,1)} fusion(bf16[512,1536]{1,0:T(8,128)(2,1)S(1)} %get-tuple-element.34.normed_ref, bf16[512,1536]{1,0:T(8,128)(2,1)S(1)} %get-tuple-element.56), kind=kOutput, calls=%fused_computation | convolution fusion | flops 2418278400 | bytes 7864320 | tf_op jit(solution)/shard_map/dot_general | solution.py:312
  105.1 1.7 %collective-permute-done.36 = bf16[64,1536]{1,0:T(8,128)(2,1)S(1)} collective-permute-done((bf16[64,1536]{1,0:T(8,128)(2,1)S(1)}, bf16[64,1536]{1,0:T(8,128)(2,1)S(1)}, u32[]{:S(2)}, u32[]{:S(2)}) %collective-permute-start.36) | collective-permute-done | bytes 196640 | tf_op jit(solution)/shard_map/ppermute | solution.py:33
  107.0 1.6 %collective-permute-start.39 = (bf16[16,1536]{1,0:T(8,128)(2,1)S(1)}, bf16[16,1536]{1,0:T(8,128)(2,1)S(1)}, u32[]{:S(2)}, u32[]{:S(2)}) collective-permute-start(bf16[16,1536]{1,0:T(8,128)(2,1)S(1)} %get-tuple-element.61), channel_id=1, source_target_pairs={{0,192},{1,193},{2,194},{3,195},{4,196},{5,197},{6,198},{7,199},{8... | collective-permute-start | bytes 147464 | tf_op jit(solution)/shard_map/ppermute | solution.py:33
  108.6 3.1 %collective-permute-start.41 = (bf16[16,1536]{1,0:T(8,128)(2,1)S(1)}, bf16[16,1536]{1,0:T(8,128)(2,1)S(1)}, u32[]{:S(2)}, u32[]{:S(2)}) collective-permute-start(bf16[16,1536]{1,0:T(8,128)(2,1)S(1)} %get-tuple-element.62), channel_id=1, source_target_pairs={{0,128},{1,129},{2,130},{3,131},{4,132},{5,133},{6,134},{7,135},{8... | collective-permute-start | bytes 147464 | tf_op jit(solution)/shard_map/ppermute | solution.py:33
  111.7 0.8 fusion.17
  112.5 1.7 %collective-permute-done.41 = bf16[16,1536]{1,0:T(8,128)(2,1)S(1)} collective-permute-done((bf16[16,1536]{1,0:T(8,128)(2,1)S(1)}, bf16[16,1536]{1,0:T(8,128)(2,1)S(1)}, u32[]{:S(2)}, u32[]{:S(2)}) %collective-permute-start.41) | collective-permute-done | bytes 49184 | tf_op jit(solution)/shard_map/ppermute | solution.py:33
  114.2 1.6 %collective-permute-done.40 = bf16[16,1536]{1,0:T(8,128)(2,1)S(1)} collective-permute-done((bf16[16,1536]{1,0:T(8,128)(2,1)S(1)}, bf16[16,1536]{1,0:T(8,128)(2,1)S(1)}, u32[]{:S(2)}, u32[]{:S(2)}) %collective-permute-start.40) | collective-permute-done | bytes 49184 | tf_op jit(solution)/shard_map/ppermute | solution.py:33
  115.8 0.6 add_convert_fusion.11
  (59 shorter events, 3.2 us)
Async XLA Ops:
  19.8 5.7 %collective-permute-start.2 = (bf16[16,1536]{1,0:T(8,128)(2,1)S(1)}, bf16[16,1536]{1,0:T(8,128)(2,1)S(1)}, u32[]{:S(2)}, u32[]{:S(2)}) collective-permute-start(bf16[16,1536]{1,0:T(8,128)(2,1)S(1)} %add_convert_fusion.12), channel_id=1, source_target_pairs={{0,128},{1,129},{2,130},{3,131},{4,132},{5,133},{6,134},{7,135},{8... | collective-permute-start | bytes 147464 | tf_op jit(solution)/shard_map/ppermute | solution.py:33
  22.1 4.1 %collective-permute-start.1 = (bf16[16,1536]{1,0:T(8,128)(2,1)S(1)}, bf16[16,1536]{1,0:T(8,128)(2,1)S(1)}, u32[]{:S(2)}, u32[]{:S(2)}) collective-permute-start(bf16[16,1536]{1,0:T(8,128)(2,1)S(1)} %add_convert_fusion.12), channel_id=1, source_target_pairs={{0,192},{1,193},{2,194},{3,195},{4,196},{5,197},{6,198},{7,199},{8... | collective-permute-start | bytes 147464 | tf_op jit(solution)/shard_map/ppermute | solution.py:33
  22.1 4.6 %collective-permute-start = (bf16[16,1536]{1,0:T(8,128)(2,1)S(1)}, bf16[16,1536]{1,0:T(8,128)(2,1)S(1)}, u32[]{:S(2)}, u32[]{:S(2)}) collective-permute-start(bf16[16,1536]{1,0:T(8,128)(2,1)S(1)} %add_convert_fusion.12), channel_id=1, source_target_pairs={{0,64},{1,65},{2,66},{3,67},{4,68},{5,69},{6,70},{7,71},{8,72},{9,... | collective-permute-start | bytes 147464 | tf_op jit(solution)/shard_map/ppermute | solution.py:33
  26.7 8.4 %collective-permute-start.5 = (bf16[64,1536]{1,0:T(8,128)(2,1)S(1)}, bf16[64,1536]{1,0:T(8,128)(2,1)S(1)}, u32[]{:S(2)}, u32[]{:S(2)}) collective-permute-start(bf16[64,1536]{1,0:T(8,128)(2,1)S(1)} %pad_maximum_fusion.refs_0_), channel_id=1, source_target_pairs={{0,16},{1,17},{2,18},{3,19},{4,20},{5,21},{6,22},{7,23},{8,24},{9,... | collective-permute-start | bytes 589832 | tf_op jit(solution)/shard_map/ppermute | solution.py:33
  28.4 6.8 %collective-permute-start.4 = (bf16[64,1536]{1,0:T(8,128)(2,1)S(1)}, bf16[64,1536]{1,0:T(8,128)(2,1)S(1)}, u32[]{:S(2)}, u32[]{:S(2)}) collective-permute-start(bf16[64,1536]{1,0:T(8,128)(2,1)S(1)} %pad_maximum_fusion.refs_0_), channel_id=1, source_target_pairs={{0,48},{1,49},{2,50},{3,51},{4,52},{5,53},{6,54},{7,55},{8,56},{9,... | collective-permute-start | bytes 589832 | tf_op jit(solution)/shard_map/ppermute | solution.py:33
  30.0 7.2 %collective-permute-start.3 = (bf16[64,1536]{1,0:T(8,128)(2,1)S(1)}, bf16[64,1536]{1,0:T(8,128)(2,1)S(1)}, u32[]{:S(2)}, u32[]{:S(2)}) collective-permute-start(bf16[64,1536]{1,0:T(8,128)(2,1)S(1)} %pad_maximum_fusion.refs_0_), channel_id=1, source_target_pairs={{0,32},{1,33},{2,34},{3,35},{4,36},{5,37},{6,38},{7,39},{8,40},{9,... | collective-permute-start | bytes 589832 | tf_op jit(solution)/shard_map/ppermute | solution.py:33
  32.0 5.7 %collective-permute-start.6 = (bf16[64,1536]{1,0:T(8,128)(2,1)S(1)}, bf16[64,1536]{1,0:T(8,128)(2,1)S(1)}, u32[]{:S(2)}, u32[]{:S(2)}) collective-permute-start(bf16[64,1536]{1,0:T(8,128)(2,1)S(1)} %pad_maximum_fusion.refs_0_), channel_id=1, source_target_pairs={{0,8},{1,9},{2,10},{3,11},{4,12},{5,13},{6,14},{7,15},{8,0},{9,1},... | collective-permute-start | bytes 589832 | tf_op jit(solution)/shard_map/ppermute | solution.py:33
  35.1 2.6 %collective-permute-start.8 = (bf16[64,1536]{1,0:T(8,128)(2,1)S(1)}, bf16[64,1536]{1,0:T(8,128)(2,1)S(1)}, u32[]{:S(2)}, u32[]{:S(2)}) collective-permute-start(bf16[64,1536]{1,0:T(8,128)(2,1)S(1)} %collective-permute-done.4.refs_2_), channel_id=1, source_target_pairs={{0,8},{1,9},{2,10},{3,11},{4,12},{5,13},{6,14},{7,15},{8,0},{9,1},... | collective-permute-start | bytes 589832 | tf_op jit(solution)/shard_map/ppermute | solution.py:33
  37.2 1.4 %collective-permute-start.7 = (bf16[64,1536]{1,0:T(8,128)(2,1)S(1)}, bf16[64,1536]{1,0:T(8,128)(2,1)S(1)}, u32[]{:S(2)}, u32[]{:S(2)}) collective-permute-start(bf16[64,1536]{1,0:T(8,128)(2,1)S(1)} %collective-permute-done.3.refs_1_), channel_id=1, source_target_pairs={{0,8},{1,9},{2,10},{3,11},{4,12},{5,13},{6,14},{7,15},{8,0},{9,1},... | collective-permute-start | bytes 589832 | tf_op jit(solution)/shard_map/ppermute | solution.py:33
  37.2 1.7 %collective-permute-start.9 = (bf16[64,1536]{1,0:T(8,128)(2,1)S(1)}, bf16[64,1536]{1,0:T(8,128)(2,1)S(1)}, u32[]{:S(2)}, u32[]{:S(2)}) collective-permute-start(bf16[64,1536]{1,0:T(8,128)(2,1)S(1)} %collective-permute-done.5.refs_3_), channel_id=1, source_target_pairs={{0,8},{1,9},{2,10},{3,11},{4,12},{5,13},{6,14},{7,15},{8,0},{9,1},... | collective-permute-start | bytes 589832 | tf_op jit(solution)/shard_map/ppermute | solution.py:33
  40.7 4.7 %collective-permute-start.10 = (bf16[64,768]{1,0:T(8,128)(2,1)S(1)}, bf16[64,768]{1,0:T(8,128)(2,1)S(1)}, u32[]{:S(2)}, u32[]{:S(2)}) collective-permute-start(bf16[64,768]{1,0:T(8,128)(2,1)S(1)} %get-tuple-element.39), channel_id=1, source_target_pairs={{0,1},{1,0},{2,3},{3,2},{4,5},{5,4},{6,7},{7,6},{8,15},{9,10},{10,... | collective-permute-start | bytes 294920 | tf_op jit(solution)/shard_map/ppermute | solution.py:33
  41.4 5.1 %collective-permute-start.14 = (bf16[64,768]{1,0:T(8,128)(2,1)S(1)}, bf16[64,768]{1,0:T(8,128)(2,1)S(1)}, u32[]{:S(2)}, u32[]{:S(2)}) collective-permute-start(bf16[64,768]{1,0:T(8,128)(2,1)S(1)} %get-tuple-element.43), channel_id=1, source_target_pairs={{0,1},{1,0},{2,3},{3,2},{4,5},{5,4},{6,7},{7,6},{8,15},{9,10},{10,... | collective-permute-start | bytes 294920 | tf_op jit(solution)/shard_map/ppermute | solution.py:33
  42.8 6.1 %collective-permute-start.18 = (bf16[64,1536]{1,0:T(8,128)(2,1)S(1)}, bf16[64,1536]{1,0:T(8,128)(2,1)S(1)}, u32[]{:S(2)}, u32[]{:S(2)}) collective-permute-start(bf16[64,1536]{1,0:T(8,128)(2,1)S(1)} %get-tuple-element.46), channel_id=1, source_target_pairs={{0,1},{1,0},{2,3},{3,2},{4,5},{5,4},{6,7},{7,6},{8,15},{9,10},{10,... | collective-permute-start | bytes 589832 | tf_op jit(solution)/shard_map/ppermute | solution.py:33
  44.8 19.6 %copy-start = (bf16[64,1536]{1,0:T(8,128)(2,1)S(1)}, bf16[64,1536]{1,0:T(8,128)(2,1)}, u32[]{:S(2)}) copy-start(bf16[64,1536]{1,0:T(8,128)(2,1)} %param.9) | copy-start | bytes 589828
  45.4 5.9 %collective-permute-start.11 = (bf16[64,768]{1,0:T(8,128)(2,1)S(1)}, bf16[64,768]{1,0:T(8,128)(2,1)S(1)}, u32[]{:S(2)}, u32[]{:S(2)}) collective-permute-start(bf16[64,768]{1,0:T(8,128)(2,1)S(1)} %add_convert_fusion.10), channel_id=1, source_target_pairs={{0,7},{1,2},{2,1},{3,4},{4,3},{5,6},{6,5},{7,0},{8,9},{9,8},{10,11... | collective-permute-start | bytes 294920 | tf_op jit(solution)/shard_map/ppermute | solution.py:33
  46.5 5.9 %collective-permute-start.15 = (bf16[64,768]{1,0:T(8,128)(2,1)S(1)}, bf16[64,768]{1,0:T(8,128)(2,1)S(1)}, u32[]{:S(2)}, u32[]{:S(2)}) collective-permute-start(bf16[64,768]{1,0:T(8,128)(2,1)S(1)} %add_convert_fusion.7), channel_id=1, source_target_pairs={{0,7},{1,2},{2,1},{3,4},{4,3},{5,6},{6,5},{7,0},{8,9},{9,8},{10,11... | collective-permute-start | bytes 294920 | tf_op jit(solution)/shard_map/ppermute | solution.py:33
  48.9 8.8 %collective-permute-start.19 = (bf16[64,1536]{1,0:T(8,128)(2,1)S(1)}, bf16[64,1536]{1,0:T(8,128)(2,1)S(1)}, u32[]{:S(2)}, u32[]{:S(2)}) collective-permute-start(bf16[64,1536]{1,0:T(8,128)(2,1)S(1)} %add_convert_fusion.4), channel_id=1, source_target_pairs={{0,7},{1,2},{2,1},{3,4},{4,3},{5,6},{6,5},{7,0},{8,9},{9,8},{10,11... | collective-permute-start | bytes 589832 | tf_op jit(solution)/shard_map/ppermute | solution.py:33
  51.4 4.9 %collective-permute-start.12 = (bf16[64,768]{1,0:T(8,128)(2,1)S(1)}, bf16[64,768]{1,0:T(8,128)(2,1)S(1)}, u32[]{:S(2)}, u32[]{:S(2)}) collective-permute-start(bf16[64,768]{1,0:T(8,128)(2,1)S(1)} %add_convert_fusion.9), channel_id=1, source_target_pairs={{0,1},{1,0},{2,3},{3,2},{4,5},{5,4},{6,7},{7,6},{8,15},{9,10},{10,... | collective-permute-start | bytes 294920 | tf_op jit(solution)/shard_map/ppermute | solution.py:33
  52.4 5.8 %collective-permute-start.16 = (bf16[64,768]{1,0:T(8,128)(2,1)S(1)}, bf16[64,768]{1,0:T(8,128)(2,1)S(1)}, u32[]{:S(2)}, u32[]{:S(2)}) collective-permute-start(bf16[64,768]{1,0:T(8,128)(2,1)S(1)} %add_convert_fusion.6), channel_id=1, source_target_pairs={{0,1},{1,0},{2,3},{3,2},{4,5},{5,4},{6,7},{7,6},{8,15},{9,10},{10,... | collective-permute-start | bytes 294920 | tf_op jit(solution)/shard_map/ppermute | solution.py:33
  56.3 7.0 %collective-permute-start.13 = (bf16[64,768]{1,0:T(8,128)(2,1)S(1)}, bf16[64,768]{1,0:T(8,128)(2,1)S(1)}, u32[]{:S(2)}, u32[]{:S(2)}) collective-permute-start(bf16[64,768]{1,0:T(8,128)(2,1)S(1)} %add_convert_fusion.8), channel_id=1, source_target_pairs={{0,7},{1,2},{2,1},{3,4},{4,3},{5,6},{6,5},{7,0},{8,9},{9,8},{10,11... | collective-permute-start | bytes 294920 | tf_op jit(solution)/shard_map/ppermute | solution.py:33
  57.8 6.6 %collective-permute-start.20 = (bf16[64,1536]{1,0:T(8,128)(2,1)S(1)}, bf16[64,1536]{1,0:T(8,128)(2,1)S(1)}, u32[]{:S(2)}, u32[]{:S(2)}) collective-permute-start(bf16[64,1536]{1,0:T(8,128)(2,1)S(1)} %add_convert_fusion.3), channel_id=1, source_target_pairs={{0,1},{1,0},{2,3},{3,2},{4,5},{5,4},{6,7},{7,6},{8,15},{9,10},{10,... | collective-permute-start | bytes 589832 | tf_op jit(solution)/shard_map/ppermute | solution.py:33
  58.2 6.2 %collective-permute-start.17 = (bf16[64,768]{1,0:T(8,128)(2,1)S(1)}, bf16[64,768]{1,0:T(8,128)(2,1)S(1)}, u32[]{:S(2)}, u32[]{:S(2)}) collective-permute-start(bf16[64,768]{1,0:T(8,128)(2,1)S(1)} %add_convert_fusion.5), channel_id=1, source_target_pairs={{0,7},{1,2},{2,1},{3,4},{4,3},{5,6},{6,5},{7,0},{8,9},{9,8},{10,11... | collective-permute-start | bytes 294920 | tf_op jit(solution)/shard_map/ppermute | solution.py:33
  64.8 7.8 %collective-permute-start.25 = (bf16[64,1536]{1,0:T(8,128)(2,1)S(1)}, bf16[64,1536]{1,0:T(8,128)(2,1)S(1)}, u32[]{:S(2)}, u32[]{:S(2)}) collective-permute-start(bf16[64,1536]{1,0:T(8,128)(2,1)S(1)} %get-tuple-element.59.refs_1_), channel_id=1, source_target_pairs={{0,7},{1,2},{2,1},{3,4},{4,3},{5,6},{6,5},{7,0},{8,9},{9,8},{10,11... | collective-permute-start | bytes 589832 | tf_op jit(solution)/shard_map/ppermute | solution.py:33
  66.5 6.4 %collective-permute-start.26 = (bf16[64,768]{1,0:T(8,128)(2,1)S(1)}, bf16[64,768]{1,0:T(8,128)(2,1)S(1)}, u32[]{:S(2)}, u32[]{:S(2)}) collective-permute-start(bf16[64,768]{1,0:T(8,128)(2,1)S(1)} %get-tuple-element.64), channel_id=1, source_target_pairs={{0,1},{1,0},{2,3},{3,2},{4,5},{5,4},{6,7},{7,6},{8,15},{9,10},{10,... | collective-permute-start | bytes 294920 | tf_op jit(solution)/shard_map/ppermute | solution.py:33
  66.6 8.1 %collective-permute-start.21 = (bf16[64,768]{1,0:T(8,128)(2,1)S(1)}, bf16[64,768]{1,0:T(8,128)(2,1)S(1)}, u32[]{:S(2)}, u32[]{:S(2)}) collective-permute-start(bf16[64,768]{1,0:T(8,128)(2,1)S(1)} %get-tuple-element.65), channel_id=1, source_target_pairs={{0,1},{1,0},{2,3},{3,2},{4,5},{5,4},{6,7},{7,6},{8,15},{9,10},{10,... | collective-permute-start | bytes 294920 | tf_op jit(solution)/shard_map/ppermute | solution.py:33
  72.6 9.1 %collective-permute-start.27 = (bf16[64,1536]{1,0:T(8,128)(2,1)S(1)}, bf16[64,1536]{1,0:T(8,128)(2,1)S(1)}, u32[]{:S(2)}, u32[]{:S(2)}) collective-permute-start(bf16[64,1536]{1,0:T(8,128)(2,1)S(1)} %collective-permute-done.25.refs_0_), channel_id=1, source_target_pairs={{0,1},{1,0},{2,3},{3,2},{4,5},{5,4},{6,7},{7,6},{8,15},{9,10},{10,... | collective-permute-start | bytes 589832 | tf_op jit(solution)/shard_map/ppermute | solution.py:33
  72.9 6.8 %collective-permute-start.28 = (bf16[64,768]{1,0:T(8,128)(2,1)S(1)}, bf16[64,768]{1,0:T(8,128)(2,1)S(1)}, u32[]{:S(2)}, u32[]{:S(2)}) collective-permute-start(bf16[64,768]{1,0:T(8,128)(2,1)S(1)} %collective-permute-done.26.refs_3_), channel_id=1, source_target_pairs={{0,7},{1,2},{2,1},{3,4},{4,3},{5,6},{6,5},{7,0},{8,9},{9,8},{10,11... | collective-permute-start | bytes 294920 | tf_op jit(solution)/shard_map/ppermute | solution.py:33
  74.7 6.8 %collective-permute-start.22 = (bf16[64,768]{1,0:T(8,128)(2,1)S(1)}, bf16[64,768]{1,0:T(8,128)(2,1)S(1)}, u32[]{:S(2)}, u32[]{:S(2)}) collective-permute-start(bf16[64,768]{1,0:T(8,128)(2,1)S(1)} %collective-permute-done.21.refs_2_), channel_id=1, source_target_pairs={{0,7},{1,2},{2,1},{3,4},{4,3},{5,6},{6,5},{7,0},{8,9},{9,8},{10,11... | collective-permute-start | bytes 294920 | tf_op jit(solution)/shard_map/ppermute | solution.py:33
  79.7 5.2 %collective-permute-start.29 = (bf16[64,768]{1,0:T(8,128)(2,1)S(1)}, bf16[64,768]{1,0:T(8,128)(2,1)S(1)}, u32[]{:S(2)}, u32[]{:S(2)}) collective-permute-start(bf16[64,768]{1,0:T(8,128)(2,1)S(1)} %collective-permute-done.28.refs_11_), channel_id=1, source_target_pairs={{0,1},{1,0},{2,3},{3,2},{4,5},{5,4},{6,7},{7,6},{8,15},{9,10},{10,... | collective-permute-start | bytes 294920 | tf_op jit(solution)/shard_map/ppermute | solution.py:33
  81.4 5.6 %collective-permute-start.23 = (bf16[64,768]{1,0:T(8,128)(2,1)S(1)}, bf16[64,768]{1,0:T(8,128)(2,1)S(1)}, u32[]{:S(2)}, u32[]{:S(2)}) collective-permute-start(bf16[64,768]{1,0:T(8,128)(2,1)S(1)} %collective-permute-done.22.refs_10_), channel_id=1, source_target_pairs={{0,1},{1,0},{2,3},{3,2},{4,5},{5,4},{6,7},{7,6},{8,15},{9,10},{10,... | collective-permute-start | bytes 294920 | tf_op jit(solution)/shard_map/ppermute | solution.py:33
  81.7 11.2 %collective-permute-start.31 = (bf16[64,1536]{1,0:T(8,128)(2,1)S(1)}, bf16[64,1536]{1,0:T(8,128)(2,1)S(1)}, u32[]{:S(2)}, u32[]{:S(2)}) collective-permute-start(bf16[64,1536]{1,0:T(8,128)(2,1)S(1)} %collective-permute-done.27.refs_4_), channel_id=1, source_target_pairs={{0,7},{1,2},{2,1},{3,4},{4,3},{5,6},{6,5},{7,0},{8,9},{9,8},{10,11... | collective-permute-start | bytes 589832 | tf_op jit(solution)/shard_map/ppermute | solution.py:33
  84.8 5.8 %collective-permute-start.30 = (bf16[64,768]{1,0:T(8,128)(2,1)S(1)}, bf16[64,768]{1,0:T(8,128)(2,1)S(1)}, u32[]{:S(2)}, u32[]{:S(2)}) collective-permute-start(bf16[64,768]{1,0:T(8,128)(2,1)S(1)} %collective-permute-done.29.refs_6_), channel_id=1, source_target_pairs={{0,7},{1,2},{2,1},{3,4},{4,3},{5,6},{6,5},{7,0},{8,9},{9,8},{10,11... | collective-permute-start | bytes 294920 | tf_op jit(solution)/shard_map/ppermute | solution.py:33
  87.1 5.8 %collective-permute-start.24 = (bf16[64,768]{1,0:T(8,128)(2,1)S(1)}, bf16[64,768]{1,0:T(8,128)(2,1)S(1)}, u32[]{:S(2)}, u32[]{:S(2)}) collective-permute-start(bf16[64,768]{1,0:T(8,128)(2,1)S(1)} %collective-permute-done.23.refs_5_), channel_id=1, source_target_pairs={{0,7},{1,2},{2,1},{3,4},{4,3},{5,6},{6,5},{7,0},{8,9},{9,8},{10,11... | collective-permute-start | bytes 294920 | tf_op jit(solution)/shard_map/ppermute | solution.py:33
  94.8 1.5 %collective-permute-start.33 = (bf16[64,1536]{1,0:T(8,128)(2,1)S(1)}, bf16[64,1536]{1,0:T(8,128)(2,1)S(1)}, u32[]{:S(2)}, u32[]{:S(2)}) collective-permute-start(bf16[64,1536]{1,0:T(8,128)(2,1)S(1)} %get-tuple-element.51), channel_id=1, source_target_pairs={{0,8},{1,9},{2,10},{3,11},{4,12},{5,13},{6,14},{7,15},{8,0},{9,1},... | collective-permute-start | bytes 589832 | tf_op jit(solution)/shard_map/ppermute | solution.py:33
  94.9 10.2 %collective-permute-start.32 = (bf16[64,1536]{1,0:T(8,128)(2,1)S(1)}, bf16[64,1536]{1,0:T(8,128)(2,1)S(1)}, u32[]{:S(2)}, u32[]{:S(2)}) collective-permute-start(bf16[64,1536]{1,0:T(8,128)(2,1)S(1)} %get-tuple-element.49), channel_id=1, source_target_pairs={{0,8},{1,9},{2,10},{3,11},{4,12},{5,13},{6,14},{7,15},{8,0},{9,1},... | collective-permute-start | bytes 589832 | tf_op jit(solution)/shard_map/ppermute | solution.py:33
  95.4 2.3 %collective-permute-start.35 = (bf16[64,1536]{1,0:T(8,128)(2,1)S(1)}, bf16[64,1536]{1,0:T(8,128)(2,1)S(1)}, u32[]{:S(2)}, u32[]{:S(2)}) collective-permute-start(bf16[64,1536]{1,0:T(8,128)(2,1)S(1)} %get-tuple-element.53), channel_id=1, source_target_pairs={{0,8},{1,9},{2,10},{3,11},{4,12},{5,13},{6,14},{7,15},{8,0},{9,1},... | collective-permute-start | bytes 589832 | tf_op jit(solution)/shard_map/ppermute | solution.py:33
  95.7 3.4 %collective-permute-start.37 = (bf16[64,1536]{1,0:T(8,128)(2,1)S(1)}, bf16[64,1536]{1,0:T(8,128)(2,1)S(1)}, u32[]{:S(2)}, u32[]{:S(2)}) collective-permute-start(bf16[64,1536]{1,0:T(8,128)(2,1)S(1)} %get-tuple-element.55), channel_id=1, source_target_pairs={{0,8},{1,9},{2,10},{3,11},{4,12},{5,13},{6,14},{7,15},{8,0},{9,1},... | collective-permute-start | bytes 589832 | tf_op jit(solution)/shard_map/ppermute | solution.py:33
  96.4 8.7 %collective-permute-start.34 = (bf16[64,1536]{1,0:T(8,128)(2,1)S(1)}, bf16[64,1536]{1,0:T(8,128)(2,1)S(1)}, u32[]{:S(2)}, u32[]{:S(2)}) collective-permute-start(bf16[64,1536]{1,0:T(8,128)(2,1)S(1)} %add_convert_fusion.2), channel_id=1, source_target_pairs={{0,16},{1,17},{2,18},{3,19},{4,20},{5,21},{6,22},{7,23},{8,72},{9,... | collective-permute-start | bytes 589832 | tf_op jit(solution)/shard_map/ppermute | solution.py:33
  97.8 9.1 %collective-permute-start.36 = (bf16[64,1536]{1,0:T(8,128)(2,1)S(1)}, bf16[64,1536]{1,0:T(8,128)(2,1)S(1)}, u32[]{:S(2)}, u32[]{:S(2)}) collective-permute-start(bf16[64,1536]{1,0:T(8,128)(2,1)S(1)} %add_convert_fusion.1), channel_id=1, source_target_pairs={{0,48},{1,49},{2,50},{3,51},{4,52},{5,53},{6,54},{7,55},{8,200},{9... | collective-permute-start | bytes 589832 | tf_op jit(solution)/shard_map/ppermute | solution.py:33
  99.2 7.6 %collective-permute-start.38 = (bf16[64,1536]{1,0:T(8,128)(2,1)S(1)}, bf16[64,1536]{1,0:T(8,128)(2,1)S(1)}, u32[]{:S(2)}, u32[]{:S(2)}) collective-permute-start(bf16[64,1536]{1,0:T(8,128)(2,1)S(1)} %add_convert_fusion), channel_id=1, source_target_pairs={{0,32},{1,33},{2,34},{3,35},{4,36},{5,37},{6,38},{7,39},{8,136},{9... | collective-permute-start | bytes 589832 | tf_op jit(solution)/shard_map/ppermute | solution.py:33
  107.0 5.5 %collective-permute-start.39 = (bf16[16,1536]{1,0:T(8,128)(2,1)S(1)}, bf16[16,1536]{1,0:T(8,128)(2,1)S(1)}, u32[]{:S(2)}, u32[]{:S(2)}) collective-permute-start(bf16[16,1536]{1,0:T(8,128)(2,1)S(1)} %get-tuple-element.61), channel_id=1, source_target_pairs={{0,192},{1,193},{2,194},{3,195},{4,196},{5,197},{6,198},{7,199},{8... | collective-permute-start | bytes 147464 | tf_op jit(solution)/shard_map/ppermute | solution.py:33
  108.6 5.6 %collective-permute-start.41 = (bf16[16,1536]{1,0:T(8,128)(2,1)S(1)}, bf16[16,1536]{1,0:T(8,128)(2,1)S(1)}, u32[]{:S(2)}, u32[]{:S(2)}) collective-permute-start(bf16[16,1536]{1,0:T(8,128)(2,1)S(1)} %get-tuple-element.62), channel_id=1, source_target_pairs={{0,128},{1,129},{2,130},{3,131},{4,132},{5,133},{6,134},{7,135},{8... | collective-permute-start | bytes 147464 | tf_op jit(solution)/shard_map/ppermute | solution.py:33
  111.7 4.1 %collective-permute-start.40 = (bf16[16,1536]{1,0:T(8,128)(2,1)S(1)}, bf16[16,1536]{1,0:T(8,128)(2,1)S(1)}, u32[]{:S(2)}, u32[]{:S(2)}) collective-permute-start(bf16[16,1536]{1,0:T(8,128)(2,1)S(1)} %get-tuple-element.63), channel_id=1, source_target_pairs={{0,64},{1,65},{2,66},{3,67},{4,68},{5,69},{6,70},{7,71},{8,24},{9,... | collective-permute-start | bytes 147464 | tf_op jit(solution)/shard_map/ppermute | solution.py:33

commit v6 on v5

--- a/solution.py
+++ b/solution.py
@@ -9,7 +9,7 @@
 F32, BF16 = jnp.float32, jnp.bfloat16
 
 NX, NY, NC, NZ = 4, 4, 2, 8
-GATHER_X, GATHER_Y, SUM_FIRST, SUM_LAST = (0, 1, 3, 2), (0, 2, 3, 1), (0, 1, 3, 2), (0, 3, 1, 2)
+GATHER_X, GATHER_Y, SUM_FIRST, SUM_LAST = (0, 1, 3, 2), (0, 1, 2, 3), (0, 3, 2, 1), (0, 3, 1, 2)
 TOKENS_OWN = 16
 TOKENS_Z = 64
 TOKENS = 512
@@ -37,8 +37,8 @@
     return send(value, lambda x, y, c, z: (x ^ k, y, c, z))
 
 
-def send_y(value, shift):
-    return send(value, lambda x, y, c, z: (x, y + shift, c, z))
+def send_y(value, k):
+    return send(value, lambda x, y, c, z: (x, y ^ k, c, z))
 
 
 def send_plane(value, k, x_core):
@@ -63,7 +63,7 @@
 def gathered_row(core_shift, i, p):
     row = lax.axis_index("row")
     x, y, c = row // (NY * NC), (row // NC) % NY, row % NC
-    x, y = x ^ GATHER_X[p], (y + NY - GATHER_Y[i]) % NY
+    x, y = x ^ GATHER_X[p], y ^ GATHER_Y[i]
     return row_of((x * NY + y) * NC + (c + core_shift) % NC)
 
 
@@ -133,8 +133,7 @@
     ]
 
 
-SUM_CUT = (1, 0, 0, 1, 0, 1, 1, 0)
-GATHER_CUT = (0, 0, 1, 0, 1, 1, 0, 1)
+CUT = (1, 0, 0, 1, 0, 1, 1, 0)
 
 
 def far_kernel(*refs):
@@ -146,11 +145,11 @@
                 normed_ref[rows, :] = pieces[core_shift * 4 + i][
                     p * TOKENS_OWN : (p + 1) * TOKENS_OWN, :
                 ]
-    multiply(normed_ref[HALF:, :], w_ref, halves_of(SUM_CUT[4:], outs))
+    multiply(normed_ref[HALF:, :], w_ref, halves_of(CUT[4:], outs))
 
 
 def near_kernel(normed_ref, w_ref, *outs):
-    multiply(normed_ref[:HALF, :], w_ref, halves_of(SUM_CUT[:4], outs))
+    multiply(normed_ref[:HALF, :], w_ref, halves_of(CUT[:4], outs))
 
 
 def far_pre(pieces, weight):
@@ -158,8 +157,8 @@
     return pl.pallas_call(
         far_kernel,
         in_specs=[WHOLE] * 9,
-        out_specs=[WHOLE] * (5 + sum(SUM_CUT[4:])),
-        out_shape=[jax.ShapeDtypeStruct((TOKENS, depth), BF16)] + shapes_of(SUM_CUT[4:], width),
+        out_specs=[WHOLE] * (5 + sum(CUT[4:])),
+        out_shape=[jax.ShapeDtypeStruct((TOKENS, depth), BF16)] + shapes_of(CUT[4:], width),
         **settings(weight, 16),
     )(*pieces, weight)
 
@@ -168,8 +167,8 @@
     return pl.pallas_call(
         near_kernel,
         in_specs=[WHOLE] * 2,
-        out_specs=[WHOLE] * (4 + sum(SUM_CUT[:4])),
-        out_shape=shapes_of(SUM_CUT[:4], weight.shape[1]),
+        out_specs=[WHOLE] * (4 + sum(CUT[:4])),
+        out_shape=shapes_of(CUT[:4], weight.shape[1]),
         **settings(weight, 16),
     )(normed, weight)
 
@@ -191,7 +190,7 @@
 
 def near_back_kernel(*refs):
     *pieces, w_ref, out_ref, rows_ref = refs
-    fill(rows_ref, halves_of(GATHER_CUT[:4], pieces))
+    fill(rows_ref, halves_of(CUT[:4], pieces))
     rows = rows_ref[...]
     for start in range(0, w_ref.shape[0], TILE):
         part = slice(start, start + TILE)
@@ -212,7 +211,7 @@
 def far_back_kernel(*refs):
     *pieces, near_ref, w_ref, slopes_ref = refs[:-9]
     outs, product = refs[-9:-1], refs[-1]
-    fill(slopes_ref, halves_of(GATHER_CUT, pieces))
+    fill(slopes_ref, halves_of(CUT, pieces))
     product[:HALF, :] = near_ref[...].astype(F32)
     rows = slopes_ref[HALF:, :]
     for start in range(0, w_ref.shape[0], TILE):
@@ -250,19 +249,65 @@
     return total
 
 
+LANES = 128
+
+
+def center_kernel(*refs):
+    sources, (centered_ref, stats_ref, *vectors), sems = refs[:3], refs[3:7], refs[7]
+    copies = [
+        pltpu.make_async_copy(source, target, sems.at[i])
+        for i, (source, target) in enumerate(zip(sources, [centered_ref] + vectors))
+    ]
+    for copy in copies:
+        copy.start()
+    copies[0].wait()
+    rows = centered_ref[...]
+    mean = jnp.sum(rows, axis=1, keepdims=True) / rows.shape[1]
+    centered = rows - mean
+    centered_ref[...] = centered
+    square = jnp.sum(centered * centered, axis=1, keepdims=True)
+    lane = lax.broadcasted_iota(jnp.int32, (rows.shape[0], LANES), 1)
+    stats = jnp.where(lane < LANES // 2, mean, square)
+    for k in range(NZ):
+        stats_ref[k] = stats
+    for copy in copies[1:]:
+        copy.wait()
+
+
+def scale_kernel(centered_ref, own_ref, every_ref, gain_ref, bias_ref, normed_ref):
+    centered = centered_ref[...]
+    local = centered.shape[1]
+    means = [every_ref[k][:, :1] for k in range(NZ)]
+    squares = [every_ref[k][:, LANES // 2 : LANES // 2 + 1] for k in range(NZ)]
+    mean = sum(means) / NZ
+    spread = sum(square + local * (m - mean) * (m - mean) for m, square in zip(means, squares))
+    scale = lax.rsqrt(spread / D + 1e-05)
+    moved = centered + (own_ref[0][:, :1] - mean)
+    normed_ref[...] = (moved * scale * gain_ref[...][None, :] + bias_ref[...][None, :]).astype(BF16)
+
+
 def normalize(inputs, gain, bias):
-    local = inputs.shape[1]
-    local_mean = jnp.sum(inputs, axis=1) / local
-    centered = inputs - local_mean[:, None]
-    local_square = jnp.sum(centered * centered, axis=1)
-    stats = jnp.stack([local_mean, local_square])
-    every = lax.all_to_all(jnp.broadcast_to(stats[None], (NZ,) + stats.shape), "col", 0, 0)
-    mean = jnp.mean(every[:, 0, :], axis=0)
-    offset = every[:, 0, :] - mean[None, :]
-    spread = (jnp.sum(every[:, 1, :], axis=0) + local * jnp.sum(offset * offset, axis=0)) / D
-    scale = lax.rsqrt(spread + 1e-05)
-    moved = centered + (local_mean - mean)[:, None]
-    return (moved * scale[:, None] * gain[None, :] + bias[None, :]).astype(BF16)
+    rows = inputs.shape[0]
+    centered, own, gain, bias = pl.pallas_call(
+        center_kernel,
+        in_specs=[pl.BlockSpec(memory_space=pl.ANY)] * 3,
+        out_specs=[WHOLE] * 4,
+        out_shape=[
+            jax.ShapeDtypeStruct(inputs.shape, F32),
+            jax.ShapeDtypeStruct((NZ, rows, LANES), F32),
+            jax.ShapeDtypeStruct(gain.shape, F32),
+            jax.ShapeDtypeStruct(bias.shape, F32),
+        ],
+        scratch_shapes=[pltpu.SemaphoreType.DMA((3,))],
+        compiler_params=pltpu.CompilerParams(vmem_limit_bytes=60 << 20),
+    )(inputs, gain, bias)
+    every = lax.all_to_all(own, "col", 0, 0)
+    return pl.pallas_call(
+        scale_kernel,
+        in_specs=[WHOLE] * 5,
+        out_specs=WHOLE,
+        out_shape=jax.ShapeDtypeStruct(inputs.shape, BF16),
+    )(centered, own, every, gain, bias)
 
 
 def reduce_chain(parts):
@@ -291,17 +336,18 @@
     other = [send_core(v) for v in along_y]
 
     gathered, *far = far_pre(along_y + other, weight)
-    three, four, five, six = halves_of(SUM_CUT[4:], far)
-    back, own, one, two = halves_of(SUM_CUT[:4], near_pre(gathered, weight))
+    three, four, five, six = halves_of(CUT[4:], far)
+    back, own, one, two = halves_of(CUT[:4], near_pre(gathered, weight))
     longer = [reduce_chain([four[h], five[h], two[h], back[h]]) for h in range(2)]
     shorter = reduce_chain([three[0], six[0], one[0]])
     pre = add(own[0], jnp.concatenate(longer, axis=1), shorter)
     slopes = jax.vjp(gelu_tanh, pre)[1](d_act.astype(F32))[0].astype(BF16)
 
     half = weight.shape[1] // 2
-    longer = [gather_chain(slopes[:, h * half : (h + 1) * half], 1, 4) for h in range(2)]
-    block_1, block_6, block_3, block_4 = ([chain[i] for chain in longer] for i in range(4))
-    block_7, block_2, block_5 = ([v] for v in gather_chain(slopes, -1, 3))
+    slopes, *cut = lax.optimization_barrier((slopes, slopes[:, :half], slopes[:, half:]))
+    longer = [gather_chain(part, -1, 4) for part in cut]
+    block_7, block_2, block_5, block_4 = ([chain[i] for chain in longer] for i in range(4))
+    block_1, block_6, block_3 = ([v] for v in gather_chain(slopes, 1, 3))
     nearest = block_7 + [slopes] + block_1 + block_2
     pieces = nearest + block_3 + block_4 + block_5 + block_6
     pre, _ = lax.optimization_barrier((pre, block_4[0]))

time: 117 us -> 117 us (level)
  starting transfers between devices: 45.4 us -> 41.6 us
  Pallas kernels: 8.77 us -> 12.3 us
  waiting for transfers between devices: 35.6 us -> 38.1 us
  other arithmetic: 5.55 us -> 3.14 us
    ppermute x42, starting transfers between devices: 45.4 us -> 41.6 us  [send(): return lax.ppermute(value, ('row', 'col'), pairs_of(target))]
    pallas_call x0 -> x2, Pallas kernels: none -> 3.53 us  [the longest x1 1.77 us: normalize(): pl.pallas_call(center_kernel, in_specs=[pl.BlockSpec(memory_space=pl.ANY)...]
    ppermute x42, waiting for transfers between devices: 35.6 us -> 38.1 us  [send(): return lax.ppermute(value, ('row', 'col'), pairs_of(target))]
    reduce_sum x4 -> x0, other arithmetic: 2.15 us -> none  [the longest x1 1.09 us: normalize(): local_square = jnp.sum(centered * centered, axis=1)]
  transfers between devices with their start and end apart: 42 -> 42, of which waited for: 25 -> 26; matrix products, arithmetic and copies ran while one was open for 5% -> 5% of each run, Pallas kernels for 4% -> 4%
where the time goes in v6:
time: 117 us
  starting transfers between devices  41.6 us (36%)
  waiting for transfers between devices  38.1 us (33%)
  blocking collectives  17 us (15%)
  Pallas kernels  12.3 us (11%)
  matrix products  4.27 us (4%)
  other arithmetic  3.14 us (3%)
    ppermute x42, starting transfers between devices, send(): return lax.ppermute(value, ('row', 'col'), pairs_of(target))  41.6 us
    ppermute x42, waiting for transfers between devices, send(): return lax.ppermute(value, ('row', 'col'), pairs_of(target))  38.1 us
    all_to_all x1, blocking collectives, normalize(): every = lax.all_to_all(own, 'col', 0, 0)  17 us
    dot_general x1, matrix products, per_device(): lax.dot_general(gathered, slopes_all, (((0,), (0,)), ((), ())), preferred...  4.27 us
    pallas_call x1, Pallas kernels, stage(): pl.pallas_call(stage_kernel, in_specs=[pl.BlockSpec(memory_space=pl.ANY)]...  2.34 us
  transfers between devices with their start and end apart: 42, of which 26 were waited for; matrix products, arithmetic and copies ran while one was open for 5% of the time, Pallas kernels for 4%

profile of v6, /device:TPU:2, one launch (start us, length us, event | category | flops | bytes accessed | tf_op | source)
XLA Modules:
  0.0 117.2 jit_solution(17410429827876945234)
XLA Ops:
  0.6 1.8 %shard_map.76 = (f32[16,1536]{1,0:T(8,128)}, f32[8,16,128]{2,1,0:T(8,128)}, f32[1536]{0:T(1024)}, f32[1536]{0:T(1024)}) custom-call(f32[16,1536]{1,0:T(8,128)} %refs_0_.1, f32[1536]{0:T(1024)} %refs_1_.1, f32[1536]{0:T(1024)} %refs_2_.1), custom_call_target="tpu_custom_call" | custom-call | tf_op jit(solution)/shard_map/pallas_call | solution.py:291
  2.4 17.0 %all_to_all.5.every_ref = f32[8,16,128]{2,1,0:T(8,128)} all-to-all(f32[8,16,128]{2,1,0:T(8,128)} %get-tuple-element.39.own_ref), channel_id=1, replica_groups=mesh['row'=32,'col'=8] {'col'}, dimensions={0} | all-to-all | bytes 131072 | tf_op jit(solution)/shard_map/all_to_all | solution.py:304
  19.4 1.8 %shard_map.77 = bf16[16,1536]{1,0:T(8,128)(2,1)} custom-call(f32[16,1536]{1,0:T(8,128)} %get-tuple-element.38.centered_ref, f32[8,16,128]{2,1,0:T(8,128)} %get-tuple-element.39.own_ref, f32[8,16,128]{2,1,0:T(8,128)} %all_to_all.5.every_ref, f32[1536]{0:T(1024)} %get-tuple-element.40.gain_ref, f32[1536]{0:T(1024)} %get-tuple-element.41.bias_ref), custom_call_target="tpu_custom_call" | custom-call | tf_op jit(solution)/shard_map/pallas_call | solution.py:305
  21.1 2.1 %collective-permute-start.2 = (bf16[16,1536]{1,0:T(8,128)(2,1)}, bf16[16,1536]{1,0:T(8,128)(2,1)S(1)}, u32[]{:S(2)}, u32[]{:S(2)}) collective-permute-start(bf16[16,1536]{1,0:T(8,128)(2,1)} %shard_map.77), channel_id=1, source_target_pairs={{0,128},{1,129},{2,130},{3,131},{4,132},{5,133},{6,134},{7,135},{8... | collective-permute-start | bytes 147464 | tf_op jit(solution)/shard_map/ppermute | solution.py:33
  23.3 2.6 %collective-permute-start = (bf16[16,1536]{1,0:T(8,128)(2,1)}, bf16[16,1536]{1,0:T(8,128)(2,1)S(1)}, u32[]{:S(2)}, u32[]{:S(2)}) collective-permute-start(bf16[16,1536]{1,0:T(8,128)(2,1)} %shard_map.77), channel_id=1, source_target_pairs={{0,64},{1,65},{2,66},{3,67},{4,68},{5,69},{6,70},{7,71},{8,72},{9,... | collective-permute-start | bytes 147464 | tf_op jit(solution)/shard_map/ppermute | solution.py:33
  25.8 1.1 collective-permute-done.2
  26.9 0.6 collective-permute-done.1
  27.6 0.6 collective-permute-done
  28.1 0.8 pad_maximum_fusion.refs_0_
  28.9 3.1 %collective-permute-start.5 = (bf16[64,1536]{1,0:T(8,128)(2,1)S(1)}, bf16[64,1536]{1,0:T(8,128)(2,1)S(1)}, u32[]{:S(2)}, u32[]{:S(2)}) collective-permute-start(bf16[64,1536]{1,0:T(8,128)(2,1)S(1)} %pad_maximum_fusion.refs_0_), channel_id=1, source_target_pairs={{0,48},{1,49},{2,50},{3,51},{4,52},{5,53},{6,54},{7,55},{8,56},{9,... | collective-permute-start | bytes 589832 | tf_op jit(solution)/shard_map/ppermute | solution.py:33
  32.0 0.6 collective-permute-start.4
  32.7 0.5 collective-permute-start.3
  33.1 2.3 %shard_map.78.refs_8_.w_ref.refs_6_.refs_13_ = bf16[1536,1536]{1,0:T(8,128)(2,1)S(1)} custom-call(bf16[1536,1536]{1,0:T(8,128)(2,1)} %w_ref), custom_call_target="tpu_custom_call" | custom-call | flops 1207959552 | bytes 4718592 | tf_op jit(solution)/shard_map/pallas_call | solution.py:100
  35.5 2.1 %collective-permute-done.5.refs_3_ = bf16[64,1536]{1,0:T(8,128)(2,1)S(1)} collective-permute-done((bf16[64,1536]{1,0:T(8,128)(2,1)S(1)}, bf16[64,1536]{1,0:T(8,128)(2,1)S(1)}, u32[]{:S(2)}, u32[]{:S(2)}) %collective-permute-start.5) | collective-permute-done | bytes 196640 | tf_op jit(solution)/shard_map/ppermute | solution.py:33
  37.6 1.6 %collective-permute-done.4.refs_2_ = bf16[64,1536]{1,0:T(8,128)(2,1)S(1)} collective-permute-done((bf16[64,1536]{1,0:T(8,128)(2,1)S(1)}, bf16[64,1536]{1,0:T(8,128)(2,1)S(1)}, u32[]{:S(2)}, u32[]{:S(2)}) %collective-permute-start.4) | collective-permute-done | bytes 196640 | tf_op jit(solution)/shard_map/ppermute | solution.py:33
  39.2 0.5 collective-permute-start.7
  39.7 0.9 collective-permute-done.8.refs_6_
  41.2 1.7 %shard_map.79 = (bf16[512,1536]{1,0:T(8,128)(2,1)S(1)}, bf16[64,1536]{1,0:T(8,128)(2,1)S(1)}, bf16[64,768]{1,0:T(8,128)(2,1)S(1)}, bf16[64,768]{1,0:T(8,128)(2,1...) custom-call(bf16[64,1536]{1,0:T(8,128)(2,1)S(1)} %pad_maximum_fusion.refs_0_, ...), custom_call_target="tpu_custom_call" | custom-call | flops 1207959552 | bytes 4718592 | tf_op jit(solution)/shard_map/pallas_call | solution.py:157
  42.9 0.7 collective-permute-start.10
  43.6 1.5 %collective-permute-start.14 = (bf16[64,768]{1,0:T(8,128)(2,1)S(1)}, bf16[64,768]{1,0:T(8,128)(2,1)S(1)}, u32[]{:S(2)}, u32[]{:S(2)}) collective-permute-start(bf16[64,768]{1,0:T(8,128)(2,1)S(1)} %get-tuple-element.54), channel_id=1, source_target_pairs={{0,1},{1,0},{2,3},{3,2},{4,5},{5,4},{6,7},{7,6},{8,15},{9,10},{10,... | collective-permute-start | bytes 294920 | tf_op jit(solution)/shard_map/ppermute | solution.py:33
  45.1 0.6 collective-permute-start.18
  45.6 1.4 %shard_map.80 = (bf16[64,768]{1,0:T(8,128)(2,1)S(1)}, bf16[64,768]{1,0:T(8,128)(2,1)S(1)}, bf16[64,1536]{1,0:T(8,128)(2,1)S(1)}, bf16[64,1536]{1,0:T(8,128)(2,1)...) custom-call(bf16[512,1536]{1,0:T(8,128)(2,1)S(1)} %get-tuple-element.45.normed_ref, ...), custom_call_target="tpu_custom_call" | custom-call | flops 1207959552 | bytes 4718592 | tf_op jit(solution)/shard_map/pallas_call | solution.py:167
  47.0 0.6 collective-permute-done.10
  48.0 0.7 collective-permute-done.14
  48.7 2.4 %collective-permute-start.15 = (bf16[64,768]{1,0:T(8,128)(2,1)S(1)}, bf16[64,768]{1,0:T(8,128)(2,1)S(1)}, u32[]{:S(2)}, u32[]{:S(2)}) collective-permute-start(bf16[64,768]{1,0:T(8,128)(2,1)S(1)} %add_convert_fusion.7), channel_id=1, source_target_pairs={{0,7},{1,2},{2,1},{3,4},{4,3},{5,6},{6,5},{7,0},{8,9},{9,8},{10,11... | collective-permute-start | bytes 294920 | tf_op jit(solution)/shard_map/ppermute | solution.py:33
  51.2 1.0 collective-permute-start.19
  52.2 1.4 %collective-permute-done.11 = bf16[64,768]{1,0:T(8,128)(2,1)S(1)} collective-permute-done((bf16[64,768]{1,0:T(8,128)(2,1)S(1)}, bf16[64,768]{1,0:T(8,128)(2,1)S(1)}, u32[]{:S(2)}, u32[]{:S(2)}) %collective-permute-start.11) | collective-permute-done | bytes 98336 | tf_op jit(solution)/shard_map/ppermute | solution.py:33
  53.7 0.9 collective-permute-done.15
  54.7 1.4 %collective-permute-start.16 = (bf16[64,768]{1,0:T(8,128)(2,1)S(1)}, bf16[64,768]{1,0:T(8,128)(2,1)S(1)}, u32[]{:S(2)}, u32[]{:S(2)}) collective-permute-start(bf16[64,768]{1,0:T(8,128)(2,1)S(1)} %add_convert_fusion.6), channel_id=1, source_target_pairs={{0,1},{1,0},{2,3},{3,2},{4,5},{5,4},{6,7},{7,6},{8,15},{9,10},{10,... | collective-permute-start | bytes 294920 | tf_op jit(solution)/shard_map/ppermute | solution.py:33
  56.0 2.3 %collective-permute-done.12 = bf16[64,768]{1,0:T(8,128)(2,1)S(1)} collective-permute-done((bf16[64,768]{1,0:T(8,128)(2,1)S(1)}, bf16[64,768]{1,0:T(8,128)(2,1)S(1)}, u32[]{:S(2)}, u32[]{:S(2)}) %collective-permute-start.12) | collective-permute-done | bytes 98336 | tf_op jit(solution)/shard_map/ppermute | solution.py:33
  58.4 1.3 %collective-permute-start.13 = (bf16[64,768]{1,0:T(8,128)(2,1)S(1)}, bf16[64,768]{1,0:T(8,128)(2,1)S(1)}, u32[]{:S(2)}, u32[]{:S(2)}) collective-permute-start(bf16[64,768]{1,0:T(8,128)(2,1)S(1)} %add_convert_fusion.8), channel_id=1, source_target_pairs={{0,7},{1,2},{2,1},{3,4},{4,3},{5,6},{6,5},{7,0},{8,9},{9,8},{10,11... | collective-permute-start | bytes 294920 | tf_op jit(solution)/shard_map/ppermute | solution.py:33
  59.7 0.9 collective-permute-start.20
  60.6 1.4 %collective-permute-start.17 = (bf16[64,768]{1,0:T(8,128)(2,1)S(1)}, bf16[64,768]{1,0:T(8,128)(2,1)S(1)}, u32[]{:S(2)}, u32[]{:S(2)}) collective-permute-start(bf16[64,768]{1,0:T(8,128)(2,1)S(1)} %add_convert_fusion.5), channel_id=1, source_target_pairs={{0,7},{1,2},{2,1},{3,4},{4,3},{5,6},{6,5},{7,0},{8,9},{9,8},{10,11... | collective-permute-start | bytes 294920 | tf_op jit(solution)/shard_map/ppermute | solution.py:33
  62.0 3.3 %collective-permute-done.13 = bf16[64,768]{1,0:T(8,128)(2,1)S(1)} collective-permute-done((bf16[64,768]{1,0:T(8,128)(2,1)S(1)}, bf16[64,768]{1,0:T(8,128)(2,1)S(1)}, u32[]{:S(2)}, u32[]{:S(2)}) %collective-permute-start.13) | collective-permute-done | bytes 98336 | tf_op jit(solution)/shard_map/ppermute | solution.py:33
  65.3 1.2 %collective-permute-done.17 = bf16[64,768]{1,0:T(8,128)(2,1)S(1)} collective-permute-done((bf16[64,768]{1,0:T(8,128)(2,1)S(1)}, bf16[64,768]{1,0:T(8,128)(2,1)S(1)}, u32[]{:S(2)}, u32[]{:S(2)}) %collective-permute-start.17) | collective-permute-done | bytes 98336 | tf_op jit(solution)/shard_map/ppermute | solution.py:33
  66.6 0.3 fusion.2
  67.1 2.0 %collective-permute-start.21 = (bf16[64,768]{1,0:T(8,128)(2,1)S(1)}, bf16[64,768]{1,0:T(8,128)(2,1)S(1)}, u32[]{:S(2)}, u32[]{:S(2)}) collective-permute-start(bf16[64,768]{1,0:T(8,128)(2,1)S(1)} %get-tuple-element.58), channel_id=1, source_target_pairs={{0,7},{1,2},{2,1},{3,4},{4,3},{5,6},{6,5},{7,0},{8,9},{9,8},{10,11... | collective-permute-start | bytes 294920 | tf_op jit(solution)/shard_map/ppermute | solution.py:33
  69.1 1.3 %collective-permute-start.25 = (bf16[64,768]{1,0:T(8,128)(2,1)S(1)}, bf16[64,768]{1,0:T(8,128)(2,1)S(1)}, u32[]{:S(2)}, u32[]{:S(2)}) collective-permute-start(bf16[64,768]{1,0:T(8,128)(2,1)S(1)} %get-tuple-element.60), channel_id=1, source_target_pairs={{0,7},{1,2},{2,1},{3,4},{4,3},{5,6},{6,5},{7,0},{8,9},{9,8},{10,11... | collective-permute-start | bytes 294920 | tf_op jit(solution)/shard_map/ppermute | solution.py:33
  70.4 4.2 %collective-permute-done.26.refs_3_ = bf16[64,1536]{1,0:T(8,128)(2,1)S(1)} collective-permute-done((bf16[64,1536]{1,0:T(8,128)(2,1)S(1)}, bf16[64,1536]{1,0:T(8,128)(2,1)S(1)}, u32[]{:S(2)}, u32[]{:S(2)}) %collective-permute-start.26) | collective-permute-done | bytes 196640 | tf_op jit(solution)/shard_map/ppermute | solution.py:33
  74.5 1.2 %collective-permute-start.28 = (bf16[64,1536]{1,0:T(8,128)(2,1)S(1)}, bf16[64,1536]{1,0:T(8,128)(2,1)S(1)}, u32[]{:S(2)}, u32[]{:S(2)}) collective-permute-start(bf16[64,1536]{1,0:T(8,128)(2,1)S(1)} %collective-permute-done.26.refs_3_), channel_id=1, source_target_pairs={{0,7},{1,2},{2,1},{3,4},{4,3},{5,6},{6,5},{7,0},{8,9},{9,8},{10,11... | collective-permute-start | bytes 589832 | tf_op jit(solution)/shard_map/ppermute | solution.py:33
  75.7 2.0 %collective-permute-start.27 = (bf16[64,768]{1,0:T(8,128)(2,1)S(1)}, bf16[64,768]{1,0:T(8,128)(2,1)S(1)}, u32[]{:S(2)}, u32[]{:S(2)}) collective-permute-start(bf16[64,768]{1,0:T(8,128)(2,1)S(1)} %collective-permute-done.25.refs_1_), channel_id=1, source_target_pairs={{0,1},{1,0},{2,3},{3,2},{4,5},{5,4},{6,7},{7,6},{8,15},{9,10},{10,... | collective-permute-start | bytes 294920 | tf_op jit(solution)/shard_map/ppermute | solution.py:33
  77.7 2.6 %collective-permute-done.22.refs_4_ = bf16[64,768]{1,0:T(8,128)(2,1)S(1)} collective-permute-done((bf16[64,768]{1,0:T(8,128)(2,1)S(1)}, bf16[64,768]{1,0:T(8,128)(2,1)S(1)}, u32[]{:S(2)}, u32[]{:S(2)}) %collective-permute-start.22) | collective-permute-done | bytes 98336 | tf_op jit(solution)/shard_map/ppermute | solution.py:33
  80.3 2.1 %collective-permute-start.23 = (bf16[64,768]{1,0:T(8,128)(2,1)S(1)}, bf16[64,768]{1,0:T(8,128)(2,1)S(1)}, u32[]{:S(2)}, u32[]{:S(2)}) collective-permute-start(bf16[64,768]{1,0:T(8,128)(2,1)S(1)} %collective-permute-done.22.refs_4_), channel_id=1, source_target_pairs={{0,7},{1,2},{2,1},{3,4},{4,3},{5,6},{6,5},{7,0},{8,9},{9,8},{10,11... | collective-permute-start | bytes 294920 | tf_op jit(solution)/shard_map/ppermute | solution.py:33
  82.4 1.9 %collective-permute-start.30 = (bf16[64,768]{1,0:T(8,128)(2,1)S(1)}, bf16[64,768]{1,0:T(8,128)(2,1)S(1)}, u32[]{:S(2)}, u32[]{:S(2)}) collective-permute-start(bf16[64,768]{1,0:T(8,128)(2,1)S(1)} %collective-permute-done.27.refs_5_), channel_id=1, source_target_pairs={{0,7},{1,2},{2,1},{3,4},{4,3},{5,6},{6,5},{7,0},{8,9},{9,8},{10,11... | collective-permute-start | bytes 294920 | tf_op jit(solution)/shard_map/ppermute | solution.py:33
  84.3 2.8 %collective-permute-done.23.refs_9_ = bf16[64,768]{1,0:T(8,128)(2,1)S(1)} collective-permute-done((bf16[64,768]{1,0:T(8,128)(2,1)S(1)}, bf16[64,768]{1,0:T(8,128)(2,1)S(1)}, u32[]{:S(2)}, u32[]{:S(2)}) %collective-permute-start.23) | collective-permute-done | bytes 98336 | tf_op jit(solution)/shard_map/ppermute | solution.py:33
  87.1 2.2 %collective-permute-done.30.refs_10_ = bf16[64,768]{1,0:T(8,128)(2,1)S(1)} collective-permute-done((bf16[64,768]{1,0:T(8,128)(2,1)S(1)}, bf16[64,768]{1,0:T(8,128)(2,1)S(1)}, u32[]{:S(2)}, u32[]{:S(2)}) %collective-permute-start.30) | collective-permute-done | bytes 98336 | tf_op jit(solution)/shard_map/ppermute | solution.py:33
  89.3 1.4 %shard_map.81.refs_12_ = bf16[256,1536]{1,0:T(8,128)(2,1)S(1)} custom-call(bf16[64,768]{1,0:T(8,128)(2,1)S(1)} %collective-permute-done.21.refs_0_, bf16[64,768]{1,0:T(8,128)(2,1)S(1)} %collective-permute-done.25.refs_1_, bf16[64,1536]{1,0:T(8,128)(2,1)S(1)} %get-tuple-element.61.refs_2_, bf16[64,1536]{1,0:T(8,128)(2,1)S(1)} %collective-permute-done.26.refs_3_, ...), custom_call_target="tpu_custom_call" | custom-call | flops 1207959552 | bytes 4718592 | tf_op jit(solution)/shard_map/pallas_call | solution.py:201
  90.7 1.0 collective-permute-done.24.refs_7_
  91.8 2.2 %collective-permute-done.31.refs_8_ = bf16[64,768]{1,0:T(8,128)(2,1)S(1)} collective-permute-done((bf16[64,768]{1,0:T(8,128)(2,1)S(1)}, bf16[64,768]{1,0:T(8,128)(2,1)S(1)}, u32[]{:S(2)}, u32[]{:S(2)}) %collective-permute-start.31) | collective-permute-done | bytes 98336 | tf_op jit(solution)/shard_map/ppermute | solution.py:33
  93.9 1.9 %shard_map.82 = (bf16[512,1536]{1,0:T(8,128)(2,1)S(1)}, bf16[64,1536]{1,0:T(8,128)(2,1)S(1)}, bf16[64,1536]{1,0:T(8,128)(2,1)S(1)}, bf16[64,1536]{1,0:T(8,128)(2...) custom-call(bf16[64,768]{1,0:T(8,128)(2,1)S(1)} %collective-permute-, ...), custom_call_target="tpu_custom_call" | custom-call | flops 1207959552 | bytes 4718592 | tf_op jit(solution)/shard_map/pallas_call | solution.py:230
  96.0 0.5 collective-permute-start.32
  96.6 0.4 collective-permute-start.37
  97.0 0.4 collective-permute-done.33
  97.4 2.5 %collective-permute-start.34 = (bf16[64,1536]{1,0:T(8,128)(2,1)S(1)}, bf16[64,1536]{1,0:T(8,128)(2,1)S(1)}, u32[]{:S(2)}, u32[]{:S(2)}) collective-permute-start(bf16[64,1536]{1,0:T(8,128)(2,1)S(1)} %add_convert_fusion.2), channel_id=1, source_target_pairs={{0,48},{1,49},{2,50},{3,51},{4,52},{5,53},{6,54},{7,55},{8,200},{9... | collective-permute-start | bytes 589832 | tf_op jit(solution)/shard_map/ppermute | solution.py:33
  100.0 0.8 collective-permute-start.36
  100.8 1.1 collective-permute-start.38
  101.9 4.3 %convolution_convert_fusion = bf16[1536,1536]{1,0:T(8,128)(2,1)} fusion(bf16[512,1536]{1,0:T(8,128)(2,1)S(1)} %get-tuple-element.45.normed_ref, bf16[512,1536]{1,0:T(8,128)(2,1)S(1)} %get-tuple-element.70), kind=kOutput, calls=%fused_computation | convolution fusion | flops 2418278400 | bytes 7864320 | tf_op jit(solution)/shard_map/dot_general | solution.py:358
  106.2 1.1 collective-permute-done.36
  107.7 1.6 %collective-permute-start.39 = (bf16[16,1536]{1,0:T(8,128)(2,1)S(1)}, bf16[16,1536]{1,0:T(8,128)(2,1)S(1)}, u32[]{:S(2)}, u32[]{:S(2)}) collective-permute-start(bf16[16,1536]{1,0:T(8,128)(2,1)S(1)} %get-tuple-element.75), channel_id=1, source_target_pairs={{0,192},{1,193},{2,194},{3,195},{4,196},{5,197},{6,198},{7,199},{8... | collective-permute-start | bytes 147464 | tf_op jit(solution)/shard_map/ppermute | solution.py:33
  109.3 3.1 %collective-permute-start.41 = (bf16[16,1536]{1,0:T(8,128)(2,1)S(1)}, bf16[16,1536]{1,0:T(8,128)(2,1)S(1)}, u32[]{:S(2)}, u32[]{:S(2)}) collective-permute-start(bf16[16,1536]{1,0:T(8,128)(2,1)S(1)} %get-tuple-element.76), channel_id=1, source_target_pairs={{0,128},{1,129},{2,130},{3,131},{4,132},{5,133},{6,134},{7,135},{8... | collective-permute-start | bytes 147464 | tf_op jit(solution)/shard_map/ppermute | solution.py:33
  112.4 0.8 fusion.17
  113.2 1.6 %collective-permute-done.41 = bf16[16,1536]{1,0:T(8,128)(2,1)S(1)} collective-permute-done((bf16[16,1536]{1,0:T(8,128)(2,1)S(1)}, bf16[16,1536]{1,0:T(8,128)(2,1)S(1)}, u32[]{:S(2)}, u32[]{:S(2)}) %collective-permute-start.41) | collective-permute-done | bytes 49184 | tf_op jit(solution)/shard_map/ppermute | solution.py:33
  114.9 1.6 %collective-permute-done.40 = bf16[16,1536]{1,0:T(8,128)(2,1)S(1)} collective-permute-done((bf16[16,1536]{1,0:T(8,128)(2,1)S(1)}, bf16[16,1536]{1,0:T(8,128)(2,1)S(1)}, u32[]{:S(2)}, u32[]{:S(2)}) %collective-permute-start.40) | collective-permute-done | bytes 49184 | tf_op jit(solution)/shard_map/ppermute | solution.py:33
  116.5 0.6 add_convert_fusion.11
  (50 shorter events, 2.2 us)
Async XLA Ops:
  21.1 5.8 %collective-permute-start.2 = (bf16[16,1536]{1,0:T(8,128)(2,1)}, bf16[16,1536]{1,0:T(8,128)(2,1)S(1)}, u32[]{:S(2)}, u32[]{:S(2)}) collective-permute-start(bf16[16,1536]{1,0:T(8,128)(2,1)} %shard_map.77), channel_id=1, source_target_pairs={{0,128},{1,129},{2,130},{3,131},{4,132},{5,133},{6,134},{7,135},{8... | collective-permute-start | bytes 147464 | tf_op jit(solution)/shard_map/ppermute | solution.py:33
  23.2 4.3 %collective-permute-start.1 = (bf16[16,1536]{1,0:T(8,128)(2,1)}, bf16[16,1536]{1,0:T(8,128)(2,1)S(1)}, u32[]{:S(2)}, u32[]{:S(2)}) collective-permute-start(bf16[16,1536]{1,0:T(8,128)(2,1)} %shard_map.77), channel_id=1, source_target_pairs={{0,192},{1,193},{2,194},{3,195},{4,196},{5,197},{6,198},{7,199},{8... | collective-permute-start | bytes 147464 | tf_op jit(solution)/shard_map/ppermute | solution.py:33
  23.3 4.9 %collective-permute-start = (bf16[16,1536]{1,0:T(8,128)(2,1)}, bf16[16,1536]{1,0:T(8,128)(2,1)S(1)}, u32[]{:S(2)}, u32[]{:S(2)}) collective-permute-start(bf16[16,1536]{1,0:T(8,128)(2,1)} %shard_map.77), channel_id=1, source_target_pairs={{0,64},{1,65},{2,66},{3,67},{4,68},{5,69},{6,70},{7,71},{8,72},{9,... | collective-permute-start | bytes 147464 | tf_op jit(solution)/shard_map/ppermute | solution.py:33
  28.9 8.6 %collective-permute-start.5 = (bf16[64,1536]{1,0:T(8,128)(2,1)S(1)}, bf16[64,1536]{1,0:T(8,128)(2,1)S(1)}, u32[]{:S(2)}, u32[]{:S(2)}) collective-permute-start(bf16[64,1536]{1,0:T(8,128)(2,1)S(1)} %pad_maximum_fusion.refs_0_), channel_id=1, source_target_pairs={{0,48},{1,49},{2,50},{3,51},{4,52},{5,53},{6,54},{7,55},{8,56},{9,... | collective-permute-start | bytes 589832 | tf_op jit(solution)/shard_map/ppermute | solution.py:33
  32.0 7.2 %collective-permute-start.4 = (bf16[64,1536]{1,0:T(8,128)(2,1)S(1)}, bf16[64,1536]{1,0:T(8,128)(2,1)S(1)}, u32[]{:S(2)}, u32[]{:S(2)}) collective-permute-start(bf16[64,1536]{1,0:T(8,128)(2,1)S(1)} %pad_maximum_fusion.refs_0_), channel_id=1, source_target_pairs={{0,32},{1,33},{2,34},{3,35},{4,36},{5,37},{6,38},{7,39},{8,40},{9,... | collective-permute-start | bytes 589832 | tf_op jit(solution)/shard_map/ppermute | solution.py:33
  32.7 6.6 %collective-permute-start.3 = (bf16[64,1536]{1,0:T(8,128)(2,1)S(1)}, bf16[64,1536]{1,0:T(8,128)(2,1)S(1)}, u32[]{:S(2)}, u32[]{:S(2)}) collective-permute-start(bf16[64,1536]{1,0:T(8,128)(2,1)S(1)} %pad_maximum_fusion.refs_0_), channel_id=1, source_target_pairs={{0,16},{1,17},{2,18},{3,19},{4,20},{5,21},{6,22},{7,23},{8,24},{9,... | collective-permute-start | bytes 589832 | tf_op jit(solution)/shard_map/ppermute | solution.py:33
  33.1 6.6 %collective-permute-start.6 = (bf16[64,1536]{1,0:T(8,128)(2,1)S(1)}, bf16[64,1536]{1,0:T(8,128)(2,1)S(1)}, u32[]{:S(2)}, u32[]{:S(2)}) collective-permute-start(bf16[64,1536]{1,0:T(8,128)(2,1)S(1)} %pad_maximum_fusion.refs_0_), channel_id=1, source_target_pairs={{0,8},{1,9},{2,10},{3,11},{4,12},{5,13},{6,14},{7,15},{8,0},{9,1},... | collective-permute-start | bytes 589832 | tf_op jit(solution)/shard_map/ppermute | solution.py:33
  39.2 1.4 %collective-permute-start.8 = (bf16[64,1536]{1,0:T(8,128)(2,1)S(1)}, bf16[64,1536]{1,0:T(8,128)(2,1)S(1)}, u32[]{:S(2)}, u32[]{:S(2)}) collective-permute-start(bf16[64,1536]{1,0:T(8,128)(2,1)S(1)} %collective-permute-done.4.refs_2_), channel_id=1, source_target_pairs={{0,8},{1,9},{2,10},{3,11},{4,12},{5,13},{6,14},{7,15},{8,0},{9,1},... | collective-permute-start | bytes 589832 | tf_op jit(solution)/shard_map/ppermute | solution.py:33
  39.2 1.7 %collective-permute-start.7 = (bf16[64,1536]{1,0:T(8,128)(2,1)S(1)}, bf16[64,1536]{1,0:T(8,128)(2,1)S(1)}, u32[]{:S(2)}, u32[]{:S(2)}) collective-permute-start(bf16[64,1536]{1,0:T(8,128)(2,1)S(1)} %collective-permute-done.3.refs_1_), channel_id=1, source_target_pairs={{0,8},{1,9},{2,10},{3,11},{4,12},{5,13},{6,14},{7,15},{8,0},{9,1},... | collective-permute-start | bytes 589832 | tf_op jit(solution)/shard_map/ppermute | solution.py:33
  39.7 1.5 %collective-permute-start.9 = (bf16[64,1536]{1,0:T(8,128)(2,1)S(1)}, bf16[64,1536]{1,0:T(8,128)(2,1)S(1)}, u32[]{:S(2)}, u32[]{:S(2)}) collective-permute-start(bf16[64,1536]{1,0:T(8,128)(2,1)S(1)} %collective-permute-done.5.refs_3_), channel_id=1, source_target_pairs={{0,8},{1,9},{2,10},{3,11},{4,12},{5,13},{6,14},{7,15},{8,0},{9,1},... | collective-permute-start | bytes 589832 | tf_op jit(solution)/shard_map/ppermute | solution.py:33
  42.9 4.7 %collective-permute-start.10 = (bf16[64,768]{1,0:T(8,128)(2,1)S(1)}, bf16[64,768]{1,0:T(8,128)(2,1)S(1)}, u32[]{:S(2)}, u32[]{:S(2)}) collective-permute-start(bf16[64,768]{1,0:T(8,128)(2,1)S(1)} %get-tuple-element.50), channel_id=1, source_target_pairs={{0,1},{1,0},{2,3},{3,2},{4,5},{5,4},{6,7},{7,6},{8,15},{9,10},{10,... | collective-permute-start | bytes 294920 | tf_op jit(solution)/shard_map/ppermute | solution.py:33
  43.6 5.1 %collective-permute-start.14 = (bf16[64,768]{1,0:T(8,128)(2,1)S(1)}, bf16[64,768]{1,0:T(8,128)(2,1)S(1)}, u32[]{:S(2)}, u32[]{:S(2)}) collective-permute-start(bf16[64,768]{1,0:T(8,128)(2,1)S(1)} %get-tuple-element.54), channel_id=1, source_target_pairs={{0,1},{1,0},{2,3},{3,2},{4,5},{5,4},{6,7},{7,6},{8,15},{9,10},{10,... | collective-permute-start | bytes 294920 | tf_op jit(solution)/shard_map/ppermute | solution.py:33
  45.1 6.1 %collective-permute-start.18 = (bf16[64,1536]{1,0:T(8,128)(2,1)S(1)}, bf16[64,1536]{1,0:T(8,128)(2,1)S(1)}, u32[]{:S(2)}, u32[]{:S(2)}) collective-permute-start(bf16[64,1536]{1,0:T(8,128)(2,1)S(1)} %get-tuple-element.57), channel_id=1, source_target_pairs={{0,1},{1,0},{2,3},{3,2},{4,5},{5,4},{6,7},{7,6},{8,15},{9,10},{10,... | collective-permute-start | bytes 589832 | tf_op jit(solution)/shard_map/ppermute | solution.py:33
  47.0 19.5 %copy-start = (bf16[64,1536]{1,0:T(8,128)(2,1)S(1)}, bf16[64,1536]{1,0:T(8,128)(2,1)}, u32[]{:S(2)}) copy-start(bf16[64,1536]{1,0:T(8,128)(2,1)} %param.9) | copy-start | bytes 589828
  47.7 5.9 %collective-permute-start.11 = (bf16[64,768]{1,0:T(8,128)(2,1)S(1)}, bf16[64,768]{1,0:T(8,128)(2,1)S(1)}, u32[]{:S(2)}, u32[]{:S(2)}) collective-permute-start(bf16[64,768]{1,0:T(8,128)(2,1)S(1)} %add_convert_fusion.10), channel_id=1, source_target_pairs={{0,7},{1,2},{2,1},{3,4},{4,3},{5,6},{6,5},{7,0},{8,9},{9,8},{10,11... | collective-permute-start | bytes 294920 | tf_op jit(solution)/shard_map/ppermute | solution.py:33
  48.7 5.9 %collective-permute-start.15 = (bf16[64,768]{1,0:T(8,128)(2,1)S(1)}, bf16[64,768]{1,0:T(8,128)(2,1)S(1)}, u32[]{:S(2)}, u32[]{:S(2)}) collective-permute-start(bf16[64,768]{1,0:T(8,128)(2,1)S(1)} %add_convert_fusion.7), channel_id=1, source_target_pairs={{0,7},{1,2},{2,1},{3,4},{4,3},{5,6},{6,5},{7,0},{8,9},{9,8},{10,11... | collective-permute-start | bytes 294920 | tf_op jit(solution)/shard_map/ppermute | solution.py:33
  51.2 8.5 %collective-permute-start.19 = (bf16[64,1536]{1,0:T(8,128)(2,1)S(1)}, bf16[64,1536]{1,0:T(8,128)(2,1)S(1)}, u32[]{:S(2)}, u32[]{:S(2)}) collective-permute-start(bf16[64,1536]{1,0:T(8,128)(2,1)S(1)} %add_convert_fusion.4), channel_id=1, source_target_pairs={{0,7},{1,2},{2,1},{3,4},{4,3},{5,6},{6,5},{7,0},{8,9},{9,8},{10,11... | collective-permute-start | bytes 589832 | tf_op jit(solution)/shard_map/ppermute | solution.py:33
  53.6 4.7 %collective-permute-start.12 = (bf16[64,768]{1,0:T(8,128)(2,1)S(1)}, bf16[64,768]{1,0:T(8,128)(2,1)S(1)}, u32[]{:S(2)}, u32[]{:S(2)}) collective-permute-start(bf16[64,768]{1,0:T(8,128)(2,1)S(1)} %add_convert_fusion.9), channel_id=1, source_target_pairs={{0,1},{1,0},{2,3},{3,2},{4,5},{5,4},{6,7},{7,6},{8,15},{9,10},{10,... | collective-permute-start | bytes 294920 | tf_op jit(solution)/shard_map/ppermute | solution.py:33
  54.7 5.9 %collective-permute-start.16 = (bf16[64,768]{1,0:T(8,128)(2,1)S(1)}, bf16[64,768]{1,0:T(8,128)(2,1)S(1)}, u32[]{:S(2)}, u32[]{:S(2)}) collective-permute-start(bf16[64,768]{1,0:T(8,128)(2,1)S(1)} %add_convert_fusion.6), channel_id=1, source_target_pairs={{0,1},{1,0},{2,3},{3,2},{4,5},{5,4},{6,7},{7,6},{8,15},{9,10},{10,... | collective-permute-start | bytes 294920 | tf_op jit(solution)/shard_map/ppermute | solution.py:33
  58.4 7.0 %collective-permute-start.13 = (bf16[64,768]{1,0:T(8,128)(2,1)S(1)}, bf16[64,768]{1,0:T(8,128)(2,1)S(1)}, u32[]{:S(2)}, u32[]{:S(2)}) collective-permute-start(bf16[64,768]{1,0:T(8,128)(2,1)S(1)} %add_convert_fusion.8), channel_id=1, source_target_pairs={{0,7},{1,2},{2,1},{3,4},{4,3},{5,6},{6,5},{7,0},{8,9},{9,8},{10,11... | collective-permute-start | bytes 294920 | tf_op jit(solution)/shard_map/ppermute | solution.py:33
  59.7 6.8 %collective-permute-start.20 = (bf16[64,1536]{1,0:T(8,128)(2,1)S(1)}, bf16[64,1536]{1,0:T(8,128)(2,1)S(1)}, u32[]{:S(2)}, u32[]{:S(2)}) collective-permute-start(bf16[64,1536]{1,0:T(8,128)(2,1)S(1)} %add_convert_fusion.3), channel_id=1, source_target_pairs={{0,1},{1,0},{2,3},{3,2},{4,5},{5,4},{6,7},{7,6},{8,15},{9,10},{10,... | collective-permute-start | bytes 589832 | tf_op jit(solution)/shard_map/ppermute | solution.py:33
  60.6 5.9 %collective-permute-start.17 = (bf16[64,768]{1,0:T(8,128)(2,1)S(1)}, bf16[64,768]{1,0:T(8,128)(2,1)S(1)}, u32[]{:S(2)}, u32[]{:S(2)}) collective-permute-start(bf16[64,768]{1,0:T(8,128)(2,1)S(1)} %add_convert_fusion.5), channel_id=1, source_target_pairs={{0,7},{1,2},{2,1},{3,4},{4,3},{5,6},{6,5},{7,0},{8,9},{9,8},{10,11... | collective-permute-start | bytes 294920 | tf_op jit(solution)/shard_map/ppermute | solution.py:33
  66.9 7.6 %collective-permute-start.26 = (bf16[64,1536]{1,0:T(8,128)(2,1)S(1)}, bf16[64,1536]{1,0:T(8,128)(2,1)S(1)}, u32[]{:S(2)}, u32[]{:S(2)}) collective-permute-start(bf16[64,1536]{1,0:T(8,128)(2,1)S(1)} %get-tuple-element.61.refs_2_), channel_id=1, source_target_pairs={{0,1},{1,0},{2,3},{3,2},{4,5},{5,4},{6,7},{7,6},{8,15},{9,10},{10,... | collective-permute-start | bytes 589832 | tf_op jit(solution)/shard_map/ppermute | solution.py:33
  67.1 8.6 %collective-permute-start.21 = (bf16[64,768]{1,0:T(8,128)(2,1)S(1)}, bf16[64,768]{1,0:T(8,128)(2,1)S(1)}, u32[]{:S(2)}, u32[]{:S(2)}) collective-permute-start(bf16[64,768]{1,0:T(8,128)(2,1)S(1)} %get-tuple-element.58), channel_id=1, source_target_pairs={{0,7},{1,2},{2,1},{3,4},{4,3},{5,6},{6,5},{7,0},{8,9},{9,8},{10,11... | collective-permute-start | bytes 294920 | tf_op jit(solution)/shard_map/ppermute | solution.py:33
  69.1 6.6 %collective-permute-start.25 = (bf16[64,768]{1,0:T(8,128)(2,1)S(1)}, bf16[64,768]{1,0:T(8,128)(2,1)S(1)}, u32[]{:S(2)}, u32[]{:S(2)}) collective-permute-start(bf16[64,768]{1,0:T(8,128)(2,1)S(1)} %get-tuple-element.60), channel_id=1, source_target_pairs={{0,7},{1,2},{2,1},{3,4},{4,3},{5,6},{6,5},{7,0},{8,9},{9,8},{10,11... | collective-permute-start | bytes 294920 | tf_op jit(solution)/shard_map/ppermute | solution.py:33
  74.5 9.8 %collective-permute-start.28 = (bf16[64,1536]{1,0:T(8,128)(2,1)S(1)}, bf16[64,1536]{1,0:T(8,128)(2,1)S(1)}, u32[]{:S(2)}, u32[]{:S(2)}) collective-permute-start(bf16[64,1536]{1,0:T(8,128)(2,1)S(1)} %collective-permute-done.26.refs_3_), channel_id=1, source_target_pairs={{0,7},{1,2},{2,1},{3,4},{4,3},{5,6},{6,5},{7,0},{8,9},{9,8},{10,11... | collective-permute-start | bytes 589832 | tf_op jit(solution)/shard_map/ppermute | solution.py:33
  75.7 4.6 %collective-permute-start.22 = (bf16[64,768]{1,0:T(8,128)(2,1)S(1)}, bf16[64,768]{1,0:T(8,128)(2,1)S(1)}, u32[]{:S(2)}, u32[]{:S(2)}) collective-permute-start(bf16[64,768]{1,0:T(8,128)(2,1)S(1)} %collective-permute-done.21.refs_0_), channel_id=1, source_target_pairs={{0,1},{1,0},{2,3},{3,2},{4,5},{5,4},{6,7},{7,6},{8,15},{9,10},{10,... | collective-permute-start | bytes 294920 | tf_op jit(solution)/shard_map/ppermute | solution.py:33
  75.7 6.7 %collective-permute-start.27 = (bf16[64,768]{1,0:T(8,128)(2,1)S(1)}, bf16[64,768]{1,0:T(8,128)(2,1)S(1)}, u32[]{:S(2)}, u32[]{:S(2)}) collective-permute-start(bf16[64,768]{1,0:T(8,128)(2,1)S(1)} %collective-permute-done.25.refs_1_), channel_id=1, source_target_pairs={{0,1},{1,0},{2,3},{3,2},{4,5},{5,4},{6,7},{7,6},{8,15},{9,10},{10,... | collective-permute-start | bytes 294920 | tf_op jit(solution)/shard_map/ppermute | solution.py:33
  80.3 6.8 %collective-permute-start.23 = (bf16[64,768]{1,0:T(8,128)(2,1)S(1)}, bf16[64,768]{1,0:T(8,128)(2,1)S(1)}, u32[]{:S(2)}, u32[]{:S(2)}) collective-permute-start(bf16[64,768]{1,0:T(8,128)(2,1)S(1)} %collective-permute-done.22.refs_4_), channel_id=1, source_target_pairs={{0,7},{1,2},{2,1},{3,4},{4,3},{5,6},{6,5},{7,0},{8,9},{9,8},{10,11... | collective-permute-start | bytes 294920 | tf_op jit(solution)/shard_map/ppermute | solution.py:33
  82.4 6.9 %collective-permute-start.30 = (bf16[64,768]{1,0:T(8,128)(2,1)S(1)}, bf16[64,768]{1,0:T(8,128)(2,1)S(1)}, u32[]{:S(2)}, u32[]{:S(2)}) collective-permute-start(bf16[64,768]{1,0:T(8,128)(2,1)S(1)} %collective-permute-done.27.refs_5_), channel_id=1, source_target_pairs={{0,7},{1,2},{2,1},{3,4},{4,3},{5,6},{6,5},{7,0},{8,9},{9,8},{10,11... | collective-permute-start | bytes 294920 | tf_op jit(solution)/shard_map/ppermute | solution.py:33
  84.3 9.6 %collective-permute-start.29 = (bf16[64,1536]{1,0:T(8,128)(2,1)S(1)}, bf16[64,1536]{1,0:T(8,128)(2,1)S(1)}, u32[]{:S(2)}, u32[]{:S(2)}) collective-permute-start(bf16[64,1536]{1,0:T(8,128)(2,1)S(1)} %collective-permute-done.28.refs_11_), channel_id=1, source_target_pairs={{0,1},{1,0},{2,3},{3,2},{4,5},{5,4},{6,7},{7,6},{8,15},{9,10},{10,... | collective-permute-start | bytes 589832 | tf_op jit(solution)/shard_map/ppermute | solution.py:33
  87.1 4.6 %collective-permute-start.24 = (bf16[64,768]{1,0:T(8,128)(2,1)S(1)}, bf16[64,768]{1,0:T(8,128)(2,1)S(1)}, u32[]{:S(2)}, u32[]{:S(2)}) collective-permute-start(bf16[64,768]{1,0:T(8,128)(2,1)S(1)} %collective-permute-done.23.refs_9_), channel_id=1, source_target_pairs={{0,1},{1,0},{2,3},{3,2},{4,5},{5,4},{6,7},{7,6},{8,15},{9,10},{10,... | collective-permute-start | bytes 294920 | tf_op jit(solution)/shard_map/ppermute | solution.py:33
  89.3 4.6 %collective-permute-start.31 = (bf16[64,768]{1,0:T(8,128)(2,1)S(1)}, bf16[64,768]{1,0:T(8,128)(2,1)S(1)}, u32[]{:S(2)}, u32[]{:S(2)}) collective-permute-start(bf16[64,768]{1,0:T(8,128)(2,1)S(1)} %collective-permute-done.30.refs_10_), channel_id=1, source_target_pairs={{0,1},{1,0},{2,3},{3,2},{4,5},{5,4},{6,7},{7,6},{8,15},{9,10},{10,... | collective-permute-start | bytes 294920 | tf_op jit(solution)/shard_map/ppermute | solution.py:33
  95.9 1.5 %collective-permute-start.33 = (bf16[64,1536]{1,0:T(8,128)(2,1)S(1)}, bf16[64,1536]{1,0:T(8,128)(2,1)S(1)}, u32[]{:S(2)}, u32[]{:S(2)}) collective-permute-start(bf16[64,1536]{1,0:T(8,128)(2,1)S(1)} %get-tuple-element.65), channel_id=1, source_target_pairs={{0,8},{1,9},{2,10},{3,11},{4,12},{5,13},{6,14},{7,15},{8,0},{9,1},... | collective-permute-start | bytes 589832 | tf_op jit(solution)/shard_map/ppermute | solution.py:33
  96.0 10.2 %collective-permute-start.32 = (bf16[64,1536]{1,0:T(8,128)(2,1)S(1)}, bf16[64,1536]{1,0:T(8,128)(2,1)S(1)}, u32[]{:S(2)}, u32[]{:S(2)}) collective-permute-start(bf16[64,1536]{1,0:T(8,128)(2,1)S(1)} %get-tuple-element.63), channel_id=1, source_target_pairs={{0,8},{1,9},{2,10},{3,11},{4,12},{5,13},{6,14},{7,15},{8,0},{9,1},... | collective-permute-start | bytes 589832 | tf_op jit(solution)/shard_map/ppermute | solution.py:33
  96.5 3.5 %collective-permute-start.35 = (bf16[64,1536]{1,0:T(8,128)(2,1)S(1)}, bf16[64,1536]{1,0:T(8,128)(2,1)S(1)}, u32[]{:S(2)}, u32[]{:S(2)}) collective-permute-start(bf16[64,1536]{1,0:T(8,128)(2,1)S(1)} %get-tuple-element.67), channel_id=1, source_target_pairs={{0,8},{1,9},{2,10},{3,11},{4,12},{5,13},{6,14},{7,15},{8,0},{9,1},... | collective-permute-start | bytes 589832 | tf_op jit(solution)/shard_map/ppermute | solution.py:33
  96.6 4.2 %collective-permute-start.37 = (bf16[64,1536]{1,0:T(8,128)(2,1)S(1)}, bf16[64,1536]{1,0:T(8,128)(2,1)S(1)}, u32[]{:S(2)}, u32[]{:S(2)}) collective-permute-start(bf16[64,1536]{1,0:T(8,128)(2,1)S(1)} %get-tuple-element.69), channel_id=1, source_target_pairs={{0,8},{1,9},{2,10},{3,11},{4,12},{5,13},{6,14},{7,15},{8,0},{9,1},... | collective-permute-start | bytes 589832 | tf_op jit(solution)/shard_map/ppermute | solution.py:33
  97.4 8.7 %collective-permute-start.34 = (bf16[64,1536]{1,0:T(8,128)(2,1)S(1)}, bf16[64,1536]{1,0:T(8,128)(2,1)S(1)}, u32[]{:S(2)}, u32[]{:S(2)}) collective-permute-start(bf16[64,1536]{1,0:T(8,128)(2,1)S(1)} %add_convert_fusion.2), channel_id=1, source_target_pairs={{0,48},{1,49},{2,50},{3,51},{4,52},{5,53},{6,54},{7,55},{8,200},{9... | collective-permute-start | bytes 589832 | tf_op jit(solution)/shard_map/ppermute | solution.py:33
  100.0 7.3 %collective-permute-start.36 = (bf16[64,1536]{1,0:T(8,128)(2,1)S(1)}, bf16[64,1536]{1,0:T(8,128)(2,1)S(1)}, u32[]{:S(2)}, u32[]{:S(2)}) collective-permute-start(bf16[64,1536]{1,0:T(8,128)(2,1)S(1)} %add_convert_fusion.1), channel_id=1, source_target_pairs={{0,32},{1,33},{2,34},{3,35},{4,36},{5,37},{6,38},{7,39},{8,136},{9... | collective-permute-start | bytes 589832 | tf_op jit(solution)/shard_map/ppermute | solution.py:33
  100.8 6.8 %collective-permute-start.38 = (bf16[64,1536]{1,0:T(8,128)(2,1)S(1)}, bf16[64,1536]{1,0:T(8,128)(2,1)S(1)}, u32[]{:S(2)}, u32[]{:S(2)}) collective-permute-start(bf16[64,1536]{1,0:T(8,128)(2,1)S(1)} %add_convert_fusion), channel_id=1, source_target_pairs={{0,16},{1,17},{2,18},{3,19},{4,20},{5,21},{6,22},{7,23},{8,72},{9,... | collective-permute-start | bytes 589832 | tf_op jit(solution)/shard_map/ppermute | solution.py:33
  107.7 5.5 %collective-permute-start.39 = (bf16[16,1536]{1,0:T(8,128)(2,1)S(1)}, bf16[16,1536]{1,0:T(8,128)(2,1)S(1)}, u32[]{:S(2)}, u32[]{:S(2)}) collective-permute-start(bf16[16,1536]{1,0:T(8,128)(2,1)S(1)} %get-tuple-element.75), channel_id=1, source_target_pairs={{0,192},{1,193},{2,194},{3,195},{4,196},{5,197},{6,198},{7,199},{8... | collective-permute-start | bytes 147464 | tf_op jit(solution)/shard_map/ppermute | solution.py:33
  109.3 5.6 %collective-permute-start.41 = (bf16[16,1536]{1,0:T(8,128)(2,1)S(1)}, bf16[16,1536]{1,0:T(8,128)(2,1)S(1)}, u32[]{:S(2)}, u32[]{:S(2)}) collective-permute-start(bf16[16,1536]{1,0:T(8,128)(2,1)S(1)} %get-tuple-element.76), channel_id=1, source_target_pairs={{0,128},{1,129},{2,130},{3,131},{4,132},{5,133},{6,134},{7,135},{8... | collective-permute-start | bytes 147464 | tf_op jit(solution)/shard_map/ppermute | solution.py:33
  112.4 4.1 %collective-permute-start.40 = (bf16[16,1536]{1,0:T(8,128)(2,1)S(1)}, bf16[16,1536]{1,0:T(8,128)(2,1)S(1)}, u32[]{:S(2)}, u32[]{:S(2)}) collective-permute-start(bf16[16,1536]{1,0:T(8,128)(2,1)S(1)} %get-tuple-element.77), channel_id=1, source_target_pairs={{0,64},{1,65},{2,66},{3,67},{4,68},{5,69},{6,70},{7,71},{8,24},{9,... | collective-permute-start | bytes 147464 | tf_op jit(solution)/shard_map/ppermute | solution.py:33

commit v7 on v5

--- a/solution.py
+++ b/solution.py
@@ -1,3 +1,5 @@
+import functools
+
 import jax
 import jax.numpy as jnp
 from jax import lax
@@ -9,11 +11,10 @@
 F32, BF16 = jnp.float32, jnp.bfloat16
 
 NX, NY, NC, NZ = 4, 4, 2, 8
-GATHER_X, GATHER_Y, SUM_FIRST, SUM_LAST = (0, 1, 3, 2), (0, 2, 3, 1), (0, 1, 3, 2), (0, 3, 1, 2)
+GATHER_X, GATHER_Y, SUM_FIRST, SUM_LAST = (0, 1, 3, 2), (0, 1, 2, 3), (0, 3, 2, 1), (0, 3, 1, 2)
 TOKENS_OWN = 16
 TOKENS_Z = 64
 TOKENS = 512
-HALF = TOKENS // 2
 
 
 def pairs_of(target):
@@ -37,8 +38,8 @@
     return send(value, lambda x, y, c, z: (x ^ k, y, c, z))
 
 
-def send_y(value, shift):
-    return send(value, lambda x, y, c, z: (x, y + shift, c, z))
+def send_y(value, k):
+    return send(value, lambda x, y, c, z: (x, y ^ k, c, z))
 
 
 def send_plane(value, k, x_core):
@@ -63,7 +64,7 @@
 def gathered_row(core_shift, i, p):
     row = lax.axis_index("row")
     x, y, c = row // (NY * NC), (row // NC) % NY, row % NC
-    x, y = x ^ GATHER_X[p], (y + NY - GATHER_Y[i]) % NY
+    x, y = x ^ GATHER_X[p], y ^ GATHER_Y[i]
     return row_of((x * NY + y) * NC + (c + core_shift) % NC)
 
 
@@ -134,10 +135,15 @@
 
 
 SUM_CUT = (1, 0, 0, 1, 0, 1, 1, 0)
-GATHER_CUT = (0, 0, 1, 0, 1, 1, 0, 1)
-
-
-def far_kernel(*refs):
+FIRST, REST = (4, 6), (0, 4, 6, 8)
+GATHER_CUT = (1, 0, 1, 1, 1, 1, 1, 1)
+
+
+def z_rows(start, stop):
+    return slice(start * TOKENS_Z, stop * TOKENS_Z)
+
+
+def first_kernel(*refs):
     pieces, w_ref, normed_ref, outs = refs[:8], refs[8], refs[9], refs[10:]
     for core_shift in range(2):
         for i in range(4):
@@ -146,30 +152,37 @@
                 normed_ref[rows, :] = pieces[core_shift * 4 + i][
                     p * TOKENS_OWN : (p + 1) * TOKENS_OWN, :
                 ]
-    multiply(normed_ref[HALF:, :], w_ref, halves_of(SUM_CUT[4:], outs))
-
-
-def near_kernel(normed_ref, w_ref, *outs):
-    multiply(normed_ref[:HALF, :], w_ref, halves_of(SUM_CUT[:4], outs))
-
-
-def far_pre(pieces, weight):
+    multiply(normed_ref[z_rows(*FIRST), :], w_ref, halves_of(SUM_CUT[slice(*FIRST)], outs))
+
+
+def rest_kernel(normed_ref, w_ref, *outs):
+    outs = list(outs)
+    for part in (REST[:2], REST[2:]):
+        cut = SUM_CUT[slice(*part)]
+        count = len(cut) + sum(cut)
+        multiply(normed_ref[z_rows(*part), :], w_ref, halves_of(cut, outs[:count]))
+        outs = outs[count:]
+
+
+def first_pre(pieces, weight):
     depth, width = weight.shape
-    return pl.pallas_call(
-        far_kernel,
+    shapes = shapes_of(SUM_CUT[slice(*FIRST)], width)
+    return pl.pallas_call(
+        first_kernel,
         in_specs=[WHOLE] * 9,
-        out_specs=[WHOLE] * (5 + sum(SUM_CUT[4:])),
-        out_shape=[jax.ShapeDtypeStruct((TOKENS, depth), BF16)] + shapes_of(SUM_CUT[4:], width),
+        out_specs=[WHOLE] * (1 + len(shapes)),
+        out_shape=[jax.ShapeDtypeStruct((TOKENS, depth), BF16)] + shapes,
         **settings(weight, 16),
     )(*pieces, weight)
 
 
-def near_pre(normed, weight):
-    return pl.pallas_call(
-        near_kernel,
+def rest_pre(normed, weight):
+    shapes = shapes_of(SUM_CUT[slice(*REST[:2])] + SUM_CUT[slice(*REST[2:])], weight.shape[1])
+    return pl.pallas_call(
+        rest_kernel,
         in_specs=[WHOLE] * 2,
-        out_specs=[WHOLE] * (4 + sum(SUM_CUT[:4])),
-        out_shape=shapes_of(SUM_CUT[:4], weight.shape[1]),
+        out_specs=[WHOLE] * len(shapes),
+        out_shape=shapes,
         **settings(weight, 16),
     )(normed, weight)
 
@@ -181,43 +194,47 @@
 def fill(rows_ref, blocks):
     half = rows_ref.shape[1] // 2
     for k, block in enumerate(blocks):
-        rows = slice(k * TOKENS_Z, (k + 1) * TOKENS_Z)
         if len(block) == 2:
-            rows_ref[rows, :half] = block[0][...]
-            rows_ref[rows, half:] = block[1][...]
+            rows_ref[z_rows(k, k + 1), :half] = block[0][...]
+            rows_ref[z_rows(k, k + 1), half:] = block[1][...]
         else:
-            rows_ref[rows, :] = block[0][...]
-
-
-def near_back_kernel(*refs):
+            rows_ref[z_rows(k, k + 1), :] = block[0][...]
+
+
+def some_back_kernel(cut, *refs):
     *pieces, w_ref, out_ref, rows_ref = refs
-    fill(rows_ref, halves_of(GATHER_CUT[:4], pieces))
+    fill(rows_ref, halves_of(cut, pieces))
     rows = rows_ref[...]
     for start in range(0, w_ref.shape[0], TILE):
         part = slice(start, start + TILE)
         out_ref[:, part] = transposed_dot(rows, w_ref[part, :]).astype(out_ref.dtype)
 
 
-def near_back(pieces, weight):
-    return pl.pallas_call(
-        near_back_kernel,
+def some_back(blocks, weight):
+    cut = [len(block) - 1 for block in blocks]
+    pieces = sum(blocks, [])
+    rows = len(blocks) * TOKENS_Z
+    return pl.pallas_call(
+        functools.partial(some_back_kernel, cut),
         in_specs=[WHOLE] * (len(pieces) + 1),
         out_specs=WHOLE,
-        out_shape=jax.ShapeDtypeStruct((HALF, weight.shape[0]), BF16),
-        scratch_shapes=[pltpu.VMEM((HALF, weight.shape[1]), BF16)],
+        out_shape=jax.ShapeDtypeStruct((rows, weight.shape[0]), BF16),
+        scratch_shapes=[pltpu.VMEM((rows, weight.shape[1]), BF16)],
         **settings(weight, 16),
     )(*pieces, weight)
 
 
-def far_back_kernel(*refs):
-    *pieces, near_ref, w_ref, slopes_ref = refs[:-9]
+def last_back_kernel(*refs):
+    *pieces, near_ref, middle_ref, w_ref, slopes_ref = refs[:-9]
     outs, product = refs[-9:-1], refs[-1]
     fill(slopes_ref, halves_of(GATHER_CUT, pieces))
-    product[:HALF, :] = near_ref[...].astype(F32)
-    rows = slopes_ref[HALF:, :]
+    product[z_rows(0, 4), :] = near_ref[...].astype(F32)
+    product[z_rows(4, 5), :] = middle_ref[z_rows(0, 1), :].astype(F32)
+    product[z_rows(7, 8), :] = middle_ref[z_rows(1, 2), :].astype(F32)
+    rows = slopes_ref[z_rows(5, 7), :]
     for start in range(0, w_ref.shape[0], TILE):
         part = slice(start, start + TILE)
-        product[HALF:, part] = transposed_dot(rows, w_ref[part, :])
+        product[z_rows(5, 7), part] = transposed_dot(rows, w_ref[part, :])
     for core_shift in (1, 0):
         for i in range(4):
             for p in range(4):
@@ -226,17 +243,18 @@
                 ].astype(BF16)
 
 
-def far_back(pieces, near, weight):
+def last_back(blocks, near, middle, weight):
     depth, width = weight.shape
-    return pl.pallas_call(
-        far_back_kernel,
-        in_specs=[WHOLE] * (len(pieces) + 2),
+    pieces = sum(blocks, [])
+    return pl.pallas_call(
+        last_back_kernel,
+        in_specs=[WHOLE] * (len(pieces) + 3),
         out_specs=[WHOLE] * 9,
         out_shape=[jax.ShapeDtypeStruct((TOKENS, width), BF16)]
         + [jax.ShapeDtypeStruct((TOKENS_Z, depth), BF16)] * 8,
         scratch_shapes=[pltpu.VMEM((TOKENS, depth), F32)],
         **settings(weight, 16),
-    )(*pieces, near, weight)
+    )(*pieces, near, middle, weight)
 
 
 def gelu_tanh(value):
@@ -290,25 +308,29 @@
     along_y[3], weight = lax.optimization_barrier((along_y[3], stage(weight)))
     other = [send_core(v) for v in along_y]
 
-    gathered, *far = far_pre(along_y + other, weight)
-    three, four, five, six = halves_of(SUM_CUT[4:], far)
-    back, own, one, two = halves_of(SUM_CUT[:4], near_pre(gathered, weight))
+    gathered, *first = first_pre(along_y + other, weight)
+    rest = rest_pre(gathered, weight)
+    three, four = halves_of(SUM_CUT[4:6], first)
+    back, own, one, two, five, six = halves_of(SUM_CUT[:4] + SUM_CUT[6:], rest)
     longer = [reduce_chain([four[h], five[h], two[h], back[h]]) for h in range(2)]
     shorter = reduce_chain([three[0], six[0], one[0]])
     pre = add(own[0], jnp.concatenate(longer, axis=1), shorter)
     slopes = jax.vjp(gelu_tanh, pre)[1](d_act.astype(F32))[0].astype(BF16)
 
     half = weight.shape[1] // 2
-    longer = [gather_chain(slopes[:, h * half : (h + 1) * half], 1, 4) for h in range(2)]
+    cut = lax.optimization_barrier((slopes[:, :half], slopes[:, half:]))
+    longer = [gather_chain(part, 1, 4) for part in cut]
+    shorter = [gather_chain(part, -1, 3) for part in cut]
     block_1, block_6, block_3, block_4 = ([chain[i] for chain in longer] for i in range(4))
-    block_7, block_2, block_5 = ([v] for v in gather_chain(slopes, -1, 3))
-    nearest = block_7 + [slopes] + block_1 + block_2
-    pieces = nearest + block_3 + block_4 + block_5 + block_6
+    block_7, block_2, block_5 = ([chain[i] for chain in shorter] for i in range(3))
+    nearest = [block_7, [slopes], block_1, block_2]
+    near = some_back(nearest, weight)
+    middle = some_back([block_3, block_6], weight)
+    blocks = nearest + [block_3, block_4, block_5, block_6]
+    slopes_all, *parts = last_back(blocks, near, middle, weight)
     pre, _ = lax.optimization_barrier((pre, block_4[0]))
     activated = gelu_tanh(pre).astype(BF16)
 
-    near = near_back(nearest, weight)
-    slopes_all, *parts = far_back(pieces, near, weight)
     d_weight = lax.dot_general(
         gathered, slopes_all, (((0,), (0,)), ((), ())), preferred_element_type=F32
     ).astype(BF16)

time: 117 us -> 117 us (level)
  waiting for transfers between devices: 35.6 us -> 33 us
  Pallas kernels: 8.77 us -> 10.7 us
  starting transfers between devices: 45.4 us -> 46.7 us
    ppermute x42 -> x45, waiting for transfers between devices: 35.6 us -> 33 us  [send(): return lax.ppermute(value, ('row', 'col'), pairs_of(target))]
    pallas_call x4 -> x5, Pallas kernels: 6.42 us -> 8.37 us  [the longest x2 3.04 us: some_back(): pl.pallas_call(functools.partial(some_back_kernel, cut), in_specs=[WHOLE]...]
    ppermute x42 -> x45, starting transfers between devices: 45.4 us -> 46.7 us  [send(): return lax.ppermute(value, ('row', 'col'), pairs_of(target))]
  transfers between devices with their start and end apart: 42 -> 45, of which waited for: 25 -> 28; matrix products, arithmetic and copies ran while one was open for 5% -> 5% of each run, Pallas kernels for 4% -> 6%
where the time goes in v7:
time: 117 us
  starting transfers between devices  46.7 us (40%)
  waiting for transfers between devices  33 us (28%)
  blocking collectives  16 us (14%)
  Pallas kernels  10.7 us (9%)
  other arithmetic  5.56 us (5%)
  matrix products  4.27 us (4%)
    ppermute x45, starting transfers between devices, send(): return lax.ppermute(value, ('row', 'col'), pairs_of(target))  46.7 us
    ppermute x45, waiting for transfers between devices, send(): return lax.ppermute(value, ('row', 'col'), pairs_of(target))  33 us
    all_to_all x1, blocking collectives, normalize(): lax.all_to_all(jnp.broadcast_to(stats[None], (NZ,) + stats.shape), 'col',...  16 us
    dot_general x1, matrix products, per_device(): lax.dot_general(gathered, slopes_all, (((0,), (0,)), ((), ())), preferred...  4.27 us
    pallas_call x2, Pallas kernels, some_back(): pl.pallas_call(functools.partial(some_back_kernel, cut), in_specs=[WHOLE]...  3.04 us
    pallas_call x1, Pallas kernels, stage(): pl.pallas_call(stage_kernel, in_specs=[pl.BlockSpec(memory_space=pl.ANY)]...  2.34 us
  transfers between devices with their start and end apart: 45, of which 28 were waited for; matrix products, arithmetic and copies ran while one was open for 5% of the time, Pallas kernels for 6%

profile of v7, /device:TPU:2, one launch (start us, length us, event | category | flops | bytes accessed | tf_op | source)
XLA Modules:
  0.0 117.1 jit_solution(5795758545923833350)
XLA Ops:
  0.6 1.0 reduce_sum.45
  1.7 1.1 multiply_reduce_fusion
  2.8 16.0 %all_to_all.5 = f32[8,2,16]{2,1,0:T(2,128)S(1)} all-to-all(f32[8,2,16]{2,1,0:T(2,128)S(1)} %broadcast_in_dim.2), channel_id=1, replica_groups=mesh['row'=32,'col'=8] {'col'}, dimensions={0} | all-to-all | bytes 2048 | tf_op jit(solution)/shard_map/all_to_all | solution.py:277
  18.8 1.0 add_convert_fusion.12
  19.8 2.2 %collective-permute-start.2 = (bf16[16,1536]{1,0:T(8,128)(2,1)S(1)}, bf16[16,1536]{1,0:T(8,128)(2,1)S(1)}, u32[]{:S(2)}, u32[]{:S(2)}) collective-permute-start(bf16[16,1536]{1,0:T(8,128)(2,1)S(1)} %add_convert_fusion.12), channel_id=1, source_target_pairs={{0,128},{1,129},{2,130},{3,131},{4,132},{5,133},{6,134},{7,135},{8... | collective-permute-start | bytes 147464 | tf_op jit(solution)/shard_map/ppermute | solution.py:34
  22.1 2.6 %collective-permute-start = (bf16[16,1536]{1,0:T(8,128)(2,1)S(1)}, bf16[16,1536]{1,0:T(8,128)(2,1)S(1)}, u32[]{:S(2)}, u32[]{:S(2)}) collective-permute-start(bf16[16,1536]{1,0:T(8,128)(2,1)S(1)} %add_convert_fusion.12), channel_id=1, source_target_pairs={{0,64},{1,65},{2,66},{3,67},{4,68},{5,69},{6,70},{7,71},{8,72},{9,... | collective-permute-start | bytes 147464 | tf_op jit(solution)/shard_map/ppermute | solution.py:34
  24.6 0.9 collective-permute-done.2
  25.5 0.6 collective-permute-done.1
  26.2 0.6 collective-permute-done
  26.7 3.1 %collective-permute-start.5 = (bf16[64,1536]{1,0:T(8,128)(2,1)S(1)}, bf16[64,1536]{1,0:T(8,128)(2,1)S(1)}, u32[]{:S(2)}, u32[]{:S(2)}) collective-permute-start(bf16[64,1536]{1,0:T(8,128)(2,1)S(1)} %pad_maximum_fusion.refs_0_), channel_id=1, source_target_pairs={{0,48},{1,49},{2,50},{3,51},{4,52},{5,53},{6,54},{7,55},{8,56},{9,... | collective-permute-start | bytes 589832 | tf_op jit(solution)/shard_map/ppermute | solution.py:34
  29.8 0.6 collective-permute-start.4
  30.5 0.5 collective-permute-start.3
  30.9 2.3 %shard_map.76.refs_8_.w_ref.refs_7_.refs_4_.refs_17_ = bf16[1536,1536]{1,0:T(8,128)(2,1)S(1)} custom-call(bf16[1536,1536]{1,0:T(8,128)(2,1)} %w_ref), custom_call_target="tpu_custom_call" | custom-call | flops 1207959552 | bytes 4718592 | tf_op jit(solution)/shard_map/pallas_call | solution.py:101
  33.3 2.1 %collective-permute-done.5.refs_3_ = bf16[64,1536]{1,0:T(8,128)(2,1)S(1)} collective-permute-done((bf16[64,1536]{1,0:T(8,128)(2,1)S(1)}, bf16[64,1536]{1,0:T(8,128)(2,1)S(1)}, u32[]{:S(2)}, u32[]{:S(2)}) %collective-permute-start.5) | collective-permute-done | bytes 196640 | tf_op jit(solution)/shard_map/ppermute | solution.py:34
  35.3 1.7 %collective-permute-done.4.refs_2_ = bf16[64,1536]{1,0:T(8,128)(2,1)S(1)} collective-permute-done((bf16[64,1536]{1,0:T(8,128)(2,1)S(1)}, bf16[64,1536]{1,0:T(8,128)(2,1)S(1)}, u32[]{:S(2)}, u32[]{:S(2)}) %collective-permute-start.4) | collective-permute-done | bytes 196640 | tf_op jit(solution)/shard_map/ppermute | solution.py:34
  37.0 0.5 collective-permute-start.7
  37.5 0.9 collective-permute-done.8.refs_6_
  39.0 1.1 shard_map.77
  40.1 0.7 collective-permute-start.10
  40.8 1.4 %collective-permute-start.14 = (bf16[64,768]{1,0:T(8,128)(2,1)S(1)}, bf16[64,768]{1,0:T(8,128)(2,1)S(1)}, u32[]{:S(2)}, u32[]{:S(2)}) collective-permute-start(bf16[64,768]{1,0:T(8,128)(2,1)S(1)} %get-tuple-element.45), channel_id=1, source_target_pairs={{0,1},{1,0},{2,3},{3,2},{4,5},{5,4},{6,7},{7,6},{8,15},{9,10},{10,... | collective-permute-start | bytes 294920 | tf_op jit(solution)/shard_map/ppermute | solution.py:34
  42.2 0.6 collective-permute-start.18
  42.8 2.0 %shard_map.78 = (bf16[64,768]{1,0:T(8,128)(2,1)S(1)}, bf16[64,768]{1,0:T(8,128)(2,1)S(1)}, bf16[64,1536]{1,0:T(8,128)(2,1)S(1)}, bf16[64,1536]{1,0:T(8,128)(2,1)...) custom-call(bf16[512,1536]{1,0:T(8,128)(2,1)S(1)} %get-tuple-element, ...), custom_call_target="tpu_custom_call" | custom-call | flops 1207959552 | bytes 4718592 | tf_op jit(solution)/shard_map/pallas_call | solution.py:181
  44.9 0.8 collective-permute-start.11
  45.9 2.4 %collective-permute-start.15 = (bf16[64,768]{1,0:T(8,128)(2,1)S(1)}, bf16[64,768]{1,0:T(8,128)(2,1)S(1)}, u32[]{:S(2)}, u32[]{:S(2)}) collective-permute-start(bf16[64,768]{1,0:T(8,128)(2,1)S(1)} %add_convert_fusion.7), channel_id=1, source_target_pairs={{0,7},{1,2},{2,1},{3,4},{4,3},{5,6},{6,5},{7,0},{8,9},{9,8},{10,11... | collective-permute-start | bytes 294920 | tf_op jit(solution)/shard_map/ppermute | solution.py:34
  48.3 2.5 %collective-permute-done.11 = bf16[64,768]{1,0:T(8,128)(2,1)S(1)} collective-permute-done((bf16[64,768]{1,0:T(8,128)(2,1)S(1)}, bf16[64,768]{1,0:T(8,128)(2,1)S(1)}, u32[]{:S(2)}, u32[]{:S(2)}) %collective-permute-start.11) | collective-permute-done | bytes 98336 | tf_op jit(solution)/shard_map/ppermute | solution.py:34
  51.1 0.7 collective-permute-done.15
  51.9 1.4 %collective-permute-start.16 = (bf16[64,768]{1,0:T(8,128)(2,1)S(1)}, bf16[64,768]{1,0:T(8,128)(2,1)S(1)}, u32[]{:S(2)}, u32[]{:S(2)}) collective-permute-start(bf16[64,768]{1,0:T(8,128)(2,1)S(1)} %add_convert_fusion.6), channel_id=1, source_target_pairs={{0,1},{1,0},{2,3},{3,2},{4,5},{5,4},{6,7},{7,6},{8,15},{9,10},{10,... | collective-permute-start | bytes 294920 | tf_op jit(solution)/shard_map/ppermute | solution.py:34
  53.3 1.3 %collective-permute-start.19 = (bf16[64,1536]{1,0:T(8,128)(2,1)S(1)}, bf16[64,1536]{1,0:T(8,128)(2,1)S(1)}, u32[]{:S(2)}, u32[]{:S(2)}) collective-permute-start(bf16[64,1536]{1,0:T(8,128)(2,1)S(1)} %add_convert_fusion.4), channel_id=1, source_target_pairs={{0,7},{1,2},{2,1},{3,4},{4,3},{5,6},{6,5},{7,0},{8,9},{9,8},{10,11... | collective-permute-start | bytes 589832 | tf_op jit(solution)/shard_map/ppermute | solution.py:34
  54.6 0.9 collective-permute-done.12
  55.6 1.2 collective-permute-start.13
  56.7 3.5 %collective-permute-done.19 = bf16[64,1536]{1,0:T(8,128)(2,1)S(1)} collective-permute-done((bf16[64,1536]{1,0:T(8,128)(2,1)S(1)}, bf16[64,1536]{1,0:T(8,128)(2,1)S(1)}, u32[]{:S(2)}, u32[]{:S(2)}) %collective-permute-start.19) | collective-permute-done | bytes 196640 | tf_op jit(solution)/shard_map/ppermute | solution.py:34
  60.5 2.1 %collective-permute-start.17 = (bf16[64,768]{1,0:T(8,128)(2,1)S(1)}, bf16[64,768]{1,0:T(8,128)(2,1)S(1)}, u32[]{:S(2)}, u32[]{:S(2)}) collective-permute-start(bf16[64,768]{1,0:T(8,128)(2,1)S(1)} %add_convert_fusion.5), channel_id=1, source_target_pairs={{0,7},{1,2},{2,1},{3,4},{4,3},{5,6},{6,5},{7,0},{8,9},{9,8},{10,11... | collective-permute-start | bytes 294920 | tf_op jit(solution)/shard_map/ppermute | solution.py:34
  62.5 3.8 %collective-permute-done.17 = bf16[64,768]{1,0:T(8,128)(2,1)S(1)} collective-permute-done((bf16[64,768]{1,0:T(8,128)(2,1)S(1)}, bf16[64,768]{1,0:T(8,128)(2,1)S(1)}, u32[]{:S(2)}, u32[]{:S(2)}) %collective-permute-start.17) | collective-permute-done | bytes 98336 | tf_op jit(solution)/shard_map/ppermute | solution.py:34
  66.9 1.9 %collective-permute-start.25 = (bf16[64,768]{1,0:T(8,128)(2,1)S(1)}, bf16[64,768]{1,0:T(8,128)(2,1)S(1)}, u32[]{:S(2)}, u32[]{:S(2)}) collective-permute-start(bf16[64,768]{1,0:T(8,128)(2,1)S(1)} %get-tuple-element.49), channel_id=1, source_target_pairs={{0,7},{1,2},{2,1},{3,4},{4,3},{5,6},{6,5},{7,0},{8,9},{9,8},{10,11... | collective-permute-start | bytes 294920 | tf_op jit(solution)/shard_map/ppermute | solution.py:34
  68.8 2.0 %collective-permute-start.27 = (bf16[64,768]{1,0:T(8,128)(2,1)S(1)}, bf16[64,768]{1,0:T(8,128)(2,1)S(1)}, u32[]{:S(2)}, u32[]{:S(2)}) collective-permute-start(bf16[64,768]{1,0:T(8,128)(2,1)S(1)} %get-tuple-element.51), channel_id=1, source_target_pairs={{0,1},{1,0},{2,3},{3,2},{4,5},{5,4},{6,7},{7,6},{8,15},{9,10},{10,... | collective-permute-start | bytes 294920 | tf_op jit(solution)/shard_map/ppermute | solution.py:34
  70.9 1.4 %collective-permute-start.26 = (bf16[64,768]{1,0:T(8,128)(2,1)S(1)}, bf16[64,768]{1,0:T(8,128)(2,1)S(1)}, u32[]{:S(2)}, u32[]{:S(2)}) collective-permute-start(bf16[64,768]{1,0:T(8,128)(2,1)S(1)} %get-tuple-element.51), channel_id=1, source_target_pairs={{0,7},{1,2},{2,1},{3,4},{4,3},{5,6},{6,5},{7,0},{8,9},{9,8},{10,11... | collective-permute-start | bytes 294920 | tf_op jit(solution)/shard_map/ppermute | solution.py:34
  72.2 0.7 collective-permute-done.25.refs_0_
  73.2 0.8 collective-permute-done.21.refs_3_
  73.9 1.3 %collective-permute-start.22 = (bf16[64,768]{1,0:T(8,128)(2,1)S(1)}, bf16[64,768]{1,0:T(8,128)(2,1)S(1)}, u32[]{:S(2)}, u32[]{:S(2)}) collective-permute-start(bf16[64,768]{1,0:T(8,128)(2,1)S(1)} %collective-permute-done.21.refs_3_), channel_id=1, source_target_pairs={{0,7},{1,2},{2,1},{3,4},{4,3},{5,6},{6,5},{7,0},{8,9},{9,8},{10,11... | collective-permute-start | bytes 294920 | tf_op jit(solution)/shard_map/ppermute | solution.py:34
  75.2 0.8 collective-permute-done.27.refs_4_
  76.0 1.3 %collective-permute-start.30 = (bf16[64,768]{1,0:T(8,128)(2,1)S(1)}, bf16[64,768]{1,0:T(8,128)(2,1)S(1)}, u32[]{:S(2)}, u32[]{:S(2)}) collective-permute-start(bf16[64,768]{1,0:T(8,128)(2,1)S(1)} %collective-permute-done.27.refs_4_), channel_id=1, source_target_pairs={{0,7},{1,2},{2,1},{3,4},{4,3},{5,6},{6,5},{7,0},{8,9},{9,8},{10,11... | collective-permute-start | bytes 294920 | tf_op jit(solution)/shard_map/ppermute | solution.py:34
  77.3 1.2 %collective-permute-done.28.refs_5_ = bf16[64,768]{1,0:T(8,128)(2,1)S(1)} collective-permute-done((bf16[64,768]{1,0:T(8,128)(2,1)S(1)}, bf16[64,768]{1,0:T(8,128)(2,1)S(1)}, u32[]{:S(2)}, u32[]{:S(2)}) %collective-permute-start.28) | collective-permute-done | bytes 98336 | tf_op jit(solution)/shard_map/ppermute | solution.py:34
  78.5 1.7 %collective-permute-start.33 = (bf16[64,768]{1,0:T(8,128)(2,1)S(1)}, bf16[64,768]{1,0:T(8,128)(2,1)S(1)}, u32[]{:S(2)}, u32[]{:S(2)}) collective-permute-start(bf16[64,768]{1,0:T(8,128)(2,1)S(1)} %collective-permute-done.28.refs_5_), channel_id=1, source_target_pairs={{0,7},{1,2},{2,1},{3,4},{4,3},{5,6},{6,5},{7,0},{8,9},{9,8},{10,11... | collective-permute-start | bytes 294920 | tf_op jit(solution)/shard_map/ppermute | solution.py:34
  80.6 2.3 %collective-permute-done.30.refs_3_.refs_14_ = bf16[64,768]{1,0:T(8,128)(2,1)S(1)} collective-permute-done((bf16[64,768]{1,0:T(8,128)(2,1)S(1)}, bf16[64,768]{1,0:T(8,128)(2,1)S(1)}, u32[]{:S(2)}, u32[]{:S(2)}) %collective-permute-start.30) | collective-permute-done | bytes 98336 | tf_op jit(solution)/shard_map/ppermute | solution.py:34
  82.9 1.5 %collective-permute-start.34 = (bf16[64,768]{1,0:T(8,128)(2,1)S(1)}, bf16[64,768]{1,0:T(8,128)(2,1)S(1)}, u32[]{:S(2)}, u32[]{:S(2)}) collective-permute-start(bf16[64,768]{1,0:T(8,128)(2,1)S(1)} %collective-permute-done.29.refs_6_), channel_id=1, source_target_pairs={{0,7},{1,2},{2,1},{3,4},{4,3},{5,6},{6,5},{7,0},{8,9},{9,8},{10,11... | collective-permute-start | bytes 294920 | tf_op jit(solution)/shard_map/ppermute | solution.py:34
  84.4 1.4 %shard_map.79.refs_15_ = bf16[256,1536]{1,0:T(8,128)(2,1)S(1)} custom-call(bf16[64,768]{1,0:T(8,128)(2,1)S(1)} %collective-permute-done.25.refs_0_, bf16[64,768]{1,0:T(8,128)(2,1)S(1)} %collective-permute-done.26.refs_1_, bf16[64,1536]{1,0:T(8,128)(2,1)S(1)} %get-tuple-element.63.refs_2_, bf16[64,768]{1,0:T(8,128)(2,1)S(1)} %collective-permute-done.21.refs_3_, ...), custom_call_target="tpu_custom_call" | custom-call | flops 1207959552 | bytes 4718592 | tf_op jit(solution)/shard_map/pallas_call | solution.py:217
  85.9 1.8 %collective-permute-start.24 = (bf16[64,768]{1,0:T(8,128)(2,1)S(1)}, bf16[64,768]{1,0:T(8,128)(2,1)S(1)}, u32[]{:S(2)}, u32[]{:S(2)}) collective-permute-start(bf16[64,768]{1,0:T(8,128)(2,1)S(1)} %collective-permute-done.23.refs_0_.refs_7_), channel_id=1, source_target_pairs={{0,7},{1,2},{2,1},{3,4},{4,3},{5,6},{6,5},{7,0},{8,9},{9,8},{10,11... | collective-permute-start | bytes 294920 | tf_op jit(solution)/shard_map/ppermute | solution.py:34
  87.7 1.5 %collective-permute-start.32 = (bf16[64,768]{1,0:T(8,128)(2,1)S(1)}, bf16[64,768]{1,0:T(8,128)(2,1)S(1)}, u32[]{:S(2)}, u32[]{:S(2)}) collective-permute-start(bf16[64,768]{1,0:T(8,128)(2,1)S(1)} %collective-permute-done.31.refs_1_.refs_8_), channel_id=1, source_target_pairs={{0,7},{1,2},{2,1},{3,4},{4,3},{5,6},{6,5},{7,0},{8,9},{9,8},{10,11... | collective-permute-start | bytes 294920 | tf_op jit(solution)/shard_map/ppermute | solution.py:34
  89.2 1.6 %shard_map.80.refs_16_ = bf16[128,1536]{1,0:T(8,128)(2,1)S(1)} custom-call(bf16[64,768]{1,0:T(8,128)(2,1)S(1)} %collective-permute-done.23.refs_0_.refs_7_, bf16[64,768]{1,0:T(8,128)(2,1)S(1)} %collective-permute-done.31.refs_1_.refs_8_, bf16[64,768]{1,0:T(8,128)(2,1)S(1)} %collective-permute-done.22.refs_2_.refs_13_, ...), custom_call_target="tpu_custom_call" | custom-call | flops 1207959552 | bytes 4718592 | tf_op jit(solution)/shard_map/pallas_call | solution.py:217
  90.9 0.9 collective-permute-done.24.refs_9_
  91.8 1.7 %collective-permute-done.32.refs_10_ = bf16[64,768]{1,0:T(8,128)(2,1)S(1)} collective-permute-done((bf16[64,768]{1,0:T(8,128)(2,1)S(1)}, bf16[64,768]{1,0:T(8,128)(2,1)S(1)}, u32[]{:S(2)}, u32[]{:S(2)}) %collective-permute-start.32) | collective-permute-done | bytes 98336 | tf_op jit(solution)/shard_map/ppermute | solution.py:34
  93.5 2.2 %shard_map.81 = (bf16[512,1536]{1,0:T(8,128)(2,1)S(1)}, bf16[64,1536]{1,0:T(8,128)(2,1)S(1)}, bf16[64,1536]{1,0:T(8,128)(2,1)S(1)}, bf16[64,1536]{1,0:T(8,128)(2...) custom-call(bf16[64,768]{1,0:T(8,128)(2,1)S(1)} %collective-permute-, ...), custom_call_target="tpu_custom_call" | custom-call | flops 1207959552 | bytes 4718592 | tf_op jit(solution)/shard_map/pallas_call | solution.py:249
  95.9 0.5 collective-permute-start.35
  97.3 2.5 %collective-permute-start.37 = (bf16[64,1536]{1,0:T(8,128)(2,1)S(1)}, bf16[64,1536]{1,0:T(8,128)(2,1)S(1)}, u32[]{:S(2)}, u32[]{:S(2)}) collective-permute-start(bf16[64,1536]{1,0:T(8,128)(2,1)S(1)} %add_convert_fusion.2), channel_id=1, source_target_pairs={{0,48},{1,49},{2,50},{3,51},{4,52},{5,53},{6,54},{7,55},{8,200},{9... | collective-permute-start | bytes 589832 | tf_op jit(solution)/shard_map/ppermute | solution.py:34
  99.9 0.7 collective-permute-start.39
  100.7 1.1 collective-permute-start.41
  101.8 4.3 %convolution_convert_fusion = bf16[1536,1536]{1,0:T(8,128)(2,1)} fusion(bf16[512,1536]{1,0:T(8,128)(2,1)S(1)} %get-tuple-element.36.normed_ref, bf16[512,1536]{1,0:T(8,128)(2,1)S(1)} %get-tuple-element.60), kind=kOutput, calls=%fused_computation | convolution fusion | flops 2418278400 | bytes 7864320 | tf_op jit(solution)/shard_map/dot_general | solution.py:334
  106.1 1.1 collective-permute-done.39
  107.6 1.7 %collective-permute-start.42 = (bf16[16,1536]{1,0:T(8,128)(2,1)S(1)}, bf16[16,1536]{1,0:T(8,128)(2,1)S(1)}, u32[]{:S(2)}, u32[]{:S(2)}) collective-permute-start(bf16[16,1536]{1,0:T(8,128)(2,1)S(1)} %get-tuple-element.65), channel_id=1, source_target_pairs={{0,192},{1,193},{2,194},{3,195},{4,196},{5,197},{6,198},{7,199},{8... | collective-permute-start | bytes 147464 | tf_op jit(solution)/shard_map/ppermute | solution.py:34
  109.4 3.0 %collective-permute-start.44 = (bf16[16,1536]{1,0:T(8,128)(2,1)S(1)}, bf16[16,1536]{1,0:T(8,128)(2,1)S(1)}, u32[]{:S(2)}, u32[]{:S(2)}) collective-permute-start(bf16[16,1536]{1,0:T(8,128)(2,1)S(1)} %get-tuple-element.66), channel_id=1, source_target_pairs={{0,128},{1,129},{2,130},{3,131},{4,132},{5,133},{6,134},{7,135},{8... | collective-permute-start | bytes 147464 | tf_op jit(solution)/shard_map/ppermute | solution.py:34
  112.4 0.8 fusion.17
  113.2 1.8 %collective-permute-done.44 = bf16[16,1536]{1,0:T(8,128)(2,1)S(1)} collective-permute-done((bf16[16,1536]{1,0:T(8,128)(2,1)S(1)}, bf16[16,1536]{1,0:T(8,128)(2,1)S(1)}, u32[]{:S(2)}, u32[]{:S(2)}) %collective-permute-start.44) | collective-permute-done | bytes 49184 | tf_op jit(solution)/shard_map/ppermute | solution.py:34
  115.0 1.5 %collective-permute-done.43 = bf16[16,1536]{1,0:T(8,128)(2,1)S(1)} collective-permute-done((bf16[16,1536]{1,0:T(8,128)(2,1)S(1)}, bf16[16,1536]{1,0:T(8,128)(2,1)S(1)}, u32[]{:S(2)}, u32[]{:S(2)}) %collective-permute-start.43) | collective-permute-done | bytes 49184 | tf_op jit(solution)/shard_map/ppermute | solution.py:34
  116.5 0.6 add_convert_fusion.11
  (66 shorter events, 4.3 us)
Async XLA Ops:
  19.8 5.7 %collective-permute-start.2 = (bf16[16,1536]{1,0:T(8,128)(2,1)S(1)}, bf16[16,1536]{1,0:T(8,128)(2,1)S(1)}, u32[]{:S(2)}, u32[]{:S(2)}) collective-permute-start(bf16[16,1536]{1,0:T(8,128)(2,1)S(1)} %add_convert_fusion.12), channel_id=1, source_target_pairs={{0,128},{1,129},{2,130},{3,131},{4,132},{5,133},{6,134},{7,135},{8... | collective-permute-start | bytes 147464 | tf_op jit(solution)/shard_map/ppermute | solution.py:34
  22.1 4.1 %collective-permute-start.1 = (bf16[16,1536]{1,0:T(8,128)(2,1)S(1)}, bf16[16,1536]{1,0:T(8,128)(2,1)S(1)}, u32[]{:S(2)}, u32[]{:S(2)}) collective-permute-start(bf16[16,1536]{1,0:T(8,128)(2,1)S(1)} %add_convert_fusion.12), channel_id=1, source_target_pairs={{0,192},{1,193},{2,194},{3,195},{4,196},{5,197},{6,198},{7,199},{8... | collective-permute-start | bytes 147464 | tf_op jit(solution)/shard_map/ppermute | solution.py:34
  22.1 4.6 %collective-permute-start = (bf16[16,1536]{1,0:T(8,128)(2,1)S(1)}, bf16[16,1536]{1,0:T(8,128)(2,1)S(1)}, u32[]{:S(2)}, u32[]{:S(2)}) collective-permute-start(bf16[16,1536]{1,0:T(8,128)(2,1)S(1)} %add_convert_fusion.12), channel_id=1, source_target_pairs={{0,64},{1,65},{2,66},{3,67},{4,68},{5,69},{6,70},{7,71},{8,72},{9,... | collective-permute-start | bytes 147464 | tf_op jit(solution)/shard_map/ppermute | solution.py:34
  26.7 8.6 %collective-permute-start.5 = (bf16[64,1536]{1,0:T(8,128)(2,1)S(1)}, bf16[64,1536]{1,0:T(8,128)(2,1)S(1)}, u32[]{:S(2)}, u32[]{:S(2)}) collective-permute-start(bf16[64,1536]{1,0:T(8,128)(2,1)S(1)} %pad_maximum_fusion.refs_0_), channel_id=1, source_target_pairs={{0,48},{1,49},{2,50},{3,51},{4,52},{5,53},{6,54},{7,55},{8,56},{9,... | collective-permute-start | bytes 589832 | tf_op jit(solution)/shard_map/ppermute | solution.py:34
  29.8 7.2 %collective-permute-start.4 = (bf16[64,1536]{1,0:T(8,128)(2,1)S(1)}, bf16[64,1536]{1,0:T(8,128)(2,1)S(1)}, u32[]{:S(2)}, u32[]{:S(2)}) collective-permute-start(bf16[64,1536]{1,0:T(8,128)(2,1)S(1)} %pad_maximum_fusion.refs_0_), channel_id=1, source_target_pairs={{0,32},{1,33},{2,34},{3,35},{4,36},{5,37},{6,38},{7,39},{8,40},{9,... | collective-permute-start | bytes 589832 | tf_op jit(solution)/shard_map/ppermute | solution.py:34
  30.5 6.6 %collective-permute-start.3 = (bf16[64,1536]{1,0:T(8,128)(2,1)S(1)}, bf16[64,1536]{1,0:T(8,128)(2,1)S(1)}, u32[]{:S(2)}, u32[]{:S(2)}) collective-permute-start(bf16[64,1536]{1,0:T(8,128)(2,1)S(1)} %pad_maximum_fusion.refs_0_), channel_id=1, source_target_pairs={{0,16},{1,17},{2,18},{3,19},{4,20},{5,21},{6,22},{7,23},{8,24},{9,... | collective-permute-start | bytes 589832 | tf_op jit(solution)/shard_map/ppermute | solution.py:34
  30.9 6.6 %collective-permute-start.6 = (bf16[64,1536]{1,0:T(8,128)(2,1)S(1)}, bf16[64,1536]{1,0:T(8,128)(2,1)S(1)}, u32[]{:S(2)}, u32[]{:S(2)}) collective-permute-start(bf16[64,1536]{1,0:T(8,128)(2,1)S(1)} %pad_maximum_fusion.refs_0_), channel_id=1, source_target_pairs={{0,8},{1,9},{2,10},{3,11},{4,12},{5,13},{6,14},{7,15},{8,0},{9,1},... | collective-permute-start | bytes 589832 | tf_op jit(solution)/shard_map/ppermute | solution.py:34
  37.0 1.4 %collective-permute-start.8 = (bf16[64,1536]{1,0:T(8,128)(2,1)S(1)}, bf16[64,1536]{1,0:T(8,128)(2,1)S(1)}, u32[]{:S(2)}, u32[]{:S(2)}) collective-permute-start(bf16[64,1536]{1,0:T(8,128)(2,1)S(1)} %collective-permute-done.4.refs_2_), channel_id=1, source_target_pairs={{0,8},{1,9},{2,10},{3,11},{4,12},{5,13},{6,14},{7,15},{8,0},{9,1},... | collective-permute-start | bytes 589832 | tf_op jit(solution)/shard_map/ppermute | solution.py:34
  37.0 1.7 %collective-permute-start.7 = (bf16[64,1536]{1,0:T(8,128)(2,1)S(1)}, bf16[64,1536]{1,0:T(8,128)(2,1)S(1)}, u32[]{:S(2)}, u32[]{:S(2)}) collective-permute-start(bf16[64,1536]{1,0:T(8,128)(2,1)S(1)} %collective-permute-done.3.refs_1_), channel_id=1, source_target_pairs={{0,8},{1,9},{2,10},{3,11},{4,12},{5,13},{6,14},{7,15},{8,0},{9,1},... | collective-permute-start | bytes 589832 | tf_op jit(solution)/shard_map/ppermute | solution.py:34
  37.5 1.5 %collective-permute-start.9 = (bf16[64,1536]{1,0:T(8,128)(2,1)S(1)}, bf16[64,1536]{1,0:T(8,128)(2,1)S(1)}, u32[]{:S(2)}, u32[]{:S(2)}) collective-permute-start(bf16[64,1536]{1,0:T(8,128)(2,1)S(1)} %collective-permute-done.5.refs_3_), channel_id=1, source_target_pairs={{0,8},{1,9},{2,10},{3,11},{4,12},{5,13},{6,14},{7,15},{8,0},{9,1},... | collective-permute-start | bytes 589832 | tf_op jit(solution)/shard_map/ppermute | solution.py:34
  40.1 4.7 %collective-permute-start.10 = (bf16[64,768]{1,0:T(8,128)(2,1)S(1)}, bf16[64,768]{1,0:T(8,128)(2,1)S(1)}, u32[]{:S(2)}, u32[]{:S(2)}) collective-permute-start(bf16[64,768]{1,0:T(8,128)(2,1)S(1)} %get-tuple-element.41), channel_id=1, source_target_pairs={{0,1},{1,0},{2,3},{3,2},{4,5},{5,4},{6,7},{7,6},{8,15},{9,10},{10,... | collective-permute-start | bytes 294920 | tf_op jit(solution)/shard_map/ppermute | solution.py:34
  40.8 5.1 %collective-permute-start.14 = (bf16[64,768]{1,0:T(8,128)(2,1)S(1)}, bf16[64,768]{1,0:T(8,128)(2,1)S(1)}, u32[]{:S(2)}, u32[]{:S(2)}) collective-permute-start(bf16[64,768]{1,0:T(8,128)(2,1)S(1)} %get-tuple-element.45), channel_id=1, source_target_pairs={{0,1},{1,0},{2,3},{3,2},{4,5},{5,4},{6,7},{7,6},{8,15},{9,10},{10,... | collective-permute-start | bytes 294920 | tf_op jit(solution)/shard_map/ppermute | solution.py:34
  42.2 11.0 %collective-permute-start.18 = (bf16[64,1536]{1,0:T(8,128)(2,1)S(1)}, bf16[64,1536]{1,0:T(8,128)(2,1)S(1)}, u32[]{:S(2)}, u32[]{:S(2)}) collective-permute-start(bf16[64,1536]{1,0:T(8,128)(2,1)S(1)} %get-tuple-element.48), channel_id=1, source_target_pairs={{0,1},{1,0},{2,3},{3,2},{4,5},{5,4},{6,7},{7,6},{8,15},{9,10},{10,... | collective-permute-start | bytes 589832 | tf_op jit(solution)/shard_map/ppermute | solution.py:34
  44.8 21.7 %copy-start = (bf16[64,1536]{1,0:T(8,128)(2,1)S(1)}, bf16[64,1536]{1,0:T(8,128)(2,1)}, u32[]{:S(2)}) copy-start(bf16[64,1536]{1,0:T(8,128)(2,1)} %param.9) | copy-start | bytes 589828
  44.9 5.9 %collective-permute-start.11 = (bf16[64,768]{1,0:T(8,128)(2,1)S(1)}, bf16[64,768]{1,0:T(8,128)(2,1)S(1)}, u32[]{:S(2)}, u32[]{:S(2)}) collective-permute-start(bf16[64,768]{1,0:T(8,128)(2,1)S(1)} %add_convert_fusion.10), channel_id=1, source_target_pairs={{0,7},{1,2},{2,1},{3,4},{4,3},{5,6},{6,5},{7,0},{8,9},{9,8},{10,11... | collective-permute-start | bytes 294920 | tf_op jit(solution)/shard_map/ppermute | solution.py:34
  45.9 5.9 %collective-permute-start.15 = (bf16[64,768]{1,0:T(8,128)(2,1)S(1)}, bf16[64,768]{1,0:T(8,128)(2,1)S(1)}, u32[]{:S(2)}, u32[]{:S(2)}) collective-permute-start(bf16[64,768]{1,0:T(8,128)(2,1)S(1)} %add_convert_fusion.7), channel_id=1, source_target_pairs={{0,7},{1,2},{2,1},{3,4},{4,3},{5,6},{6,5},{7,0},{8,9},{9,8},{10,11... | collective-permute-start | bytes 294920 | tf_op jit(solution)/shard_map/ppermute | solution.py:34
  50.8 4.7 %collective-permute-start.12 = (bf16[64,768]{1,0:T(8,128)(2,1)S(1)}, bf16[64,768]{1,0:T(8,128)(2,1)S(1)}, u32[]{:S(2)}, u32[]{:S(2)}) collective-permute-start(bf16[64,768]{1,0:T(8,128)(2,1)S(1)} %add_convert_fusion.9), channel_id=1, source_target_pairs={{0,1},{1,0},{2,3},{3,2},{4,5},{5,4},{6,7},{7,6},{8,15},{9,10},{10,... | collective-permute-start | bytes 294920 | tf_op jit(solution)/shard_map/ppermute | solution.py:34
  51.9 8.5 %collective-permute-start.16 = (bf16[64,768]{1,0:T(8,128)(2,1)S(1)}, bf16[64,768]{1,0:T(8,128)(2,1)S(1)}, u32[]{:S(2)}, u32[]{:S(2)}) collective-permute-start(bf16[64,768]{1,0:T(8,128)(2,1)S(1)} %add_convert_fusion.6), channel_id=1, source_target_pairs={{0,1},{1,0},{2,3},{3,2},{4,5},{5,4},{6,7},{7,6},{8,15},{9,10},{10,... | collective-permute-start | bytes 294920 | tf_op jit(solution)/shard_map/ppermute | solution.py:34
  53.3 7.0 %collective-permute-start.19 = (bf16[64,1536]{1,0:T(8,128)(2,1)S(1)}, bf16[64,1536]{1,0:T(8,128)(2,1)S(1)}, u32[]{:S(2)}, u32[]{:S(2)}) collective-permute-start(bf16[64,1536]{1,0:T(8,128)(2,1)S(1)} %add_convert_fusion.4), channel_id=1, source_target_pairs={{0,7},{1,2},{2,1},{3,4},{4,3},{5,6},{6,5},{7,0},{8,9},{9,8},{10,11... | collective-permute-start | bytes 589832 | tf_op jit(solution)/shard_map/ppermute | solution.py:34
  55.6 7.0 %collective-permute-start.13 = (bf16[64,768]{1,0:T(8,128)(2,1)S(1)}, bf16[64,768]{1,0:T(8,128)(2,1)S(1)}, u32[]{:S(2)}, u32[]{:S(2)}) collective-permute-start(bf16[64,768]{1,0:T(8,128)(2,1)S(1)} %add_convert_fusion.8), channel_id=1, source_target_pairs={{0,7},{1,2},{2,1},{3,4},{4,3},{5,6},{6,5},{7,0},{8,9},{9,8},{10,11... | collective-permute-start | bytes 294920 | tf_op jit(solution)/shard_map/ppermute | solution.py:34
  60.3 6.2 %collective-permute-start.20 = (bf16[64,1536]{1,0:T(8,128)(2,1)S(1)}, bf16[64,1536]{1,0:T(8,128)(2,1)S(1)}, u32[]{:S(2)}, u32[]{:S(2)}) collective-permute-start(bf16[64,1536]{1,0:T(8,128)(2,1)S(1)} %add_convert_fusion.3), channel_id=1, source_target_pairs={{0,1},{1,0},{2,3},{3,2},{4,5},{5,4},{6,7},{7,6},{8,15},{9,10},{10,... | collective-permute-start | bytes 589832 | tf_op jit(solution)/shard_map/ppermute | solution.py:34
  60.5 5.9 %collective-permute-start.17 = (bf16[64,768]{1,0:T(8,128)(2,1)S(1)}, bf16[64,768]{1,0:T(8,128)(2,1)S(1)}, u32[]{:S(2)}, u32[]{:S(2)}) collective-permute-start(bf16[64,768]{1,0:T(8,128)(2,1)S(1)} %add_convert_fusion.5), channel_id=1, source_target_pairs={{0,7},{1,2},{2,1},{3,4},{4,3},{5,6},{6,5},{7,0},{8,9},{9,8},{10,11... | collective-permute-start | bytes 294920 | tf_op jit(solution)/shard_map/ppermute | solution.py:34
  66.9 6.0 %collective-permute-start.25 = (bf16[64,768]{1,0:T(8,128)(2,1)S(1)}, bf16[64,768]{1,0:T(8,128)(2,1)S(1)}, u32[]{:S(2)}, u32[]{:S(2)}) collective-permute-start(bf16[64,768]{1,0:T(8,128)(2,1)S(1)} %get-tuple-element.49), channel_id=1, source_target_pairs={{0,7},{1,2},{2,1},{3,4},{4,3},{5,6},{6,5},{7,0},{8,9},{9,8},{10,11... | collective-permute-start | bytes 294920 | tf_op jit(solution)/shard_map/ppermute | solution.py:34
  68.8 5.1 %collective-permute-start.21 = (bf16[64,768]{1,0:T(8,128)(2,1)S(1)}, bf16[64,768]{1,0:T(8,128)(2,1)S(1)}, u32[]{:S(2)}, u32[]{:S(2)}) collective-permute-start(bf16[64,768]{1,0:T(8,128)(2,1)S(1)} %get-tuple-element.49), channel_id=1, source_target_pairs={{0,1},{1,0},{2,3},{3,2},{4,5},{5,4},{6,7},{7,6},{8,15},{9,10},{10,... | collective-permute-start | bytes 294920 | tf_op jit(solution)/shard_map/ppermute | solution.py:34
  68.8 7.2 %collective-permute-start.27 = (bf16[64,768]{1,0:T(8,128)(2,1)S(1)}, bf16[64,768]{1,0:T(8,128)(2,1)S(1)}, u32[]{:S(2)}, u32[]{:S(2)}) collective-permute-start(bf16[64,768]{1,0:T(8,128)(2,1)S(1)} %get-tuple-element.51), channel_id=1, source_target_pairs={{0,1},{1,0},{2,3},{3,2},{4,5},{5,4},{6,7},{7,6},{8,15},{9,10},{10,... | collective-permute-start | bytes 294920 | tf_op jit(solution)/shard_map/ppermute | solution.py:34
  70.9 6.5 %collective-permute-start.26 = (bf16[64,768]{1,0:T(8,128)(2,1)S(1)}, bf16[64,768]{1,0:T(8,128)(2,1)S(1)}, u32[]{:S(2)}, u32[]{:S(2)}) collective-permute-start(bf16[64,768]{1,0:T(8,128)(2,1)S(1)} %get-tuple-element.51), channel_id=1, source_target_pairs={{0,7},{1,2},{2,1},{3,4},{4,3},{5,6},{6,5},{7,0},{8,9},{9,8},{10,11... | collective-permute-start | bytes 294920 | tf_op jit(solution)/shard_map/ppermute | solution.py:34
  72.9 5.6 %collective-permute-start.28 = (bf16[64,768]{1,0:T(8,128)(2,1)S(1)}, bf16[64,768]{1,0:T(8,128)(2,1)S(1)}, u32[]{:S(2)}, u32[]{:S(2)}) collective-permute-start(bf16[64,768]{1,0:T(8,128)(2,1)S(1)} %collective-permute-done.25.refs_0_), channel_id=1, source_target_pairs={{0,1},{1,0},{2,3},{3,2},{4,5},{5,4},{6,7},{7,6},{8,15},{9,10},{10,... | collective-permute-start | bytes 294920 | tf_op jit(solution)/shard_map/ppermute | solution.py:34
  73.9 6.6 %collective-permute-start.22 = (bf16[64,768]{1,0:T(8,128)(2,1)S(1)}, bf16[64,768]{1,0:T(8,128)(2,1)S(1)}, u32[]{:S(2)}, u32[]{:S(2)}) collective-permute-start(bf16[64,768]{1,0:T(8,128)(2,1)S(1)} %collective-permute-done.21.refs_3_), channel_id=1, source_target_pairs={{0,7},{1,2},{2,1},{3,4},{4,3},{5,6},{6,5},{7,0},{8,9},{9,8},{10,11... | collective-permute-start | bytes 294920 | tf_op jit(solution)/shard_map/ppermute | solution.py:34
  76.0 6.9 %collective-permute-start.30 = (bf16[64,768]{1,0:T(8,128)(2,1)S(1)}, bf16[64,768]{1,0:T(8,128)(2,1)S(1)}, u32[]{:S(2)}, u32[]{:S(2)}) collective-permute-start(bf16[64,768]{1,0:T(8,128)(2,1)S(1)} %collective-permute-done.27.refs_4_), channel_id=1, source_target_pairs={{0,7},{1,2},{2,1},{3,4},{4,3},{5,6},{6,5},{7,0},{8,9},{9,8},{10,11... | collective-permute-start | bytes 294920 | tf_op jit(solution)/shard_map/ppermute | solution.py:34
  77.3 5.6 %collective-permute-start.29 = (bf16[64,768]{1,0:T(8,128)(2,1)S(1)}, bf16[64,768]{1,0:T(8,128)(2,1)S(1)}, u32[]{:S(2)}, u32[]{:S(2)}) collective-permute-start(bf16[64,768]{1,0:T(8,128)(2,1)S(1)} %collective-permute-done.26.refs_1_), channel_id=1, source_target_pairs={{0,1},{1,0},{2,3},{3,2},{4,5},{5,4},{6,7},{7,6},{8,15},{9,10},{10,... | collective-permute-start | bytes 294920 | tf_op jit(solution)/shard_map/ppermute | solution.py:34
  78.5 12.3 %collective-permute-start.33 = (bf16[64,768]{1,0:T(8,128)(2,1)S(1)}, bf16[64,768]{1,0:T(8,128)(2,1)S(1)}, u32[]{:S(2)}, u32[]{:S(2)}) collective-permute-start(bf16[64,768]{1,0:T(8,128)(2,1)S(1)} %collective-permute-done.28.refs_5_), channel_id=1, source_target_pairs={{0,7},{1,2},{2,1},{3,4},{4,3},{5,6},{6,5},{7,0},{8,9},{9,8},{10,11... | collective-permute-start | bytes 294920 | tf_op jit(solution)/shard_map/ppermute | solution.py:34
  80.6 5.3 %collective-permute-start.23 = (bf16[64,768]{1,0:T(8,128)(2,1)S(1)}, bf16[64,768]{1,0:T(8,128)(2,1)S(1)}, u32[]{:S(2)}, u32[]{:S(2)}) collective-permute-start(bf16[64,768]{1,0:T(8,128)(2,1)S(1)} %collective-permute-done.22.refs_2_.refs_13_), channel_id=1, source_target_pairs={{0,1},{1,0},{2,3},{3,2},{4,5},{5,4},{6,7},{7,6},{8,15},{9,10},{10,... | collective-permute-start | bytes 294920 | tf_op jit(solution)/shard_map/ppermute | solution.py:34
  82.9 4.8 %collective-permute-start.31 = (bf16[64,768]{1,0:T(8,128)(2,1)S(1)}, bf16[64,768]{1,0:T(8,128)(2,1)S(1)}, u32[]{:S(2)}, u32[]{:S(2)}) collective-permute-start(bf16[64,768]{1,0:T(8,128)(2,1)S(1)} %collective-permute-done.30.refs_3_.refs_14_), channel_id=1, source_target_pairs={{0,1},{1,0},{2,3},{3,2},{4,5},{5,4},{6,7},{7,6},{8,15},{9,10},{10,... | collective-permute-start | bytes 294920 | tf_op jit(solution)/shard_map/ppermute | solution.py:34
  82.9 7.9 %collective-permute-start.34 = (bf16[64,768]{1,0:T(8,128)(2,1)S(1)}, bf16[64,768]{1,0:T(8,128)(2,1)S(1)}, u32[]{:S(2)}, u32[]{:S(2)}) collective-permute-start(bf16[64,768]{1,0:T(8,128)(2,1)S(1)} %collective-permute-done.29.refs_6_), channel_id=1, source_target_pairs={{0,7},{1,2},{2,1},{3,4},{4,3},{5,6},{6,5},{7,0},{8,9},{9,8},{10,11... | collective-permute-start | bytes 294920 | tf_op jit(solution)/shard_map/ppermute | solution.py:34
  85.9 5.9 %collective-permute-start.24 = (bf16[64,768]{1,0:T(8,128)(2,1)S(1)}, bf16[64,768]{1,0:T(8,128)(2,1)S(1)}, u32[]{:S(2)}, u32[]{:S(2)}) collective-permute-start(bf16[64,768]{1,0:T(8,128)(2,1)S(1)} %collective-permute-done.23.refs_0_.refs_7_), channel_id=1, source_target_pairs={{0,7},{1,2},{2,1},{3,4},{4,3},{5,6},{6,5},{7,0},{8,9},{9,8},{10,11... | collective-permute-start | bytes 294920 | tf_op jit(solution)/shard_map/ppermute | solution.py:34
  87.7 5.8 %collective-permute-start.32 = (bf16[64,768]{1,0:T(8,128)(2,1)S(1)}, bf16[64,768]{1,0:T(8,128)(2,1)S(1)}, u32[]{:S(2)}, u32[]{:S(2)}) collective-permute-start(bf16[64,768]{1,0:T(8,128)(2,1)S(1)} %collective-permute-done.31.refs_1_.refs_8_), channel_id=1, source_target_pairs={{0,7},{1,2},{2,1},{3,4},{4,3},{5,6},{6,5},{7,0},{8,9},{9,8},{10,11... | collective-permute-start | bytes 294920 | tf_op jit(solution)/shard_map/ppermute | solution.py:34
  95.8 1.5 %collective-permute-start.36 = (bf16[64,1536]{1,0:T(8,128)(2,1)S(1)}, bf16[64,1536]{1,0:T(8,128)(2,1)S(1)}, u32[]{:S(2)}, u32[]{:S(2)}) collective-permute-start(bf16[64,1536]{1,0:T(8,128)(2,1)S(1)} %get-tuple-element.55), channel_id=1, source_target_pairs={{0,8},{1,9},{2,10},{3,11},{4,12},{5,13},{6,14},{7,15},{8,0},{9,1},... | collective-permute-start | bytes 589832 | tf_op jit(solution)/shard_map/ppermute | solution.py:34
  95.9 10.2 %collective-permute-start.35 = (bf16[64,1536]{1,0:T(8,128)(2,1)S(1)}, bf16[64,1536]{1,0:T(8,128)(2,1)S(1)}, u32[]{:S(2)}, u32[]{:S(2)}) collective-permute-start(bf16[64,1536]{1,0:T(8,128)(2,1)S(1)} %get-tuple-element.53), channel_id=1, source_target_pairs={{0,8},{1,9},{2,10},{3,11},{4,12},{5,13},{6,14},{7,15},{8,0},{9,1},... | collective-permute-start | bytes 589832 | tf_op jit(solution)/shard_map/ppermute | solution.py:34
  96.4 3.5 %collective-permute-start.38 = (bf16[64,1536]{1,0:T(8,128)(2,1)S(1)}, bf16[64,1536]{1,0:T(8,128)(2,1)S(1)}, u32[]{:S(2)}, u32[]{:S(2)}) collective-permute-start(bf16[64,1536]{1,0:T(8,128)(2,1)S(1)} %get-tuple-element.57), channel_id=1, source_target_pairs={{0,8},{1,9},{2,10},{3,11},{4,12},{5,13},{6,14},{7,15},{8,0},{9,1},... | collective-permute-start | bytes 589832 | tf_op jit(solution)/shard_map/ppermute | solution.py:34
  96.5 4.2 %collective-permute-start.40 = (bf16[64,1536]{1,0:T(8,128)(2,1)S(1)}, bf16[64,1536]{1,0:T(8,128)(2,1)S(1)}, u32[]{:S(2)}, u32[]{:S(2)}) collective-permute-start(bf16[64,1536]{1,0:T(8,128)(2,1)S(1)} %get-tuple-element.59), channel_id=1, source_target_pairs={{0,8},{1,9},{2,10},{3,11},{4,12},{5,13},{6,14},{7,15},{8,0},{9,1},... | collective-permute-start | bytes 589832 | tf_op jit(solution)/shard_map/ppermute | solution.py:34
  97.3 8.7 %collective-permute-start.37 = (bf16[64,1536]{1,0:T(8,128)(2,1)S(1)}, bf16[64,1536]{1,0:T(8,128)(2,1)S(1)}, u32[]{:S(2)}, u32[]{:S(2)}) collective-permute-start(bf16[64,1536]{1,0:T(8,128)(2,1)S(1)} %add_convert_fusion.2), channel_id=1, source_target_pairs={{0,48},{1,49},{2,50},{3,51},{4,52},{5,53},{6,54},{7,55},{8,200},{9... | collective-permute-start | bytes 589832 | tf_op jit(solution)/shard_map/ppermute | solution.py:34
  99.9 7.3 %collective-permute-start.39 = (bf16[64,1536]{1,0:T(8,128)(2,1)S(1)}, bf16[64,1536]{1,0:T(8,128)(2,1)S(1)}, u32[]{:S(2)}, u32[]{:S(2)}) collective-permute-start(bf16[64,1536]{1,0:T(8,128)(2,1)S(1)} %add_convert_fusion.1), channel_id=1, source_target_pairs={{0,32},{1,33},{2,34},{3,35},{4,36},{5,37},{6,38},{7,39},{8,136},{9... | collective-permute-start | bytes 589832 | tf_op jit(solution)/shard_map/ppermute | solution.py:34
  100.7 6.8 %collective-permute-start.41 = (bf16[64,1536]{1,0:T(8,128)(2,1)S(1)}, bf16[64,1536]{1,0:T(8,128)(2,1)S(1)}, u32[]{:S(2)}, u32[]{:S(2)}) collective-permute-start(bf16[64,1536]{1,0:T(8,128)(2,1)S(1)} %add_convert_fusion), channel_id=1, source_target_pairs={{0,16},{1,17},{2,18},{3,19},{4,20},{5,21},{6,22},{7,23},{8,72},{9,... | collective-permute-start | bytes 589832 | tf_op jit(solution)/shard_map/ppermute | solution.py:34
  107.6 5.6 %collective-permute-start.42 = (bf16[16,1536]{1,0:T(8,128)(2,1)S(1)}, bf16[16,1536]{1,0:T(8,128)(2,1)S(1)}, u32[]{:S(2)}, u32[]{:S(2)}) collective-permute-start(bf16[16,1536]{1,0:T(8,128)(2,1)S(1)} %get-tuple-element.65), channel_id=1, source_target_pairs={{0,192},{1,193},{2,194},{3,195},{4,196},{5,197},{6,198},{7,199},{8... | collective-permute-start | bytes 147464 | tf_op jit(solution)/shard_map/ppermute | solution.py:34
  109.4 5.6 %collective-permute-start.44 = (bf16[16,1536]{1,0:T(8,128)(2,1)S(1)}, bf16[16,1536]{1,0:T(8,128)(2,1)S(1)}, u32[]{:S(2)}, u32[]{:S(2)}) collective-permute-start(bf16[16,1536]{1,0:T(8,128)(2,1)S(1)} %get-tuple-element.66), channel_id=1, source_target_pairs={{0,128},{1,129},{2,130},{3,131},{4,132},{5,133},{6,134},{7,135},{8... | collective-permute-start | bytes 147464 | tf_op jit(solution)/shard_map/ppermute | solution.py:34
  112.4 4.1 %collective-permute-start.43 = (bf16[16,1536]{1,0:T(8,128)(2,1)S(1)}, bf16[16,1536]{1,0:T(8,128)(2,1)S(1)}, u32[]{:S(2)}, u32[]{:S(2)}) collective-permute-start(bf16[16,1536]{1,0:T(8,128)(2,1)S(1)} %get-tuple-element.67), channel_id=1, source_target_pairs={{0,64},{1,65},{2,66},{3,67},{4,68},{5,69},{6,70},{7,71},{8,24},{9,... | collective-permute-start | bytes 147464 | tf_op jit(solution)/shard_map/ppermute | solution.py:34

commit v8 on v5

--- a/solution.py
+++ b/solution.py
@@ -9,7 +9,7 @@
 F32, BF16 = jnp.float32, jnp.bfloat16
 
 NX, NY, NC, NZ = 4, 4, 2, 8
-GATHER_X, GATHER_Y, SUM_FIRST, SUM_LAST = (0, 1, 3, 2), (0, 2, 3, 1), (0, 1, 3, 2), (0, 3, 1, 2)
+GATHER_X, GATHER_Y, SUM_FIRST, SUM_LAST = (0, 1, 3, 2), (0, 1, 2, 3), (0, 3, 2, 1), (0, 3, 1, 2)
 TOKENS_OWN = 16
 TOKENS_Z = 64
 TOKENS = 512
@@ -37,8 +37,8 @@
     return send(value, lambda x, y, c, z: (x ^ k, y, c, z))
 
 
-def send_y(value, shift):
-    return send(value, lambda x, y, c, z: (x, y + shift, c, z))
+def send_y(value, k):
+    return send(value, lambda x, y, c, z: (x, y ^ k, c, z))
 
 
 def send_plane(value, k, x_core):
@@ -63,7 +63,7 @@
 def gathered_row(core_shift, i, p):
     row = lax.axis_index("row")
     x, y, c = row // (NY * NC), (row // NC) % NY, row % NC
-    x, y = x ^ GATHER_X[p], (y + NY - GATHER_Y[i]) % NY
+    x, y = x ^ GATHER_X[p], y ^ GATHER_Y[i]
     return row_of((x * NY + y) * NC + (c + core_shift) % NC)
 
 
@@ -134,10 +134,15 @@
 
 
 SUM_CUT = (1, 0, 0, 1, 0, 1, 1, 0)
-GATHER_CUT = (0, 0, 1, 0, 1, 1, 0, 1)
-
-
-def far_kernel(*refs):
+FIRST, REST = (4, 8), (0, 4)
+GATHER_CUT = (1, 0, 0, 1, 0, 1, 1, 0)
+
+
+def z_rows(start, stop):
+    return slice(start * TOKENS_Z, stop * TOKENS_Z)
+
+
+def first_kernel(*refs):
     pieces, w_ref, normed_ref, outs = refs[:8], refs[8], refs[9], refs[10:]
     for core_shift in range(2):
         for i in range(4):
@@ -146,30 +151,32 @@
                 normed_ref[rows, :] = pieces[core_shift * 4 + i][
                     p * TOKENS_OWN : (p + 1) * TOKENS_OWN, :
                 ]
-    multiply(normed_ref[HALF:, :], w_ref, halves_of(SUM_CUT[4:], outs))
-
-
-def near_kernel(normed_ref, w_ref, *outs):
-    multiply(normed_ref[:HALF, :], w_ref, halves_of(SUM_CUT[:4], outs))
-
-
-def far_pre(pieces, weight):
+    multiply(normed_ref[z_rows(*FIRST), :], w_ref, halves_of(SUM_CUT[slice(*FIRST)], outs))
+
+
+def rest_kernel(normed_ref, w_ref, *outs):
+    multiply(normed_ref[z_rows(*REST), :], w_ref, halves_of(SUM_CUT[slice(*REST)], outs))
+
+
+def first_pre(pieces, weight):
     depth, width = weight.shape
-    return pl.pallas_call(
-        far_kernel,
+    shapes = shapes_of(SUM_CUT[slice(*FIRST)], width)
+    return pl.pallas_call(
+        first_kernel,
         in_specs=[WHOLE] * 9,
-        out_specs=[WHOLE] * (5 + sum(SUM_CUT[4:])),
-        out_shape=[jax.ShapeDtypeStruct((TOKENS, depth), BF16)] + shapes_of(SUM_CUT[4:], width),
+        out_specs=[WHOLE] * (1 + len(shapes)),
+        out_shape=[jax.ShapeDtypeStruct((TOKENS, depth), BF16)] + shapes,
         **settings(weight, 16),
     )(*pieces, weight)
 
 
-def near_pre(normed, weight):
-    return pl.pallas_call(
-        near_kernel,
+def rest_pre(normed, weight):
+    shapes = shapes_of(SUM_CUT[slice(*REST)], weight.shape[1])
+    return pl.pallas_call(
+        rest_kernel,
         in_specs=[WHOLE] * 2,
-        out_specs=[WHOLE] * (4 + sum(SUM_CUT[:4])),
-        out_shape=shapes_of(SUM_CUT[:4], weight.shape[1]),
+        out_specs=[WHOLE] * len(shapes),
+        out_shape=shapes,
         **settings(weight, 16),
     )(normed, weight)
 
@@ -265,13 +272,6 @@
     return (moved * scale[:, None] * gain[None, :] + bias[None, :]).astype(BF16)
 
 
-def reduce_chain(parts):
-    travelling = send_ring(parts[0], 1)
-    for step, part in enumerate(parts[1:]):
-        travelling = send_ring(add(part, travelling).astype(BF16), 2 * (step % 2) - 1)
-    return travelling
-
-
 def gather_chain(own, way, count):
     got = []
     for _ in range(count):
@@ -290,18 +290,27 @@
     along_y[3], weight = lax.optimization_barrier((along_y[3], stage(weight)))
     other = [send_core(v) for v in along_y]
 
-    gathered, *far = far_pre(along_y + other, weight)
-    three, four, five, six = halves_of(SUM_CUT[4:], far)
-    back, own, one, two = halves_of(SUM_CUT[:4], near_pre(gathered, weight))
-    longer = [reduce_chain([four[h], five[h], two[h], back[h]]) for h in range(2)]
-    shorter = reduce_chain([three[0], six[0], one[0]])
+    gathered, *first = first_pre(along_y + other, weight)
+    rest = rest_pre(gathered, weight)
+    three, four, five, six = halves_of(SUM_CUT[slice(*FIRST)], first)
+    back, own, one, two = halves_of(SUM_CUT[slice(*REST)], rest)
+    arrived_3 = send_ring(three[0], 1)
+    arrived_6 = send_ring(add(six[0], arrived_3).astype(BF16), -1)
+    shorter = send_ring(add(one[0], arrived_6).astype(BF16), 1)
+    longer = []
+    for h in range(2):
+        travelling = send_ring(four[h], 1)
+        travelling = send_ring(add(five[h], travelling).astype(BF16), -1)
+        travelling = send_ring(add(two[h], travelling).astype(BF16), 1)
+        longer.append(send_ring(add(back[h], travelling).astype(BF16), -1))
     pre = add(own[0], jnp.concatenate(longer, axis=1), shorter)
     slopes = jax.vjp(gelu_tanh, pre)[1](d_act.astype(F32))[0].astype(BF16)
 
     half = weight.shape[1] // 2
-    longer = [gather_chain(slopes[:, h * half : (h + 1) * half], 1, 4) for h in range(2)]
-    block_1, block_6, block_3, block_4 = ([chain[i] for chain in longer] for i in range(4))
-    block_7, block_2, block_5 = ([v] for v in gather_chain(slopes, -1, 3))
+    slopes, *cut = lax.optimization_barrier((slopes, slopes[:, :half], slopes[:, half:]))
+    longer = [gather_chain(part, -1, 4) for part in cut]
+    block_7, block_2, block_5, block_4 = ([chain[i] for chain in longer] for i in range(4))
+    block_1, block_6, block_3 = ([v] for v in gather_chain(slopes, 1, 3))
     nearest = block_7 + [slopes] + block_1 + block_2
     pieces = nearest + block_3 + block_4 + block_5 + block_6
     pre, _ = lax.optimization_barrier((pre, block_4[0]))

time: 117 us -> 116 us (level)
  starting transfers between devices: 45.4 us -> 42.6 us
  waiting for transfers between devices: 35.6 us -> 37.8 us
    ppermute x42, starting transfers between devices: 45.4 us -> 42.6 us  [send(): return lax.ppermute(value, ('row', 'col'), pairs_of(target))]
    ppermute x42, waiting for transfers between devices: 35.6 us -> 37.8 us  [send(): return lax.ppermute(value, ('row', 'col'), pairs_of(target))]
  transfers between devices with their start and end apart: 42 -> 42, of which waited for: 25 -> 27; matrix products, arithmetic and copies ran while one was open for 5% -> 5% of each run, Pallas kernels for 4% -> 4%
where the time goes in v8:
time: 116 us
  starting transfers between devices  42.6 us (37%)
  waiting for transfers between devices  37.8 us (33%)
  blocking collectives  16 us (14%)
  Pallas kernels  8.75 us (8%)
  other arithmetic  5.55 us (5%)
  matrix products  4.27 us (4%)
    ppermute x42, starting transfers between devices, send(): return lax.ppermute(value, ('row', 'col'), pairs_of(target))  42.6 us
    ppermute x42, waiting for transfers between devices, send(): return lax.ppermute(value, ('row', 'col'), pairs_of(target))  37.8 us
    all_to_all x1, blocking collectives, normalize(): lax.all_to_all(jnp.broadcast_to(stats[None], (NZ,) + stats.shape), 'col',...  16 us
    dot_general x1, matrix products, per_device(): lax.dot_general(gathered, slopes_all, (((0,), (0,)), ((), ())), preferred...  4.27 us
    pallas_call x1, Pallas kernels, stage(): pl.pallas_call(stage_kernel, in_specs=[pl.BlockSpec(memory_space=pl.ANY)]...  2.34 us
  transfers between devices with their start and end apart: 42, of which 27 were waited for; matrix products, arithmetic and copies ran while one was open for 5% of the time, Pallas kernels for 4%

profile of v8, /device:TPU:2, one launch (start us, length us, event | category | flops | bytes accessed | tf_op | source)
XLA Modules:
  0.0 115.8 jit_solution(10062873184930912062)
XLA Ops:
  0.6 1.0 reduce_sum.45
  1.7 1.1 multiply_reduce_fusion
  2.8 16.0 %all_to_all.5 = f32[8,2,16]{2,1,0:T(2,128)S(1)} all-to-all(f32[8,2,16]{2,1,0:T(2,128)S(1)} %broadcast_in_dim.2), channel_id=1, replica_groups=mesh['row'=32,'col'=8] {'col'}, dimensions={0} | all-to-all | bytes 2048 | tf_op jit(solution)/shard_map/all_to_all | solution.py:266
  18.8 1.0 add_convert_fusion.12
  19.8 2.2 %collective-permute-start.2 = (bf16[16,1536]{1,0:T(8,128)(2,1)S(1)}, bf16[16,1536]{1,0:T(8,128)(2,1)S(1)}, u32[]{:S(2)}, u32[]{:S(2)}) collective-permute-start(bf16[16,1536]{1,0:T(8,128)(2,1)S(1)} %add_convert_fusion.12), channel_id=1, source_target_pairs={{0,128},{1,129},{2,130},{3,131},{4,132},{5,133},{6,134},{7,135},{8... | collective-permute-start | bytes 147464 | tf_op jit(solution)/shard_map/ppermute | solution.py:33
  22.1 2.6 %collective-permute-start = (bf16[16,1536]{1,0:T(8,128)(2,1)S(1)}, bf16[16,1536]{1,0:T(8,128)(2,1)S(1)}, u32[]{:S(2)}, u32[]{:S(2)}) collective-permute-start(bf16[16,1536]{1,0:T(8,128)(2,1)S(1)} %add_convert_fusion.12), channel_id=1, source_target_pairs={{0,64},{1,65},{2,66},{3,67},{4,68},{5,69},{6,70},{7,71},{8,72},{9,... | collective-permute-start | bytes 147464 | tf_op jit(solution)/shard_map/ppermute | solution.py:33
  24.6 0.9 collective-permute-done.2
  25.5 0.6 collective-permute-done.1
  26.2 0.6 collective-permute-done
  26.7 3.1 %collective-permute-start.5 = (bf16[64,1536]{1,0:T(8,128)(2,1)S(1)}, bf16[64,1536]{1,0:T(8,128)(2,1)S(1)}, u32[]{:S(2)}, u32[]{:S(2)}) collective-permute-start(bf16[64,1536]{1,0:T(8,128)(2,1)S(1)} %pad_maximum_fusion.refs_0_), channel_id=1, source_target_pairs={{0,48},{1,49},{2,50},{3,51},{4,52},{5,53},{6,54},{7,55},{8,56},{9,... | collective-permute-start | bytes 589832 | tf_op jit(solution)/shard_map/ppermute | solution.py:33
  29.8 0.6 collective-permute-start.4
  30.5 0.5 collective-permute-start.3
  30.9 2.3 %shard_map.76.refs_8_.w_ref.refs_6_.refs_13_ = bf16[1536,1536]{1,0:T(8,128)(2,1)S(1)} custom-call(bf16[1536,1536]{1,0:T(8,128)(2,1)} %w_ref), custom_call_target="tpu_custom_call" | custom-call | flops 1207959552 | bytes 4718592 | tf_op jit(solution)/shard_map/pallas_call | solution.py:100
  33.3 2.1 %collective-permute-done.5.refs_3_ = bf16[64,1536]{1,0:T(8,128)(2,1)S(1)} collective-permute-done((bf16[64,1536]{1,0:T(8,128)(2,1)S(1)}, bf16[64,1536]{1,0:T(8,128)(2,1)S(1)}, u32[]{:S(2)}, u32[]{:S(2)}) %collective-permute-start.5) | collective-permute-done | bytes 196640 | tf_op jit(solution)/shard_map/ppermute | solution.py:33
  35.3 1.7 %collective-permute-done.4.refs_2_ = bf16[64,1536]{1,0:T(8,128)(2,1)S(1)} collective-permute-done((bf16[64,1536]{1,0:T(8,128)(2,1)S(1)}, bf16[64,1536]{1,0:T(8,128)(2,1)S(1)}, u32[]{:S(2)}, u32[]{:S(2)}) %collective-permute-start.4) | collective-permute-done | bytes 196640 | tf_op jit(solution)/shard_map/ppermute | solution.py:33
  37.0 0.5 collective-permute-start.7
  37.5 0.9 collective-permute-done.8.refs_6_
  39.0 1.7 %shard_map.77 = (bf16[512,1536]{1,0:T(8,128)(2,1)S(1)}, bf16[64,1536]{1,0:T(8,128)(2,1)S(1)}, bf16[64,768]{1,0:T(8,128)(2,1)S(1)}, bf16[64,768]{1,0:T(8,128)(2,1...) custom-call(bf16[64,1536]{1,0:T(8,128)(2,1)S(1)} %pad_maximum_fusion.refs_0_, ...), custom_call_target="tpu_custom_call" | custom-call | flops 1207959552 | bytes 4718592 | tf_op jit(solution)/shard_map/pallas_call | solution.py:164
  40.7 0.7 collective-permute-start.10
  41.4 1.4 %collective-permute-start.14 = (bf16[64,768]{1,0:T(8,128)(2,1)S(1)}, bf16[64,768]{1,0:T(8,128)(2,1)S(1)}, u32[]{:S(2)}, u32[]{:S(2)}) collective-permute-start(bf16[64,768]{1,0:T(8,128)(2,1)S(1)} %get-tuple-element.46), channel_id=1, source_target_pairs={{0,1},{1,0},{2,3},{3,2},{4,5},{5,4},{6,7},{7,6},{8,15},{9,10},{10,... | collective-permute-start | bytes 294920 | tf_op jit(solution)/shard_map/ppermute | solution.py:33
  42.8 0.6 collective-permute-start.18
  43.4 1.4 %shard_map.78 = (bf16[64,768]{1,0:T(8,128)(2,1)S(1)}, bf16[64,768]{1,0:T(8,128)(2,1)S(1)}, bf16[64,1536]{1,0:T(8,128)(2,1)S(1)}, bf16[64,1536]{1,0:T(8,128)(2,1)...) custom-call(bf16[512,1536]{1,0:T(8,128)(2,1)S(1)} %get-tuple-element.37.normed_ref, ...), custom_call_target="tpu_custom_call" | custom-call | flops 1207959552 | bytes 4718592 | tf_op jit(solution)/shard_map/pallas_call | solution.py:175
  44.8 0.6 collective-permute-done.10
  45.5 0.8 collective-permute-start.11
  46.5 2.4 %collective-permute-start.15 = (bf16[64,768]{1,0:T(8,128)(2,1)S(1)}, bf16[64,768]{1,0:T(8,128)(2,1)S(1)}, u32[]{:S(2)}, u32[]{:S(2)}) collective-permute-start(bf16[64,768]{1,0:T(8,128)(2,1)S(1)} %add_convert_fusion.7), channel_id=1, source_target_pairs={{0,7},{1,2},{2,1},{3,4},{4,3},{5,6},{6,5},{7,0},{8,9},{9,8},{10,11... | collective-permute-start | bytes 294920 | tf_op jit(solution)/shard_map/ppermute | solution.py:33
  49.0 1.0 collective-permute-start.19
  50.0 1.4 %collective-permute-done.11 = bf16[64,768]{1,0:T(8,128)(2,1)S(1)} collective-permute-done((bf16[64,768]{1,0:T(8,128)(2,1)S(1)}, bf16[64,768]{1,0:T(8,128)(2,1)S(1)}, u32[]{:S(2)}, u32[]{:S(2)}) %collective-permute-start.11) | collective-permute-done | bytes 98336 | tf_op jit(solution)/shard_map/ppermute | solution.py:33
  51.5 0.9 collective-permute-done.15
  52.5 1.4 %collective-permute-start.16 = (bf16[64,768]{1,0:T(8,128)(2,1)S(1)}, bf16[64,768]{1,0:T(8,128)(2,1)S(1)}, u32[]{:S(2)}, u32[]{:S(2)}) collective-permute-start(bf16[64,768]{1,0:T(8,128)(2,1)S(1)} %add_convert_fusion.6), channel_id=1, source_target_pairs={{0,1},{1,0},{2,3},{3,2},{4,5},{5,4},{6,7},{7,6},{8,15},{9,10},{10,... | collective-permute-start | bytes 294920 | tf_op jit(solution)/shard_map/ppermute | solution.py:33
  53.8 2.3 %collective-permute-done.12 = bf16[64,768]{1,0:T(8,128)(2,1)S(1)} collective-permute-done((bf16[64,768]{1,0:T(8,128)(2,1)S(1)}, bf16[64,768]{1,0:T(8,128)(2,1)S(1)}, u32[]{:S(2)}, u32[]{:S(2)}) %collective-permute-start.12) | collective-permute-done | bytes 98336 | tf_op jit(solution)/shard_map/ppermute | solution.py:33
  56.1 1.0 collective-permute-start.13
  57.5 0.9 collective-permute-start.20
  58.4 1.4 %collective-permute-start.17 = (bf16[64,768]{1,0:T(8,128)(2,1)S(1)}, bf16[64,768]{1,0:T(8,128)(2,1)S(1)}, u32[]{:S(2)}, u32[]{:S(2)}) collective-permute-start(bf16[64,768]{1,0:T(8,128)(2,1)S(1)} %add_convert_fusion.5), channel_id=1, source_target_pairs={{0,7},{1,2},{2,1},{3,4},{4,3},{5,6},{6,5},{7,0},{8,9},{9,8},{10,11... | collective-permute-start | bytes 294920 | tf_op jit(solution)/shard_map/ppermute | solution.py:33
  59.8 3.3 %collective-permute-done.13 = bf16[64,768]{1,0:T(8,128)(2,1)S(1)} collective-permute-done((bf16[64,768]{1,0:T(8,128)(2,1)S(1)}, bf16[64,768]{1,0:T(8,128)(2,1)S(1)}, u32[]{:S(2)}, u32[]{:S(2)}) %collective-permute-start.13) | collective-permute-done | bytes 98336 | tf_op jit(solution)/shard_map/ppermute | solution.py:33
  63.1 1.2 %collective-permute-done.17 = bf16[64,768]{1,0:T(8,128)(2,1)S(1)} collective-permute-done((bf16[64,768]{1,0:T(8,128)(2,1)S(1)}, bf16[64,768]{1,0:T(8,128)(2,1)S(1)}, u32[]{:S(2)}, u32[]{:S(2)}) %collective-permute-start.17) | collective-permute-done | bytes 98336 | tf_op jit(solution)/shard_map/ppermute | solution.py:33
  64.3 0.3 fusion.2
  64.8 2.0 %collective-permute-start.21 = (bf16[64,768]{1,0:T(8,128)(2,1)S(1)}, bf16[64,768]{1,0:T(8,128)(2,1)S(1)}, u32[]{:S(2)}, u32[]{:S(2)}) collective-permute-start(bf16[64,768]{1,0:T(8,128)(2,1)S(1)} %get-tuple-element.50), channel_id=1, source_target_pairs={{0,7},{1,2},{2,1},{3,4},{4,3},{5,6},{6,5},{7,0},{8,9},{9,8},{10,11... | collective-permute-start | bytes 294920 | tf_op jit(solution)/shard_map/ppermute | solution.py:33
  66.8 1.3 %collective-permute-start.25 = (bf16[64,768]{1,0:T(8,128)(2,1)S(1)}, bf16[64,768]{1,0:T(8,128)(2,1)S(1)}, u32[]{:S(2)}, u32[]{:S(2)}) collective-permute-start(bf16[64,768]{1,0:T(8,128)(2,1)S(1)} %get-tuple-element.52), channel_id=1, source_target_pairs={{0,7},{1,2},{2,1},{3,4},{4,3},{5,6},{6,5},{7,0},{8,9},{9,8},{10,11... | collective-permute-start | bytes 294920 | tf_op jit(solution)/shard_map/ppermute | solution.py:33
  68.1 4.4 %collective-permute-done.26.refs_3_ = bf16[64,1536]{1,0:T(8,128)(2,1)S(1)} collective-permute-done((bf16[64,1536]{1,0:T(8,128)(2,1)S(1)}, bf16[64,1536]{1,0:T(8,128)(2,1)S(1)}, u32[]{:S(2)}, u32[]{:S(2)}) %collective-permute-start.26) | collective-permute-done | bytes 196640 | tf_op jit(solution)/shard_map/ppermute | solution.py:33
  72.5 0.9 collective-permute-start.28
  73.4 2.0 %collective-permute-start.27 = (bf16[64,768]{1,0:T(8,128)(2,1)S(1)}, bf16[64,768]{1,0:T(8,128)(2,1)S(1)}, u32[]{:S(2)}, u32[]{:S(2)}) collective-permute-start(bf16[64,768]{1,0:T(8,128)(2,1)S(1)} %collective-permute-done.25.refs_1_), channel_id=1, source_target_pairs={{0,1},{1,0},{2,3},{3,2},{4,5},{5,4},{6,7},{7,6},{8,15},{9,10},{10,... | collective-permute-start | bytes 294920 | tf_op jit(solution)/shard_map/ppermute | solution.py:33
  75.5 2.7 %collective-permute-done.22.refs_4_ = bf16[64,768]{1,0:T(8,128)(2,1)S(1)} collective-permute-done((bf16[64,768]{1,0:T(8,128)(2,1)S(1)}, bf16[64,768]{1,0:T(8,128)(2,1)S(1)}, u32[]{:S(2)}, u32[]{:S(2)}) %collective-permute-start.22) | collective-permute-done | bytes 98336 | tf_op jit(solution)/shard_map/ppermute | solution.py:33
  78.2 2.8 %collective-permute-start.23 = (bf16[64,768]{1,0:T(8,128)(2,1)S(1)}, bf16[64,768]{1,0:T(8,128)(2,1)S(1)}, u32[]{:S(2)}, u32[]{:S(2)}) collective-permute-start(bf16[64,768]{1,0:T(8,128)(2,1)S(1)} %collective-permute-done.22.refs_4_), channel_id=1, source_target_pairs={{0,7},{1,2},{2,1},{3,4},{4,3},{5,6},{6,5},{7,0},{8,9},{9,8},{10,11... | collective-permute-start | bytes 294920 | tf_op jit(solution)/shard_map/ppermute | solution.py:33
  81.0 2.1 %collective-permute-start.30 = (bf16[64,768]{1,0:T(8,128)(2,1)S(1)}, bf16[64,768]{1,0:T(8,128)(2,1)S(1)}, u32[]{:S(2)}, u32[]{:S(2)}) collective-permute-start(bf16[64,768]{1,0:T(8,128)(2,1)S(1)} %collective-permute-done.27.refs_5_), channel_id=1, source_target_pairs={{0,7},{1,2},{2,1},{3,4},{4,3},{5,6},{6,5},{7,0},{8,9},{9,8},{10,11... | collective-permute-start | bytes 294920 | tf_op jit(solution)/shard_map/ppermute | solution.py:33
  83.1 2.0 %collective-permute-done.23.refs_9_ = bf16[64,768]{1,0:T(8,128)(2,1)S(1)} collective-permute-done((bf16[64,768]{1,0:T(8,128)(2,1)S(1)}, bf16[64,768]{1,0:T(8,128)(2,1)S(1)}, u32[]{:S(2)}, u32[]{:S(2)}) %collective-permute-start.23) | collective-permute-done | bytes 98336 | tf_op jit(solution)/shard_map/ppermute | solution.py:33
  85.1 2.8 %collective-permute-done.30.refs_10_ = bf16[64,768]{1,0:T(8,128)(2,1)S(1)} collective-permute-done((bf16[64,768]{1,0:T(8,128)(2,1)S(1)}, bf16[64,768]{1,0:T(8,128)(2,1)S(1)}, u32[]{:S(2)}, u32[]{:S(2)}) %collective-permute-start.30) | collective-permute-done | bytes 98336 | tf_op jit(solution)/shard_map/ppermute | solution.py:33
  88.0 1.4 %shard_map.79.refs_12_ = bf16[256,1536]{1,0:T(8,128)(2,1)S(1)} custom-call(bf16[64,768]{1,0:T(8,128)(2,1)S(1)} %collective-permute-done.21.refs_0_, bf16[64,768]{1,0:T(8,128)(2,1)S(1)} %collective-permute-done.25.refs_1_, bf16[64,1536]{1,0:T(8,128)(2,1)S(1)} %get-tuple-element.53.refs_2_, bf16[64,1536]{1,0:T(8,128)(2,1)S(1)} %collective-permute-done.26.refs_3_, ...), custom_call_target="tpu_custom_call" | custom-call | flops 1207959552 | bytes 4718592 | tf_op jit(solution)/shard_map/pallas_call | solution.py:209
  89.4 0.5 collective-permute-done.24.refs_7_
  89.8 2.7 %collective-permute-done.31.refs_8_ = bf16[64,768]{1,0:T(8,128)(2,1)S(1)} collective-permute-done((bf16[64,768]{1,0:T(8,128)(2,1)S(1)}, bf16[64,768]{1,0:T(8,128)(2,1)S(1)}, u32[]{:S(2)}, u32[]{:S(2)}) %collective-permute-start.31) | collective-permute-done | bytes 98336 | tf_op jit(solution)/shard_map/ppermute | solution.py:33
  92.6 1.9 %shard_map.80 = (bf16[512,1536]{1,0:T(8,128)(2,1)S(1)}, bf16[64,1536]{1,0:T(8,128)(2,1)S(1)}, bf16[64,1536]{1,0:T(8,128)(2,1)S(1)}, bf16[64,1536]{1,0:T(8,128)(2...) custom-call(bf16[64,768]{1,0:T(8,128)(2,1)S(1)} %collective-permute-, ...), custom_call_target="tpu_custom_call" | custom-call | flops 1207959552 | bytes 4718592 | tf_op jit(solution)/shard_map/pallas_call | solution.py:238
  94.6 0.5 collective-permute-start.32
  95.2 0.4 collective-permute-start.37
  95.6 0.4 collective-permute-done.33
  96.1 2.5 %collective-permute-start.34 = (bf16[64,1536]{1,0:T(8,128)(2,1)S(1)}, bf16[64,1536]{1,0:T(8,128)(2,1)S(1)}, u32[]{:S(2)}, u32[]{:S(2)}) collective-permute-start(bf16[64,1536]{1,0:T(8,128)(2,1)S(1)} %add_convert_fusion.2), channel_id=1, source_target_pairs={{0,48},{1,49},{2,50},{3,51},{4,52},{5,53},{6,54},{7,55},{8,200},{9... | collective-permute-start | bytes 589832 | tf_op jit(solution)/shard_map/ppermute | solution.py:33
  98.6 0.8 collective-permute-start.36
  99.5 1.1 collective-permute-start.38
  100.5 4.3 %convolution_convert_fusion = bf16[1536,1536]{1,0:T(8,128)(2,1)} fusion(bf16[512,1536]{1,0:T(8,128)(2,1)S(1)} %get-tuple-element.37.normed_ref, bf16[512,1536]{1,0:T(8,128)(2,1)S(1)} %get-tuple-element.62), kind=kOutput, calls=%fused_computation | convolution fusion | flops 2418278400 | bytes 7864320 | tf_op jit(solution)/shard_map/dot_general | solution.py:321
  104.8 1.1 collective-permute-done.36
  106.4 0.8 collective-permute-start.39
  107.1 3.9 %collective-permute-start.41 = (bf16[16,1536]{1,0:T(8,128)(2,1)S(1)}, bf16[16,1536]{1,0:T(8,128)(2,1)S(1)}, u32[]{:S(2)}, u32[]{:S(2)}) collective-permute-start(bf16[16,1536]{1,0:T(8,128)(2,1)S(1)} %get-tuple-element.68), channel_id=1, source_target_pairs={{0,128},{1,129},{2,130},{3,131},{4,132},{5,133},{6,134},{7,135},{8... | collective-permute-start | bytes 147464 | tf_op jit(solution)/shard_map/ppermute | solution.py:33
  111.1 0.8 fusion.17
  111.9 1.3 %collective-permute-done.41 = bf16[16,1536]{1,0:T(8,128)(2,1)S(1)} collective-permute-done((bf16[16,1536]{1,0:T(8,128)(2,1)S(1)}, bf16[16,1536]{1,0:T(8,128)(2,1)S(1)}, u32[]{:S(2)}, u32[]{:S(2)}) %collective-permute-start.41) | collective-permute-done | bytes 49184 | tf_op jit(solution)/shard_map/ppermute | solution.py:33
  113.1 2.0 %collective-permute-done.40 = bf16[16,1536]{1,0:T(8,128)(2,1)S(1)} collective-permute-done((bf16[16,1536]{1,0:T(8,128)(2,1)S(1)}, bf16[16,1536]{1,0:T(8,128)(2,1)S(1)}, u32[]{:S(2)}, u32[]{:S(2)}) %collective-permute-start.40) | collective-permute-done | bytes 49184 | tf_op jit(solution)/shard_map/ppermute | solution.py:33
  115.2 0.6 add_convert_fusion.11
  (59 shorter events, 2.5 us)
Async XLA Ops:
  19.8 5.7 %collective-permute-start.2 = (bf16[16,1536]{1,0:T(8,128)(2,1)S(1)}, bf16[16,1536]{1,0:T(8,128)(2,1)S(1)}, u32[]{:S(2)}, u32[]{:S(2)}) collective-permute-start(bf16[16,1536]{1,0:T(8,128)(2,1)S(1)} %add_convert_fusion.12), channel_id=1, source_target_pairs={{0,128},{1,129},{2,130},{3,131},{4,132},{5,133},{6,134},{7,135},{8... | collective-permute-start | bytes 147464 | tf_op jit(solution)/shard_map/ppermute | solution.py:33
  22.1 4.1 %collective-permute-start.1 = (bf16[16,1536]{1,0:T(8,128)(2,1)S(1)}, bf16[16,1536]{1,0:T(8,128)(2,1)S(1)}, u32[]{:S(2)}, u32[]{:S(2)}) collective-permute-start(bf16[16,1536]{1,0:T(8,128)(2,1)S(1)} %add_convert_fusion.12), channel_id=1, source_target_pairs={{0,192},{1,193},{2,194},{3,195},{4,196},{5,197},{6,198},{7,199},{8... | collective-permute-start | bytes 147464 | tf_op jit(solution)/shard_map/ppermute | solution.py:33
  22.1 4.6 %collective-permute-start = (bf16[16,1536]{1,0:T(8,128)(2,1)S(1)}, bf16[16,1536]{1,0:T(8,128)(2,1)S(1)}, u32[]{:S(2)}, u32[]{:S(2)}) collective-permute-start(bf16[16,1536]{1,0:T(8,128)(2,1)S(1)} %add_convert_fusion.12), channel_id=1, source_target_pairs={{0,64},{1,65},{2,66},{3,67},{4,68},{5,69},{6,70},{7,71},{8,72},{9,... | collective-permute-start | bytes 147464 | tf_op jit(solution)/shard_map/ppermute | solution.py:33
  26.7 8.6 %collective-permute-start.5 = (bf16[64,1536]{1,0:T(8,128)(2,1)S(1)}, bf16[64,1536]{1,0:T(8,128)(2,1)S(1)}, u32[]{:S(2)}, u32[]{:S(2)}) collective-permute-start(bf16[64,1536]{1,0:T(8,128)(2,1)S(1)} %pad_maximum_fusion.refs_0_), channel_id=1, source_target_pairs={{0,48},{1,49},{2,50},{3,51},{4,52},{5,53},{6,54},{7,55},{8,56},{9,... | collective-permute-start | bytes 589832 | tf_op jit(solution)/shard_map/ppermute | solution.py:33
  29.8 7.2 %collective-permute-start.4 = (bf16[64,1536]{1,0:T(8,128)(2,1)S(1)}, bf16[64,1536]{1,0:T(8,128)(2,1)S(1)}, u32[]{:S(2)}, u32[]{:S(2)}) collective-permute-start(bf16[64,1536]{1,0:T(8,128)(2,1)S(1)} %pad_maximum_fusion.refs_0_), channel_id=1, source_target_pairs={{0,32},{1,33},{2,34},{3,35},{4,36},{5,37},{6,38},{7,39},{8,40},{9,... | collective-permute-start | bytes 589832 | tf_op jit(solution)/shard_map/ppermute | solution.py:33
  30.5 6.6 %collective-permute-start.3 = (bf16[64,1536]{1,0:T(8,128)(2,1)S(1)}, bf16[64,1536]{1,0:T(8,128)(2,1)S(1)}, u32[]{:S(2)}, u32[]{:S(2)}) collective-permute-start(bf16[64,1536]{1,0:T(8,128)(2,1)S(1)} %pad_maximum_fusion.refs_0_), channel_id=1, source_target_pairs={{0,16},{1,17},{2,18},{3,19},{4,20},{5,21},{6,22},{7,23},{8,24},{9,... | collective-permute-start | bytes 589832 | tf_op jit(solution)/shard_map/ppermute | solution.py:33
  30.9 6.6 %collective-permute-start.6 = (bf16[64,1536]{1,0:T(8,128)(2,1)S(1)}, bf16[64,1536]{1,0:T(8,128)(2,1)S(1)}, u32[]{:S(2)}, u32[]{:S(2)}) collective-permute-start(bf16[64,1536]{1,0:T(8,128)(2,1)S(1)} %pad_maximum_fusion.refs_0_), channel_id=1, source_target_pairs={{0,8},{1,9},{2,10},{3,11},{4,12},{5,13},{6,14},{7,15},{8,0},{9,1},... | collective-permute-start | bytes 589832 | tf_op jit(solution)/shard_map/ppermute | solution.py:33
  37.0 1.4 %collective-permute-start.8 = (bf16[64,1536]{1,0:T(8,128)(2,1)S(1)}, bf16[64,1536]{1,0:T(8,128)(2,1)S(1)}, u32[]{:S(2)}, u32[]{:S(2)}) collective-permute-start(bf16[64,1536]{1,0:T(8,128)(2,1)S(1)} %collective-permute-done.4.refs_2_), channel_id=1, source_target_pairs={{0,8},{1,9},{2,10},{3,11},{4,12},{5,13},{6,14},{7,15},{8,0},{9,1},... | collective-permute-start | bytes 589832 | tf_op jit(solution)/shard_map/ppermute | solution.py:33
  37.0 1.7 %collective-permute-start.7 = (bf16[64,1536]{1,0:T(8,128)(2,1)S(1)}, bf16[64,1536]{1,0:T(8,128)(2,1)S(1)}, u32[]{:S(2)}, u32[]{:S(2)}) collective-permute-start(bf16[64,1536]{1,0:T(8,128)(2,1)S(1)} %collective-permute-done.3.refs_1_), channel_id=1, source_target_pairs={{0,8},{1,9},{2,10},{3,11},{4,12},{5,13},{6,14},{7,15},{8,0},{9,1},... | collective-permute-start | bytes 589832 | tf_op jit(solution)/shard_map/ppermute | solution.py:33
  37.5 1.5 %collective-permute-start.9 = (bf16[64,1536]{1,0:T(8,128)(2,1)S(1)}, bf16[64,1536]{1,0:T(8,128)(2,1)S(1)}, u32[]{:S(2)}, u32[]{:S(2)}) collective-permute-start(bf16[64,1536]{1,0:T(8,128)(2,1)S(1)} %collective-permute-done.5.refs_3_), channel_id=1, source_target_pairs={{0,8},{1,9},{2,10},{3,11},{4,12},{5,13},{6,14},{7,15},{8,0},{9,1},... | collective-permute-start | bytes 589832 | tf_op jit(solution)/shard_map/ppermute | solution.py:33
  40.7 4.7 %collective-permute-start.10 = (bf16[64,768]{1,0:T(8,128)(2,1)S(1)}, bf16[64,768]{1,0:T(8,128)(2,1)S(1)}, u32[]{:S(2)}, u32[]{:S(2)}) collective-permute-start(bf16[64,768]{1,0:T(8,128)(2,1)S(1)} %get-tuple-element.42), channel_id=1, source_target_pairs={{0,1},{1,0},{2,3},{3,2},{4,5},{5,4},{6,7},{7,6},{8,15},{9,10},{10,... | collective-permute-start | bytes 294920 | tf_op jit(solution)/shard_map/ppermute | solution.py:33
  41.4 5.1 %collective-permute-start.14 = (bf16[64,768]{1,0:T(8,128)(2,1)S(1)}, bf16[64,768]{1,0:T(8,128)(2,1)S(1)}, u32[]{:S(2)}, u32[]{:S(2)}) collective-permute-start(bf16[64,768]{1,0:T(8,128)(2,1)S(1)} %get-tuple-element.46), channel_id=1, source_target_pairs={{0,1},{1,0},{2,3},{3,2},{4,5},{5,4},{6,7},{7,6},{8,15},{9,10},{10,... | collective-permute-start | bytes 294920 | tf_op jit(solution)/shard_map/ppermute | solution.py:33
  42.8 6.1 %collective-permute-start.18 = (bf16[64,1536]{1,0:T(8,128)(2,1)S(1)}, bf16[64,1536]{1,0:T(8,128)(2,1)S(1)}, u32[]{:S(2)}, u32[]{:S(2)}) collective-permute-start(bf16[64,1536]{1,0:T(8,128)(2,1)S(1)} %get-tuple-element.49), channel_id=1, source_target_pairs={{0,1},{1,0},{2,3},{3,2},{4,5},{5,4},{6,7},{7,6},{8,15},{9,10},{10,... | collective-permute-start | bytes 589832 | tf_op jit(solution)/shard_map/ppermute | solution.py:33
  44.8 19.5 %copy-start = (bf16[64,1536]{1,0:T(8,128)(2,1)S(1)}, bf16[64,1536]{1,0:T(8,128)(2,1)}, u32[]{:S(2)}) copy-start(bf16[64,1536]{1,0:T(8,128)(2,1)} %param.9) | copy-start | bytes 589828
  45.5 5.9 %collective-permute-start.11 = (bf16[64,768]{1,0:T(8,128)(2,1)S(1)}, bf16[64,768]{1,0:T(8,128)(2,1)S(1)}, u32[]{:S(2)}, u32[]{:S(2)}) collective-permute-start(bf16[64,768]{1,0:T(8,128)(2,1)S(1)} %add_convert_fusion.10), channel_id=1, source_target_pairs={{0,7},{1,2},{2,1},{3,4},{4,3},{5,6},{6,5},{7,0},{8,9},{9,8},{10,11... | collective-permute-start | bytes 294920 | tf_op jit(solution)/shard_map/ppermute | solution.py:33
  46.5 5.9 %collective-permute-start.15 = (bf16[64,768]{1,0:T(8,128)(2,1)S(1)}, bf16[64,768]{1,0:T(8,128)(2,1)S(1)}, u32[]{:S(2)}, u32[]{:S(2)}) collective-permute-start(bf16[64,768]{1,0:T(8,128)(2,1)S(1)} %add_convert_fusion.7), channel_id=1, source_target_pairs={{0,7},{1,2},{2,1},{3,4},{4,3},{5,6},{6,5},{7,0},{8,9},{9,8},{10,11... | collective-permute-start | bytes 294920 | tf_op jit(solution)/shard_map/ppermute | solution.py:33
  49.0 8.5 %collective-permute-start.19 = (bf16[64,1536]{1,0:T(8,128)(2,1)S(1)}, bf16[64,1536]{1,0:T(8,128)(2,1)S(1)}, u32[]{:S(2)}, u32[]{:S(2)}) collective-permute-start(bf16[64,1536]{1,0:T(8,128)(2,1)S(1)} %add_convert_fusion.4), channel_id=1, source_target_pairs={{0,7},{1,2},{2,1},{3,4},{4,3},{5,6},{6,5},{7,0},{8,9},{9,8},{10,11... | collective-permute-start | bytes 589832 | tf_op jit(solution)/shard_map/ppermute | solution.py:33
  51.4 4.7 %collective-permute-start.12 = (bf16[64,768]{1,0:T(8,128)(2,1)S(1)}, bf16[64,768]{1,0:T(8,128)(2,1)S(1)}, u32[]{:S(2)}, u32[]{:S(2)}) collective-permute-start(bf16[64,768]{1,0:T(8,128)(2,1)S(1)} %add_convert_fusion.9), channel_id=1, source_target_pairs={{0,1},{1,0},{2,3},{3,2},{4,5},{5,4},{6,7},{7,6},{8,15},{9,10},{10,... | collective-permute-start | bytes 294920 | tf_op jit(solution)/shard_map/ppermute | solution.py:33
  52.5 5.9 %collective-permute-start.16 = (bf16[64,768]{1,0:T(8,128)(2,1)S(1)}, bf16[64,768]{1,0:T(8,128)(2,1)S(1)}, u32[]{:S(2)}, u32[]{:S(2)}) collective-permute-start(bf16[64,768]{1,0:T(8,128)(2,1)S(1)} %add_convert_fusion.6), channel_id=1, source_target_pairs={{0,1},{1,0},{2,3},{3,2},{4,5},{5,4},{6,7},{7,6},{8,15},{9,10},{10,... | collective-permute-start | bytes 294920 | tf_op jit(solution)/shard_map/ppermute | solution.py:33
  56.1 7.0 %collective-permute-start.13 = (bf16[64,768]{1,0:T(8,128)(2,1)S(1)}, bf16[64,768]{1,0:T(8,128)(2,1)S(1)}, u32[]{:S(2)}, u32[]{:S(2)}) collective-permute-start(bf16[64,768]{1,0:T(8,128)(2,1)S(1)} %add_convert_fusion.8), channel_id=1, source_target_pairs={{0,7},{1,2},{2,1},{3,4},{4,3},{5,6},{6,5},{7,0},{8,9},{9,8},{10,11... | collective-permute-start | bytes 294920 | tf_op jit(solution)/shard_map/ppermute | solution.py:33
  57.5 6.8 %collective-permute-start.20 = (bf16[64,1536]{1,0:T(8,128)(2,1)S(1)}, bf16[64,1536]{1,0:T(8,128)(2,1)S(1)}, u32[]{:S(2)}, u32[]{:S(2)}) collective-permute-start(bf16[64,1536]{1,0:T(8,128)(2,1)S(1)} %add_convert_fusion.3), channel_id=1, source_target_pairs={{0,1},{1,0},{2,3},{3,2},{4,5},{5,4},{6,7},{7,6},{8,15},{9,10},{10,... | collective-permute-start | bytes 589832 | tf_op jit(solution)/shard_map/ppermute | solution.py:33
  58.4 5.9 %collective-permute-start.17 = (bf16[64,768]{1,0:T(8,128)(2,1)S(1)}, bf16[64,768]{1,0:T(8,128)(2,1)S(1)}, u32[]{:S(2)}, u32[]{:S(2)}) collective-permute-start(bf16[64,768]{1,0:T(8,128)(2,1)S(1)} %add_convert_fusion.5), channel_id=1, source_target_pairs={{0,7},{1,2},{2,1},{3,4},{4,3},{5,6},{6,5},{7,0},{8,9},{9,8},{10,11... | collective-permute-start | bytes 294920 | tf_op jit(solution)/shard_map/ppermute | solution.py:33
  64.7 7.8 %collective-permute-start.26 = (bf16[64,1536]{1,0:T(8,128)(2,1)S(1)}, bf16[64,1536]{1,0:T(8,128)(2,1)S(1)}, u32[]{:S(2)}, u32[]{:S(2)}) collective-permute-start(bf16[64,1536]{1,0:T(8,128)(2,1)S(1)} %get-tuple-element.53.refs_2_), channel_id=1, source_target_pairs={{0,1},{1,0},{2,3},{3,2},{4,5},{5,4},{6,7},{7,6},{8,15},{9,10},{10,... | collective-permute-start | bytes 589832 | tf_op jit(solution)/shard_map/ppermute | solution.py:33
  64.8 8.6 %collective-permute-start.21 = (bf16[64,768]{1,0:T(8,128)(2,1)S(1)}, bf16[64,768]{1,0:T(8,128)(2,1)S(1)}, u32[]{:S(2)}, u32[]{:S(2)}) collective-permute-start(bf16[64,768]{1,0:T(8,128)(2,1)S(1)} %get-tuple-element.50), channel_id=1, source_target_pairs={{0,7},{1,2},{2,1},{3,4},{4,3},{5,6},{6,5},{7,0},{8,9},{9,8},{10,11... | collective-permute-start | bytes 294920 | tf_op jit(solution)/shard_map/ppermute | solution.py:33
  66.8 6.6 %collective-permute-start.25 = (bf16[64,768]{1,0:T(8,128)(2,1)S(1)}, bf16[64,768]{1,0:T(8,128)(2,1)S(1)}, u32[]{:S(2)}, u32[]{:S(2)}) collective-permute-start(bf16[64,768]{1,0:T(8,128)(2,1)S(1)} %get-tuple-element.52), channel_id=1, source_target_pairs={{0,7},{1,2},{2,1},{3,4},{4,3},{5,6},{6,5},{7,0},{8,9},{9,8},{10,11... | collective-permute-start | bytes 294920 | tf_op jit(solution)/shard_map/ppermute | solution.py:33
  72.5 10.6 %collective-permute-start.28 = (bf16[64,1536]{1,0:T(8,128)(2,1)S(1)}, bf16[64,1536]{1,0:T(8,128)(2,1)S(1)}, u32[]{:S(2)}, u32[]{:S(2)}) collective-permute-start(bf16[64,1536]{1,0:T(8,128)(2,1)S(1)} %collective-permute-done.26.refs_3_), channel_id=1, source_target_pairs={{0,7},{1,2},{2,1},{3,4},{4,3},{5,6},{6,5},{7,0},{8,9},{9,8},{10,11... | collective-permute-start | bytes 589832 | tf_op jit(solution)/shard_map/ppermute | solution.py:33
  73.4 4.8 %collective-permute-start.22 = (bf16[64,768]{1,0:T(8,128)(2,1)S(1)}, bf16[64,768]{1,0:T(8,128)(2,1)S(1)}, u32[]{:S(2)}, u32[]{:S(2)}) collective-permute-start(bf16[64,768]{1,0:T(8,128)(2,1)S(1)} %collective-permute-done.21.refs_0_), channel_id=1, source_target_pairs={{0,1},{1,0},{2,3},{3,2},{4,5},{5,4},{6,7},{7,6},{8,15},{9,10},{10,... | collective-permute-start | bytes 294920 | tf_op jit(solution)/shard_map/ppermute | solution.py:33
  73.4 7.6 %collective-permute-start.27 = (bf16[64,768]{1,0:T(8,128)(2,1)S(1)}, bf16[64,768]{1,0:T(8,128)(2,1)S(1)}, u32[]{:S(2)}, u32[]{:S(2)}) collective-permute-start(bf16[64,768]{1,0:T(8,128)(2,1)S(1)} %collective-permute-done.25.refs_1_), channel_id=1, source_target_pairs={{0,1},{1,0},{2,3},{3,2},{4,5},{5,4},{6,7},{7,6},{8,15},{9,10},{10,... | collective-permute-start | bytes 294920 | tf_op jit(solution)/shard_map/ppermute | solution.py:33
  78.2 6.9 %collective-permute-start.23 = (bf16[64,768]{1,0:T(8,128)(2,1)S(1)}, bf16[64,768]{1,0:T(8,128)(2,1)S(1)}, u32[]{:S(2)}, u32[]{:S(2)}) collective-permute-start(bf16[64,768]{1,0:T(8,128)(2,1)S(1)} %collective-permute-done.22.refs_4_), channel_id=1, source_target_pairs={{0,7},{1,2},{2,1},{3,4},{4,3},{5,6},{6,5},{7,0},{8,9},{9,8},{10,11... | collective-permute-start | bytes 294920 | tf_op jit(solution)/shard_map/ppermute | solution.py:33
  81.0 6.9 %collective-permute-start.30 = (bf16[64,768]{1,0:T(8,128)(2,1)S(1)}, bf16[64,768]{1,0:T(8,128)(2,1)S(1)}, u32[]{:S(2)}, u32[]{:S(2)}) collective-permute-start(bf16[64,768]{1,0:T(8,128)(2,1)S(1)} %collective-permute-done.27.refs_5_), channel_id=1, source_target_pairs={{0,7},{1,2},{2,1},{3,4},{4,3},{5,6},{6,5},{7,0},{8,9},{9,8},{10,11... | collective-permute-start | bytes 294920 | tf_op jit(solution)/shard_map/ppermute | solution.py:33
  83.1 9.5 %collective-permute-start.29 = (bf16[64,1536]{1,0:T(8,128)(2,1)S(1)}, bf16[64,1536]{1,0:T(8,128)(2,1)S(1)}, u32[]{:S(2)}, u32[]{:S(2)}) collective-permute-start(bf16[64,1536]{1,0:T(8,128)(2,1)S(1)} %collective-permute-done.28.refs_11_), channel_id=1, source_target_pairs={{0,1},{1,0},{2,3},{3,2},{4,5},{5,4},{6,7},{7,6},{8,15},{9,10},{10,... | collective-permute-start | bytes 589832 | tf_op jit(solution)/shard_map/ppermute | solution.py:33
  85.1 4.7 %collective-permute-start.24 = (bf16[64,768]{1,0:T(8,128)(2,1)S(1)}, bf16[64,768]{1,0:T(8,128)(2,1)S(1)}, u32[]{:S(2)}, u32[]{:S(2)}) collective-permute-start(bf16[64,768]{1,0:T(8,128)(2,1)S(1)} %collective-permute-done.23.refs_9_), channel_id=1, source_target_pairs={{0,1},{1,0},{2,3},{3,2},{4,5},{5,4},{6,7},{7,6},{8,15},{9,10},{10,... | collective-permute-start | bytes 294920 | tf_op jit(solution)/shard_map/ppermute | solution.py:33
  87.9 4.6 %collective-permute-start.31 = (bf16[64,768]{1,0:T(8,128)(2,1)S(1)}, bf16[64,768]{1,0:T(8,128)(2,1)S(1)}, u32[]{:S(2)}, u32[]{:S(2)}) collective-permute-start(bf16[64,768]{1,0:T(8,128)(2,1)S(1)} %collective-permute-done.30.refs_10_), channel_id=1, source_target_pairs={{0,1},{1,0},{2,3},{3,2},{4,5},{5,4},{6,7},{7,6},{8,15},{9,10},{10,... | collective-permute-start | bytes 294920 | tf_op jit(solution)/shard_map/ppermute | solution.py:33
  94.5 1.5 %collective-permute-start.33 = (bf16[64,1536]{1,0:T(8,128)(2,1)S(1)}, bf16[64,1536]{1,0:T(8,128)(2,1)S(1)}, u32[]{:S(2)}, u32[]{:S(2)}) collective-permute-start(bf16[64,1536]{1,0:T(8,128)(2,1)S(1)} %get-tuple-element.57), channel_id=1, source_target_pairs={{0,8},{1,9},{2,10},{3,11},{4,12},{5,13},{6,14},{7,15},{8,0},{9,1},... | collective-permute-start | bytes 589832 | tf_op jit(solution)/shard_map/ppermute | solution.py:33
  94.6 10.2 %collective-permute-start.32 = (bf16[64,1536]{1,0:T(8,128)(2,1)S(1)}, bf16[64,1536]{1,0:T(8,128)(2,1)S(1)}, u32[]{:S(2)}, u32[]{:S(2)}) collective-permute-start(bf16[64,1536]{1,0:T(8,128)(2,1)S(1)} %get-tuple-element.55), channel_id=1, source_target_pairs={{0,8},{1,9},{2,10},{3,11},{4,12},{5,13},{6,14},{7,15},{8,0},{9,1},... | collective-permute-start | bytes 589832 | tf_op jit(solution)/shard_map/ppermute | solution.py:33
  95.1 3.5 %collective-permute-start.35 = (bf16[64,1536]{1,0:T(8,128)(2,1)S(1)}, bf16[64,1536]{1,0:T(8,128)(2,1)S(1)}, u32[]{:S(2)}, u32[]{:S(2)}) collective-permute-start(bf16[64,1536]{1,0:T(8,128)(2,1)S(1)} %get-tuple-element.59), channel_id=1, source_target_pairs={{0,8},{1,9},{2,10},{3,11},{4,12},{5,13},{6,14},{7,15},{8,0},{9,1},... | collective-permute-start | bytes 589832 | tf_op jit(solution)/shard_map/ppermute | solution.py:33
  95.2 4.2 %collective-permute-start.37 = (bf16[64,1536]{1,0:T(8,128)(2,1)S(1)}, bf16[64,1536]{1,0:T(8,128)(2,1)S(1)}, u32[]{:S(2)}, u32[]{:S(2)}) collective-permute-start(bf16[64,1536]{1,0:T(8,128)(2,1)S(1)} %get-tuple-element.61), channel_id=1, source_target_pairs={{0,8},{1,9},{2,10},{3,11},{4,12},{5,13},{6,14},{7,15},{8,0},{9,1},... | collective-permute-start | bytes 589832 | tf_op jit(solution)/shard_map/ppermute | solution.py:33
  96.1 8.7 %collective-permute-start.34 = (bf16[64,1536]{1,0:T(8,128)(2,1)S(1)}, bf16[64,1536]{1,0:T(8,128)(2,1)S(1)}, u32[]{:S(2)}, u32[]{:S(2)}) collective-permute-start(bf16[64,1536]{1,0:T(8,128)(2,1)S(1)} %add_convert_fusion.2), channel_id=1, source_target_pairs={{0,48},{1,49},{2,50},{3,51},{4,52},{5,53},{6,54},{7,55},{8,200},{9... | collective-permute-start | bytes 589832 | tf_op jit(solution)/shard_map/ppermute | solution.py:33
  98.6 7.3 %collective-permute-start.36 = (bf16[64,1536]{1,0:T(8,128)(2,1)S(1)}, bf16[64,1536]{1,0:T(8,128)(2,1)S(1)}, u32[]{:S(2)}, u32[]{:S(2)}) collective-permute-start(bf16[64,1536]{1,0:T(8,128)(2,1)S(1)} %add_convert_fusion.1), channel_id=1, source_target_pairs={{0,32},{1,33},{2,34},{3,35},{4,36},{5,37},{6,38},{7,39},{8,136},{9... | collective-permute-start | bytes 589832 | tf_op jit(solution)/shard_map/ppermute | solution.py:33
  99.5 6.7 %collective-permute-start.38 = (bf16[64,1536]{1,0:T(8,128)(2,1)S(1)}, bf16[64,1536]{1,0:T(8,128)(2,1)S(1)}, u32[]{:S(2)}, u32[]{:S(2)}) collective-permute-start(bf16[64,1536]{1,0:T(8,128)(2,1)S(1)} %add_convert_fusion), channel_id=1, source_target_pairs={{0,16},{1,17},{2,18},{3,19},{4,20},{5,21},{6,22},{7,23},{8,72},{9,... | collective-permute-start | bytes 589832 | tf_op jit(solution)/shard_map/ppermute | solution.py:33
  106.4 5.5 %collective-permute-start.39 = (bf16[16,1536]{1,0:T(8,128)(2,1)S(1)}, bf16[16,1536]{1,0:T(8,128)(2,1)S(1)}, u32[]{:S(2)}, u32[]{:S(2)}) collective-permute-start(bf16[16,1536]{1,0:T(8,128)(2,1)S(1)} %get-tuple-element.67), channel_id=1, source_target_pairs={{0,192},{1,193},{2,194},{3,195},{4,196},{5,197},{6,198},{7,199},{8... | collective-permute-start | bytes 147464 | tf_op jit(solution)/shard_map/ppermute | solution.py:33
  107.1 6.0 %collective-permute-start.41 = (bf16[16,1536]{1,0:T(8,128)(2,1)S(1)}, bf16[16,1536]{1,0:T(8,128)(2,1)S(1)}, u32[]{:S(2)}, u32[]{:S(2)}) collective-permute-start(bf16[16,1536]{1,0:T(8,128)(2,1)S(1)} %get-tuple-element.68), channel_id=1, source_target_pairs={{0,128},{1,129},{2,130},{3,131},{4,132},{5,133},{6,134},{7,135},{8... | collective-permute-start | bytes 147464 | tf_op jit(solution)/shard_map/ppermute | solution.py:33
  111.1 4.1 %collective-permute-start.40 = (bf16[16,1536]{1,0:T(8,128)(2,1)S(1)}, bf16[16,1536]{1,0:T(8,128)(2,1)S(1)}, u32[]{:S(2)}, u32[]{:S(2)}) collective-permute-start(bf16[16,1536]{1,0:T(8,128)(2,1)S(1)} %get-tuple-element.69), channel_id=1, source_target_pairs={{0,64},{1,65},{2,66},{3,67},{4,68},{5,69},{6,70},{7,71},{8,24},{9,... | collective-permute-start | bytes 147464 | tf_op jit(solution)/shard_map/ppermute | solution.py:33

commit v9 on v8

--- a/solution.py
+++ b/solution.py
@@ -13,7 +13,6 @@
 TOKENS_OWN = 16
 TOKENS_Z = 64
 TOKENS = 512
-HALF = TOKENS // 2
 
 
 def pairs_of(target):
@@ -135,7 +134,6 @@
 
 SUM_CUT = (1, 0, 0, 1, 0, 1, 1, 0)
 FIRST, REST = (4, 8), (0, 4)
-GATHER_CUT = (1, 0, 0, 1, 0, 1, 1, 0)
 
 
 def z_rows(start, stop):
@@ -185,46 +183,37 @@
     return lax.dot_general(rows, weight, (((1,), (1,)), ((), ())), preferred_element_type=F32)
 
 
-def fill(rows_ref, blocks):
-    half = rows_ref.shape[1] // 2
-    for k, block in enumerate(blocks):
-        rows = slice(k * TOKENS_Z, (k + 1) * TOKENS_Z)
-        if len(block) == 2:
-            rows_ref[rows, :half] = block[0][...]
-            rows_ref[rows, half:] = block[1][...]
-        else:
-            rows_ref[rows, :] = block[0][...]
-
-
-def near_back_kernel(*refs):
-    *pieces, w_ref, out_ref, rows_ref = refs
-    fill(rows_ref, halves_of(GATHER_CUT[:4], pieces))
-    rows = rows_ref[...]
+def some_back_kernel(*refs):
+    *pieces, w_ref, out_ref = refs
+    rows = jnp.concatenate([piece[...] for piece in pieces], axis=0)
     for start in range(0, w_ref.shape[0], TILE):
         part = slice(start, start + TILE)
         out_ref[:, part] = transposed_dot(rows, w_ref[part, :]).astype(out_ref.dtype)
 
 
-def near_back(pieces, weight):
-    return pl.pallas_call(
-        near_back_kernel,
+def some_back(pieces, weight):
+    return pl.pallas_call(
+        some_back_kernel,
         in_specs=[WHOLE] * (len(pieces) + 1),
         out_specs=WHOLE,
-        out_shape=jax.ShapeDtypeStruct((HALF, weight.shape[0]), BF16),
-        scratch_shapes=[pltpu.VMEM((HALF, weight.shape[1]), BF16)],
+        out_shape=jax.ShapeDtypeStruct((len(pieces) * TOKENS_Z, weight.shape[0]), BF16),
         **settings(weight, 16),
     )(*pieces, weight)
 
 
-def far_back_kernel(*refs):
-    *pieces, near_ref, w_ref, slopes_ref = refs[:-9]
-    outs, product = refs[-9:-1], refs[-1]
-    fill(slopes_ref, halves_of(GATHER_CUT, pieces))
-    product[:HALF, :] = near_ref[...].astype(F32)
-    rows = slopes_ref[HALF:, :]
+def last_back_kernel(*refs):
+    pieces, (own_ref, near_ref, w_ref, slopes_ref), outs, product = (
+        refs[:8], refs[8:12], refs[12:20], refs[20]
+    )
+    for k, piece in enumerate(pieces):
+        slopes_ref[z_rows(k, k + 1), :] = piece[...]
+    product[z_rows(0, 1), :] = near_ref[z_rows(0, 1), :].astype(F32)
+    product[z_rows(1, 2), :] = own_ref[...].astype(F32)
+    product[z_rows(2, 4), :] = near_ref[z_rows(1, 3), :].astype(F32)
+    rows = slopes_ref[z_rows(4, 8), :]
     for start in range(0, w_ref.shape[0], TILE):
         part = slice(start, start + TILE)
-        product[HALF:, part] = transposed_dot(rows, w_ref[part, :])
+        product[z_rows(4, 8), part] = transposed_dot(rows, w_ref[part, :])
     for core_shift in (1, 0):
         for i in range(4):
             for p in range(4):
@@ -233,17 +222,17 @@
                 ].astype(BF16)
 
 
-def far_back(pieces, near, weight):
+def last_back(pieces, own, near, weight):
     depth, width = weight.shape
     return pl.pallas_call(
-        far_back_kernel,
-        in_specs=[WHOLE] * (len(pieces) + 2),
+        last_back_kernel,
+        in_specs=[WHOLE] * 11,
         out_specs=[WHOLE] * 9,
         out_shape=[jax.ShapeDtypeStruct((TOKENS, width), BF16)]
         + [jax.ShapeDtypeStruct((TOKENS_Z, depth), BF16)] * 8,
         scratch_shapes=[pltpu.VMEM((TOKENS, depth), F32)],
         **settings(weight, 16),
-    )(*pieces, near, weight)
+    )(*pieces, own, near, weight)
 
 
 def gelu_tanh(value):
@@ -306,18 +295,15 @@
     pre = add(own[0], jnp.concatenate(longer, axis=1), shorter)
     slopes = jax.vjp(gelu_tanh, pre)[1](d_act.astype(F32))[0].astype(BF16)
 
-    half = weight.shape[1] // 2
-    slopes, *cut = lax.optimization_barrier((slopes, slopes[:, :half], slopes[:, half:]))
-    longer = [gather_chain(part, -1, 4) for part in cut]
-    block_7, block_2, block_5, block_4 = ([chain[i] for chain in longer] for i in range(4))
-    block_1, block_6, block_3 = ([v] for v in gather_chain(slopes, 1, 3))
-    nearest = block_7 + [slopes] + block_1 + block_2
-    pieces = nearest + block_3 + block_4 + block_5 + block_6
-    pre, _ = lax.optimization_barrier((pre, block_4[0]))
+    block_1, block_6, block_3, block_4 = gather_chain(slopes, 1, 4)
+    pre, _ = lax.optimization_barrier((pre, slopes))
     activated = gelu_tanh(pre).astype(BF16)
-
-    near = near_back(nearest, weight)
-    slopes_all, *parts = far_back(pieces, near, weight)
+    own_back = some_back([slopes], weight)
+    later, _, _ = lax.optimization_barrier((slopes, activated, own_back))
+    block_7, block_2, block_5 = gather_chain(later, -1, 3)
+    near = some_back([block_7, block_1, block_2], weight)
+    pieces = [block_7, slopes, block_1, block_2, block_3, block_4, block_5, block_6]
+    slopes_all, *parts = last_back(pieces, own_back, near, weight)
     d_weight = lax.dot_general(
         gathered, slopes_all, (((0,), (0,)), ((), ())), preferred_element_type=F32
     ).astype(BF16)

time: 116 us -> 116 us (level)
  waiting for transfers between devices: 37.8 us -> 35.7 us
  Pallas kernels: 8.75 us -> 10.5 us
    ppermute x42 -> x38, waiting for transfers between devices: 37.8 us -> 35.7 us  [send(): return lax.ppermute(value, ('row', 'col'), pairs_of(target))]
    pallas_call x2 -> x3, Pallas kernels: 3.32 us -> 5.1 us  [the longest x2 3.2 us: some_back(): pl.pallas_call(some_back_kernel, in_specs=[WHOLE] * (len(pieces) + 1), ou...]
    ppermute x42 -> x38, starting transfers between devices: 42.6 us -> 43 us  [send(): return lax.ppermute(value, ('row', 'col'), pairs_of(target))]
  transfers between devices with their start and end apart: 42 -> 38, of which waited for: 27 -> 27; matrix products, arithmetic and copies ran while one was open for 5% -> 5% of each run, Pallas kernels for 4% -> 6%
where the time goes in v9:
time: 116 us
  starting transfers between devices  43 us (37%)
  waiting for transfers between devices  35.7 us (31%)
  blocking collectives  16 us (14%)
  Pallas kernels  10.5 us (9%)
  other arithmetic  5.55 us (5%)
  matrix products  4.27 us (4%)
    ppermute x38, starting transfers between devices, send(): return lax.ppermute(value, ('row', 'col'), pairs_of(target))  43 us
    ppermute x38, waiting for transfers between devices, send(): return lax.ppermute(value, ('row', 'col'), pairs_of(target))  35.7 us
    all_to_all x1, blocking collectives, normalize(): lax.all_to_all(jnp.broadcast_to(stats[None], (NZ,) + stats.shape), 'col',...  16 us
    dot_general x1, matrix products, per_device(): lax.dot_general(gathered, slopes_all, (((0,), (0,)), ((), ())), preferred...  4.27 us
    pallas_call x2, Pallas kernels, some_back(): pl.pallas_call(some_back_kernel, in_specs=[WHOLE] * (len(pieces) + 1), ou...  3.2 us
    pallas_call x1, Pallas kernels, stage(): pl.pallas_call(stage_kernel, in_specs=[pl.BlockSpec(memory_space=pl.ANY)]...  2.34 us
  transfers between devices with their start and end apart: 38, of which 27 were waited for; matrix products, arithmetic and copies ran while one was open for 5% of the time, Pallas kernels for 6%

profile of v9, /device:TPU:2, one launch (start us, length us, event | category | flops | bytes accessed | tf_op | source)
XLA Modules:
  0.0 115.9 jit_solution(4822861695824704608)
XLA Ops:
  0.6 1.0 reduce_sum.45
  1.7 1.1 multiply_reduce_fusion
  2.8 16.0 %all_to_all.5 = f32[8,2,16]{2,1,0:T(2,128)S(1)} all-to-all(f32[8,2,16]{2,1,0:T(2,128)S(1)} %broadcast_in_dim.2), channel_id=1, replica_groups=mesh['row'=32,'col'=8] {'col'}, dimensions={0} | all-to-all | bytes 2048 | tf_op jit(solution)/shard_map/all_to_all | solution.py:255
  18.8 1.0 add_convert_fusion.12
  19.8 2.2 %collective-permute-start.2 = (bf16[16,1536]{1,0:T(8,128)(2,1)S(1)}, bf16[16,1536]{1,0:T(8,128)(2,1)S(1)}, u32[]{:S(2)}, u32[]{:S(2)}) collective-permute-start(bf16[16,1536]{1,0:T(8,128)(2,1)S(1)} %add_convert_fusion.12), channel_id=1, source_target_pairs={{0,128},{1,129},{2,130},{3,131},{4,132},{5,133},{6,134},{7,135},{8... | collective-permute-start | bytes 147464 | tf_op jit(solution)/shard_map/ppermute | solution.py:32
  22.1 2.6 %collective-permute-start = (bf16[16,1536]{1,0:T(8,128)(2,1)S(1)}, bf16[16,1536]{1,0:T(8,128)(2,1)S(1)}, u32[]{:S(2)}, u32[]{:S(2)}) collective-permute-start(bf16[16,1536]{1,0:T(8,128)(2,1)S(1)} %add_convert_fusion.12), channel_id=1, source_target_pairs={{0,64},{1,65},{2,66},{3,67},{4,68},{5,69},{6,70},{7,71},{8,72},{9,... | collective-permute-start | bytes 147464 | tf_op jit(solution)/shard_map/ppermute | solution.py:32
  24.6 0.9 collective-permute-done.2
  25.5 0.6 collective-permute-done.1
  26.2 0.6 collective-permute-done
  26.7 3.1 %collective-permute-start.5 = (bf16[64,1536]{1,0:T(8,128)(2,1)S(1)}, bf16[64,1536]{1,0:T(8,128)(2,1)S(1)}, u32[]{:S(2)}, u32[]{:S(2)}) collective-permute-start(bf16[64,1536]{1,0:T(8,128)(2,1)S(1)} %pad_maximum_fusion.refs_0_), channel_id=1, source_target_pairs={{0,48},{1,49},{2,50},{3,51},{4,52},{5,53},{6,54},{7,55},{8,56},{9,... | collective-permute-start | bytes 589832 | tf_op jit(solution)/shard_map/ppermute | solution.py:32
  29.8 0.6 collective-permute-start.4
  30.5 0.5 collective-permute-start.3
  30.9 2.3 %shard_map.76.refs_8_.w_ref.refs_1_.refs_3_.refs_10_ = bf16[1536,1536]{1,0:T(8,128)(2,1)S(1)} custom-call(bf16[1536,1536]{1,0:T(8,128)(2,1)} %w_ref), custom_call_target="tpu_custom_call" | custom-call | flops 1207959552 | bytes 4718592 | tf_op jit(solution)/shard_map/pallas_call | solution.py:99
  33.3 2.1 %collective-permute-done.5.refs_3_ = bf16[64,1536]{1,0:T(8,128)(2,1)S(1)} collective-permute-done((bf16[64,1536]{1,0:T(8,128)(2,1)S(1)}, bf16[64,1536]{1,0:T(8,128)(2,1)S(1)}, u32[]{:S(2)}, u32[]{:S(2)}) %collective-permute-start.5) | collective-permute-done | bytes 196640 | tf_op jit(solution)/shard_map/ppermute | solution.py:32
  35.3 1.7 %collective-permute-done.4.refs_2_ = bf16[64,1536]{1,0:T(8,128)(2,1)S(1)} collective-permute-done((bf16[64,1536]{1,0:T(8,128)(2,1)S(1)}, bf16[64,1536]{1,0:T(8,128)(2,1)S(1)}, u32[]{:S(2)}, u32[]{:S(2)}) %collective-permute-start.4) | collective-permute-done | bytes 196640 | tf_op jit(solution)/shard_map/ppermute | solution.py:32
  37.0 0.5 collective-permute-start.7
  37.5 0.9 collective-permute-done.8.refs_6_
  39.0 1.7 %shard_map.77 = (bf16[512,1536]{1,0:T(8,128)(2,1)S(1)}, bf16[64,1536]{1,0:T(8,128)(2,1)S(1)}, bf16[64,768]{1,0:T(8,128)(2,1)S(1)}, bf16[64,768]{1,0:T(8,128)(2,1...) custom-call(bf16[64,1536]{1,0:T(8,128)(2,1)S(1)} %pad_maximum_fusion.refs_0_, ...), custom_call_target="tpu_custom_call" | custom-call | flops 1207959552 | bytes 4718592 | tf_op jit(solution)/shard_map/pallas_call | solution.py:162
  40.7 0.7 collective-permute-start.10
  41.4 1.4 %collective-permute-start.14 = (bf16[64,768]{1,0:T(8,128)(2,1)S(1)}, bf16[64,768]{1,0:T(8,128)(2,1)S(1)}, u32[]{:S(2)}, u32[]{:S(2)}) collective-permute-start(bf16[64,768]{1,0:T(8,128)(2,1)S(1)} %get-tuple-element.44), channel_id=1, source_target_pairs={{0,1},{1,0},{2,3},{3,2},{4,5},{5,4},{6,7},{7,6},{8,15},{9,10},{10,... | collective-permute-start | bytes 294920 | tf_op jit(solution)/shard_map/ppermute | solution.py:32
  42.8 0.6 collective-permute-start.18
  43.4 1.4 %shard_map.78 = (bf16[64,768]{1,0:T(8,128)(2,1)S(1)}, bf16[64,768]{1,0:T(8,128)(2,1)S(1)}, bf16[64,1536]{1,0:T(8,128)(2,1)S(1)}, bf16[64,1536]{1,0:T(8,128)(2,1)...) custom-call(bf16[512,1536]{1,0:T(8,128)(2,1)S(1)} %get-tuple-element.35.normed_ref, ...), custom_call_target="tpu_custom_call" | custom-call | flops 1207959552 | bytes 4718592 | tf_op jit(solution)/shard_map/pallas_call | solution.py:173
  44.8 0.6 collective-permute-done.10
  45.5 0.8 collective-permute-start.11
  46.5 2.4 %collective-permute-start.15 = (bf16[64,768]{1,0:T(8,128)(2,1)S(1)}, bf16[64,768]{1,0:T(8,128)(2,1)S(1)}, u32[]{:S(2)}, u32[]{:S(2)}) collective-permute-start(bf16[64,768]{1,0:T(8,128)(2,1)S(1)} %add_convert_fusion.7), channel_id=1, source_target_pairs={{0,7},{1,2},{2,1},{3,4},{4,3},{5,6},{6,5},{7,0},{8,9},{9,8},{10,11... | collective-permute-start | bytes 294920 | tf_op jit(solution)/shard_map/ppermute | solution.py:32
  49.0 1.0 collective-permute-start.19
  50.0 1.4 %collective-permute-done.11 = bf16[64,768]{1,0:T(8,128)(2,1)S(1)} collective-permute-done((bf16[64,768]{1,0:T(8,128)(2,1)S(1)}, bf16[64,768]{1,0:T(8,128)(2,1)S(1)}, u32[]{:S(2)}, u32[]{:S(2)}) %collective-permute-start.11) | collective-permute-done | bytes 98336 | tf_op jit(solution)/shard_map/ppermute | solution.py:32
  51.5 0.9 collective-permute-done.15
  52.5 1.4 %collective-permute-start.16 = (bf16[64,768]{1,0:T(8,128)(2,1)S(1)}, bf16[64,768]{1,0:T(8,128)(2,1)S(1)}, u32[]{:S(2)}, u32[]{:S(2)}) collective-permute-start(bf16[64,768]{1,0:T(8,128)(2,1)S(1)} %add_convert_fusion.6), channel_id=1, source_target_pairs={{0,1},{1,0},{2,3},{3,2},{4,5},{5,4},{6,7},{7,6},{8,15},{9,10},{10,... | collective-permute-start | bytes 294920 | tf_op jit(solution)/shard_map/ppermute | solution.py:32
  53.8 2.3 %collective-permute-done.12 = bf16[64,768]{1,0:T(8,128)(2,1)S(1)} collective-permute-done((bf16[64,768]{1,0:T(8,128)(2,1)S(1)}, bf16[64,768]{1,0:T(8,128)(2,1)S(1)}, u32[]{:S(2)}, u32[]{:S(2)}) %collective-permute-start.12) | collective-permute-done | bytes 98336 | tf_op jit(solution)/shard_map/ppermute | solution.py:32
  56.1 1.0 collective-permute-start.13
  57.5 0.9 collective-permute-start.20
  58.4 1.4 %collective-permute-start.17 = (bf16[64,768]{1,0:T(8,128)(2,1)S(1)}, bf16[64,768]{1,0:T(8,128)(2,1)S(1)}, u32[]{:S(2)}, u32[]{:S(2)}) collective-permute-start(bf16[64,768]{1,0:T(8,128)(2,1)S(1)} %add_convert_fusion.5), channel_id=1, source_target_pairs={{0,7},{1,2},{2,1},{3,4},{4,3},{5,6},{6,5},{7,0},{8,9},{9,8},{10,11... | collective-permute-start | bytes 294920 | tf_op jit(solution)/shard_map/ppermute | solution.py:32
  59.8 3.3 %collective-permute-done.13 = bf16[64,768]{1,0:T(8,128)(2,1)S(1)} collective-permute-done((bf16[64,768]{1,0:T(8,128)(2,1)S(1)}, bf16[64,768]{1,0:T(8,128)(2,1)S(1)}, u32[]{:S(2)}, u32[]{:S(2)}) %collective-permute-start.13) | collective-permute-done | bytes 98336 | tf_op jit(solution)/shard_map/ppermute | solution.py:32
  63.1 1.2 %collective-permute-done.17 = bf16[64,768]{1,0:T(8,128)(2,1)S(1)} collective-permute-done((bf16[64,768]{1,0:T(8,128)(2,1)S(1)}, bf16[64,768]{1,0:T(8,128)(2,1)S(1)}, u32[]{:S(2)}, u32[]{:S(2)}) %collective-permute-start.17) | collective-permute-done | bytes 98336 | tf_op jit(solution)/shard_map/ppermute | solution.py:32
  64.3 0.3 fusion.2
  64.8 0.8 fusion.17
  65.6 1.5 %shard_map.79.refs_8_ = bf16[64,1536]{1,0:T(8,128)(2,1)S(1)} custom-call(bf16[64,1536]{1,0:T(8,128)(2,1)S(1)} %get-tuple-element.49.refs_0_.refs_1_, bf16[1536,1536]{1,0:T(8,128)(2,1)S(1)} %shard_map.76.refs_8_.w_ref.refs_1_.refs_3_.refs_10_), custom_call_target="tpu_custom_call" | custom-call | flops 1207959552 | bytes 4718592 | tf_op jit(solution)/shard_map/pallas_call | solution.py:195
  67.1 2.1 %collective-permute-start.21 = (bf16[64,1536]{1,0:T(8,128)(2,1)S(1)}, bf16[64,1536]{1,0:T(8,128)(2,1)S(1)}, u32[]{:S(2)}, u32[]{:S(2)}) collective-permute-start(bf16[64,1536]{1,0:T(8,128)(2,1)S(1)} %get-tuple-element.49.refs_0_.refs_1_), channel_id=1, source_target_pairs={{0,7},{1,2},{2,1},{3,4},{4,3},{5,6},{6,5},{7,0},{8,9},{9,8},{10,11... | collective-permute-start | bytes 589832 | tf_op jit(solution)/shard_map/ppermute | solution.py:32
  69.2 1.2 %collective-permute-done.22.refs_1_.refs_2_ = bf16[64,1536]{1,0:T(8,128)(2,1)S(1)} collective-permute-done((bf16[64,1536]{1,0:T(8,128)(2,1)S(1)}, bf16[64,1536]{1,0:T(8,128)(2,1)S(1)}, u32[]{:S(2)}, u32[]{:S(2)}) %collective-permute-start.22) | collective-permute-done | bytes 196640 | tf_op jit(solution)/shard_map/ppermute | solution.py:32
  70.4 2.3 %collective-permute-start.24 = (bf16[64,1536]{1,0:T(8,128)(2,1)S(1)}, bf16[64,1536]{1,0:T(8,128)(2,1)S(1)}, u32[]{:S(2)}, u32[]{:S(2)}) collective-permute-start(bf16[64,1536]{1,0:T(8,128)(2,1)S(1)} %collective-permute-done.22.refs_1_.refs_2_), channel_id=1, source_target_pairs={{0,7},{1,2},{2,1},{3,4},{4,3},{5,6},{6,5},{7,0},{8,9},{9,8},{10,11... | collective-permute-start | bytes 589832 | tf_op jit(solution)/shard_map/ppermute | solution.py:32
  72.8 1.3 %collective-permute-done.21.refs_0_ = bf16[64,1536]{1,0:T(8,128)(2,1)S(1)} collective-permute-done((bf16[64,1536]{1,0:T(8,128)(2,1)S(1)}, bf16[64,1536]{1,0:T(8,128)(2,1)S(1)}, u32[]{:S(2)}, u32[]{:S(2)}) %collective-permute-start.21) | collective-permute-done | bytes 196640 | tf_op jit(solution)/shard_map/ppermute | solution.py:32
  74.1 0.8 collective-permute-start.23
  74.9 2.8 %collective-permute-done.24.refs_7_ = bf16[64,1536]{1,0:T(8,128)(2,1)S(1)} collective-permute-done((bf16[64,1536]{1,0:T(8,128)(2,1)S(1)}, bf16[64,1536]{1,0:T(8,128)(2,1)S(1)}, u32[]{:S(2)}, u32[]{:S(2)}) %collective-permute-start.24) | collective-permute-done | bytes 196640 | tf_op jit(solution)/shard_map/ppermute | solution.py:32
  78.0 1.8 %collective-permute-done.23.refs_2_.refs_3_ = bf16[64,1536]{1,0:T(8,128)(2,1)S(1)} collective-permute-done((bf16[64,1536]{1,0:T(8,128)(2,1)S(1)}, bf16[64,1536]{1,0:T(8,128)(2,1)S(1)}, u32[]{:S(2)}, u32[]{:S(2)}) %collective-permute-start.23) | collective-permute-done | bytes 196640 | tf_op jit(solution)/shard_map/ppermute | solution.py:32
  79.7 2.0 %collective-permute-start.27 = (bf16[64,1536]{1,0:T(8,128)(2,1)S(1)}, bf16[64,1536]{1,0:T(8,128)(2,1)S(1)}, u32[]{:S(2)}, u32[]{:S(2)}) collective-permute-start(bf16[64,1536]{1,0:T(8,128)(2,1)S(1)} %collective-permute-done.23.refs_2_.refs_3_), channel_id=1, source_target_pairs={{0,7},{1,2},{2,1},{3,4},{4,3},{5,6},{6,5},{7,0},{8,9},{9,8},{10,11... | collective-permute-start | bytes 589832 | tf_op jit(solution)/shard_map/ppermute | solution.py:32
  81.8 3.2 %collective-permute-done.25.refs_4_ = bf16[64,1536]{1,0:T(8,128)(2,1)S(1)} collective-permute-done((bf16[64,1536]{1,0:T(8,128)(2,1)S(1)}, bf16[64,1536]{1,0:T(8,128)(2,1)S(1)}, u32[]{:S(2)}, u32[]{:S(2)}) %collective-permute-start.25) | collective-permute-done | bytes 196640 | tf_op jit(solution)/shard_map/ppermute | solution.py:32
  85.0 3.8 %collective-permute-start.26 = (bf16[64,1536]{1,0:T(8,128)(2,1)S(1)}, bf16[64,1536]{1,0:T(8,128)(2,1)S(1)}, u32[]{:S(2)}, u32[]{:S(2)}) collective-permute-start(bf16[64,1536]{1,0:T(8,128)(2,1)S(1)} %collective-permute-done.25.refs_4_), channel_id=1, source_target_pairs={{0,7},{1,2},{2,1},{3,4},{4,3},{5,6},{6,5},{7,0},{8,9},{9,8},{10,11... | collective-permute-start | bytes 589832 | tf_op jit(solution)/shard_map/ppermute | solution.py:32
  88.8 1.7 %shard_map.80.refs_9_ = bf16[192,1536]{1,0:T(8,128)(2,1)S(1)} custom-call(bf16[64,1536]{1,0:T(8,128)(2,1)S(1)} %collective-permute-done.21.refs_0_, bf16[64,1536]{1,0:T(8,128)(2,1)S(1)} %collective-permute-done.22.refs_1_.refs_2_, bf16[64,1536]{1,0:T(8,128)(2,1)S(1)} %collective-permute-done.23.refs_2_.refs_3_, ...), custom_call_target="tpu_custom_call" | custom-call | flops 1207959552 | bytes 4718592 | tf_op jit(solution)/shard_map/pallas_call | solution.py:195
  90.5 2.0 %collective-permute-done.26.refs_5_ = bf16[64,1536]{1,0:T(8,128)(2,1)S(1)} collective-permute-done((bf16[64,1536]{1,0:T(8,128)(2,1)S(1)}, bf16[64,1536]{1,0:T(8,128)(2,1)S(1)}, u32[]{:S(2)}, u32[]{:S(2)}) %collective-permute-start.26) | collective-permute-done | bytes 196640 | tf_op jit(solution)/shard_map/ppermute | solution.py:32
  92.5 1.9 %shard_map.81 = (bf16[512,1536]{1,0:T(8,128)(2,1)S(1)}, bf16[64,1536]{1,0:T(8,128)(2,1)S(1)}, bf16[64,1536]{1,0:T(8,128)(2,1)S(1)}, bf16[64,1536]{1,0:T(8,128)(2...) custom-call(bf16[64,1536]{1,0:T(8,128)(2,1)S(1)} %collective-permute, ...), custom_call_target="tpu_custom_call" | custom-call | flops 1207959552 | bytes 4718592 | tf_op jit(solution)/shard_map/pallas_call | solution.py:227
  94.5 0.5 collective-permute-start.28
  95.1 0.4 collective-permute-start.33
  95.5 0.4 collective-permute-done.29
  95.9 2.7 %collective-permute-start.30 = (bf16[64,1536]{1,0:T(8,128)(2,1)S(1)}, bf16[64,1536]{1,0:T(8,128)(2,1)S(1)}, u32[]{:S(2)}, u32[]{:S(2)}) collective-permute-start(bf16[64,1536]{1,0:T(8,128)(2,1)S(1)} %add_convert_fusion.2), channel_id=1, source_target_pairs={{0,48},{1,49},{2,50},{3,51},{4,52},{5,53},{6,54},{7,55},{8,200},{9... | collective-permute-start | bytes 589832 | tf_op jit(solution)/shard_map/ppermute | solution.py:32
  98.7 0.8 collective-permute-start.32
  99.5 1.1 collective-permute-start.34
  100.6 4.3 %convolution_convert_fusion = bf16[1536,1536]{1,0:T(8,128)(2,1)} fusion(bf16[512,1536]{1,0:T(8,128)(2,1)S(1)} %get-tuple-element.35.normed_ref, bf16[512,1536]{1,0:T(8,128)(2,1)S(1)} %get-tuple-element.58), kind=kOutput, calls=%fused_computation | convolution fusion | flops 2418278400 | bytes 7864320 | tf_op jit(solution)/shard_map/dot_general | solution.py:307
  104.9 1.1 collective-permute-done.32
  106.5 2.5 %collective-permute-start.35 = (bf16[16,1536]{1,0:T(8,128)(2,1)S(1)}, bf16[16,1536]{1,0:T(8,128)(2,1)S(1)}, u32[]{:S(2)}, u32[]{:S(2)}) collective-permute-start(bf16[16,1536]{1,0:T(8,128)(2,1)S(1)} %get-tuple-element.63), channel_id=1, source_target_pairs={{0,192},{1,193},{2,194},{3,195},{4,196},{5,197},{6,198},{7,199},{8... | collective-permute-start | bytes 147464 | tf_op jit(solution)/shard_map/ppermute | solution.py:32
  108.9 2.3 %collective-permute-start.37 = (bf16[16,1536]{1,0:T(8,128)(2,1)S(1)}, bf16[16,1536]{1,0:T(8,128)(2,1)S(1)}, u32[]{:S(2)}, u32[]{:S(2)}) collective-permute-start(bf16[16,1536]{1,0:T(8,128)(2,1)S(1)} %get-tuple-element.64), channel_id=1, source_target_pairs={{0,128},{1,129},{2,130},{3,131},{4,132},{5,133},{6,134},{7,135},{8... | collective-permute-start | bytes 147464 | tf_op jit(solution)/shard_map/ppermute | solution.py:32
  111.2 3.3 %collective-permute-done.37 = bf16[16,1536]{1,0:T(8,128)(2,1)S(1)} collective-permute-done((bf16[16,1536]{1,0:T(8,128)(2,1)S(1)}, bf16[16,1536]{1,0:T(8,128)(2,1)S(1)}, u32[]{:S(2)}, u32[]{:S(2)}) %collective-permute-start.37) | collective-permute-done | bytes 49184 | tf_op jit(solution)/shard_map/ppermute | solution.py:32
  114.5 0.8 collective-permute-done.36
  115.3 0.6 add_convert_fusion.11
  (51 shorter events, 2.7 us)
Async XLA Ops:
  19.8 5.7 %collective-permute-start.2 = (bf16[16,1536]{1,0:T(8,128)(2,1)S(1)}, bf16[16,1536]{1,0:T(8,128)(2,1)S(1)}, u32[]{:S(2)}, u32[]{:S(2)}) collective-permute-start(bf16[16,1536]{1,0:T(8,128)(2,1)S(1)} %add_convert_fusion.12), channel_id=1, source_target_pairs={{0,128},{1,129},{2,130},{3,131},{4,132},{5,133},{6,134},{7,135},{8... | collective-permute-start | bytes 147464 | tf_op jit(solution)/shard_map/ppermute | solution.py:32
  22.1 4.1 %collective-permute-start.1 = (bf16[16,1536]{1,0:T(8,128)(2,1)S(1)}, bf16[16,1536]{1,0:T(8,128)(2,1)S(1)}, u32[]{:S(2)}, u32[]{:S(2)}) collective-permute-start(bf16[16,1536]{1,0:T(8,128)(2,1)S(1)} %add_convert_fusion.12), channel_id=1, source_target_pairs={{0,192},{1,193},{2,194},{3,195},{4,196},{5,197},{6,198},{7,199},{8... | collective-permute-start | bytes 147464 | tf_op jit(solution)/shard_map/ppermute | solution.py:32
  22.1 4.6 %collective-permute-start = (bf16[16,1536]{1,0:T(8,128)(2,1)S(1)}, bf16[16,1536]{1,0:T(8,128)(2,1)S(1)}, u32[]{:S(2)}, u32[]{:S(2)}) collective-permute-start(bf16[16,1536]{1,0:T(8,128)(2,1)S(1)} %add_convert_fusion.12), channel_id=1, source_target_pairs={{0,64},{1,65},{2,66},{3,67},{4,68},{5,69},{6,70},{7,71},{8,72},{9,... | collective-permute-start | bytes 147464 | tf_op jit(solution)/shard_map/ppermute | solution.py:32
  26.7 8.6 %collective-permute-start.5 = (bf16[64,1536]{1,0:T(8,128)(2,1)S(1)}, bf16[64,1536]{1,0:T(8,128)(2,1)S(1)}, u32[]{:S(2)}, u32[]{:S(2)}) collective-permute-start(bf16[64,1536]{1,0:T(8,128)(2,1)S(1)} %pad_maximum_fusion.refs_0_), channel_id=1, source_target_pairs={{0,48},{1,49},{2,50},{3,51},{4,52},{5,53},{6,54},{7,55},{8,56},{9,... | collective-permute-start | bytes 589832 | tf_op jit(solution)/shard_map/ppermute | solution.py:32
  29.8 7.2 %collective-permute-start.4 = (bf16[64,1536]{1,0:T(8,128)(2,1)S(1)}, bf16[64,1536]{1,0:T(8,128)(2,1)S(1)}, u32[]{:S(2)}, u32[]{:S(2)}) collective-permute-start(bf16[64,1536]{1,0:T(8,128)(2,1)S(1)} %pad_maximum_fusion.refs_0_), channel_id=1, source_target_pairs={{0,32},{1,33},{2,34},{3,35},{4,36},{5,37},{6,38},{7,39},{8,40},{9,... | collective-permute-start | bytes 589832 | tf_op jit(solution)/shard_map/ppermute | solution.py:32
  30.5 6.6 %collective-permute-start.3 = (bf16[64,1536]{1,0:T(8,128)(2,1)S(1)}, bf16[64,1536]{1,0:T(8,128)(2,1)S(1)}, u32[]{:S(2)}, u32[]{:S(2)}) collective-permute-start(bf16[64,1536]{1,0:T(8,128)(2,1)S(1)} %pad_maximum_fusion.refs_0_), channel_id=1, source_target_pairs={{0,16},{1,17},{2,18},{3,19},{4,20},{5,21},{6,22},{7,23},{8,24},{9,... | collective-permute-start | bytes 589832 | tf_op jit(solution)/shard_map/ppermute | solution.py:32
  30.9 6.6 %collective-permute-start.6 = (bf16[64,1536]{1,0:T(8,128)(2,1)S(1)}, bf16[64,1536]{1,0:T(8,128)(2,1)S(1)}, u32[]{:S(2)}, u32[]{:S(2)}) collective-permute-start(bf16[64,1536]{1,0:T(8,128)(2,1)S(1)} %pad_maximum_fusion.refs_0_), channel_id=1, source_target_pairs={{0,8},{1,9},{2,10},{3,11},{4,12},{5,13},{6,14},{7,15},{8,0},{9,1},... | collective-permute-start | bytes 589832 | tf_op jit(solution)/shard_map/ppermute | solution.py:32
  37.0 1.4 %collective-permute-start.8 = (bf16[64,1536]{1,0:T(8,128)(2,1)S(1)}, bf16[64,1536]{1,0:T(8,128)(2,1)S(1)}, u32[]{:S(2)}, u32[]{:S(2)}) collective-permute-start(bf16[64,1536]{1,0:T(8,128)(2,1)S(1)} %collective-permute-done.4.refs_2_), channel_id=1, source_target_pairs={{0,8},{1,9},{2,10},{3,11},{4,12},{5,13},{6,14},{7,15},{8,0},{9,1},... | collective-permute-start | bytes 589832 | tf_op jit(solution)/shard_map/ppermute | solution.py:32
  37.0 1.7 %collective-permute-start.7 = (bf16[64,1536]{1,0:T(8,128)(2,1)S(1)}, bf16[64,1536]{1,0:T(8,128)(2,1)S(1)}, u32[]{:S(2)}, u32[]{:S(2)}) collective-permute-start(bf16[64,1536]{1,0:T(8,128)(2,1)S(1)} %collective-permute-done.3.refs_1_), channel_id=1, source_target_pairs={{0,8},{1,9},{2,10},{3,11},{4,12},{5,13},{6,14},{7,15},{8,0},{9,1},... | collective-permute-start | bytes 589832 | tf_op jit(solution)/shard_map/ppermute | solution.py:32
  37.5 1.5 %collective-permute-start.9 = (bf16[64,1536]{1,0:T(8,128)(2,1)S(1)}, bf16[64,1536]{1,0:T(8,128)(2,1)S(1)}, u32[]{:S(2)}, u32[]{:S(2)}) collective-permute-start(bf16[64,1536]{1,0:T(8,128)(2,1)S(1)} %collective-permute-done.5.refs_3_), channel_id=1, source_target_pairs={{0,8},{1,9},{2,10},{3,11},{4,12},{5,13},{6,14},{7,15},{8,0},{9,1},... | collective-permute-start | bytes 589832 | tf_op jit(solution)/shard_map/ppermute | solution.py:32
  40.7 4.7 %collective-permute-start.10 = (bf16[64,768]{1,0:T(8,128)(2,1)S(1)}, bf16[64,768]{1,0:T(8,128)(2,1)S(1)}, u32[]{:S(2)}, u32[]{:S(2)}) collective-permute-start(bf16[64,768]{1,0:T(8,128)(2,1)S(1)} %get-tuple-element.40), channel_id=1, source_target_pairs={{0,1},{1,0},{2,3},{3,2},{4,5},{5,4},{6,7},{7,6},{8,15},{9,10},{10,... | collective-permute-start | bytes 294920 | tf_op jit(solution)/shard_map/ppermute | solution.py:32
  41.4 5.1 %collective-permute-start.14 = (bf16[64,768]{1,0:T(8,128)(2,1)S(1)}, bf16[64,768]{1,0:T(8,128)(2,1)S(1)}, u32[]{:S(2)}, u32[]{:S(2)}) collective-permute-start(bf16[64,768]{1,0:T(8,128)(2,1)S(1)} %get-tuple-element.44), channel_id=1, source_target_pairs={{0,1},{1,0},{2,3},{3,2},{4,5},{5,4},{6,7},{7,6},{8,15},{9,10},{10,... | collective-permute-start | bytes 294920 | tf_op jit(solution)/shard_map/ppermute | solution.py:32
  42.8 6.1 %collective-permute-start.18 = (bf16[64,1536]{1,0:T(8,128)(2,1)S(1)}, bf16[64,1536]{1,0:T(8,128)(2,1)S(1)}, u32[]{:S(2)}, u32[]{:S(2)}) collective-permute-start(bf16[64,1536]{1,0:T(8,128)(2,1)S(1)} %get-tuple-element.47), channel_id=1, source_target_pairs={{0,1},{1,0},{2,3},{3,2},{4,5},{5,4},{6,7},{7,6},{8,15},{9,10},{10,... | collective-permute-start | bytes 589832 | tf_op jit(solution)/shard_map/ppermute | solution.py:32
  44.8 19.5 %copy-start = (bf16[64,1536]{1,0:T(8,128)(2,1)S(1)}, bf16[64,1536]{1,0:T(8,128)(2,1)}, u32[]{:S(2)}) copy-start(bf16[64,1536]{1,0:T(8,128)(2,1)} %param.9) | copy-start | bytes 589828
  45.5 5.9 %collective-permute-start.11 = (bf16[64,768]{1,0:T(8,128)(2,1)S(1)}, bf16[64,768]{1,0:T(8,128)(2,1)S(1)}, u32[]{:S(2)}, u32[]{:S(2)}) collective-permute-start(bf16[64,768]{1,0:T(8,128)(2,1)S(1)} %add_convert_fusion.10), channel_id=1, source_target_pairs={{0,7},{1,2},{2,1},{3,4},{4,3},{5,6},{6,5},{7,0},{8,9},{9,8},{10,11... | collective-permute-start | bytes 294920 | tf_op jit(solution)/shard_map/ppermute | solution.py:32
  46.5 5.9 %collective-permute-start.15 = (bf16[64,768]{1,0:T(8,128)(2,1)S(1)}, bf16[64,768]{1,0:T(8,128)(2,1)S(1)}, u32[]{:S(2)}, u32[]{:S(2)}) collective-permute-start(bf16[64,768]{1,0:T(8,128)(2,1)S(1)} %add_convert_fusion.7), channel_id=1, source_target_pairs={{0,7},{1,2},{2,1},{3,4},{4,3},{5,6},{6,5},{7,0},{8,9},{9,8},{10,11... | collective-permute-start | bytes 294920 | tf_op jit(solution)/shard_map/ppermute | solution.py:32
  49.0 8.5 %collective-permute-start.19 = (bf16[64,1536]{1,0:T(8,128)(2,1)S(1)}, bf16[64,1536]{1,0:T(8,128)(2,1)S(1)}, u32[]{:S(2)}, u32[]{:S(2)}) collective-permute-start(bf16[64,1536]{1,0:T(8,128)(2,1)S(1)} %add_convert_fusion.4), channel_id=1, source_target_pairs={{0,7},{1,2},{2,1},{3,4},{4,3},{5,6},{6,5},{7,0},{8,9},{9,8},{10,11... | collective-permute-start | bytes 589832 | tf_op jit(solution)/shard_map/ppermute | solution.py:32
  51.4 4.7 %collective-permute-start.12 = (bf16[64,768]{1,0:T(8,128)(2,1)S(1)}, bf16[64,768]{1,0:T(8,128)(2,1)S(1)}, u32[]{:S(2)}, u32[]{:S(2)}) collective-permute-start(bf16[64,768]{1,0:T(8,128)(2,1)S(1)} %add_convert_fusion.9), channel_id=1, source_target_pairs={{0,1},{1,0},{2,3},{3,2},{4,5},{5,4},{6,7},{7,6},{8,15},{9,10},{10,... | collective-permute-start | bytes 294920 | tf_op jit(solution)/shard_map/ppermute | solution.py:32
  52.5 5.9 %collective-permute-start.16 = (bf16[64,768]{1,0:T(8,128)(2,1)S(1)}, bf16[64,768]{1,0:T(8,128)(2,1)S(1)}, u32[]{:S(2)}, u32[]{:S(2)}) collective-permute-start(bf16[64,768]{1,0:T(8,128)(2,1)S(1)} %add_convert_fusion.6), channel_id=1, source_target_pairs={{0,1},{1,0},{2,3},{3,2},{4,5},{5,4},{6,7},{7,6},{8,15},{9,10},{10,... | collective-permute-start | bytes 294920 | tf_op jit(solution)/shard_map/ppermute | solution.py:32
  56.1 7.0 %collective-permute-start.13 = (bf16[64,768]{1,0:T(8,128)(2,1)S(1)}, bf16[64,768]{1,0:T(8,128)(2,1)S(1)}, u32[]{:S(2)}, u32[]{:S(2)}) collective-permute-start(bf16[64,768]{1,0:T(8,128)(2,1)S(1)} %add_convert_fusion.8), channel_id=1, source_target_pairs={{0,7},{1,2},{2,1},{3,4},{4,3},{5,6},{6,5},{7,0},{8,9},{9,8},{10,11... | collective-permute-start | bytes 294920 | tf_op jit(solution)/shard_map/ppermute | solution.py:32
  57.5 6.8 %collective-permute-start.20 = (bf16[64,1536]{1,0:T(8,128)(2,1)S(1)}, bf16[64,1536]{1,0:T(8,128)(2,1)S(1)}, u32[]{:S(2)}, u32[]{:S(2)}) collective-permute-start(bf16[64,1536]{1,0:T(8,128)(2,1)S(1)} %add_convert_fusion.3), channel_id=1, source_target_pairs={{0,1},{1,0},{2,3},{3,2},{4,5},{5,4},{6,7},{7,6},{8,15},{9,10},{10,... | collective-permute-start | bytes 589832 | tf_op jit(solution)/shard_map/ppermute | solution.py:32
  58.4 5.9 %collective-permute-start.17 = (bf16[64,768]{1,0:T(8,128)(2,1)S(1)}, bf16[64,768]{1,0:T(8,128)(2,1)S(1)}, u32[]{:S(2)}, u32[]{:S(2)}) collective-permute-start(bf16[64,768]{1,0:T(8,128)(2,1)S(1)} %add_convert_fusion.5), channel_id=1, source_target_pairs={{0,7},{1,2},{2,1},{3,4},{4,3},{5,6},{6,5},{7,0},{8,9},{9,8},{10,11... | collective-permute-start | bytes 294920 | tf_op jit(solution)/shard_map/ppermute | solution.py:32
  64.7 5.8 %collective-permute-start.22 = (bf16[64,1536]{1,0:T(8,128)(2,1)S(1)}, bf16[64,1536]{1,0:T(8,128)(2,1)S(1)}, u32[]{:S(2)}, u32[]{:S(2)}) collective-permute-start(bf16[64,1536]{1,0:T(8,128)(2,1)S(1)} %get-tuple-element.49.refs_0_.refs_1_), channel_id=1, source_target_pairs={{0,1},{1,0},{2,3},{3,2},{4,5},{5,4},{6,7},{7,6},{8,15},{9,10},{10,... | collective-permute-start | bytes 589832 | tf_op jit(solution)/shard_map/ppermute | solution.py:32
  67.1 7.0 %collective-permute-start.21 = (bf16[64,1536]{1,0:T(8,128)(2,1)S(1)}, bf16[64,1536]{1,0:T(8,128)(2,1)S(1)}, u32[]{:S(2)}, u32[]{:S(2)}) collective-permute-start(bf16[64,1536]{1,0:T(8,128)(2,1)S(1)} %get-tuple-element.49.refs_0_.refs_1_), channel_id=1, source_target_pairs={{0,7},{1,2},{2,1},{3,4},{4,3},{5,6},{6,5},{7,0},{8,9},{9,8},{10,11... | collective-permute-start | bytes 589832 | tf_op jit(solution)/shard_map/ppermute | solution.py:32
  70.4 7.3 %collective-permute-start.24 = (bf16[64,1536]{1,0:T(8,128)(2,1)S(1)}, bf16[64,1536]{1,0:T(8,128)(2,1)S(1)}, u32[]{:S(2)}, u32[]{:S(2)}) collective-permute-start(bf16[64,1536]{1,0:T(8,128)(2,1)S(1)} %collective-permute-done.22.refs_1_.refs_2_), channel_id=1, source_target_pairs={{0,7},{1,2},{2,1},{3,4},{4,3},{5,6},{6,5},{7,0},{8,9},{9,8},{10,11... | collective-permute-start | bytes 589832 | tf_op jit(solution)/shard_map/ppermute | solution.py:32
  74.1 5.7 %collective-permute-start.23 = (bf16[64,1536]{1,0:T(8,128)(2,1)S(1)}, bf16[64,1536]{1,0:T(8,128)(2,1)S(1)}, u32[]{:S(2)}, u32[]{:S(2)}) collective-permute-start(bf16[64,1536]{1,0:T(8,128)(2,1)S(1)} %collective-permute-done.21.refs_0_), channel_id=1, source_target_pairs={{0,1},{1,0},{2,3},{3,2},{4,5},{5,4},{6,7},{7,6},{8,15},{9,10},{10,... | collective-permute-start | bytes 589832 | tf_op jit(solution)/shard_map/ppermute | solution.py:32
  77.7 7.3 %collective-permute-start.25 = (bf16[64,1536]{1,0:T(8,128)(2,1)S(1)}, bf16[64,1536]{1,0:T(8,128)(2,1)S(1)}, u32[]{:S(2)}, u32[]{:S(2)}) collective-permute-start(bf16[64,1536]{1,0:T(8,128)(2,1)S(1)} %collective-permute-done.24.refs_7_), channel_id=1, source_target_pairs={{0,1},{1,0},{2,3},{3,2},{4,5},{5,4},{6,7},{7,6},{8,15},{9,10},{10,... | collective-permute-start | bytes 589832 | tf_op jit(solution)/shard_map/ppermute | solution.py:32
  79.7 10.7 %collective-permute-start.27 = (bf16[64,1536]{1,0:T(8,128)(2,1)S(1)}, bf16[64,1536]{1,0:T(8,128)(2,1)S(1)}, u32[]{:S(2)}, u32[]{:S(2)}) collective-permute-start(bf16[64,1536]{1,0:T(8,128)(2,1)S(1)} %collective-permute-done.23.refs_2_.refs_3_), channel_id=1, source_target_pairs={{0,7},{1,2},{2,1},{3,4},{4,3},{5,6},{6,5},{7,0},{8,9},{9,8},{10,11... | collective-permute-start | bytes 589832 | tf_op jit(solution)/shard_map/ppermute | solution.py:32
  85.0 7.5 %collective-permute-start.26 = (bf16[64,1536]{1,0:T(8,128)(2,1)S(1)}, bf16[64,1536]{1,0:T(8,128)(2,1)S(1)}, u32[]{:S(2)}, u32[]{:S(2)}) collective-permute-start(bf16[64,1536]{1,0:T(8,128)(2,1)S(1)} %collective-permute-done.25.refs_4_), channel_id=1, source_target_pairs={{0,7},{1,2},{2,1},{3,4},{4,3},{5,6},{6,5},{7,0},{8,9},{9,8},{10,11... | collective-permute-start | bytes 589832 | tf_op jit(solution)/shard_map/ppermute | solution.py:32
  94.4 1.5 %collective-permute-start.29 = (bf16[64,1536]{1,0:T(8,128)(2,1)S(1)}, bf16[64,1536]{1,0:T(8,128)(2,1)S(1)}, u32[]{:S(2)}, u32[]{:S(2)}) collective-permute-start(bf16[64,1536]{1,0:T(8,128)(2,1)S(1)} %get-tuple-element.53), channel_id=1, source_target_pairs={{0,8},{1,9},{2,10},{3,11},{4,12},{5,13},{6,14},{7,15},{8,0},{9,1},... | collective-permute-start | bytes 589832 | tf_op jit(solution)/shard_map/ppermute | solution.py:32
  94.5 10.4 %collective-permute-start.28 = (bf16[64,1536]{1,0:T(8,128)(2,1)S(1)}, bf16[64,1536]{1,0:T(8,128)(2,1)S(1)}, u32[]{:S(2)}, u32[]{:S(2)}) collective-permute-start(bf16[64,1536]{1,0:T(8,128)(2,1)S(1)} %get-tuple-element.51), channel_id=1, source_target_pairs={{0,8},{1,9},{2,10},{3,11},{4,12},{5,13},{6,14},{7,15},{8,0},{9,1},... | collective-permute-start | bytes 589832 | tf_op jit(solution)/shard_map/ppermute | solution.py:32
  95.0 3.7 %collective-permute-start.31 = (bf16[64,1536]{1,0:T(8,128)(2,1)S(1)}, bf16[64,1536]{1,0:T(8,128)(2,1)S(1)}, u32[]{:S(2)}, u32[]{:S(2)}) collective-permute-start(bf16[64,1536]{1,0:T(8,128)(2,1)S(1)} %get-tuple-element.55), channel_id=1, source_target_pairs={{0,8},{1,9},{2,10},{3,11},{4,12},{5,13},{6,14},{7,15},{8,0},{9,1},... | collective-permute-start | bytes 589832 | tf_op jit(solution)/shard_map/ppermute | solution.py:32
  95.1 4.4 %collective-permute-start.33 = (bf16[64,1536]{1,0:T(8,128)(2,1)S(1)}, bf16[64,1536]{1,0:T(8,128)(2,1)S(1)}, u32[]{:S(2)}, u32[]{:S(2)}) collective-permute-start(bf16[64,1536]{1,0:T(8,128)(2,1)S(1)} %get-tuple-element.57), channel_id=1, source_target_pairs={{0,8},{1,9},{2,10},{3,11},{4,12},{5,13},{6,14},{7,15},{8,0},{9,1},... | collective-permute-start | bytes 589832 | tf_op jit(solution)/shard_map/ppermute | solution.py:32
  95.9 9.0 %collective-permute-start.30 = (bf16[64,1536]{1,0:T(8,128)(2,1)S(1)}, bf16[64,1536]{1,0:T(8,128)(2,1)S(1)}, u32[]{:S(2)}, u32[]{:S(2)}) collective-permute-start(bf16[64,1536]{1,0:T(8,128)(2,1)S(1)} %add_convert_fusion.2), channel_id=1, source_target_pairs={{0,48},{1,49},{2,50},{3,51},{4,52},{5,53},{6,54},{7,55},{8,200},{9... | collective-permute-start | bytes 589832 | tf_op jit(solution)/shard_map/ppermute | solution.py:32
  98.7 7.3 %collective-permute-start.32 = (bf16[64,1536]{1,0:T(8,128)(2,1)S(1)}, bf16[64,1536]{1,0:T(8,128)(2,1)S(1)}, u32[]{:S(2)}, u32[]{:S(2)}) collective-permute-start(bf16[64,1536]{1,0:T(8,128)(2,1)S(1)} %add_convert_fusion.1), channel_id=1, source_target_pairs={{0,32},{1,33},{2,34},{3,35},{4,36},{5,37},{6,38},{7,39},{8,136},{9... | collective-permute-start | bytes 589832 | tf_op jit(solution)/shard_map/ppermute | solution.py:32
  99.5 6.8 %collective-permute-start.34 = (bf16[64,1536]{1,0:T(8,128)(2,1)S(1)}, bf16[64,1536]{1,0:T(8,128)(2,1)S(1)}, u32[]{:S(2)}, u32[]{:S(2)}) collective-permute-start(bf16[64,1536]{1,0:T(8,128)(2,1)S(1)} %add_convert_fusion), channel_id=1, source_target_pairs={{0,16},{1,17},{2,18},{3,19},{4,20},{5,21},{6,22},{7,23},{8,72},{9,... | collective-permute-start | bytes 589832 | tf_op jit(solution)/shard_map/ppermute | solution.py:32
  106.5 4.8 %collective-permute-start.35 = (bf16[16,1536]{1,0:T(8,128)(2,1)S(1)}, bf16[16,1536]{1,0:T(8,128)(2,1)S(1)}, u32[]{:S(2)}, u32[]{:S(2)}) collective-permute-start(bf16[16,1536]{1,0:T(8,128)(2,1)S(1)} %get-tuple-element.63), channel_id=1, source_target_pairs={{0,192},{1,193},{2,194},{3,195},{4,196},{5,197},{6,198},{7,199},{8... | collective-permute-start | bytes 147464 | tf_op jit(solution)/shard_map/ppermute | solution.py:32
  108.9 5.6 %collective-permute-start.37 = (bf16[16,1536]{1,0:T(8,128)(2,1)S(1)}, bf16[16,1536]{1,0:T(8,128)(2,1)S(1)}, u32[]{:S(2)}, u32[]{:S(2)}) collective-permute-start(bf16[16,1536]{1,0:T(8,128)(2,1)S(1)} %get-tuple-element.64), channel_id=1, source_target_pairs={{0,128},{1,129},{2,130},{3,131},{4,132},{5,133},{6,134},{7,135},{8... | collective-permute-start | bytes 147464 | tf_op jit(solution)/shard_map/ppermute | solution.py:32
  111.2 4.1 %collective-permute-start.36 = (bf16[16,1536]{1,0:T(8,128)(2,1)S(1)}, bf16[16,1536]{1,0:T(8,128)(2,1)S(1)}, u32[]{:S(2)}, u32[]{:S(2)}) collective-permute-start(bf16[16,1536]{1,0:T(8,128)(2,1)S(1)} %get-tuple-element.65), channel_id=1, source_target_pairs={{0,64},{1,65},{2,66},{3,67},{4,68},{5,69},{6,70},{7,71},{8,24},{9,... | collective-permute-start | bytes 147464 | tf_op jit(solution)/shard_map/ppermute | solution.py:32

commit v10 on v8

--- a/solution.py
+++ b/solution.py
@@ -135,7 +135,7 @@
 
 SUM_CUT = (1, 0, 0, 1, 0, 1, 1, 0)
 FIRST, REST = (4, 8), (0, 4)
-GATHER_CUT = (1, 0, 0, 1, 0, 1, 1, 0)
+GATHER_CUT = (1, 0, 1, 1, 1, 1, 1, 1)
 
 
 def z_rows(start, stop):
@@ -307,12 +307,14 @@
     slopes = jax.vjp(gelu_tanh, pre)[1](d_act.astype(F32))[0].astype(BF16)
 
     half = weight.shape[1] // 2
-    slopes, *cut = lax.optimization_barrier((slopes, slopes[:, :half], slopes[:, half:]))
-    longer = [gather_chain(part, -1, 4) for part in cut]
-    block_7, block_2, block_5, block_4 = ([chain[i] for chain in longer] for i in range(4))
-    block_1, block_6, block_3 = ([v] for v in gather_chain(slopes, 1, 3))
-    nearest = block_7 + [slopes] + block_1 + block_2
-    pieces = nearest + block_3 + block_4 + block_5 + block_6
+    cut = lax.optimization_barrier((slopes[:, :half], slopes[:, half:]))
+    longer = [gather_chain(part, 1, 4) for part in cut]
+    shorter = [gather_chain(part, -1, 3) for part in cut]
+    block_1, block_6, block_3, block_4 = ([chain[i] for chain in longer] for i in range(4))
+    block_7, block_2, block_5 = ([chain[i] for chain in shorter] for i in range(3))
+    after, _ = lax.optimization_barrier((block_2[1], block_3[1]))
+    nearest = block_7 + [slopes] + block_1 + [block_2[0], after]
+    pieces = block_7 + [slopes] + block_1 + block_2 + block_3 + block_4 + block_5 + block_6
     pre, _ = lax.optimization_barrier((pre, block_4[0]))
     activated = gelu_tanh(pre).astype(BF16)
 

time: 116 us -> 114 us (0.983)
  waiting for transfers between devices: 37.8 us -> 30.9 us
  starting transfers between devices: 42.6 us -> 47.4 us
    ppermute x42 -> x45, waiting for transfers between devices: 37.8 us -> 30.9 us  [send(): return lax.ppermute(value, ('row', 'col'), pairs_of(target))]
    ppermute x42 -> x45, starting transfers between devices: 42.6 us -> 47.4 us  [send(): return lax.ppermute(value, ('row', 'col'), pairs_of(target))]
  transfers between devices with their start and end apart: 42 -> 45, of which waited for: 27 -> 27; matrix products, arithmetic and copies ran while one was open for 5% -> 5% of each run, Pallas kernels for 4% -> 5%
where the time goes in v10:
time: 114 us
  starting transfers between devices  47.4 us (42%)
  waiting for transfers between devices  30.9 us (27%)
  blocking collectives  16 us (14%)
  Pallas kernels  8.75 us (8%)
  other arithmetic  5.55 us (5%)
  matrix products  4.27 us (4%)
    ppermute x45, starting transfers between devices, send(): return lax.ppermute(value, ('row', 'col'), pairs_of(target))  47.4 us
    ppermute x45, waiting for transfers between devices, send(): return lax.ppermute(value, ('row', 'col'), pairs_of(target))  30.9 us
    all_to_all x1, blocking collectives, normalize(): lax.all_to_all(jnp.broadcast_to(stats[None], (NZ,) + stats.shape), 'col',...  16 us
    dot_general x1, matrix products, per_device(): lax.dot_general(gathered, slopes_all, (((0,), (0,)), ((), ())), preferred...  4.27 us
    pallas_call x1, Pallas kernels, stage(): pl.pallas_call(stage_kernel, in_specs=[pl.BlockSpec(memory_space=pl.ANY)]...  2.34 us
  transfers between devices with their start and end apart: 45, of which 27 were waited for; matrix products, arithmetic and copies ran while one was open for 5% of the time, Pallas kernels for 5%

profile of v10, /device:TPU:2, one launch (start us, length us, event | category | flops | bytes accessed | tf_op | source)
XLA Modules:
  0.0 113.7 jit_solution(11413351767647521262)
XLA Ops:
  0.6 1.0 reduce_sum.45
  1.7 1.1 multiply_reduce_fusion
  2.8 16.0 %all_to_all.5 = f32[8,2,16]{2,1,0:T(2,128)S(1)} all-to-all(f32[8,2,16]{2,1,0:T(2,128)S(1)} %broadcast_in_dim.2), channel_id=1, replica_groups=mesh['row'=32,'col'=8] {'col'}, dimensions={0} | all-to-all | bytes 2048 | tf_op jit(solution)/shard_map/all_to_all | solution.py:266
  18.8 1.0 add_convert_fusion.12
  19.8 2.2 %collective-permute-start.2 = (bf16[16,1536]{1,0:T(8,128)(2,1)S(1)}, bf16[16,1536]{1,0:T(8,128)(2,1)S(1)}, u32[]{:S(2)}, u32[]{:S(2)}) collective-permute-start(bf16[16,1536]{1,0:T(8,128)(2,1)S(1)} %add_convert_fusion.12), channel_id=1, source_target_pairs={{0,128},{1,129},{2,130},{3,131},{4,132},{5,133},{6,134},{7,135},{8... | collective-permute-start | bytes 147464 | tf_op jit(solution)/shard_map/ppermute | solution.py:33
  22.1 2.6 %collective-permute-start = (bf16[16,1536]{1,0:T(8,128)(2,1)S(1)}, bf16[16,1536]{1,0:T(8,128)(2,1)S(1)}, u32[]{:S(2)}, u32[]{:S(2)}) collective-permute-start(bf16[16,1536]{1,0:T(8,128)(2,1)S(1)} %add_convert_fusion.12), channel_id=1, source_target_pairs={{0,64},{1,65},{2,66},{3,67},{4,68},{5,69},{6,70},{7,71},{8,72},{9,... | collective-permute-start | bytes 147464 | tf_op jit(solution)/shard_map/ppermute | solution.py:33
  24.6 0.9 collective-permute-done.2
  25.5 0.6 collective-permute-done.1
  26.2 0.6 collective-permute-done
  26.7 3.1 %collective-permute-start.5 = (bf16[64,1536]{1,0:T(8,128)(2,1)S(1)}, bf16[64,1536]{1,0:T(8,128)(2,1)S(1)}, u32[]{:S(2)}, u32[]{:S(2)}) collective-permute-start(bf16[64,1536]{1,0:T(8,128)(2,1)S(1)} %pad_maximum_fusion.refs_0_), channel_id=1, source_target_pairs={{0,48},{1,49},{2,50},{3,51},{4,52},{5,53},{6,54},{7,55},{8,56},{9,... | collective-permute-start | bytes 589832 | tf_op jit(solution)/shard_map/ppermute | solution.py:33
  29.8 0.6 collective-permute-start.4
  30.5 0.5 collective-permute-start.3
  30.9 2.3 %shard_map.76.refs_8_.w_ref.refs_7_.refs_16_ = bf16[1536,1536]{1,0:T(8,128)(2,1)S(1)} custom-call(bf16[1536,1536]{1,0:T(8,128)(2,1)} %w_ref), custom_call_target="tpu_custom_call" | custom-call | flops 1207959552 | bytes 4718592 | tf_op jit(solution)/shard_map/pallas_call | solution.py:100
  33.3 2.1 %collective-permute-done.5.refs_3_ = bf16[64,1536]{1,0:T(8,128)(2,1)S(1)} collective-permute-done((bf16[64,1536]{1,0:T(8,128)(2,1)S(1)}, bf16[64,1536]{1,0:T(8,128)(2,1)S(1)}, u32[]{:S(2)}, u32[]{:S(2)}) %collective-permute-start.5) | collective-permute-done | bytes 196640 | tf_op jit(solution)/shard_map/ppermute | solution.py:33
  35.3 1.7 %collective-permute-done.4.refs_2_ = bf16[64,1536]{1,0:T(8,128)(2,1)S(1)} collective-permute-done((bf16[64,1536]{1,0:T(8,128)(2,1)S(1)}, bf16[64,1536]{1,0:T(8,128)(2,1)S(1)}, u32[]{:S(2)}, u32[]{:S(2)}) %collective-permute-start.4) | collective-permute-done | bytes 196640 | tf_op jit(solution)/shard_map/ppermute | solution.py:33
  37.0 0.5 collective-permute-start.7
  37.5 0.9 collective-permute-done.8.refs_6_
  39.0 1.7 %shard_map.77 = (bf16[512,1536]{1,0:T(8,128)(2,1)S(1)}, bf16[64,1536]{1,0:T(8,128)(2,1)S(1)}, bf16[64,768]{1,0:T(8,128)(2,1)S(1)}, bf16[64,768]{1,0:T(8,128)(2,1...) custom-call(bf16[64,1536]{1,0:T(8,128)(2,1)S(1)} %pad_maximum_fusion.refs_0_, ...), custom_call_target="tpu_custom_call" | custom-call | flops 1207959552 | bytes 4718592 | tf_op jit(solution)/shard_map/pallas_call | solution.py:164
  40.7 0.7 collective-permute-start.10
  41.4 1.4 %collective-permute-start.14 = (bf16[64,768]{1,0:T(8,128)(2,1)S(1)}, bf16[64,768]{1,0:T(8,128)(2,1)S(1)}, u32[]{:S(2)}, u32[]{:S(2)}) collective-permute-start(bf16[64,768]{1,0:T(8,128)(2,1)S(1)} %get-tuple-element.46), channel_id=1, source_target_pairs={{0,1},{1,0},{2,3},{3,2},{4,5},{5,4},{6,7},{7,6},{8,15},{9,10},{10,... | collective-permute-start | bytes 294920 | tf_op jit(solution)/shard_map/ppermute | solution.py:33
  42.8 0.6 collective-permute-start.18
  43.4 1.4 %shard_map.78 = (bf16[64,768]{1,0:T(8,128)(2,1)S(1)}, bf16[64,768]{1,0:T(8,128)(2,1)S(1)}, bf16[64,1536]{1,0:T(8,128)(2,1)S(1)}, bf16[64,1536]{1,0:T(8,128)(2,1)...) custom-call(bf16[512,1536]{1,0:T(8,128)(2,1)S(1)} %get-tuple-element.37.normed_ref, ...), custom_call_target="tpu_custom_call" | custom-call | flops 1207959552 | bytes 4718592 | tf_op jit(solution)/shard_map/pallas_call | solution.py:175
  44.8 0.6 collective-permute-done.10
  45.5 0.8 collective-permute-start.11
  46.5 2.4 %collective-permute-start.15 = (bf16[64,768]{1,0:T(8,128)(2,1)S(1)}, bf16[64,768]{1,0:T(8,128)(2,1)S(1)}, u32[]{:S(2)}, u32[]{:S(2)}) collective-permute-start(bf16[64,768]{1,0:T(8,128)(2,1)S(1)} %add_convert_fusion.7), channel_id=1, source_target_pairs={{0,7},{1,2},{2,1},{3,4},{4,3},{5,6},{6,5},{7,0},{8,9},{9,8},{10,11... | collective-permute-start | bytes 294920 | tf_op jit(solution)/shard_map/ppermute | solution.py:33
  49.0 1.0 collective-permute-start.19
  50.0 1.4 %collective-permute-done.11 = bf16[64,768]{1,0:T(8,128)(2,1)S(1)} collective-permute-done((bf16[64,768]{1,0:T(8,128)(2,1)S(1)}, bf16[64,768]{1,0:T(8,128)(2,1)S(1)}, u32[]{:S(2)}, u32[]{:S(2)}) %collective-permute-start.11) | collective-permute-done | bytes 98336 | tf_op jit(solution)/shard_map/ppermute | solution.py:33
  51.5 0.9 collective-permute-done.15
  52.5 1.4 %collective-permute-start.16 = (bf16[64,768]{1,0:T(8,128)(2,1)S(1)}, bf16[64,768]{1,0:T(8,128)(2,1)S(1)}, u32[]{:S(2)}, u32[]{:S(2)}) collective-permute-start(bf16[64,768]{1,0:T(8,128)(2,1)S(1)} %add_convert_fusion.6), channel_id=1, source_target_pairs={{0,1},{1,0},{2,3},{3,2},{4,5},{5,4},{6,7},{7,6},{8,15},{9,10},{10,... | collective-permute-start | bytes 294920 | tf_op jit(solution)/shard_map/ppermute | solution.py:33
  53.8 2.3 %collective-permute-done.12 = bf16[64,768]{1,0:T(8,128)(2,1)S(1)} collective-permute-done((bf16[64,768]{1,0:T(8,128)(2,1)S(1)}, bf16[64,768]{1,0:T(8,128)(2,1)S(1)}, u32[]{:S(2)}, u32[]{:S(2)}) %collective-permute-start.12) | collective-permute-done | bytes 98336 | tf_op jit(solution)/shard_map/ppermute | solution.py:33
  56.1 1.0 collective-permute-start.13
  57.5 0.9 collective-permute-start.20
  58.4 1.4 %collective-permute-start.17 = (bf16[64,768]{1,0:T(8,128)(2,1)S(1)}, bf16[64,768]{1,0:T(8,128)(2,1)S(1)}, u32[]{:S(2)}, u32[]{:S(2)}) collective-permute-start(bf16[64,768]{1,0:T(8,128)(2,1)S(1)} %add_convert_fusion.5), channel_id=1, source_target_pairs={{0,7},{1,2},{2,1},{3,4},{4,3},{5,6},{6,5},{7,0},{8,9},{9,8},{10,11... | collective-permute-start | bytes 294920 | tf_op jit(solution)/shard_map/ppermute | solution.py:33
  59.8 3.3 %collective-permute-done.13 = bf16[64,768]{1,0:T(8,128)(2,1)S(1)} collective-permute-done((bf16[64,768]{1,0:T(8,128)(2,1)S(1)}, bf16[64,768]{1,0:T(8,128)(2,1)S(1)}, u32[]{:S(2)}, u32[]{:S(2)}) %collective-permute-start.13) | collective-permute-done | bytes 98336 | tf_op jit(solution)/shard_map/ppermute | solution.py:33
  63.1 1.2 %collective-permute-done.17 = bf16[64,768]{1,0:T(8,128)(2,1)S(1)} collective-permute-done((bf16[64,768]{1,0:T(8,128)(2,1)S(1)}, bf16[64,768]{1,0:T(8,128)(2,1)S(1)}, u32[]{:S(2)}, u32[]{:S(2)}) %collective-permute-start.17) | collective-permute-done | bytes 98336 | tf_op jit(solution)/shard_map/ppermute | solution.py:33
  64.8 2.0 %collective-permute-start.21 = (bf16[64,768]{1,0:T(8,128)(2,1)S(1)}, bf16[64,768]{1,0:T(8,128)(2,1)S(1)}, u32[]{:S(2)}, u32[]{:S(2)}) collective-permute-start(bf16[64,768]{1,0:T(8,128)(2,1)S(1)} %get-tuple-element.50), channel_id=1, source_target_pairs={{0,1},{1,0},{2,3},{3,2},{4,5},{5,4},{6,7},{7,6},{8,15},{9,10},{10,... | collective-permute-start | bytes 294920 | tf_op jit(solution)/shard_map/ppermute | solution.py:33
  66.8 1.8 %collective-permute-start.25 = (bf16[64,768]{1,0:T(8,128)(2,1)S(1)}, bf16[64,768]{1,0:T(8,128)(2,1)S(1)}, u32[]{:S(2)}, u32[]{:S(2)}) collective-permute-start(bf16[64,768]{1,0:T(8,128)(2,1)S(1)} %get-tuple-element.50), channel_id=1, source_target_pairs={{0,7},{1,2},{2,1},{3,4},{4,3},{5,6},{6,5},{7,0},{8,9},{9,8},{10,11... | collective-permute-start | bytes 294920 | tf_op jit(solution)/shard_map/ppermute | solution.py:33
  68.6 1.4 %collective-permute-start.26 = (bf16[64,768]{1,0:T(8,128)(2,1)S(1)}, bf16[64,768]{1,0:T(8,128)(2,1)S(1)}, u32[]{:S(2)}, u32[]{:S(2)}) collective-permute-start(bf16[64,768]{1,0:T(8,128)(2,1)S(1)} %get-tuple-element.52), channel_id=1, source_target_pairs={{0,7},{1,2},{2,1},{3,4},{4,3},{5,6},{6,5},{7,0},{8,9},{9,8},{10,11... | collective-permute-start | bytes 294920 | tf_op jit(solution)/shard_map/ppermute | solution.py:33
  70.1 1.8 %collective-permute-start.30 = (bf16[64,768]{1,0:T(8,128)(2,1)S(1)}, bf16[64,768]{1,0:T(8,128)(2,1)S(1)}, u32[]{:S(2)}, u32[]{:S(2)}) collective-permute-start(bf16[64,768]{1,0:T(8,128)(2,1)S(1)} %collective-permute-done.27.refs_4_), channel_id=1, source_target_pairs={{0,7},{1,2},{2,1},{3,4},{4,3},{5,6},{6,5},{7,0},{8,9},{9,8},{10,11... | collective-permute-start | bytes 294920 | tf_op jit(solution)/shard_map/ppermute | solution.py:33
  72.0 1.3 %collective-permute-start.22 = (bf16[64,768]{1,0:T(8,128)(2,1)S(1)}, bf16[64,768]{1,0:T(8,128)(2,1)S(1)}, u32[]{:S(2)}, u32[]{:S(2)}) collective-permute-start(bf16[64,768]{1,0:T(8,128)(2,1)S(1)} %collective-permute-done.21.refs_3_), channel_id=1, source_target_pairs={{0,7},{1,2},{2,1},{3,4},{4,3},{5,6},{6,5},{7,0},{8,9},{9,8},{10,11... | collective-permute-start | bytes 294920 | tf_op jit(solution)/shard_map/ppermute | solution.py:33
  73.3 1.1 %collective-permute-done.26.refs_1_ = bf16[64,768]{1,0:T(8,128)(2,1)S(1)} collective-permute-done((bf16[64,768]{1,0:T(8,128)(2,1)S(1)}, bf16[64,768]{1,0:T(8,128)(2,1)S(1)}, u32[]{:S(2)}, u32[]{:S(2)}) %collective-permute-start.26) | collective-permute-done | bytes 98336 | tf_op jit(solution)/shard_map/ppermute | solution.py:33
  74.4 0.9 collective-permute-start.29
  75.3 1.5 %collective-permute-done.30.refs_14_ = bf16[64,768]{1,0:T(8,128)(2,1)S(1)} collective-permute-done((bf16[64,768]{1,0:T(8,128)(2,1)S(1)}, bf16[64,768]{1,0:T(8,128)(2,1)S(1)}, u32[]{:S(2)}, u32[]{:S(2)}) %collective-permute-start.30) | collective-permute-done | bytes 98336 | tf_op jit(solution)/shard_map/ppermute | solution.py:33
  76.9 2.1 %collective-permute-done.22.refs_13_ = bf16[64,768]{1,0:T(8,128)(2,1)S(1)} collective-permute-done((bf16[64,768]{1,0:T(8,128)(2,1)S(1)}, bf16[64,768]{1,0:T(8,128)(2,1)S(1)}, u32[]{:S(2)}, u32[]{:S(2)}) %collective-permute-start.22) | collective-permute-done | bytes 98336 | tf_op jit(solution)/shard_map/ppermute | solution.py:33
  79.0 1.6 %collective-permute-start.33 = (bf16[64,768]{1,0:T(8,128)(2,1)S(1)}, bf16[64,768]{1,0:T(8,128)(2,1)S(1)}, u32[]{:S(2)}, u32[]{:S(2)}) collective-permute-start(bf16[64,768]{1,0:T(8,128)(2,1)S(1)} %collective-permute-done.28.refs_5_), channel_id=1, source_target_pairs={{0,7},{1,2},{2,1},{3,4},{4,3},{5,6},{6,5},{7,0},{8,9},{9,8},{10,11... | collective-permute-start | bytes 294920 | tf_op jit(solution)/shard_map/ppermute | solution.py:33
  80.5 1.7 %collective-permute-start.34 = (bf16[64,768]{1,0:T(8,128)(2,1)S(1)}, bf16[64,768]{1,0:T(8,128)(2,1)S(1)}, u32[]{:S(2)}, u32[]{:S(2)}) collective-permute-start(bf16[64,768]{1,0:T(8,128)(2,1)S(1)} %collective-permute-done.29.refs_6_), channel_id=1, source_target_pairs={{0,7},{1,2},{2,1},{3,4},{4,3},{5,6},{6,5},{7,0},{8,9},{9,8},{10,11... | collective-permute-start | bytes 294920 | tf_op jit(solution)/shard_map/ppermute | solution.py:33
  82.2 1.9 %collective-permute-start.32 = (bf16[64,768]{1,0:T(8,128)(2,1)S(1)}, bf16[64,768]{1,0:T(8,128)(2,1)S(1)}, u32[]{:S(2)}, u32[]{:S(2)}) collective-permute-start(bf16[64,768]{1,0:T(8,128)(2,1)S(1)} %collective-permute-done.31.refs_8_), channel_id=1, source_target_pairs={{0,7},{1,2},{2,1},{3,4},{4,3},{5,6},{6,5},{7,0},{8,9},{9,8},{10,11... | collective-permute-start | bytes 294920 | tf_op jit(solution)/shard_map/ppermute | solution.py:33
  84.1 0.5 collective-permute-done.23.refs_7_
  84.6 1.7 %collective-permute-start.24 = (bf16[64,768]{1,0:T(8,128)(2,1)S(1)}, bf16[64,768]{1,0:T(8,128)(2,1)S(1)}, u32[]{:S(2)}, u32[]{:S(2)}) collective-permute-start(bf16[64,768]{1,0:T(8,128)(2,1)S(1)} %collective-permute-done.23.refs_7_), channel_id=1, source_target_pairs={{0,7},{1,2},{2,1},{3,4},{4,3},{5,6},{6,5},{7,0},{8,9},{9,8},{10,11... | collective-permute-start | bytes 294920 | tf_op jit(solution)/shard_map/ppermute | solution.py:33
  86.3 1.4 %shard_map.79.refs_15_ = bf16[256,1536]{1,0:T(8,128)(2,1)S(1)} custom-call(bf16[64,768]{1,0:T(8,128)(2,1)S(1)} %collective-permute-done.25.refs_0_, bf16[64,768]{1,0:T(8,128)(2,1)S(1)} %collective-permute-done.26.refs_1_, bf16[64,1536]{1,0:T(8,128)(2,1)S(1)} %get-tuple-element.65.refs_2_, bf16[64,768]{1,0:T(8,128)(2,1)S(1)} %collective-permute-done.21.refs_3_, ...), custom_call_target="tpu_custom_call" | custom-call | flops 1207959552 | bytes 4718592 | tf_op jit(solution)/shard_map/pallas_call | solution.py:209
  87.7 2.7 %collective-permute-done.24.refs_9_ = bf16[64,768]{1,0:T(8,128)(2,1)S(1)} collective-permute-done((bf16[64,768]{1,0:T(8,128)(2,1)S(1)}, bf16[64,768]{1,0:T(8,128)(2,1)S(1)}, u32[]{:S(2)}, u32[]{:S(2)}) %collective-permute-start.24) | collective-permute-done | bytes 98336 | tf_op jit(solution)/shard_map/ppermute | solution.py:33
  90.4 1.9 %shard_map.80 = (bf16[512,1536]{1,0:T(8,128)(2,1)S(1)}, bf16[64,1536]{1,0:T(8,128)(2,1)S(1)}, bf16[64,1536]{1,0:T(8,128)(2,1)S(1)}, bf16[64,1536]{1,0:T(8,128)(2...) custom-call(bf16[64,768]{1,0:T(8,128)(2,1)S(1)} %collective-permute-, ...), custom_call_target="tpu_custom_call" | custom-call | flops 1207959552 | bytes 4718592 | tf_op jit(solution)/shard_map/pallas_call | solution.py:238
  92.5 0.5 collective-permute-start.35
  93.9 2.5 %collective-permute-start.37 = (bf16[64,1536]{1,0:T(8,128)(2,1)S(1)}, bf16[64,1536]{1,0:T(8,128)(2,1)S(1)}, u32[]{:S(2)}, u32[]{:S(2)}) collective-permute-start(bf16[64,1536]{1,0:T(8,128)(2,1)S(1)} %add_convert_fusion.2), channel_id=1, source_target_pairs={{0,48},{1,49},{2,50},{3,51},{4,52},{5,53},{6,54},{7,55},{8,200},{9... | collective-permute-start | bytes 589832 | tf_op jit(solution)/shard_map/ppermute | solution.py:33
  96.5 0.8 collective-permute-start.39
  97.3 1.1 collective-permute-start.41
  98.4 4.3 %convolution_convert_fusion = bf16[1536,1536]{1,0:T(8,128)(2,1)} fusion(bf16[512,1536]{1,0:T(8,128)(2,1)S(1)} %get-tuple-element.37.normed_ref, bf16[512,1536]{1,0:T(8,128)(2,1)S(1)} %get-tuple-element.62), kind=kOutput, calls=%fused_computation | convolution fusion | flops 2418278400 | bytes 7864320 | tf_op jit(solution)/shard_map/dot_general | solution.py:323
  102.7 1.1 collective-permute-done.39
  104.2 1.6 %collective-permute-start.42 = (bf16[16,1536]{1,0:T(8,128)(2,1)S(1)}, bf16[16,1536]{1,0:T(8,128)(2,1)S(1)}, u32[]{:S(2)}, u32[]{:S(2)}) collective-permute-start(bf16[16,1536]{1,0:T(8,128)(2,1)S(1)} %get-tuple-element.67), channel_id=1, source_target_pairs={{0,192},{1,193},{2,194},{3,195},{4,196},{5,197},{6,198},{7,199},{8... | collective-permute-start | bytes 147464 | tf_op jit(solution)/shard_map/ppermute | solution.py:33
  105.8 3.1 %collective-permute-start.44 = (bf16[16,1536]{1,0:T(8,128)(2,1)S(1)}, bf16[16,1536]{1,0:T(8,128)(2,1)S(1)}, u32[]{:S(2)}, u32[]{:S(2)}) collective-permute-start(bf16[16,1536]{1,0:T(8,128)(2,1)S(1)} %get-tuple-element.68), channel_id=1, source_target_pairs={{0,128},{1,129},{2,130},{3,131},{4,132},{5,133},{6,134},{7,135},{8... | collective-permute-start | bytes 147464 | tf_op jit(solution)/shard_map/ppermute | solution.py:33
  109.0 0.8 fusion.17
  109.8 1.6 %collective-permute-done.44 = bf16[16,1536]{1,0:T(8,128)(2,1)S(1)} collective-permute-done((bf16[16,1536]{1,0:T(8,128)(2,1)S(1)}, bf16[16,1536]{1,0:T(8,128)(2,1)S(1)}, u32[]{:S(2)}, u32[]{:S(2)}) %collective-permute-start.44) | collective-permute-done | bytes 49184 | tf_op jit(solution)/shard_map/ppermute | solution.py:33
  111.4 1.6 %collective-permute-done.43 = bf16[16,1536]{1,0:T(8,128)(2,1)S(1)} collective-permute-done((bf16[16,1536]{1,0:T(8,128)(2,1)S(1)}, bf16[16,1536]{1,0:T(8,128)(2,1)S(1)}, u32[]{:S(2)}, u32[]{:S(2)}) %collective-permute-start.43) | collective-permute-done | bytes 49184 | tf_op jit(solution)/shard_map/ppermute | solution.py:33
  113.1 0.6 add_convert_fusion.11
  (65 shorter events, 3.8 us)
Async XLA Ops:
  19.8 5.7 %collective-permute-start.2 = (bf16[16,1536]{1,0:T(8,128)(2,1)S(1)}, bf16[16,1536]{1,0:T(8,128)(2,1)S(1)}, u32[]{:S(2)}, u32[]{:S(2)}) collective-permute-start(bf16[16,1536]{1,0:T(8,128)(2,1)S(1)} %add_convert_fusion.12), channel_id=1, source_target_pairs={{0,128},{1,129},{2,130},{3,131},{4,132},{5,133},{6,134},{7,135},{8... | collective-permute-start | bytes 147464 | tf_op jit(solution)/shard_map/ppermute | solution.py:33
  22.1 4.1 %collective-permute-start.1 = (bf16[16,1536]{1,0:T(8,128)(2,1)S(1)}, bf16[16,1536]{1,0:T(8,128)(2,1)S(1)}, u32[]{:S(2)}, u32[]{:S(2)}) collective-permute-start(bf16[16,1536]{1,0:T(8,128)(2,1)S(1)} %add_convert_fusion.12), channel_id=1, source_target_pairs={{0,192},{1,193},{2,194},{3,195},{4,196},{5,197},{6,198},{7,199},{8... | collective-permute-start | bytes 147464 | tf_op jit(solution)/shard_map/ppermute | solution.py:33
  22.1 4.6 %collective-permute-start = (bf16[16,1536]{1,0:T(8,128)(2,1)S(1)}, bf16[16,1536]{1,0:T(8,128)(2,1)S(1)}, u32[]{:S(2)}, u32[]{:S(2)}) collective-permute-start(bf16[16,1536]{1,0:T(8,128)(2,1)S(1)} %add_convert_fusion.12), channel_id=1, source_target_pairs={{0,64},{1,65},{2,66},{3,67},{4,68},{5,69},{6,70},{7,71},{8,72},{9,... | collective-permute-start | bytes 147464 | tf_op jit(solution)/shard_map/ppermute | solution.py:33
  26.7 8.6 %collective-permute-start.5 = (bf16[64,1536]{1,0:T(8,128)(2,1)S(1)}, bf16[64,1536]{1,0:T(8,128)(2,1)S(1)}, u32[]{:S(2)}, u32[]{:S(2)}) collective-permute-start(bf16[64,1536]{1,0:T(8,128)(2,1)S(1)} %pad_maximum_fusion.refs_0_), channel_id=1, source_target_pairs={{0,48},{1,49},{2,50},{3,51},{4,52},{5,53},{6,54},{7,55},{8,56},{9,... | collective-permute-start | bytes 589832 | tf_op jit(solution)/shard_map/ppermute | solution.py:33
  29.8 7.2 %collective-permute-start.4 = (bf16[64,1536]{1,0:T(8,128)(2,1)S(1)}, bf16[64,1536]{1,0:T(8,128)(2,1)S(1)}, u32[]{:S(2)}, u32[]{:S(2)}) collective-permute-start(bf16[64,1536]{1,0:T(8,128)(2,1)S(1)} %pad_maximum_fusion.refs_0_), channel_id=1, source_target_pairs={{0,32},{1,33},{2,34},{3,35},{4,36},{5,37},{6,38},{7,39},{8,40},{9,... | collective-permute-start | bytes 589832 | tf_op jit(solution)/shard_map/ppermute | solution.py:33
  30.5 6.6 %collective-permute-start.3 = (bf16[64,1536]{1,0:T(8,128)(2,1)S(1)}, bf16[64,1536]{1,0:T(8,128)(2,1)S(1)}, u32[]{:S(2)}, u32[]{:S(2)}) collective-permute-start(bf16[64,1536]{1,0:T(8,128)(2,1)S(1)} %pad_maximum_fusion.refs_0_), channel_id=1, source_target_pairs={{0,16},{1,17},{2,18},{3,19},{4,20},{5,21},{6,22},{7,23},{8,24},{9,... | collective-permute-start | bytes 589832 | tf_op jit(solution)/shard_map/ppermute | solution.py:33
  30.9 6.6 %collective-permute-start.6 = (bf16[64,1536]{1,0:T(8,128)(2,1)S(1)}, bf16[64,1536]{1,0:T(8,128)(2,1)S(1)}, u32[]{:S(2)}, u32[]{:S(2)}) collective-permute-start(bf16[64,1536]{1,0:T(8,128)(2,1)S(1)} %pad_maximum_fusion.refs_0_), channel_id=1, source_target_pairs={{0,8},{1,9},{2,10},{3,11},{4,12},{5,13},{6,14},{7,15},{8,0},{9,1},... | collective-permute-start | bytes 589832 | tf_op jit(solution)/shard_map/ppermute | solution.py:33
  37.0 1.4 %collective-permute-start.8 = (bf16[64,1536]{1,0:T(8,128)(2,1)S(1)}, bf16[64,1536]{1,0:T(8,128)(2,1)S(1)}, u32[]{:S(2)}, u32[]{:S(2)}) collective-permute-start(bf16[64,1536]{1,0:T(8,128)(2,1)S(1)} %collective-permute-done.4.refs_2_), channel_id=1, source_target_pairs={{0,8},{1,9},{2,10},{3,11},{4,12},{5,13},{6,14},{7,15},{8,0},{9,1},... | collective-permute-start | bytes 589832 | tf_op jit(solution)/shard_map/ppermute | solution.py:33
  37.0 1.7 %collective-permute-start.7 = (bf16[64,1536]{1,0:T(8,128)(2,1)S(1)}, bf16[64,1536]{1,0:T(8,128)(2,1)S(1)}, u32[]{:S(2)}, u32[]{:S(2)}) collective-permute-start(bf16[64,1536]{1,0:T(8,128)(2,1)S(1)} %collective-permute-done.3.refs_1_), channel_id=1, source_target_pairs={{0,8},{1,9},{2,10},{3,11},{4,12},{5,13},{6,14},{7,15},{8,0},{9,1},... | collective-permute-start | bytes 589832 | tf_op jit(solution)/shard_map/ppermute | solution.py:33
  37.5 1.5 %collective-permute-start.9 = (bf16[64,1536]{1,0:T(8,128)(2,1)S(1)}, bf16[64,1536]{1,0:T(8,128)(2,1)S(1)}, u32[]{:S(2)}, u32[]{:S(2)}) collective-permute-start(bf16[64,1536]{1,0:T(8,128)(2,1)S(1)} %collective-permute-done.5.refs_3_), channel_id=1, source_target_pairs={{0,8},{1,9},{2,10},{3,11},{4,12},{5,13},{6,14},{7,15},{8,0},{9,1},... | collective-permute-start | bytes 589832 | tf_op jit(solution)/shard_map/ppermute | solution.py:33
  40.7 4.7 %collective-permute-start.10 = (bf16[64,768]{1,0:T(8,128)(2,1)S(1)}, bf16[64,768]{1,0:T(8,128)(2,1)S(1)}, u32[]{:S(2)}, u32[]{:S(2)}) collective-permute-start(bf16[64,768]{1,0:T(8,128)(2,1)S(1)} %get-tuple-element.42), channel_id=1, source_target_pairs={{0,1},{1,0},{2,3},{3,2},{4,5},{5,4},{6,7},{7,6},{8,15},{9,10},{10,... | collective-permute-start | bytes 294920 | tf_op jit(solution)/shard_map/ppermute | solution.py:33
  41.4 5.1 %collective-permute-start.14 = (bf16[64,768]{1,0:T(8,128)(2,1)S(1)}, bf16[64,768]{1,0:T(8,128)(2,1)S(1)}, u32[]{:S(2)}, u32[]{:S(2)}) collective-permute-start(bf16[64,768]{1,0:T(8,128)(2,1)S(1)} %get-tuple-element.46), channel_id=1, source_target_pairs={{0,1},{1,0},{2,3},{3,2},{4,5},{5,4},{6,7},{7,6},{8,15},{9,10},{10,... | collective-permute-start | bytes 294920 | tf_op jit(solution)/shard_map/ppermute | solution.py:33
  42.8 6.1 %collective-permute-start.18 = (bf16[64,1536]{1,0:T(8,128)(2,1)S(1)}, bf16[64,1536]{1,0:T(8,128)(2,1)S(1)}, u32[]{:S(2)}, u32[]{:S(2)}) collective-permute-start(bf16[64,1536]{1,0:T(8,128)(2,1)S(1)} %get-tuple-element.49), channel_id=1, source_target_pairs={{0,1},{1,0},{2,3},{3,2},{4,5},{5,4},{6,7},{7,6},{8,15},{9,10},{10,... | collective-permute-start | bytes 589832 | tf_op jit(solution)/shard_map/ppermute | solution.py:33
  44.8 19.5 %copy-start = (bf16[64,1536]{1,0:T(8,128)(2,1)S(1)}, bf16[64,1536]{1,0:T(8,128)(2,1)}, u32[]{:S(2)}) copy-start(bf16[64,1536]{1,0:T(8,128)(2,1)} %param.9) | copy-start | bytes 589828
  45.5 5.9 %collective-permute-start.11 = (bf16[64,768]{1,0:T(8,128)(2,1)S(1)}, bf16[64,768]{1,0:T(8,128)(2,1)S(1)}, u32[]{:S(2)}, u32[]{:S(2)}) collective-permute-start(bf16[64,768]{1,0:T(8,128)(2,1)S(1)} %add_convert_fusion.10), channel_id=1, source_target_pairs={{0,7},{1,2},{2,1},{3,4},{4,3},{5,6},{6,5},{7,0},{8,9},{9,8},{10,11... | collective-permute-start | bytes 294920 | tf_op jit(solution)/shard_map/ppermute | solution.py:33
  46.5 5.9 %collective-permute-start.15 = (bf16[64,768]{1,0:T(8,128)(2,1)S(1)}, bf16[64,768]{1,0:T(8,128)(2,1)S(1)}, u32[]{:S(2)}, u32[]{:S(2)}) collective-permute-start(bf16[64,768]{1,0:T(8,128)(2,1)S(1)} %add_convert_fusion.7), channel_id=1, source_target_pairs={{0,7},{1,2},{2,1},{3,4},{4,3},{5,6},{6,5},{7,0},{8,9},{9,8},{10,11... | collective-permute-start | bytes 294920 | tf_op jit(solution)/shard_map/ppermute | solution.py:33
  49.0 8.5 %collective-permute-start.19 = (bf16[64,1536]{1,0:T(8,128)(2,1)S(1)}, bf16[64,1536]{1,0:T(8,128)(2,1)S(1)}, u32[]{:S(2)}, u32[]{:S(2)}) collective-permute-start(bf16[64,1536]{1,0:T(8,128)(2,1)S(1)} %add_convert_fusion.4), channel_id=1, source_target_pairs={{0,7},{1,2},{2,1},{3,4},{4,3},{5,6},{6,5},{7,0},{8,9},{9,8},{10,11... | collective-permute-start | bytes 589832 | tf_op jit(solution)/shard_map/ppermute | solution.py:33
  51.4 4.7 %collective-permute-start.12 = (bf16[64,768]{1,0:T(8,128)(2,1)S(1)}, bf16[64,768]{1,0:T(8,128)(2,1)S(1)}, u32[]{:S(2)}, u32[]{:S(2)}) collective-permute-start(bf16[64,768]{1,0:T(8,128)(2,1)S(1)} %add_convert_fusion.9), channel_id=1, source_target_pairs={{0,1},{1,0},{2,3},{3,2},{4,5},{5,4},{6,7},{7,6},{8,15},{9,10},{10,... | collective-permute-start | bytes 294920 | tf_op jit(solution)/shard_map/ppermute | solution.py:33
  52.5 5.9 %collective-permute-start.16 = (bf16[64,768]{1,0:T(8,128)(2,1)S(1)}, bf16[64,768]{1,0:T(8,128)(2,1)S(1)}, u32[]{:S(2)}, u32[]{:S(2)}) collective-permute-start(bf16[64,768]{1,0:T(8,128)(2,1)S(1)} %add_convert_fusion.6), channel_id=1, source_target_pairs={{0,1},{1,0},{2,3},{3,2},{4,5},{5,4},{6,7},{7,6},{8,15},{9,10},{10,... | collective-permute-start | bytes 294920 | tf_op jit(solution)/shard_map/ppermute | solution.py:33
  56.1 7.0 %collective-permute-start.13 = (bf16[64,768]{1,0:T(8,128)(2,1)S(1)}, bf16[64,768]{1,0:T(8,128)(2,1)S(1)}, u32[]{:S(2)}, u32[]{:S(2)}) collective-permute-start(bf16[64,768]{1,0:T(8,128)(2,1)S(1)} %add_convert_fusion.8), channel_id=1, source_target_pairs={{0,7},{1,2},{2,1},{3,4},{4,3},{5,6},{6,5},{7,0},{8,9},{9,8},{10,11... | collective-permute-start | bytes 294920 | tf_op jit(solution)/shard_map/ppermute | solution.py:33
  57.5 6.8 %collective-permute-start.20 = (bf16[64,1536]{1,0:T(8,128)(2,1)S(1)}, bf16[64,1536]{1,0:T(8,128)(2,1)S(1)}, u32[]{:S(2)}, u32[]{:S(2)}) collective-permute-start(bf16[64,1536]{1,0:T(8,128)(2,1)S(1)} %add_convert_fusion.3), channel_id=1, source_target_pairs={{0,1},{1,0},{2,3},{3,2},{4,5},{5,4},{6,7},{7,6},{8,15},{9,10},{10,... | collective-permute-start | bytes 589832 | tf_op jit(solution)/shard_map/ppermute | solution.py:33
  58.4 5.9 %collective-permute-start.17 = (bf16[64,768]{1,0:T(8,128)(2,1)S(1)}, bf16[64,768]{1,0:T(8,128)(2,1)S(1)}, u32[]{:S(2)}, u32[]{:S(2)}) collective-permute-start(bf16[64,768]{1,0:T(8,128)(2,1)S(1)} %add_convert_fusion.5), channel_id=1, source_target_pairs={{0,7},{1,2},{2,1},{3,4},{4,3},{5,6},{6,5},{7,0},{8,9},{9,8},{10,11... | collective-permute-start | bytes 294920 | tf_op jit(solution)/shard_map/ppermute | solution.py:33
  64.7 5.4 %collective-permute-start.27 = (bf16[64,768]{1,0:T(8,128)(2,1)S(1)}, bf16[64,768]{1,0:T(8,128)(2,1)S(1)}, u32[]{:S(2)}, u32[]{:S(2)}) collective-permute-start(bf16[64,768]{1,0:T(8,128)(2,1)S(1)} %get-tuple-element.52), channel_id=1, source_target_pairs={{0,1},{1,0},{2,3},{3,2},{4,5},{5,4},{6,7},{7,6},{8,15},{9,10},{10,... | collective-permute-start | bytes 294920 | tf_op jit(solution)/shard_map/ppermute | solution.py:33
  64.8 7.2 %collective-permute-start.21 = (bf16[64,768]{1,0:T(8,128)(2,1)S(1)}, bf16[64,768]{1,0:T(8,128)(2,1)S(1)}, u32[]{:S(2)}, u32[]{:S(2)}) collective-permute-start(bf16[64,768]{1,0:T(8,128)(2,1)S(1)} %get-tuple-element.50), channel_id=1, source_target_pairs={{0,1},{1,0},{2,3},{3,2},{4,5},{5,4},{6,7},{7,6},{8,15},{9,10},{10,... | collective-permute-start | bytes 294920 | tf_op jit(solution)/shard_map/ppermute | solution.py:33
  66.8 6.5 %collective-permute-start.25 = (bf16[64,768]{1,0:T(8,128)(2,1)S(1)}, bf16[64,768]{1,0:T(8,128)(2,1)S(1)}, u32[]{:S(2)}, u32[]{:S(2)}) collective-permute-start(bf16[64,768]{1,0:T(8,128)(2,1)S(1)} %get-tuple-element.50), channel_id=1, source_target_pairs={{0,7},{1,2},{2,1},{3,4},{4,3},{5,6},{6,5},{7,0},{8,9},{9,8},{10,11... | collective-permute-start | bytes 294920 | tf_op jit(solution)/shard_map/ppermute | solution.py:33
  68.6 5.8 %collective-permute-start.26 = (bf16[64,768]{1,0:T(8,128)(2,1)S(1)}, bf16[64,768]{1,0:T(8,128)(2,1)S(1)}, u32[]{:S(2)}, u32[]{:S(2)}) collective-permute-start(bf16[64,768]{1,0:T(8,128)(2,1)S(1)} %get-tuple-element.52), channel_id=1, source_target_pairs={{0,7},{1,2},{2,1},{3,4},{4,3},{5,6},{6,5},{7,0},{8,9},{9,8},{10,11... | collective-permute-start | bytes 294920 | tf_op jit(solution)/shard_map/ppermute | solution.py:33
  70.1 6.8 %collective-permute-start.30 = (bf16[64,768]{1,0:T(8,128)(2,1)S(1)}, bf16[64,768]{1,0:T(8,128)(2,1)S(1)}, u32[]{:S(2)}, u32[]{:S(2)}) collective-permute-start(bf16[64,768]{1,0:T(8,128)(2,1)S(1)} %collective-permute-done.27.refs_4_), channel_id=1, source_target_pairs={{0,7},{1,2},{2,1},{3,4},{4,3},{5,6},{6,5},{7,0},{8,9},{9,8},{10,11... | collective-permute-start | bytes 294920 | tf_op jit(solution)/shard_map/ppermute | solution.py:33
  72.0 6.9 %collective-permute-start.22 = (bf16[64,768]{1,0:T(8,128)(2,1)S(1)}, bf16[64,768]{1,0:T(8,128)(2,1)S(1)}, u32[]{:S(2)}, u32[]{:S(2)}) collective-permute-start(bf16[64,768]{1,0:T(8,128)(2,1)S(1)} %collective-permute-done.21.refs_3_), channel_id=1, source_target_pairs={{0,7},{1,2},{2,1},{3,4},{4,3},{5,6},{6,5},{7,0},{8,9},{9,8},{10,11... | collective-permute-start | bytes 294920 | tf_op jit(solution)/shard_map/ppermute | solution.py:33
  73.3 5.7 %collective-permute-start.28 = (bf16[64,768]{1,0:T(8,128)(2,1)S(1)}, bf16[64,768]{1,0:T(8,128)(2,1)S(1)}, u32[]{:S(2)}, u32[]{:S(2)}) collective-permute-start(bf16[64,768]{1,0:T(8,128)(2,1)S(1)} %collective-permute-done.25.refs_0_), channel_id=1, source_target_pairs={{0,1},{1,0},{2,3},{3,2},{4,5},{5,4},{6,7},{7,6},{8,15},{9,10},{10,... | collective-permute-start | bytes 294920 | tf_op jit(solution)/shard_map/ppermute | solution.py:33
  74.4 6.1 %collective-permute-start.29 = (bf16[64,768]{1,0:T(8,128)(2,1)S(1)}, bf16[64,768]{1,0:T(8,128)(2,1)S(1)}, u32[]{:S(2)}, u32[]{:S(2)}) collective-permute-start(bf16[64,768]{1,0:T(8,128)(2,1)S(1)} %collective-permute-done.26.refs_1_), channel_id=1, source_target_pairs={{0,1},{1,0},{2,3},{3,2},{4,5},{5,4},{6,7},{7,6},{8,15},{9,10},{10,... | collective-permute-start | bytes 294920 | tf_op jit(solution)/shard_map/ppermute | solution.py:33
  76.9 5.4 %collective-permute-start.31 = (bf16[64,768]{1,0:T(8,128)(2,1)S(1)}, bf16[64,768]{1,0:T(8,128)(2,1)S(1)}, u32[]{:S(2)}, u32[]{:S(2)}) collective-permute-start(bf16[64,768]{1,0:T(8,128)(2,1)S(1)} %collective-permute-done.30.refs_14_), channel_id=1, source_target_pairs={{0,1},{1,0},{2,3},{3,2},{4,5},{5,4},{6,7},{7,6},{8,15},{9,10},{10,... | collective-permute-start | bytes 294920 | tf_op jit(solution)/shard_map/ppermute | solution.py:33
  79.0 5.6 %collective-permute-start.23 = (bf16[64,768]{1,0:T(8,128)(2,1)S(1)}, bf16[64,768]{1,0:T(8,128)(2,1)S(1)}, u32[]{:S(2)}, u32[]{:S(2)}) collective-permute-start(bf16[64,768]{1,0:T(8,128)(2,1)S(1)} %collective-permute-done.22.refs_13_), channel_id=1, source_target_pairs={{0,1},{1,0},{2,3},{3,2},{4,5},{5,4},{6,7},{7,6},{8,15},{9,10},{10,... | collective-permute-start | bytes 294920 | tf_op jit(solution)/shard_map/ppermute | solution.py:33
  79.0 8.7 %collective-permute-start.33 = (bf16[64,768]{1,0:T(8,128)(2,1)S(1)}, bf16[64,768]{1,0:T(8,128)(2,1)S(1)}, u32[]{:S(2)}, u32[]{:S(2)}) collective-permute-start(bf16[64,768]{1,0:T(8,128)(2,1)S(1)} %collective-permute-done.28.refs_5_), channel_id=1, source_target_pairs={{0,7},{1,2},{2,1},{3,4},{4,3},{5,6},{6,5},{7,0},{8,9},{9,8},{10,11... | collective-permute-start | bytes 294920 | tf_op jit(solution)/shard_map/ppermute | solution.py:33
  80.5 7.2 %collective-permute-start.34 = (bf16[64,768]{1,0:T(8,128)(2,1)S(1)}, bf16[64,768]{1,0:T(8,128)(2,1)S(1)}, u32[]{:S(2)}, u32[]{:S(2)}) collective-permute-start(bf16[64,768]{1,0:T(8,128)(2,1)S(1)} %collective-permute-done.29.refs_6_), channel_id=1, source_target_pairs={{0,7},{1,2},{2,1},{3,4},{4,3},{5,6},{6,5},{7,0},{8,9},{9,8},{10,11... | collective-permute-start | bytes 294920 | tf_op jit(solution)/shard_map/ppermute | solution.py:33
  82.2 8.2 %collective-permute-start.32 = (bf16[64,768]{1,0:T(8,128)(2,1)S(1)}, bf16[64,768]{1,0:T(8,128)(2,1)S(1)}, u32[]{:S(2)}, u32[]{:S(2)}) collective-permute-start(bf16[64,768]{1,0:T(8,128)(2,1)S(1)} %collective-permute-done.31.refs_8_), channel_id=1, source_target_pairs={{0,7},{1,2},{2,1},{3,4},{4,3},{5,6},{6,5},{7,0},{8,9},{9,8},{10,11... | collective-permute-start | bytes 294920 | tf_op jit(solution)/shard_map/ppermute | solution.py:33
  84.6 5.8 %collective-permute-start.24 = (bf16[64,768]{1,0:T(8,128)(2,1)S(1)}, bf16[64,768]{1,0:T(8,128)(2,1)S(1)}, u32[]{:S(2)}, u32[]{:S(2)}) collective-permute-start(bf16[64,768]{1,0:T(8,128)(2,1)S(1)} %collective-permute-done.23.refs_7_), channel_id=1, source_target_pairs={{0,7},{1,2},{2,1},{3,4},{4,3},{5,6},{6,5},{7,0},{8,9},{9,8},{10,11... | collective-permute-start | bytes 294920 | tf_op jit(solution)/shard_map/ppermute | solution.py:33
  92.4 1.5 %collective-permute-start.36 = (bf16[64,1536]{1,0:T(8,128)(2,1)S(1)}, bf16[64,1536]{1,0:T(8,128)(2,1)S(1)}, u32[]{:S(2)}, u32[]{:S(2)}) collective-permute-start(bf16[64,1536]{1,0:T(8,128)(2,1)S(1)} %get-tuple-element.57), channel_id=1, source_target_pairs={{0,8},{1,9},{2,10},{3,11},{4,12},{5,13},{6,14},{7,15},{8,0},{9,1},... | collective-permute-start | bytes 589832 | tf_op jit(solution)/shard_map/ppermute | solution.py:33
  92.5 10.2 %collective-permute-start.35 = (bf16[64,1536]{1,0:T(8,128)(2,1)S(1)}, bf16[64,1536]{1,0:T(8,128)(2,1)S(1)}, u32[]{:S(2)}, u32[]{:S(2)}) collective-permute-start(bf16[64,1536]{1,0:T(8,128)(2,1)S(1)} %get-tuple-element.55), channel_id=1, source_target_pairs={{0,8},{1,9},{2,10},{3,11},{4,12},{5,13},{6,14},{7,15},{8,0},{9,1},... | collective-permute-start | bytes 589832 | tf_op jit(solution)/shard_map/ppermute | solution.py:33
  93.0 3.5 %collective-permute-start.38 = (bf16[64,1536]{1,0:T(8,128)(2,1)S(1)}, bf16[64,1536]{1,0:T(8,128)(2,1)S(1)}, u32[]{:S(2)}, u32[]{:S(2)}) collective-permute-start(bf16[64,1536]{1,0:T(8,128)(2,1)S(1)} %get-tuple-element.59), channel_id=1, source_target_pairs={{0,8},{1,9},{2,10},{3,11},{4,12},{5,13},{6,14},{7,15},{8,0},{9,1},... | collective-permute-start | bytes 589832 | tf_op jit(solution)/shard_map/ppermute | solution.py:33
  93.1 4.2 %collective-permute-start.40 = (bf16[64,1536]{1,0:T(8,128)(2,1)S(1)}, bf16[64,1536]{1,0:T(8,128)(2,1)S(1)}, u32[]{:S(2)}, u32[]{:S(2)}) collective-permute-start(bf16[64,1536]{1,0:T(8,128)(2,1)S(1)} %get-tuple-element.61), channel_id=1, source_target_pairs={{0,8},{1,9},{2,10},{3,11},{4,12},{5,13},{6,14},{7,15},{8,0},{9,1},... | collective-permute-start | bytes 589832 | tf_op jit(solution)/shard_map/ppermute | solution.py:33
  93.9 8.7 %collective-permute-start.37 = (bf16[64,1536]{1,0:T(8,128)(2,1)S(1)}, bf16[64,1536]{1,0:T(8,128)(2,1)S(1)}, u32[]{:S(2)}, u32[]{:S(2)}) collective-permute-start(bf16[64,1536]{1,0:T(8,128)(2,1)S(1)} %add_convert_fusion.2), channel_id=1, source_target_pairs={{0,48},{1,49},{2,50},{3,51},{4,52},{5,53},{6,54},{7,55},{8,200},{9... | collective-permute-start | bytes 589832 | tf_op jit(solution)/shard_map/ppermute | solution.py:33
  96.5 7.3 %collective-permute-start.39 = (bf16[64,1536]{1,0:T(8,128)(2,1)S(1)}, bf16[64,1536]{1,0:T(8,128)(2,1)S(1)}, u32[]{:S(2)}, u32[]{:S(2)}) collective-permute-start(bf16[64,1536]{1,0:T(8,128)(2,1)S(1)} %add_convert_fusion.1), channel_id=1, source_target_pairs={{0,32},{1,33},{2,34},{3,35},{4,36},{5,37},{6,38},{7,39},{8,136},{9... | collective-permute-start | bytes 589832 | tf_op jit(solution)/shard_map/ppermute | solution.py:33
  97.3 6.7 %collective-permute-start.41 = (bf16[64,1536]{1,0:T(8,128)(2,1)S(1)}, bf16[64,1536]{1,0:T(8,128)(2,1)S(1)}, u32[]{:S(2)}, u32[]{:S(2)}) collective-permute-start(bf16[64,1536]{1,0:T(8,128)(2,1)S(1)} %add_convert_fusion), channel_id=1, source_target_pairs={{0,16},{1,17},{2,18},{3,19},{4,20},{5,21},{6,22},{7,23},{8,72},{9,... | collective-permute-start | bytes 589832 | tf_op jit(solution)/shard_map/ppermute | solution.py:33
  104.2 5.5 %collective-permute-start.42 = (bf16[16,1536]{1,0:T(8,128)(2,1)S(1)}, bf16[16,1536]{1,0:T(8,128)(2,1)S(1)}, u32[]{:S(2)}, u32[]{:S(2)}) collective-permute-start(bf16[16,1536]{1,0:T(8,128)(2,1)S(1)} %get-tuple-element.67), channel_id=1, source_target_pairs={{0,192},{1,193},{2,194},{3,195},{4,196},{5,197},{6,198},{7,199},{8... | collective-permute-start | bytes 147464 | tf_op jit(solution)/shard_map/ppermute | solution.py:33
  105.8 5.6 %collective-permute-start.44 = (bf16[16,1536]{1,0:T(8,128)(2,1)S(1)}, bf16[16,1536]{1,0:T(8,128)(2,1)S(1)}, u32[]{:S(2)}, u32[]{:S(2)}) collective-permute-start(bf16[16,1536]{1,0:T(8,128)(2,1)S(1)} %get-tuple-element.68), channel_id=1, source_target_pairs={{0,128},{1,129},{2,130},{3,131},{4,132},{5,133},{6,134},{7,135},{8... | collective-permute-start | bytes 147464 | tf_op jit(solution)/shard_map/ppermute | solution.py:33
  109.0 4.1 %collective-permute-start.43 = (bf16[16,1536]{1,0:T(8,128)(2,1)S(1)}, bf16[16,1536]{1,0:T(8,128)(2,1)S(1)}, u32[]{:S(2)}, u32[]{:S(2)}) collective-permute-start(bf16[16,1536]{1,0:T(8,128)(2,1)S(1)} %get-tuple-element.69), channel_id=1, source_target_pairs={{0,64},{1,65},{2,66},{3,67},{4,68},{5,69},{6,70},{7,71},{8,24},{9,... | collective-permute-start | bytes 147464 | tf_op jit(solution)/shard_map/ppermute | solution.py:33

commit v11 on v10

--- a/solution.py
+++ b/solution.py
@@ -134,7 +134,7 @@
 
 
 SUM_CUT = (1, 0, 0, 1, 0, 1, 1, 0)
-FIRST, REST = (4, 8), (0, 4)
+FIRST, REST = (4, 6), (0, 4, 6, 8)
 GATHER_CUT = (1, 0, 1, 1, 1, 1, 1, 1)
 
 
@@ -155,7 +155,12 @@
 
 
 def rest_kernel(normed_ref, w_ref, *outs):
-    multiply(normed_ref[z_rows(*REST), :], w_ref, halves_of(SUM_CUT[slice(*REST)], outs))
+    outs = list(outs)
+    for part in (REST[:2], REST[2:]):
+        cut = SUM_CUT[slice(*part)]
+        count = len(cut) + sum(cut)
+        multiply(normed_ref[z_rows(*part), :], w_ref, halves_of(cut, outs[:count]))
+        outs = outs[count:]
 
 
 def first_pre(pieces, weight):
@@ -171,7 +176,7 @@
 
 
 def rest_pre(normed, weight):
-    shapes = shapes_of(SUM_CUT[slice(*REST)], weight.shape[1])
+    shapes = shapes_of(SUM_CUT[slice(*REST[:2])] + SUM_CUT[slice(*REST[2:])], weight.shape[1])
     return pl.pallas_call(
         rest_kernel,
         in_specs=[WHOLE] * 2,
@@ -209,9 +214,8 @@
     return pl.pallas_call(
         near_back_kernel,
         in_specs=[WHOLE] * (len(pieces) + 1),
-        out_specs=WHOLE,
-        out_shape=jax.ShapeDtypeStruct((HALF, weight.shape[0]), BF16),
-        scratch_shapes=[pltpu.VMEM((HALF, weight.shape[1]), BF16)],
+        out_specs=[WHOLE] * 2,
+        out_shape=[jax.ShapeDtypeStruct((HALF, width), BF16) for width in weight.shape],
         **settings(weight, 16),
     )(*pieces, weight)
 
@@ -219,18 +223,18 @@
 def far_back_kernel(*refs):
     *pieces, near_ref, w_ref, slopes_ref = refs[:-9]
     outs, product = refs[-9:-1], refs[-1]
-    fill(slopes_ref, halves_of(GATHER_CUT, pieces))
-    product[:HALF, :] = near_ref[...].astype(F32)
-    rows = slopes_ref[HALF:, :]
+    fill(slopes_ref, halves_of(GATHER_CUT[4:], pieces))
+    product[:HALF, :] = near_ref[...]
+    rows = slopes_ref[...]
     for start in range(0, w_ref.shape[0], TILE):
         part = slice(start, start + TILE)
-        product[HALF:, part] = transposed_dot(rows, w_ref[part, :])
+        product[HALF:, part] = transposed_dot(rows, w_ref[part, :]).astype(BF16)
     for core_shift in (1, 0):
         for i in range(4):
             for p in range(4):
                 outs[core_shift * 4 + i][p * TOKENS_OWN : (p + 1) * TOKENS_OWN, :] = product[
                     pl.ds(summed_row(core_shift, i, p), TOKENS_OWN), :
-                ].astype(BF16)
+                ]
 
 
 def far_back(pieces, near, weight):
@@ -239,9 +243,9 @@
         far_back_kernel,
         in_specs=[WHOLE] * (len(pieces) + 2),
         out_specs=[WHOLE] * 9,
-        out_shape=[jax.ShapeDtypeStruct((TOKENS, width), BF16)]
+        out_shape=[jax.ShapeDtypeStruct((HALF, width), BF16)]
         + [jax.ShapeDtypeStruct((TOKENS_Z, depth), BF16)] * 8,
-        scratch_shapes=[pltpu.VMEM((TOKENS, depth), F32)],
+        scratch_shapes=[pltpu.VMEM((TOKENS, depth), BF16)],
         **settings(weight, 16),
     )(*pieces, near, weight)
 
@@ -292,15 +296,17 @@
 
     gathered, *first = first_pre(along_y + other, weight)
     rest = rest_pre(gathered, weight)
-    three, four, five, six = halves_of(SUM_CUT[slice(*FIRST)], first)
-    back, own, one, two = halves_of(SUM_CUT[slice(*REST)], rest)
+    three, four = halves_of(SUM_CUT[4:6], first)
+    back, own, one, two, five, six = halves_of(SUM_CUT[:4] + SUM_CUT[6:], rest)
     arrived_3 = send_ring(three[0], 1)
-    arrived_6 = send_ring(add(six[0], arrived_3).astype(BF16), -1)
+    sum_6 = add(six[0], arrived_3).astype(BF16)
+    arrived_6 = send_ring(sum_6, -1)
     shorter = send_ring(add(one[0], arrived_6).astype(BF16), 1)
     longer = []
     for h in range(2):
         travelling = send_ring(four[h], 1)
         travelling = send_ring(add(five[h], travelling).astype(BF16), -1)
+        travelling, _ = lax.optimization_barrier((travelling, sum_6))
         travelling = send_ring(add(two[h], travelling).astype(BF16), 1)
         longer.append(send_ring(add(back[h], travelling).astype(BF16), -1))
     pre = add(own[0], jnp.concatenate(longer, axis=1), shorter)
@@ -314,12 +320,13 @@
     block_7, block_2, block_5 = ([chain[i] for chain in shorter] for i in range(3))
     after, _ = lax.optimization_barrier((block_2[1], block_3[1]))
     nearest = block_7 + [slopes] + block_1 + [block_2[0], after]
-    pieces = block_7 + [slopes] + block_1 + block_2 + block_3 + block_4 + block_5 + block_6
+    farthest = block_3 + block_4 + block_5 + block_6
     pre, _ = lax.optimization_barrier((pre, block_4[0]))
     activated = gelu_tanh(pre).astype(BF16)
 
-    near = near_back(nearest, weight)
-    slopes_all, *parts = far_back(pieces, near, weight)
+    near, near_slopes = near_back(nearest, weight)
+    far_slopes, *parts = far_back(farthest, near, weight)
+    slopes_all = jnp.concatenate([near_slopes, far_slopes])
     d_weight = lax.dot_general(
         gathered, slopes_all, (((0,), (0,)), ((), ())), preferred_element_type=F32
     ).astype(BF16)

time: 114 us -> 113 us (level)
  no operation moved by 1% of the time
where the time goes in v11:
time: 113 us
  starting transfers between devices  47.6 us (42%)
  waiting for transfers between devices  30 us (27%)
  blocking collectives  16 us (14%)
  Pallas kernels  8.71 us (8%)
  other arithmetic  5.56 us (5%)
  matrix products  4.29 us (4%)
    ppermute x45, starting transfers between devices, send(): return lax.ppermute(value, ('row', 'col'), pairs_of(target))  47.6 us
    ppermute x45, waiting for transfers between devices, send(): return lax.ppermute(value, ('row', 'col'), pairs_of(target))  30 us
    all_to_all x1, blocking collectives, normalize(): lax.all_to_all(jnp.broadcast_to(stats[None], (NZ,) + stats.shape), 'col',...  16 us
    dot_general x1, matrix products, per_device(): lax.dot_general(gathered, slopes_all, (((0,), (0,)), ((), ())), preferred...  4.29 us
    pallas_call x1, Pallas kernels, stage(): pl.pallas_call(stage_kernel, in_specs=[pl.BlockSpec(memory_space=pl.ANY)]...  2.34 us
  transfers between devices with their start and end apart: 45, of which 27 were waited for; matrix products, arithmetic and copies ran while one was open for 5% of the time, Pallas kernels for 5%

profile of v11, /device:TPU:2, one launch (start us, length us, event | category | flops | bytes accessed | tf_op | source)
XLA Modules:
  0.0 113.0 jit_solution(9063995236681349852)
XLA Ops:
  0.6 1.0 reduce_sum.45
  1.7 1.1 multiply_reduce_fusion
  2.8 16.0 %all_to_all.5 = f32[8,2,16]{2,1,0:T(2,128)S(1)} all-to-all(f32[8,2,16]{2,1,0:T(2,128)S(1)} %broadcast_in_dim.2), channel_id=1, replica_groups=mesh['row'=32,'col'=8] {'col'}, dimensions={0} | all-to-all | bytes 2048 | tf_op jit(solution)/shard_map/all_to_all | solution.py:270
  18.8 1.0 add_convert_fusion.12
  19.8 2.2 %collective-permute-start.2 = (bf16[16,1536]{1,0:T(8,128)(2,1)S(1)}, bf16[16,1536]{1,0:T(8,128)(2,1)S(1)}, u32[]{:S(2)}, u32[]{:S(2)}) collective-permute-start(bf16[16,1536]{1,0:T(8,128)(2,1)S(1)} %add_convert_fusion.12), channel_id=1, source_target_pairs={{0,128},{1,129},{2,130},{3,131},{4,132},{5,133},{6,134},{7,135},{8... | collective-permute-start | bytes 147464 | tf_op jit(solution)/shard_map/ppermute | solution.py:33
  22.1 2.6 %collective-permute-start = (bf16[16,1536]{1,0:T(8,128)(2,1)S(1)}, bf16[16,1536]{1,0:T(8,128)(2,1)S(1)}, u32[]{:S(2)}, u32[]{:S(2)}) collective-permute-start(bf16[16,1536]{1,0:T(8,128)(2,1)S(1)} %add_convert_fusion.12), channel_id=1, source_target_pairs={{0,64},{1,65},{2,66},{3,67},{4,68},{5,69},{6,70},{7,71},{8,72},{9,... | collective-permute-start | bytes 147464 | tf_op jit(solution)/shard_map/ppermute | solution.py:33
  24.6 0.9 collective-permute-done.2
  25.5 0.6 collective-permute-done.1
  26.2 0.6 collective-permute-done
  26.7 3.1 %collective-permute-start.5 = (bf16[64,1536]{1,0:T(8,128)(2,1)S(1)}, bf16[64,1536]{1,0:T(8,128)(2,1)S(1)}, u32[]{:S(2)}, u32[]{:S(2)}) collective-permute-start(bf16[64,1536]{1,0:T(8,128)(2,1)S(1)} %pad_maximum_fusion.refs_0_), channel_id=1, source_target_pairs={{0,48},{1,49},{2,50},{3,51},{4,52},{5,53},{6,54},{7,55},{8,56},{9,... | collective-permute-start | bytes 589832 | tf_op jit(solution)/shard_map/ppermute | solution.py:33
  29.8 0.6 collective-permute-start.4
  30.5 0.5 collective-permute-start.3
  30.9 2.3 %shard_map.76.refs_8_.w_ref.refs_7_.refs_9_ = bf16[1536,1536]{1,0:T(8,128)(2,1)S(1)} custom-call(bf16[1536,1536]{1,0:T(8,128)(2,1)} %w_ref), custom_call_target="tpu_custom_call" | custom-call | flops 1207959552 | bytes 4718592 | tf_op jit(solution)/shard_map/pallas_call | solution.py:100
  33.3 2.1 %collective-permute-done.5.refs_3_ = bf16[64,1536]{1,0:T(8,128)(2,1)S(1)} collective-permute-done((bf16[64,1536]{1,0:T(8,128)(2,1)S(1)}, bf16[64,1536]{1,0:T(8,128)(2,1)S(1)}, u32[]{:S(2)}, u32[]{:S(2)}) %collective-permute-start.5) | collective-permute-done | bytes 196640 | tf_op jit(solution)/shard_map/ppermute | solution.py:33
  35.3 1.7 %collective-permute-done.4.refs_2_ = bf16[64,1536]{1,0:T(8,128)(2,1)S(1)} collective-permute-done((bf16[64,1536]{1,0:T(8,128)(2,1)S(1)}, bf16[64,1536]{1,0:T(8,128)(2,1)S(1)}, u32[]{:S(2)}, u32[]{:S(2)}) %collective-permute-start.4) | collective-permute-done | bytes 196640 | tf_op jit(solution)/shard_map/ppermute | solution.py:33
  37.0 0.5 collective-permute-start.7
  37.5 0.9 collective-permute-done.8.refs_6_
  39.0 1.1 %shard_map.77 = (bf16[512,1536]{1,0:T(8,128)(2,1)S(1)}, bf16[64,1536]{1,0:T(8,128)(2,1)S(1)}, bf16[64,768]{1,0:T(8,128)(2,1)S(1)}, bf16[64,768]{1,0:T(8,128)(2,1)S(1)}) custom-call(bf16[64,1536]{1,0:T(8,128)(2,1)S(1)} %pad_maximum_fusion.refs_0_, bf16[64,1536]{1,0:T(8,128)(2,1)S(1)} %collective-permute-done.3.refs_1_, ...), custom_call_target="tpu_custom_call" | custom-call | flops 1207959552 | bytes 4718592 | tf_op jit(solution)/shard_map/pallas_call | solution.py:169
  40.1 0.7 collective-permute-start.10
  40.8 1.5 %collective-permute-start.15 = (bf16[64,768]{1,0:T(8,128)(2,1)S(1)}, bf16[64,768]{1,0:T(8,128)(2,1)S(1)}, u32[]{:S(2)}, u32[]{:S(2)}) collective-permute-start(bf16[64,768]{1,0:T(8,128)(2,1)S(1)} %get-tuple-element.53), channel_id=1, source_target_pairs={{0,1},{1,0},{2,3},{3,2},{4,5},{5,4},{6,7},{7,6},{8,15},{9,10},{10,... | collective-permute-start | bytes 294920 | tf_op jit(solution)/shard_map/ppermute | solution.py:33
  42.3 0.6 collective-permute-start.12
  42.8 2.0 %shard_map.78 = (bf16[64,768]{1,0:T(8,128)(2,1)S(1)}, bf16[64,768]{1,0:T(8,128)(2,1)S(1)}, bf16[64,1536]{1,0:T(8,128)(2,1)S(1)}, bf16[64,1536]{1,0:T(8,128)(2,1)...) custom-call(bf16[512,1536]{1,0:T(8,128)(2,1)S(1)} %get-tuple-element, ...), custom_call_target="tpu_custom_call" | custom-call | flops 1207959552 | bytes 4718592 | tf_op jit(solution)/shard_map/pallas_call | solution.py:180
  44.9 0.8 collective-permute-start.11
  45.9 2.4 %collective-permute-start.16 = (bf16[64,768]{1,0:T(8,128)(2,1)S(1)}, bf16[64,768]{1,0:T(8,128)(2,1)S(1)}, u32[]{:S(2)}, u32[]{:S(2)}) collective-permute-start(bf16[64,768]{1,0:T(8,128)(2,1)S(1)} %add_convert_fusion.7), channel_id=1, source_target_pairs={{0,7},{1,2},{2,1},{3,4},{4,3},{5,6},{6,5},{7,0},{8,9},{9,8},{10,11... | collective-permute-start | bytes 294920 | tf_op jit(solution)/shard_map/ppermute | solution.py:33
  48.4 1.0 collective-permute-start.19
  49.4 1.4 %collective-permute-done.11 = bf16[64,768]{1,0:T(8,128)(2,1)S(1)} collective-permute-done((bf16[64,768]{1,0:T(8,128)(2,1)S(1)}, bf16[64,768]{1,0:T(8,128)(2,1)S(1)}, u32[]{:S(2)}, u32[]{:S(2)}) %collective-permute-start.11) | collective-permute-done | bytes 98336 | tf_op jit(solution)/shard_map/ppermute | solution.py:33
  50.9 0.5 collective-permute-start.13
  51.4 0.5 collective-permute-done.16
  51.9 1.4 %collective-permute-start.17 = (bf16[64,768]{1,0:T(8,128)(2,1)S(1)}, bf16[64,768]{1,0:T(8,128)(2,1)S(1)}, u32[]{:S(2)}, u32[]{:S(2)}) collective-permute-start(bf16[64,768]{1,0:T(8,128)(2,1)S(1)} %add_convert_fusion.6), channel_id=1, source_target_pairs={{0,1},{1,0},{2,3},{3,2},{4,5},{5,4},{6,7},{7,6},{8,15},{9,10},{10,... | collective-permute-start | bytes 294920 | tf_op jit(solution)/shard_map/ppermute | solution.py:33
  53.3 2.5 %collective-permute-done.13 = bf16[64,768]{1,0:T(8,128)(2,1)S(1)} collective-permute-done((bf16[64,768]{1,0:T(8,128)(2,1)S(1)}, bf16[64,768]{1,0:T(8,128)(2,1)S(1)}, u32[]{:S(2)}, u32[]{:S(2)}) %collective-permute-start.13) | collective-permute-done | bytes 98336 | tf_op jit(solution)/shard_map/ppermute | solution.py:33
  55.8 1.0 collective-permute-start.14
  57.3 2.0 %collective-permute-start.18 = (bf16[64,768]{1,0:T(8,128)(2,1)S(1)}, bf16[64,768]{1,0:T(8,128)(2,1)S(1)}, u32[]{:S(2)}, u32[]{:S(2)}) collective-permute-start(bf16[64,768]{1,0:T(8,128)(2,1)S(1)} %add_convert_fusion.5), channel_id=1, source_target_pairs={{0,7},{1,2},{2,1},{3,4},{4,3},{5,6},{6,5},{7,0},{8,9},{9,8},{10,11... | collective-permute-start | bytes 294920 | tf_op jit(solution)/shard_map/ppermute | solution.py:33
  59.4 3.4 %collective-permute-done.14 = bf16[64,768]{1,0:T(8,128)(2,1)S(1)} collective-permute-done((bf16[64,768]{1,0:T(8,128)(2,1)S(1)}, bf16[64,768]{1,0:T(8,128)(2,1)S(1)}, u32[]{:S(2)}, u32[]{:S(2)}) %collective-permute-start.14) | collective-permute-done | bytes 98336 | tf_op jit(solution)/shard_map/ppermute | solution.py:33
  62.7 1.1 %collective-permute-done.18 = bf16[64,768]{1,0:T(8,128)(2,1)S(1)} collective-permute-done((bf16[64,768]{1,0:T(8,128)(2,1)S(1)}, bf16[64,768]{1,0:T(8,128)(2,1)S(1)}, u32[]{:S(2)}, u32[]{:S(2)}) %collective-permute-start.18) | collective-permute-done | bytes 98336 | tf_op jit(solution)/shard_map/ppermute | solution.py:33
  64.5 1.8 %collective-permute-start.21 = (bf16[64,768]{1,0:T(8,128)(2,1)S(1)}, bf16[64,768]{1,0:T(8,128)(2,1)S(1)}, u32[]{:S(2)}, u32[]{:S(2)}) collective-permute-start(bf16[64,768]{1,0:T(8,128)(2,1)S(1)} %get-tuple-element.56), channel_id=1, source_target_pairs={{0,1},{1,0},{2,3},{3,2},{4,5},{5,4},{6,7},{7,6},{8,15},{9,10},{10,... | collective-permute-start | bytes 294920 | tf_op jit(solution)/shard_map/ppermute | solution.py:33
  66.4 1.6 %collective-permute-start.29 = (bf16[64,768]{1,0:T(8,128)(2,1)S(1)}, bf16[64,768]{1,0:T(8,128)(2,1)S(1)}, u32[]{:S(2)}, u32[]{:S(2)}) collective-permute-start(bf16[64,768]{1,0:T(8,128)(2,1)S(1)} %get-tuple-element.56), channel_id=1, source_target_pairs={{0,7},{1,2},{2,1},{3,4},{4,3},{5,6},{6,5},{7,0},{8,9},{9,8},{10,11... | collective-permute-start | bytes 294920 | tf_op jit(solution)/shard_map/ppermute | solution.py:33
  68.0 1.6 %collective-permute-start.32 = (bf16[64,768]{1,0:T(8,128)(2,1)S(1)}, bf16[64,768]{1,0:T(8,128)(2,1)S(1)}, u32[]{:S(2)}, u32[]{:S(2)}) collective-permute-start(bf16[64,768]{1,0:T(8,128)(2,1)S(1)} %get-tuple-element.58), channel_id=1, source_target_pairs={{0,7},{1,2},{2,1},{3,4},{4,3},{5,6},{6,5},{7,0},{8,9},{9,8},{10,11... | collective-permute-start | bytes 294920 | tf_op jit(solution)/shard_map/ppermute | solution.py:33
  69.6 1.6 %collective-permute-start.26 = (bf16[64,768]{1,0:T(8,128)(2,1)S(1)}, bf16[64,768]{1,0:T(8,128)(2,1)S(1)}, u32[]{:S(2)}, u32[]{:S(2)}) collective-permute-start(bf16[64,768]{1,0:T(8,128)(2,1)S(1)} %collective-permute-done.25.refs_4_), channel_id=1, source_target_pairs={{0,7},{1,2},{2,1},{3,4},{4,3},{5,6},{6,5},{7,0},{8,9},{9,8},{10,11... | collective-permute-start | bytes 294920 | tf_op jit(solution)/shard_map/ppermute | solution.py:33
  71.3 1.5 %collective-permute-start.22 = (bf16[64,768]{1,0:T(8,128)(2,1)S(1)}, bf16[64,768]{1,0:T(8,128)(2,1)S(1)}, u32[]{:S(2)}, u32[]{:S(2)}) collective-permute-start(bf16[64,768]{1,0:T(8,128)(2,1)S(1)} %collective-permute-done.21.refs_3_), channel_id=1, source_target_pairs={{0,7},{1,2},{2,1},{3,4},{4,3},{5,6},{6,5},{7,0},{8,9},{9,8},{10,11... | collective-permute-start | bytes 294920 | tf_op jit(solution)/shard_map/ppermute | solution.py:33
  73.1 0.7 collective-permute-done.32.refs_1_
  73.8 1.1 collective-permute-start.33
  74.9 1.3 %collective-permute-done.26.refs_7_ = bf16[64,768]{1,0:T(8,128)(2,1)S(1)} collective-permute-done((bf16[64,768]{1,0:T(8,128)(2,1)S(1)}, bf16[64,768]{1,0:T(8,128)(2,1)S(1)}, u32[]{:S(2)}, u32[]{:S(2)}) %collective-permute-start.26) | collective-permute-done | bytes 98336 | tf_op jit(solution)/shard_map/ppermute | solution.py:33
  76.2 2.1 %collective-permute-done.22.refs_6_ = bf16[64,768]{1,0:T(8,128)(2,1)S(1)} collective-permute-done((bf16[64,768]{1,0:T(8,128)(2,1)S(1)}, bf16[64,768]{1,0:T(8,128)(2,1)S(1)}, u32[]{:S(2)}, u32[]{:S(2)}) %collective-permute-start.22) | collective-permute-done | bytes 98336 | tf_op jit(solution)/shard_map/ppermute | solution.py:33
  78.3 1.5 %collective-permute-start.31 = (bf16[64,768]{1,0:T(8,128)(2,1)S(1)}, bf16[64,768]{1,0:T(8,128)(2,1)S(1)}, u32[]{:S(2)}, u32[]{:S(2)}) collective-permute-start(bf16[64,768]{1,0:T(8,128)(2,1)S(1)} %collective-permute-done.30.refs_5_), channel_id=1, source_target_pairs={{0,7},{1,2},{2,1},{3,4},{4,3},{5,6},{6,5},{7,0},{8,9},{9,8},{10,11... | collective-permute-start | bytes 294920 | tf_op jit(solution)/shard_map/ppermute | solution.py:33
  79.8 1.8 %collective-permute-start.34 = (bf16[64,768]{1,0:T(8,128)(2,1)S(1)}, bf16[64,768]{1,0:T(8,128)(2,1)S(1)}, u32[]{:S(2)}, u32[]{:S(2)}) collective-permute-start(bf16[64,768]{1,0:T(8,128)(2,1)S(1)} %collective-permute-done.33.refs_6_), channel_id=1, source_target_pairs={{0,7},{1,2},{2,1},{3,4},{4,3},{5,6},{6,5},{7,0},{8,9},{9,8},{10,11... | collective-permute-start | bytes 294920 | tf_op jit(solution)/shard_map/ppermute | solution.py:33
  81.9 1.5 %collective-permute-start.28 = (bf16[64,768]{1,0:T(8,128)(2,1)S(1)}, bf16[64,768]{1,0:T(8,128)(2,1)S(1)}, u32[]{:S(2)}, u32[]{:S(2)}) collective-permute-start(bf16[64,768]{1,0:T(8,128)(2,1)S(1)} %collective-permute-done.27.refs_1_), channel_id=1, source_target_pairs={{0,7},{1,2},{2,1},{3,4},{4,3},{5,6},{6,5},{7,0},{8,9},{9,8},{10,11... | collective-permute-start | bytes 294920 | tf_op jit(solution)/shard_map/ppermute | solution.py:33
  83.3 0.7 collective-permute-done.23.refs_0_
  84.1 1.5 %collective-permute-start.24 = (bf16[64,768]{1,0:T(8,128)(2,1)S(1)}, bf16[64,768]{1,0:T(8,128)(2,1)S(1)}, u32[]{:S(2)}, u32[]{:S(2)}) collective-permute-start(bf16[64,768]{1,0:T(8,128)(2,1)S(1)} %collective-permute-done.23.refs_0_), channel_id=1, source_target_pairs={{0,7},{1,2},{2,1},{3,4},{4,3},{5,6},{6,5},{7,0},{8,9},{9,8},{10,11... | collective-permute-start | bytes 294920 | tf_op jit(solution)/shard_map/ppermute | solution.py:33
  85.5 1.4 %shard_map.79 = (bf16[256,1536]{1,0:T(8,128)(2,1)S(1)}, bf16[256,1536]{1,0:T(8,128)(2,1)S(1)}) custom-call(bf16[64,768]{1,0:T(8,128)(2,1)S(1)} %collective-permute-done.29.refs_0_, bf16[64,768]{1,0:T(8,128)(2,1)S(1)} %collective-permute-done.32.refs_1_, bf16[64,1536]{1,0:T(8,128)(2,1)S(1)} %get-tuple-element.73.refs_2_, ...), custom_call_target="tpu_custom_call" | custom-call | flops 1207959552 | bytes 4718592 | tf_op jit(solution)/shard_map/pallas_call | solution.py:214
  87.0 2.9 %collective-permute-done.24.refs_2_ = bf16[64,768]{1,0:T(8,128)(2,1)S(1)} collective-permute-done((bf16[64,768]{1,0:T(8,128)(2,1)S(1)}, bf16[64,768]{1,0:T(8,128)(2,1)S(1)}, u32[]{:S(2)}, u32[]{:S(2)}) %collective-permute-start.24) | collective-permute-done | bytes 98336 | tf_op jit(solution)/shard_map/ppermute | solution.py:33
  89.9 1.8 %shard_map.80 = (bf16[256,1536]{1,0:T(8,128)(2,1)S(1)}, bf16[64,1536]{1,0:T(8,128)(2,1)S(1)}, bf16[64,1536]{1,0:T(8,128)(2,1)S(1)}, bf16[64,1536]{1,0:T(8,128)(2...) custom-call(bf16[64,768]{1,0:T(8,128)(2,1)S(1)} %collective-permute-, ...), custom_call_target="tpu_custom_call" | custom-call | flops 1207959552 | bytes 4718592 | tf_op jit(solution)/shard_map/pallas_call | solution.py:242
  91.8 0.5 collective-permute-start.35
  92.8 0.4 collective-permute-done.36
  93.3 2.4 %collective-permute-start.37 = (bf16[64,1536]{1,0:T(8,128)(2,1)S(1)}, bf16[64,1536]{1,0:T(8,128)(2,1)S(1)}, u32[]{:S(2)}, u32[]{:S(2)}) collective-permute-start(bf16[64,1536]{1,0:T(8,128)(2,1)S(1)} %add_convert_fusion.2), channel_id=1, source_target_pairs={{0,48},{1,49},{2,50},{3,51},{4,52},{5,53},{6,54},{7,55},{8,200},{9... | collective-permute-start | bytes 589832 | tf_op jit(solution)/shard_map/ppermute | solution.py:33
  95.7 0.8 collective-permute-start.39
  96.6 1.1 %collective-permute-start.41 = (bf16[64,1536]{1,0:T(8,128)(2,1)S(1)}, bf16[64,1536]{1,0:T(8,128)(2,1)S(1)}, u32[]{:S(2)}, u32[]{:S(2)}) collective-permute-start(bf16[64,1536]{1,0:T(8,128)(2,1)S(1)} %add_convert_fusion), channel_id=1, source_target_pairs={{0,16},{1,17},{2,18},{3,19},{4,20},{5,21},{6,22},{7,23},{8,72},{9,... | collective-permute-start | bytes 589832 | tf_op jit(solution)/shard_map/ppermute | solution.py:33
  97.7 4.3 %convolution_convert_fusion = bf16[1536,1536]{1,0:T(8,128)(2,1)} fusion(bf16[512,1536]{1,0:T(8,128)(2,1)S(1)} %get-tuple-element.41.normed_ref, bf16[256,1536]{1,0:T(8,128)(2,1)S(1)} %get-tuple-element.70, bf16[256,1536]{1,0:T(8,128)(2,1)S(1)} %get-tuple-element.69), kind=kOutput, calls=%fused_computation | convolution fusion | flops 2421424128 | bytes 7864320 | tf_op jit(solution)/shard_map/dot_general | solution.py:330
  102.0 1.0 collective-permute-done.39
  103.6 2.3 %collective-permute-start.42 = (bf16[16,1536]{1,0:T(8,128)(2,1)S(1)}, bf16[16,1536]{1,0:T(8,128)(2,1)S(1)}, u32[]{:S(2)}, u32[]{:S(2)}) collective-permute-start(bf16[16,1536]{1,0:T(8,128)(2,1)S(1)} %get-tuple-element.75), channel_id=1, source_target_pairs={{0,192},{1,193},{2,194},{3,195},{4,196},{5,197},{6,198},{7,199},{8... | collective-permute-start | bytes 147464 | tf_op jit(solution)/shard_map/ppermute | solution.py:33
  105.8 2.4 %collective-permute-start.44 = (bf16[16,1536]{1,0:T(8,128)(2,1)S(1)}, bf16[16,1536]{1,0:T(8,128)(2,1)S(1)}, u32[]{:S(2)}, u32[]{:S(2)}) collective-permute-start(bf16[16,1536]{1,0:T(8,128)(2,1)S(1)} %get-tuple-element.76), channel_id=1, source_target_pairs={{0,128},{1,129},{2,130},{3,131},{4,132},{5,133},{6,134},{7,135},{8... | collective-permute-start | bytes 147464 | tf_op jit(solution)/shard_map/ppermute | solution.py:33
  108.2 0.8 fusion.20
  109.0 2.4 %collective-permute-done.44 = bf16[16,1536]{1,0:T(8,128)(2,1)S(1)} collective-permute-done((bf16[16,1536]{1,0:T(8,128)(2,1)S(1)}, bf16[16,1536]{1,0:T(8,128)(2,1)S(1)}, u32[]{:S(2)}, u32[]{:S(2)}) %collective-permute-start.44) | collective-permute-done | bytes 49184 | tf_op jit(solution)/shard_map/ppermute | solution.py:33
  111.4 0.9 collective-permute-done.43
  112.3 0.6 add_convert_fusion.11
  (65 shorter events, 4.2 us)
Async XLA Ops:
  19.8 5.7 %collective-permute-start.2 = (bf16[16,1536]{1,0:T(8,128)(2,1)S(1)}, bf16[16,1536]{1,0:T(8,128)(2,1)S(1)}, u32[]{:S(2)}, u32[]{:S(2)}) collective-permute-start(bf16[16,1536]{1,0:T(8,128)(2,1)S(1)} %add_convert_fusion.12), channel_id=1, source_target_pairs={{0,128},{1,129},{2,130},{3,131},{4,132},{5,133},{6,134},{7,135},{8... | collective-permute-start | bytes 147464 | tf_op jit(solution)/shard_map/ppermute | solution.py:33
  22.1 4.1 %collective-permute-start.1 = (bf16[16,1536]{1,0:T(8,128)(2,1)S(1)}, bf16[16,1536]{1,0:T(8,128)(2,1)S(1)}, u32[]{:S(2)}, u32[]{:S(2)}) collective-permute-start(bf16[16,1536]{1,0:T(8,128)(2,1)S(1)} %add_convert_fusion.12), channel_id=1, source_target_pairs={{0,192},{1,193},{2,194},{3,195},{4,196},{5,197},{6,198},{7,199},{8... | collective-permute-start | bytes 147464 | tf_op jit(solution)/shard_map/ppermute | solution.py:33
  22.1 4.6 %collective-permute-start = (bf16[16,1536]{1,0:T(8,128)(2,1)S(1)}, bf16[16,1536]{1,0:T(8,128)(2,1)S(1)}, u32[]{:S(2)}, u32[]{:S(2)}) collective-permute-start(bf16[16,1536]{1,0:T(8,128)(2,1)S(1)} %add_convert_fusion.12), channel_id=1, source_target_pairs={{0,64},{1,65},{2,66},{3,67},{4,68},{5,69},{6,70},{7,71},{8,72},{9,... | collective-permute-start | bytes 147464 | tf_op jit(solution)/shard_map/ppermute | solution.py:33
  26.7 8.6 %collective-permute-start.5 = (bf16[64,1536]{1,0:T(8,128)(2,1)S(1)}, bf16[64,1536]{1,0:T(8,128)(2,1)S(1)}, u32[]{:S(2)}, u32[]{:S(2)}) collective-permute-start(bf16[64,1536]{1,0:T(8,128)(2,1)S(1)} %pad_maximum_fusion.refs_0_), channel_id=1, source_target_pairs={{0,48},{1,49},{2,50},{3,51},{4,52},{5,53},{6,54},{7,55},{8,56},{9,... | collective-permute-start | bytes 589832 | tf_op jit(solution)/shard_map/ppermute | solution.py:33
  29.8 7.2 %collective-permute-start.4 = (bf16[64,1536]{1,0:T(8,128)(2,1)S(1)}, bf16[64,1536]{1,0:T(8,128)(2,1)S(1)}, u32[]{:S(2)}, u32[]{:S(2)}) collective-permute-start(bf16[64,1536]{1,0:T(8,128)(2,1)S(1)} %pad_maximum_fusion.refs_0_), channel_id=1, source_target_pairs={{0,32},{1,33},{2,34},{3,35},{4,36},{5,37},{6,38},{7,39},{8,40},{9,... | collective-permute-start | bytes 589832 | tf_op jit(solution)/shard_map/ppermute | solution.py:33
  30.5 6.6 %collective-permute-start.3 = (bf16[64,1536]{1,0:T(8,128)(2,1)S(1)}, bf16[64,1536]{1,0:T(8,128)(2,1)S(1)}, u32[]{:S(2)}, u32[]{:S(2)}) collective-permute-start(bf16[64,1536]{1,0:T(8,128)(2,1)S(1)} %pad_maximum_fusion.refs_0_), channel_id=1, source_target_pairs={{0,16},{1,17},{2,18},{3,19},{4,20},{5,21},{6,22},{7,23},{8,24},{9,... | collective-permute-start | bytes 589832 | tf_op jit(solution)/shard_map/ppermute | solution.py:33
  30.9 6.6 %collective-permute-start.6 = (bf16[64,1536]{1,0:T(8,128)(2,1)S(1)}, bf16[64,1536]{1,0:T(8,128)(2,1)S(1)}, u32[]{:S(2)}, u32[]{:S(2)}) collective-permute-start(bf16[64,1536]{1,0:T(8,128)(2,1)S(1)} %pad_maximum_fusion.refs_0_), channel_id=1, source_target_pairs={{0,8},{1,9},{2,10},{3,11},{4,12},{5,13},{6,14},{7,15},{8,0},{9,1},... | collective-permute-start | bytes 589832 | tf_op jit(solution)/shard_map/ppermute | solution.py:33
  37.0 1.4 %collective-permute-start.8 = (bf16[64,1536]{1,0:T(8,128)(2,1)S(1)}, bf16[64,1536]{1,0:T(8,128)(2,1)S(1)}, u32[]{:S(2)}, u32[]{:S(2)}) collective-permute-start(bf16[64,1536]{1,0:T(8,128)(2,1)S(1)} %collective-permute-done.4.refs_2_), channel_id=1, source_target_pairs={{0,8},{1,9},{2,10},{3,11},{4,12},{5,13},{6,14},{7,15},{8,0},{9,1},... | collective-permute-start | bytes 589832 | tf_op jit(solution)/shard_map/ppermute | solution.py:33
  37.0 1.7 %collective-permute-start.7 = (bf16[64,1536]{1,0:T(8,128)(2,1)S(1)}, bf16[64,1536]{1,0:T(8,128)(2,1)S(1)}, u32[]{:S(2)}, u32[]{:S(2)}) collective-permute-start(bf16[64,1536]{1,0:T(8,128)(2,1)S(1)} %collective-permute-done.3.refs_1_), channel_id=1, source_target_pairs={{0,8},{1,9},{2,10},{3,11},{4,12},{5,13},{6,14},{7,15},{8,0},{9,1},... | collective-permute-start | bytes 589832 | tf_op jit(solution)/shard_map/ppermute | solution.py:33
  37.5 1.5 %collective-permute-start.9 = (bf16[64,1536]{1,0:T(8,128)(2,1)S(1)}, bf16[64,1536]{1,0:T(8,128)(2,1)S(1)}, u32[]{:S(2)}, u32[]{:S(2)}) collective-permute-start(bf16[64,1536]{1,0:T(8,128)(2,1)S(1)} %collective-permute-done.5.refs_3_), channel_id=1, source_target_pairs={{0,8},{1,9},{2,10},{3,11},{4,12},{5,13},{6,14},{7,15},{8,0},{9,1},... | collective-permute-start | bytes 589832 | tf_op jit(solution)/shard_map/ppermute | solution.py:33
  40.1 4.7 %collective-permute-start.10 = (bf16[64,768]{1,0:T(8,128)(2,1)S(1)}, bf16[64,768]{1,0:T(8,128)(2,1)S(1)}, u32[]{:S(2)}, u32[]{:S(2)}) collective-permute-start(bf16[64,768]{1,0:T(8,128)(2,1)S(1)} %get-tuple-element.46), channel_id=1, source_target_pairs={{0,1},{1,0},{2,3},{3,2},{4,5},{5,4},{6,7},{7,6},{8,15},{9,10},{10,... | collective-permute-start | bytes 294920 | tf_op jit(solution)/shard_map/ppermute | solution.py:33
  40.8 5.1 %collective-permute-start.15 = (bf16[64,768]{1,0:T(8,128)(2,1)S(1)}, bf16[64,768]{1,0:T(8,128)(2,1)S(1)}, u32[]{:S(2)}, u32[]{:S(2)}) collective-permute-start(bf16[64,768]{1,0:T(8,128)(2,1)S(1)} %get-tuple-element.53), channel_id=1, source_target_pairs={{0,1},{1,0},{2,3},{3,2},{4,5},{5,4},{6,7},{7,6},{8,15},{9,10},{10,... | collective-permute-start | bytes 294920 | tf_op jit(solution)/shard_map/ppermute | solution.py:33
  42.3 6.1 %collective-permute-start.12 = (bf16[64,1536]{1,0:T(8,128)(2,1)S(1)}, bf16[64,1536]{1,0:T(8,128)(2,1)S(1)}, u32[]{:S(2)}, u32[]{:S(2)}) collective-permute-start(bf16[64,1536]{1,0:T(8,128)(2,1)S(1)} %get-tuple-element.48), channel_id=1, source_target_pairs={{0,1},{1,0},{2,3},{3,2},{4,5},{5,4},{6,7},{7,6},{8,15},{9,10},{10,... | collective-permute-start | bytes 589832 | tf_op jit(solution)/shard_map/ppermute | solution.py:33
  42.8 21.0 %copy-start = (bf16[64,1536]{1,0:T(8,128)(2,1)S(1)}, bf16[64,1536]{1,0:T(8,128)(2,1)}, u32[]{:S(2)}) copy-start(bf16[64,1536]{1,0:T(8,128)(2,1)} %param.9) | copy-start | bytes 589828
  44.9 5.9 %collective-permute-start.11 = (bf16[64,768]{1,0:T(8,128)(2,1)S(1)}, bf16[64,768]{1,0:T(8,128)(2,1)S(1)}, u32[]{:S(2)}, u32[]{:S(2)}) collective-permute-start(bf16[64,768]{1,0:T(8,128)(2,1)S(1)} %add_convert_fusion.10), channel_id=1, source_target_pairs={{0,7},{1,2},{2,1},{3,4},{4,3},{5,6},{6,5},{7,0},{8,9},{9,8},{10,11... | collective-permute-start | bytes 294920 | tf_op jit(solution)/shard_map/ppermute | solution.py:33
  45.9 5.9 %collective-permute-start.16 = (bf16[64,768]{1,0:T(8,128)(2,1)S(1)}, bf16[64,768]{1,0:T(8,128)(2,1)S(1)}, u32[]{:S(2)}, u32[]{:S(2)}) collective-permute-start(bf16[64,768]{1,0:T(8,128)(2,1)S(1)} %add_convert_fusion.7), channel_id=1, source_target_pairs={{0,7},{1,2},{2,1},{3,4},{4,3},{5,6},{6,5},{7,0},{8,9},{9,8},{10,11... | collective-permute-start | bytes 294920 | tf_op jit(solution)/shard_map/ppermute | solution.py:33
  48.4 8.7 %collective-permute-start.19 = (bf16[64,1536]{1,0:T(8,128)(2,1)S(1)}, bf16[64,1536]{1,0:T(8,128)(2,1)S(1)}, u32[]{:S(2)}, u32[]{:S(2)}) collective-permute-start(bf16[64,1536]{1,0:T(8,128)(2,1)S(1)} %add_convert_fusion.4), channel_id=1, source_target_pairs={{0,7},{1,2},{2,1},{3,4},{4,3},{5,6},{6,5},{7,0},{8,9},{9,8},{10,11... | collective-permute-start | bytes 589832 | tf_op jit(solution)/shard_map/ppermute | solution.py:33
  50.9 4.9 %collective-permute-start.13 = (bf16[64,768]{1,0:T(8,128)(2,1)S(1)}, bf16[64,768]{1,0:T(8,128)(2,1)S(1)}, u32[]{:S(2)}, u32[]{:S(2)}) collective-permute-start(bf16[64,768]{1,0:T(8,128)(2,1)S(1)} %add_convert_fusion.9), channel_id=1, source_target_pairs={{0,1},{1,0},{2,3},{3,2},{4,5},{5,4},{6,7},{7,6},{8,15},{9,10},{10,... | collective-permute-start | bytes 294920 | tf_op jit(solution)/shard_map/ppermute | solution.py:33
  51.9 5.4 %collective-permute-start.17 = (bf16[64,768]{1,0:T(8,128)(2,1)S(1)}, bf16[64,768]{1,0:T(8,128)(2,1)S(1)}, u32[]{:S(2)}, u32[]{:S(2)}) collective-permute-start(bf16[64,768]{1,0:T(8,128)(2,1)S(1)} %add_convert_fusion.6), channel_id=1, source_target_pairs={{0,1},{1,0},{2,3},{3,2},{4,5},{5,4},{6,7},{7,6},{8,15},{9,10},{10,... | collective-permute-start | bytes 294920 | tf_op jit(solution)/shard_map/ppermute | solution.py:33
  55.8 7.0 %collective-permute-start.14 = (bf16[64,768]{1,0:T(8,128)(2,1)S(1)}, bf16[64,768]{1,0:T(8,128)(2,1)S(1)}, u32[]{:S(2)}, u32[]{:S(2)}) collective-permute-start(bf16[64,768]{1,0:T(8,128)(2,1)S(1)} %add_convert_fusion.8), channel_id=1, source_target_pairs={{0,7},{1,2},{2,1},{3,4},{4,3},{5,6},{6,5},{7,0},{8,9},{9,8},{10,11... | collective-permute-start | bytes 294920 | tf_op jit(solution)/shard_map/ppermute | solution.py:33
  57.2 6.7 %collective-permute-start.20 = (bf16[64,1536]{1,0:T(8,128)(2,1)S(1)}, bf16[64,1536]{1,0:T(8,128)(2,1)S(1)}, u32[]{:S(2)}, u32[]{:S(2)}) collective-permute-start(bf16[64,1536]{1,0:T(8,128)(2,1)S(1)} %add_convert_fusion.3), channel_id=1, source_target_pairs={{0,1},{1,0},{2,3},{3,2},{4,5},{5,4},{6,7},{7,6},{8,15},{9,10},{10,... | collective-permute-start | bytes 589832 | tf_op jit(solution)/shard_map/ppermute | solution.py:33
  57.3 6.5 %collective-permute-start.18 = (bf16[64,768]{1,0:T(8,128)(2,1)S(1)}, bf16[64,768]{1,0:T(8,128)(2,1)S(1)}, u32[]{:S(2)}, u32[]{:S(2)}) collective-permute-start(bf16[64,768]{1,0:T(8,128)(2,1)S(1)} %add_convert_fusion.5), channel_id=1, source_target_pairs={{0,7},{1,2},{2,1},{3,4},{4,3},{5,6},{6,5},{7,0},{8,9},{9,8},{10,11... | collective-permute-start | bytes 294920 | tf_op jit(solution)/shard_map/ppermute | solution.py:33
  64.2 5.4 %collective-permute-start.25 = (bf16[64,768]{1,0:T(8,128)(2,1)S(1)}, bf16[64,768]{1,0:T(8,128)(2,1)S(1)}, u32[]{:S(2)}, u32[]{:S(2)}) collective-permute-start(bf16[64,768]{1,0:T(8,128)(2,1)S(1)} %get-tuple-element.58), channel_id=1, source_target_pairs={{0,1},{1,0},{2,3},{3,2},{4,5},{5,4},{6,7},{7,6},{8,15},{9,10},{10,... | collective-permute-start | bytes 294920 | tf_op jit(solution)/shard_map/ppermute | solution.py:33
  64.5 6.8 %collective-permute-start.21 = (bf16[64,768]{1,0:T(8,128)(2,1)S(1)}, bf16[64,768]{1,0:T(8,128)(2,1)S(1)}, u32[]{:S(2)}, u32[]{:S(2)}) collective-permute-start(bf16[64,768]{1,0:T(8,128)(2,1)S(1)} %get-tuple-element.56), channel_id=1, source_target_pairs={{0,1},{1,0},{2,3},{3,2},{4,5},{5,4},{6,7},{7,6},{8,15},{9,10},{10,... | collective-permute-start | bytes 294920 | tf_op jit(solution)/shard_map/ppermute | solution.py:33
  66.4 6.5 %collective-permute-start.29 = (bf16[64,768]{1,0:T(8,128)(2,1)S(1)}, bf16[64,768]{1,0:T(8,128)(2,1)S(1)}, u32[]{:S(2)}, u32[]{:S(2)}) collective-permute-start(bf16[64,768]{1,0:T(8,128)(2,1)S(1)} %get-tuple-element.56), channel_id=1, source_target_pairs={{0,7},{1,2},{2,1},{3,4},{4,3},{5,6},{6,5},{7,0},{8,9},{9,8},{10,11... | collective-permute-start | bytes 294920 | tf_op jit(solution)/shard_map/ppermute | solution.py:33
  68.0 5.8 %collective-permute-start.32 = (bf16[64,768]{1,0:T(8,128)(2,1)S(1)}, bf16[64,768]{1,0:T(8,128)(2,1)S(1)}, u32[]{:S(2)}, u32[]{:S(2)}) collective-permute-start(bf16[64,768]{1,0:T(8,128)(2,1)S(1)} %get-tuple-element.58), channel_id=1, source_target_pairs={{0,7},{1,2},{2,1},{3,4},{4,3},{5,6},{6,5},{7,0},{8,9},{9,8},{10,11... | collective-permute-start | bytes 294920 | tf_op jit(solution)/shard_map/ppermute | solution.py:33
  69.6 6.6 %collective-permute-start.26 = (bf16[64,768]{1,0:T(8,128)(2,1)S(1)}, bf16[64,768]{1,0:T(8,128)(2,1)S(1)}, u32[]{:S(2)}, u32[]{:S(2)}) collective-permute-start(bf16[64,768]{1,0:T(8,128)(2,1)S(1)} %collective-permute-done.25.refs_4_), channel_id=1, source_target_pairs={{0,7},{1,2},{2,1},{3,4},{4,3},{5,6},{6,5},{7,0},{8,9},{9,8},{10,11... | collective-permute-start | bytes 294920 | tf_op jit(solution)/shard_map/ppermute | solution.py:33
  71.3 7.0 %collective-permute-start.22 = (bf16[64,768]{1,0:T(8,128)(2,1)S(1)}, bf16[64,768]{1,0:T(8,128)(2,1)S(1)}, u32[]{:S(2)}, u32[]{:S(2)}) collective-permute-start(bf16[64,768]{1,0:T(8,128)(2,1)S(1)} %collective-permute-done.21.refs_3_), channel_id=1, source_target_pairs={{0,7},{1,2},{2,1},{3,4},{4,3},{5,6},{6,5},{7,0},{8,9},{9,8},{10,11... | collective-permute-start | bytes 294920 | tf_op jit(solution)/shard_map/ppermute | solution.py:33
  72.8 5.5 %collective-permute-start.30 = (bf16[64,768]{1,0:T(8,128)(2,1)S(1)}, bf16[64,768]{1,0:T(8,128)(2,1)S(1)}, u32[]{:S(2)}, u32[]{:S(2)}) collective-permute-start(bf16[64,768]{1,0:T(8,128)(2,1)S(1)} %collective-permute-done.29.refs_0_), channel_id=1, source_target_pairs={{0,1},{1,0},{2,3},{3,2},{4,5},{5,4},{6,7},{7,6},{8,15},{9,10},{10,... | collective-permute-start | bytes 294920 | tf_op jit(solution)/shard_map/ppermute | solution.py:33
  73.8 6.0 %collective-permute-start.33 = (bf16[64,768]{1,0:T(8,128)(2,1)S(1)}, bf16[64,768]{1,0:T(8,128)(2,1)S(1)}, u32[]{:S(2)}, u32[]{:S(2)}) collective-permute-start(bf16[64,768]{1,0:T(8,128)(2,1)S(1)} %collective-permute-done.32.refs_1_), channel_id=1, source_target_pairs={{0,1},{1,0},{2,3},{3,2},{4,5},{5,4},{6,7},{7,6},{8,15},{9,10},{10,... | collective-permute-start | bytes 294920 | tf_op jit(solution)/shard_map/ppermute | solution.py:33
  76.2 5.7 %collective-permute-start.27 = (bf16[64,768]{1,0:T(8,128)(2,1)S(1)}, bf16[64,768]{1,0:T(8,128)(2,1)S(1)}, u32[]{:S(2)}, u32[]{:S(2)}) collective-permute-start(bf16[64,768]{1,0:T(8,128)(2,1)S(1)} %collective-permute-done.26.refs_7_), channel_id=1, source_target_pairs={{0,1},{1,0},{2,3},{3,2},{4,5},{5,4},{6,7},{7,6},{8,15},{9,10},{10,... | collective-permute-start | bytes 294920 | tf_op jit(solution)/shard_map/ppermute | solution.py:33
  78.3 5.7 %collective-permute-start.23 = (bf16[64,768]{1,0:T(8,128)(2,1)S(1)}, bf16[64,768]{1,0:T(8,128)(2,1)S(1)}, u32[]{:S(2)}, u32[]{:S(2)}) collective-permute-start(bf16[64,768]{1,0:T(8,128)(2,1)S(1)} %collective-permute-done.22.refs_6_), channel_id=1, source_target_pairs={{0,1},{1,0},{2,3},{3,2},{4,5},{5,4},{6,7},{7,6},{8,15},{9,10},{10,... | collective-permute-start | bytes 294920 | tf_op jit(solution)/shard_map/ppermute | solution.py:33
  78.3 8.6 %collective-permute-start.31 = (bf16[64,768]{1,0:T(8,128)(2,1)S(1)}, bf16[64,768]{1,0:T(8,128)(2,1)S(1)}, u32[]{:S(2)}, u32[]{:S(2)}) collective-permute-start(bf16[64,768]{1,0:T(8,128)(2,1)S(1)} %collective-permute-done.30.refs_5_), channel_id=1, source_target_pairs={{0,7},{1,2},{2,1},{3,4},{4,3},{5,6},{6,5},{7,0},{8,9},{9,8},{10,11... | collective-permute-start | bytes 294920 | tf_op jit(solution)/shard_map/ppermute | solution.py:33
  79.8 7.2 %collective-permute-start.34 = (bf16[64,768]{1,0:T(8,128)(2,1)S(1)}, bf16[64,768]{1,0:T(8,128)(2,1)S(1)}, u32[]{:S(2)}, u32[]{:S(2)}) collective-permute-start(bf16[64,768]{1,0:T(8,128)(2,1)S(1)} %collective-permute-done.33.refs_6_), channel_id=1, source_target_pairs={{0,7},{1,2},{2,1},{3,4},{4,3},{5,6},{6,5},{7,0},{8,9},{9,8},{10,11... | collective-permute-start | bytes 294920 | tf_op jit(solution)/shard_map/ppermute | solution.py:33
  81.9 8.0 %collective-permute-start.28 = (bf16[64,768]{1,0:T(8,128)(2,1)S(1)}, bf16[64,768]{1,0:T(8,128)(2,1)S(1)}, u32[]{:S(2)}, u32[]{:S(2)}) collective-permute-start(bf16[64,768]{1,0:T(8,128)(2,1)S(1)} %collective-permute-done.27.refs_1_), channel_id=1, source_target_pairs={{0,7},{1,2},{2,1},{3,4},{4,3},{5,6},{6,5},{7,0},{8,9},{9,8},{10,11... | collective-permute-start | bytes 294920 | tf_op jit(solution)/shard_map/ppermute | solution.py:33
  84.1 5.8 %collective-permute-start.24 = (bf16[64,768]{1,0:T(8,128)(2,1)S(1)}, bf16[64,768]{1,0:T(8,128)(2,1)S(1)}, u32[]{:S(2)}, u32[]{:S(2)}) collective-permute-start(bf16[64,768]{1,0:T(8,128)(2,1)S(1)} %collective-permute-done.23.refs_0_), channel_id=1, source_target_pairs={{0,7},{1,2},{2,1},{3,4},{4,3},{5,6},{6,5},{7,0},{8,9},{9,8},{10,11... | collective-permute-start | bytes 294920 | tf_op jit(solution)/shard_map/ppermute | solution.py:33
  91.7 1.5 %collective-permute-start.36 = (bf16[64,1536]{1,0:T(8,128)(2,1)S(1)}, bf16[64,1536]{1,0:T(8,128)(2,1)S(1)}, u32[]{:S(2)}, u32[]{:S(2)}) collective-permute-start(bf16[64,1536]{1,0:T(8,128)(2,1)S(1)} %get-tuple-element.64), channel_id=1, source_target_pairs={{0,8},{1,9},{2,10},{3,11},{4,12},{5,13},{6,14},{7,15},{8,0},{9,1},... | collective-permute-start | bytes 589832 | tf_op jit(solution)/shard_map/ppermute | solution.py:33
  91.8 10.2 %collective-permute-start.35 = (bf16[64,1536]{1,0:T(8,128)(2,1)S(1)}, bf16[64,1536]{1,0:T(8,128)(2,1)S(1)}, u32[]{:S(2)}, u32[]{:S(2)}) collective-permute-start(bf16[64,1536]{1,0:T(8,128)(2,1)S(1)} %get-tuple-element.62), channel_id=1, source_target_pairs={{0,8},{1,9},{2,10},{3,11},{4,12},{5,13},{6,14},{7,15},{8,0},{9,1},... | collective-permute-start | bytes 589832 | tf_op jit(solution)/shard_map/ppermute | solution.py:33
  92.3 3.4 %collective-permute-start.38 = (bf16[64,1536]{1,0:T(8,128)(2,1)S(1)}, bf16[64,1536]{1,0:T(8,128)(2,1)S(1)}, u32[]{:S(2)}, u32[]{:S(2)}) collective-permute-start(bf16[64,1536]{1,0:T(8,128)(2,1)S(1)} %get-tuple-element.66), channel_id=1, source_target_pairs={{0,8},{1,9},{2,10},{3,11},{4,12},{5,13},{6,14},{7,15},{8,0},{9,1},... | collective-permute-start | bytes 589832 | tf_op jit(solution)/shard_map/ppermute | solution.py:33
  92.4 4.2 %collective-permute-start.40 = (bf16[64,1536]{1,0:T(8,128)(2,1)S(1)}, bf16[64,1536]{1,0:T(8,128)(2,1)S(1)}, u32[]{:S(2)}, u32[]{:S(2)}) collective-permute-start(bf16[64,1536]{1,0:T(8,128)(2,1)S(1)} %get-tuple-element.68), channel_id=1, source_target_pairs={{0,8},{1,9},{2,10},{3,11},{4,12},{5,13},{6,14},{7,15},{8,0},{9,1},... | collective-permute-start | bytes 589832 | tf_op jit(solution)/shard_map/ppermute | solution.py:33
  93.3 8.8 %collective-permute-start.37 = (bf16[64,1536]{1,0:T(8,128)(2,1)S(1)}, bf16[64,1536]{1,0:T(8,128)(2,1)S(1)}, u32[]{:S(2)}, u32[]{:S(2)}) collective-permute-start(bf16[64,1536]{1,0:T(8,128)(2,1)S(1)} %add_convert_fusion.2), channel_id=1, source_target_pairs={{0,48},{1,49},{2,50},{3,51},{4,52},{5,53},{6,54},{7,55},{8,200},{9... | collective-permute-start | bytes 589832 | tf_op jit(solution)/shard_map/ppermute | solution.py:33
  95.7 7.3 %collective-permute-start.39 = (bf16[64,1536]{1,0:T(8,128)(2,1)S(1)}, bf16[64,1536]{1,0:T(8,128)(2,1)S(1)}, u32[]{:S(2)}, u32[]{:S(2)}) collective-permute-start(bf16[64,1536]{1,0:T(8,128)(2,1)S(1)} %add_convert_fusion.1), channel_id=1, source_target_pairs={{0,32},{1,33},{2,34},{3,35},{4,36},{5,37},{6,38},{7,39},{8,136},{9... | collective-permute-start | bytes 589832 | tf_op jit(solution)/shard_map/ppermute | solution.py:33
  96.6 6.8 %collective-permute-start.41 = (bf16[64,1536]{1,0:T(8,128)(2,1)S(1)}, bf16[64,1536]{1,0:T(8,128)(2,1)S(1)}, u32[]{:S(2)}, u32[]{:S(2)}) collective-permute-start(bf16[64,1536]{1,0:T(8,128)(2,1)S(1)} %add_convert_fusion), channel_id=1, source_target_pairs={{0,16},{1,17},{2,18},{3,19},{4,20},{5,21},{6,22},{7,23},{8,72},{9,... | collective-permute-start | bytes 589832 | tf_op jit(solution)/shard_map/ppermute | solution.py:33
  103.6 5.5 %collective-permute-start.42 = (bf16[16,1536]{1,0:T(8,128)(2,1)S(1)}, bf16[16,1536]{1,0:T(8,128)(2,1)S(1)}, u32[]{:S(2)}, u32[]{:S(2)}) collective-permute-start(bf16[16,1536]{1,0:T(8,128)(2,1)S(1)} %get-tuple-element.75), channel_id=1, source_target_pairs={{0,192},{1,193},{2,194},{3,195},{4,196},{5,197},{6,198},{7,199},{8... | collective-permute-start | bytes 147464 | tf_op jit(solution)/shard_map/ppermute | solution.py:33
  105.8 5.6 %collective-permute-start.44 = (bf16[16,1536]{1,0:T(8,128)(2,1)S(1)}, bf16[16,1536]{1,0:T(8,128)(2,1)S(1)}, u32[]{:S(2)}, u32[]{:S(2)}) collective-permute-start(bf16[16,1536]{1,0:T(8,128)(2,1)S(1)} %get-tuple-element.76), channel_id=1, source_target_pairs={{0,128},{1,129},{2,130},{3,131},{4,132},{5,133},{6,134},{7,135},{8... | collective-permute-start | bytes 147464 | tf_op jit(solution)/shard_map/ppermute | solution.py:33
  108.2 4.1 %collective-permute-start.43 = (bf16[16,1536]{1,0:T(8,128)(2,1)S(1)}, bf16[16,1536]{1,0:T(8,128)(2,1)S(1)}, u32[]{:S(2)}, u32[]{:S(2)}) collective-permute-start(bf16[16,1536]{1,0:T(8,128)(2,1)S(1)} %get-tuple-element.77), channel_id=1, source_target_pairs={{0,64},{1,65},{2,66},{3,67},{4,68},{5,69},{6,70},{7,71},{8,24},{9,... | collective-permute-start | bytes 147464 | tf_op jit(solution)/shard_map/ppermute | solution.py:33

commit v12 on v11

--- a/solution.py
+++ b/solution.py
@@ -135,7 +135,7 @@
 
 SUM_CUT = (1, 0, 0, 1, 0, 1, 1, 0)
 FIRST, REST = (4, 6), (0, 4, 6, 8)
-GATHER_CUT = (1, 0, 1, 1, 1, 1, 1, 1)
+GATHER_CUT = (1, 1, 1, 1, 1, 1, 1, 1)
 
 
 def z_rows(start, stop):
@@ -309,20 +309,26 @@
         travelling, _ = lax.optimization_barrier((travelling, sum_6))
         travelling = send_ring(add(two[h], travelling).astype(BF16), 1)
         longer.append(send_ring(add(back[h], travelling).astype(BF16), -1))
-    pre = add(own[0], jnp.concatenate(longer, axis=1), shorter)
-    slopes = jax.vjp(gelu_tanh, pre)[1](d_act.astype(F32))[0].astype(BF16)
-
     half = weight.shape[1] // 2
-    cut = lax.optimization_barrier((slopes[:, :half], slopes[:, half:]))
-    longer = [gather_chain(part, 1, 4) for part in cut]
-    shorter = [gather_chain(part, -1, 3) for part in cut]
+
+    def split(value):
+        return lax.optimization_barrier((value[:, :half], value[:, half:]))
+
+    parts_of = zip(split(own[0]), longer, split(shorter))
+    pres = [add(*parts) for parts in parts_of]
+    cut = [
+        jax.vjp(gelu_tanh, pre)[1](cotangent.astype(F32))[0].astype(BF16)
+        for pre, cotangent in zip(pres, split(d_act))
+    ]
+    longer = [gather_chain(part, 1, 4) for part in cut[::-1]][::-1]
+    shorter = [gather_chain(part, -1, 3) for part in cut[::-1]][::-1]
     block_1, block_6, block_3, block_4 = ([chain[i] for chain in longer] for i in range(4))
     block_7, block_2, block_5 = ([chain[i] for chain in shorter] for i in range(3))
-    after, _ = lax.optimization_barrier((block_2[1], block_3[1]))
-    nearest = block_7 + [slopes] + block_1 + [block_2[0], after]
+    after, _ = lax.optimization_barrier((block_2[0], block_3[0]))
+    nearest = block_7 + cut + block_1 + [after, block_2[1]]
     farthest = block_3 + block_4 + block_5 + block_6
-    pre, _ = lax.optimization_barrier((pre, block_4[0]))
-    activated = gelu_tanh(pre).astype(BF16)
+    *pres, _ = lax.optimization_barrier((*pres, block_4[0]))
+    activated = jnp.concatenate([gelu_tanh(pre).astype(BF16) for pre in pres], axis=1)
 
     near, near_slopes = near_back(nearest, weight)
     far_slopes, *parts = far_back(farthest, near, weight)

time: 113 us -> 116 us (1.027)
  waiting for transfers between devices: 30 us -> 32.3 us
    ppermute x45, waiting for transfers between devices: 30 us -> 32.3 us  [send(): return lax.ppermute(value, ('row', 'col'), pairs_of(target))]
  transfers between devices with their start and end apart: 45 -> 45, of which waited for: 27 -> 24; matrix products, arithmetic and copies ran while one was open for 5% -> 5% of each run, Pallas kernels for 5% -> 5%
where the time goes in v12:
time: 116 us
  starting transfers between devices  48.4 us (42%)
  waiting for transfers between devices  32.3 us (28%)
  blocking collectives  16 us (14%)
  Pallas kernels  8.7 us (7%)
  other arithmetic  5.58 us (5%)
  matrix products  4.29 us (4%)
    ppermute x45, starting transfers between devices, send(): return lax.ppermute(value, ('row', 'col'), pairs_of(target))  48.4 us
    ppermute x45, waiting for transfers between devices, send(): return lax.ppermute(value, ('row', 'col'), pairs_of(target))  32.3 us
    all_to_all x1, blocking collectives, normalize(): lax.all_to_all(jnp.broadcast_to(stats[None], (NZ,) + stats.shape), 'col',...  16 us
    dot_general x1, matrix products, per_device(): lax.dot_general(gathered, slopes_all, (((0,), (0,)), ((), ())), preferred...  4.29 us
    pallas_call x1, Pallas kernels, stage(): pl.pallas_call(stage_kernel, in_specs=[pl.BlockSpec(memory_space=pl.ANY)]...  2.34 us
  transfers between devices with their start and end apart: 45, of which 24 were waited for; matrix products, arithmetic and copies ran while one was open for 5% of the time, Pallas kernels for 5%

profile of v12, /device:TPU:2, one launch (start us, length us, event | category | flops | bytes accessed | tf_op | source)
XLA Modules:
  0.0 116.2 jit_solution(2611858892361477555)
XLA Ops:
  0.6 1.0 reduce_sum.45
  1.7 1.1 multiply_reduce_fusion
  2.8 16.0 %all_to_all.5 = f32[8,2,16]{2,1,0:T(2,128)S(1)} all-to-all(f32[8,2,16]{2,1,0:T(2,128)S(1)} %broadcast_in_dim.2), channel_id=1, replica_groups=mesh['row'=32,'col'=8] {'col'}, dimensions={0} | all-to-all | bytes 2048 | tf_op jit(solution)/shard_map/all_to_all | solution.py:270
  18.8 1.0 add_convert_fusion.12
  19.8 2.2 %collective-permute-start.2 = (bf16[16,1536]{1,0:T(8,128)(2,1)S(1)}, bf16[16,1536]{1,0:T(8,128)(2,1)S(1)}, u32[]{:S(2)}, u32[]{:S(2)}) collective-permute-start(bf16[16,1536]{1,0:T(8,128)(2,1)S(1)} %add_convert_fusion.12), channel_id=1, source_target_pairs={{0,128},{1,129},{2,130},{3,131},{4,132},{5,133},{6,134},{7,135},{8... | collective-permute-start | bytes 147464 | tf_op jit(solution)/shard_map/ppermute | solution.py:33
  22.1 2.6 %collective-permute-start = (bf16[16,1536]{1,0:T(8,128)(2,1)S(1)}, bf16[16,1536]{1,0:T(8,128)(2,1)S(1)}, u32[]{:S(2)}, u32[]{:S(2)}) collective-permute-start(bf16[16,1536]{1,0:T(8,128)(2,1)S(1)} %add_convert_fusion.12), channel_id=1, source_target_pairs={{0,64},{1,65},{2,66},{3,67},{4,68},{5,69},{6,70},{7,71},{8,72},{9,... | collective-permute-start | bytes 147464 | tf_op jit(solution)/shard_map/ppermute | solution.py:33
  24.6 0.9 collective-permute-done.2
  25.5 0.6 collective-permute-done.1
  26.2 0.6 collective-permute-done
  26.7 3.1 %collective-permute-start.5 = (bf16[64,1536]{1,0:T(8,128)(2,1)S(1)}, bf16[64,1536]{1,0:T(8,128)(2,1)S(1)}, u32[]{:S(2)}, u32[]{:S(2)}) collective-permute-start(bf16[64,1536]{1,0:T(8,128)(2,1)S(1)} %pad_maximum_fusion.refs_0_), channel_id=1, source_target_pairs={{0,48},{1,49},{2,50},{3,51},{4,52},{5,53},{6,54},{7,55},{8,56},{9,... | collective-permute-start | bytes 589832 | tf_op jit(solution)/shard_map/ppermute | solution.py:33
  29.8 0.6 collective-permute-start.4
  30.5 0.5 collective-permute-start.3
  30.9 2.3 %shard_map.76.refs_8_.w_ref.refs_9_ = bf16[1536,1536]{1,0:T(8,128)(2,1)S(1)} custom-call(bf16[1536,1536]{1,0:T(8,128)(2,1)} %w_ref), custom_call_target="tpu_custom_call" | custom-call | flops 1207959552 | bytes 4718592 | tf_op jit(solution)/shard_map/pallas_call | solution.py:100
  33.3 2.1 %collective-permute-done.5.refs_3_ = bf16[64,1536]{1,0:T(8,128)(2,1)S(1)} collective-permute-done((bf16[64,1536]{1,0:T(8,128)(2,1)S(1)}, bf16[64,1536]{1,0:T(8,128)(2,1)S(1)}, u32[]{:S(2)}, u32[]{:S(2)}) %collective-permute-start.5) | collective-permute-done | bytes 196640 | tf_op jit(solution)/shard_map/ppermute | solution.py:33
  35.4 1.7 %collective-permute-done.4.refs_2_ = bf16[64,1536]{1,0:T(8,128)(2,1)S(1)} collective-permute-done((bf16[64,1536]{1,0:T(8,128)(2,1)S(1)}, bf16[64,1536]{1,0:T(8,128)(2,1)S(1)}, u32[]{:S(2)}, u32[]{:S(2)}) %collective-permute-start.4) | collective-permute-done | bytes 196640 | tf_op jit(solution)/shard_map/ppermute | solution.py:33
  37.0 0.5 collective-permute-start.7
  37.6 0.9 collective-permute-done.8.refs_6_
  38.7 1.1 shard_map.77
  39.9 0.7 collective-permute-start.10
  40.5 1.4 %collective-permute-start.17 = (bf16[64,768]{1,0:T(8,128)(2,1)S(1)}, bf16[64,768]{1,0:T(8,128)(2,1)S(1)}, u32[]{:S(2)}, u32[]{:S(2)}) collective-permute-start(bf16[64,768]{1,0:T(8,128)(2,1)S(1)} %get-tuple-element.62), channel_id=1, source_target_pairs={{0,1},{1,0},{2,3},{3,2},{4,5},{5,4},{6,7},{7,6},{8,15},{9,10},{10,... | collective-permute-start | bytes 294920 | tf_op jit(solution)/shard_map/ppermute | solution.py:33
  42.0 0.6 collective-permute-start.12
  42.6 2.0 %shard_map.78 = (bf16[64,768]{1,0:T(8,128)(2,1)S(1)}, bf16[64,768]{1,0:T(8,128)(2,1)S(1)}, bf16[64,1536]{1,0:T(8,128)(2,1)S(1)}, bf16[64,1536]{1,0:T(8,128)(2,1)...) custom-call(bf16[512,1536]{1,0:T(8,128)(2,1)S(1)} %get-tuple-element, ...), custom_call_target="tpu_custom_call" | custom-call | flops 1207959552 | bytes 4718592 | tf_op jit(solution)/shard_map/pallas_call | solution.py:180
  44.7 0.8 collective-permute-start.11
  45.7 2.5 %collective-permute-start.18 = (bf16[64,768]{1,0:T(8,128)(2,1)S(1)}, bf16[64,768]{1,0:T(8,128)(2,1)S(1)}, u32[]{:S(2)}, u32[]{:S(2)}) collective-permute-start(bf16[64,768]{1,0:T(8,128)(2,1)S(1)} %add_convert_fusion.7), channel_id=1, source_target_pairs={{0,7},{1,2},{2,1},{3,4},{4,3},{5,6},{6,5},{7,0},{8,9},{9,8},{10,11... | collective-permute-start | bytes 294920 | tf_op jit(solution)/shard_map/ppermute | solution.py:33
  48.2 1.0 collective-permute-start.15
  49.1 1.5 %collective-permute-done.11 = bf16[64,768]{1,0:T(8,128)(2,1)S(1)} collective-permute-done((bf16[64,768]{1,0:T(8,128)(2,1)S(1)}, bf16[64,768]{1,0:T(8,128)(2,1)S(1)}, u32[]{:S(2)}, u32[]{:S(2)}) %collective-permute-start.11) | collective-permute-done | bytes 98336 | tf_op jit(solution)/shard_map/ppermute | solution.py:33
  50.6 0.5 collective-permute-start.13
  51.1 0.5 collective-permute-done.18
  51.7 1.4 %collective-permute-start.19 = (bf16[64,768]{1,0:T(8,128)(2,1)S(1)}, bf16[64,768]{1,0:T(8,128)(2,1)S(1)}, u32[]{:S(2)}, u32[]{:S(2)}) collective-permute-start(bf16[64,768]{1,0:T(8,128)(2,1)S(1)} %add_convert_fusion.6), channel_id=1, source_target_pairs={{0,1},{1,0},{2,3},{3,2},{4,5},{5,4},{6,7},{7,6},{8,15},{9,10},{10,... | collective-permute-start | bytes 294920 | tf_op jit(solution)/shard_map/ppermute | solution.py:33
  53.0 2.5 %collective-permute-done.13 = bf16[64,768]{1,0:T(8,128)(2,1)S(1)} collective-permute-done((bf16[64,768]{1,0:T(8,128)(2,1)S(1)}, bf16[64,768]{1,0:T(8,128)(2,1)S(1)}, u32[]{:S(2)}, u32[]{:S(2)}) %collective-permute-start.13) | collective-permute-done | bytes 98336 | tf_op jit(solution)/shard_map/ppermute | solution.py:33
  55.5 1.0 collective-permute-start.14
  57.1 2.0 %collective-permute-start.20 = (bf16[64,768]{1,0:T(8,128)(2,1)S(1)}, bf16[64,768]{1,0:T(8,128)(2,1)S(1)}, u32[]{:S(2)}, u32[]{:S(2)}) collective-permute-start(bf16[64,768]{1,0:T(8,128)(2,1)S(1)} %add_convert_fusion.5), channel_id=1, source_target_pairs={{0,7},{1,2},{2,1},{3,4},{4,3},{5,6},{6,5},{7,0},{8,9},{9,8},{10,11... | collective-permute-start | bytes 294920 | tf_op jit(solution)/shard_map/ppermute | solution.py:33
  59.1 3.8 %collective-permute-done.16 = bf16[64,1536]{1,0:T(8,128)(2,1)S(1)} collective-permute-done((bf16[64,1536]{1,0:T(8,128)(2,1)S(1)}, bf16[64,1536]{1,0:T(8,128)(2,1)S(1)}, u32[]{:S(2)}, u32[]{:S(2)}) %collective-permute-start.16) | collective-permute-done | bytes 196640 | tf_op jit(solution)/shard_map/ppermute | solution.py:33
  63.8 1.7 %collective-permute-start.25 = (bf16[64,768]{1,0:T(8,128)(2,1)S(1)}, bf16[64,768]{1,0:T(8,128)(2,1)S(1)}, u32[]{:S(2)}, u32[]{:S(2)}) collective-permute-start(bf16[64,768]{1,0:T(8,128)(2,1)S(1)} %get-tuple-element.83.refs_3_), channel_id=1, source_target_pairs={{0,1},{1,0},{2,3},{3,2},{4,5},{5,4},{6,7},{7,6},{8,15},{9,10},{10,... | collective-permute-start | bytes 294920 | tf_op jit(solution)/shard_map/ppermute | solution.py:33
  65.5 1.7 %collective-permute-start.32 = (bf16[64,768]{1,0:T(8,128)(2,1)S(1)}, bf16[64,768]{1,0:T(8,128)(2,1)S(1)}, u32[]{:S(2)}, u32[]{:S(2)}) collective-permute-start(bf16[64,768]{1,0:T(8,128)(2,1)S(1)} %get-tuple-element.83.refs_3_), channel_id=1, source_target_pairs={{0,7},{1,2},{2,1},{3,4},{4,3},{5,6},{6,5},{7,0},{8,9},{9,8},{10,11... | collective-permute-start | bytes 294920 | tf_op jit(solution)/shard_map/ppermute | solution.py:33
  67.3 1.5 %collective-permute-start.29 = (bf16[64,768]{1,0:T(8,128)(2,1)S(1)}, bf16[64,768]{1,0:T(8,128)(2,1)S(1)}, u32[]{:S(2)}, u32[]{:S(2)}) collective-permute-start(bf16[64,768]{1,0:T(8,128)(2,1)S(1)} %get-tuple-element.85.refs_2_), channel_id=1, source_target_pairs={{0,7},{1,2},{2,1},{3,4},{4,3},{5,6},{6,5},{7,0},{8,9},{9,8},{10,11... | collective-permute-start | bytes 294920 | tf_op jit(solution)/shard_map/ppermute | solution.py:33
  68.8 1.7 %collective-permute-start.22 = (bf16[64,768]{1,0:T(8,128)(2,1)S(1)}, bf16[64,768]{1,0:T(8,128)(2,1)S(1)}, u32[]{:S(2)}, u32[]{:S(2)}) collective-permute-start(bf16[64,768]{1,0:T(8,128)(2,1)S(1)} %collective-permute-done.21.refs_4_), channel_id=1, source_target_pairs={{0,7},{1,2},{2,1},{3,4},{4,3},{5,6},{6,5},{7,0},{8,9},{9,8},{10,11... | collective-permute-start | bytes 294920 | tf_op jit(solution)/shard_map/ppermute | solution.py:33
  70.5 1.5 %collective-permute-start.26 = (bf16[64,768]{1,0:T(8,128)(2,1)S(1)}, bf16[64,768]{1,0:T(8,128)(2,1)S(1)}, u32[]{:S(2)}, u32[]{:S(2)}) collective-permute-start(bf16[64,768]{1,0:T(8,128)(2,1)S(1)} %collective-permute-done.25.refs_5_), channel_id=1, source_target_pairs={{0,7},{1,2},{2,1},{3,4},{4,3},{5,6},{6,5},{7,0},{8,9},{9,8},{10,11... | collective-permute-start | bytes 294920 | tf_op jit(solution)/shard_map/ppermute | solution.py:33
  72.0 0.6 collective-permute-start.33
  72.6 0.5 collective-permute-done.29.refs_0_
  73.1 1.0 collective-permute-start.30
  74.0 1.6 %collective-permute-done.22.refs_6_ = bf16[64,768]{1,0:T(8,128)(2,1)S(1)} collective-permute-done((bf16[64,768]{1,0:T(8,128)(2,1)S(1)}, bf16[64,768]{1,0:T(8,128)(2,1)S(1)}, u32[]{:S(2)}, u32[]{:S(2)}) %collective-permute-start.22) | collective-permute-done | bytes 98336 | tf_op jit(solution)/shard_map/ppermute | solution.py:33
  75.6 2.1 %collective-permute-done.26.refs_7_ = bf16[64,768]{1,0:T(8,128)(2,1)S(1)} collective-permute-done((bf16[64,768]{1,0:T(8,128)(2,1)S(1)}, bf16[64,768]{1,0:T(8,128)(2,1)S(1)}, u32[]{:S(2)}, u32[]{:S(2)}) %collective-permute-start.26) | collective-permute-done | bytes 98336 | tf_op jit(solution)/shard_map/ppermute | solution.py:33
  77.7 1.7 %collective-permute-start.34 = (bf16[64,768]{1,0:T(8,128)(2,1)S(1)}, bf16[64,768]{1,0:T(8,128)(2,1)S(1)}, u32[]{:S(2)}, u32[]{:S(2)}) collective-permute-start(bf16[64,768]{1,0:T(8,128)(2,1)S(1)} %collective-permute-done.33.refs_7_), channel_id=1, source_target_pairs={{0,7},{1,2},{2,1},{3,4},{4,3},{5,6},{6,5},{7,0},{8,9},{9,8},{10,11... | collective-permute-start | bytes 294920 | tf_op jit(solution)/shard_map/ppermute | solution.py:33
  79.5 1.5 %collective-permute-start.31 = (bf16[64,768]{1,0:T(8,128)(2,1)S(1)}, bf16[64,768]{1,0:T(8,128)(2,1)S(1)}, u32[]{:S(2)}, u32[]{:S(2)}) collective-permute-start(bf16[64,768]{1,0:T(8,128)(2,1)S(1)} %collective-permute-done.30.refs_6_), channel_id=1, source_target_pairs={{0,7},{1,2},{2,1},{3,4},{4,3},{5,6},{6,5},{7,0},{8,9},{9,8},{10,11... | collective-permute-start | bytes 294920 | tf_op jit(solution)/shard_map/ppermute | solution.py:33
  81.0 1.7 %collective-permute-start.24 = (bf16[64,768]{1,0:T(8,128)(2,1)S(1)}, bf16[64,768]{1,0:T(8,128)(2,1)S(1)}, u32[]{:S(2)}, u32[]{:S(2)}) collective-permute-start(bf16[64,768]{1,0:T(8,128)(2,1)S(1)} %collective-permute-done.23.refs_0_), channel_id=1, source_target_pairs={{0,7},{1,2},{2,1},{3,4},{4,3},{5,6},{6,5},{7,0},{8,9},{9,8},{10,11... | collective-permute-start | bytes 294920 | tf_op jit(solution)/shard_map/ppermute | solution.py:33
  82.7 0.7 collective-permute-done.27.refs_1_
  83.4 1.7 %collective-permute-start.28 = (bf16[64,768]{1,0:T(8,128)(2,1)S(1)}, bf16[64,768]{1,0:T(8,128)(2,1)S(1)}, u32[]{:S(2)}, u32[]{:S(2)}) collective-permute-start(bf16[64,768]{1,0:T(8,128)(2,1)S(1)} %collective-permute-done.27.refs_1_), channel_id=1, source_target_pairs={{0,7},{1,2},{2,1},{3,4},{4,3},{5,6},{6,5},{7,0},{8,9},{9,8},{10,11... | collective-permute-start | bytes 294920 | tf_op jit(solution)/shard_map/ppermute | solution.py:33
  85.1 1.4 %shard_map.79 = (bf16[256,1536]{1,0:T(8,128)(2,1)S(1)}, bf16[256,1536]{1,0:T(8,128)(2,1)S(1)}) custom-call(bf16[64,768]{1,0:T(8,128)(2,1)S(1)} %collective-permute-done.29.refs_0_, bf16[64,768]{1,0:T(8,128)(2,1)S(1)} %collective-permute-done.32.refs_1_, bf16[64,768]{1,0:T(8,128)(2,1)S(1)} %get-tuple-element.85.refs_2_, ...), custom_call_target="tpu_custom_call" | custom-call | flops 1207959552 | bytes 4718592 | tf_op jit(solution)/shard_map/pallas_call | solution.py:214
  86.5 2.7 %collective-permute-done.28.refs_3_ = bf16[64,768]{1,0:T(8,128)(2,1)S(1)} collective-permute-done((bf16[64,768]{1,0:T(8,128)(2,1)S(1)}, bf16[64,768]{1,0:T(8,128)(2,1)S(1)}, u32[]{:S(2)}, u32[]{:S(2)}) %collective-permute-start.28) | collective-permute-done | bytes 98336 | tf_op jit(solution)/shard_map/ppermute | solution.py:33
  89.2 1.8 %shard_map.80 = (bf16[256,1536]{1,0:T(8,128)(2,1)S(1)}, bf16[64,1536]{1,0:T(8,128)(2,1)S(1)}, bf16[64,1536]{1,0:T(8,128)(2,1)S(1)}, bf16[64,1536]{1,0:T(8,128)(2...) custom-call(bf16[64,768]{1,0:T(8,128)(2,1)S(1)} %collective-permute-, ...), custom_call_target="tpu_custom_call" | custom-call | flops 1207959552 | bytes 4718592 | tf_op jit(solution)/shard_map/pallas_call | solution.py:242
  91.1 0.5 collective-permute-start.36
  92.1 4.3 %convolution_convert_fusion = bf16[1536,1536]{1,0:T(8,128)(2,1)} fusion(bf16[512,1536]{1,0:T(8,128)(2,1)S(1)} %get-tuple-element.46.normed_ref, bf16[256,1536]{1,0:T(8,128)(2,1)S(1)} %get-tuple-element.80, bf16[256,1536]{1,0:T(8,128)(2,1)S(1)} %get-tuple-element.79), kind=kOutput, calls=%fused_computation | convolution fusion | flops 2421424128 | bytes 7864320 | tf_op jit(solution)/shard_map/dot_general | solution.py:336
  96.4 2.5 %collective-permute-start.37 = (bf16[64,1536]{1,0:T(8,128)(2,1)S(1)}, bf16[64,1536]{1,0:T(8,128)(2,1)S(1)}, u32[]{:S(2)}, u32[]{:S(2)}) collective-permute-start(bf16[64,1536]{1,0:T(8,128)(2,1)S(1)} %add_convert_fusion.2), channel_id=1, source_target_pairs={{0,48},{1,49},{2,50},{3,51},{4,52},{5,53},{6,54},{7,55},{8,200},{9... | collective-permute-start | bytes 589832 | tf_op jit(solution)/shard_map/ppermute | solution.py:33
  99.0 0.8 collective-permute-start.39
  99.8 1.1 collective-permute-start.41
  101.1 3.2 %collective-permute-done.37 = bf16[64,1536]{1,0:T(8,128)(2,1)S(1)} collective-permute-done((bf16[64,1536]{1,0:T(8,128)(2,1)S(1)}, bf16[64,1536]{1,0:T(8,128)(2,1)S(1)}, u32[]{:S(2)}, u32[]{:S(2)}) %collective-permute-start.37) | collective-permute-done | bytes 196640 | tf_op jit(solution)/shard_map/ppermute | solution.py:33
  104.3 2.0 %collective-permute-done.39 = bf16[64,1536]{1,0:T(8,128)(2,1)S(1)} collective-permute-done((bf16[64,1536]{1,0:T(8,128)(2,1)S(1)}, bf16[64,1536]{1,0:T(8,128)(2,1)S(1)}, u32[]{:S(2)}, u32[]{:S(2)}) %collective-permute-start.39) | collective-permute-done | bytes 196640 | tf_op jit(solution)/shard_map/ppermute | solution.py:33
  106.7 1.7 %collective-permute-start.42 = (bf16[16,1536]{1,0:T(8,128)(2,1)S(1)}, bf16[16,1536]{1,0:T(8,128)(2,1)S(1)}, u32[]{:S(2)}, u32[]{:S(2)}) collective-permute-start(bf16[16,1536]{1,0:T(8,128)(2,1)S(1)} %get-tuple-element.87), channel_id=1, source_target_pairs={{0,192},{1,193},{2,194},{3,195},{4,196},{5,197},{6,198},{7,199},{8... | collective-permute-start | bytes 147464 | tf_op jit(solution)/shard_map/ppermute | solution.py:33
  108.4 3.0 %collective-permute-start.44 = (bf16[16,1536]{1,0:T(8,128)(2,1)S(1)}, bf16[16,1536]{1,0:T(8,128)(2,1)S(1)}, u32[]{:S(2)}, u32[]{:S(2)}) collective-permute-start(bf16[16,1536]{1,0:T(8,128)(2,1)S(1)} %get-tuple-element.88), channel_id=1, source_target_pairs={{0,128},{1,129},{2,130},{3,131},{4,132},{5,133},{6,134},{7,135},{8... | collective-permute-start | bytes 147464 | tf_op jit(solution)/shard_map/ppermute | solution.py:33
  111.5 0.7 pad_maximum_fusion.1
  112.2 1.8 %collective-permute-done.44 = bf16[16,1536]{1,0:T(8,128)(2,1)S(1)} collective-permute-done((bf16[16,1536]{1,0:T(8,128)(2,1)S(1)}, bf16[16,1536]{1,0:T(8,128)(2,1)S(1)}, u32[]{:S(2)}, u32[]{:S(2)}) %collective-permute-start.44) | collective-permute-done | bytes 49184 | tf_op jit(solution)/shard_map/ppermute | solution.py:33
  114.0 1.5 %collective-permute-done.43 = bf16[16,1536]{1,0:T(8,128)(2,1)S(1)} collective-permute-done((bf16[16,1536]{1,0:T(8,128)(2,1)S(1)}, bf16[16,1536]{1,0:T(8,128)(2,1)S(1)}, u32[]{:S(2)}, u32[]{:S(2)}) %collective-permute-start.43) | collective-permute-done | bytes 49184 | tf_op jit(solution)/shard_map/ppermute | solution.py:33
  115.6 0.6 add_convert_fusion.11
  (69 shorter events, 3.5 us)
Async XLA Ops:
  19.8 5.7 %collective-permute-start.2 = (bf16[16,1536]{1,0:T(8,128)(2,1)S(1)}, bf16[16,1536]{1,0:T(8,128)(2,1)S(1)}, u32[]{:S(2)}, u32[]{:S(2)}) collective-permute-start(bf16[16,1536]{1,0:T(8,128)(2,1)S(1)} %add_convert_fusion.12), channel_id=1, source_target_pairs={{0,128},{1,129},{2,130},{3,131},{4,132},{5,133},{6,134},{7,135},{8... | collective-permute-start | bytes 147464 | tf_op jit(solution)/shard_map/ppermute | solution.py:33
  22.1 4.1 %collective-permute-start.1 = (bf16[16,1536]{1,0:T(8,128)(2,1)S(1)}, bf16[16,1536]{1,0:T(8,128)(2,1)S(1)}, u32[]{:S(2)}, u32[]{:S(2)}) collective-permute-start(bf16[16,1536]{1,0:T(8,128)(2,1)S(1)} %add_convert_fusion.12), channel_id=1, source_target_pairs={{0,192},{1,193},{2,194},{3,195},{4,196},{5,197},{6,198},{7,199},{8... | collective-permute-start | bytes 147464 | tf_op jit(solution)/shard_map/ppermute | solution.py:33
  22.1 4.6 %collective-permute-start = (bf16[16,1536]{1,0:T(8,128)(2,1)S(1)}, bf16[16,1536]{1,0:T(8,128)(2,1)S(1)}, u32[]{:S(2)}, u32[]{:S(2)}) collective-permute-start(bf16[16,1536]{1,0:T(8,128)(2,1)S(1)} %add_convert_fusion.12), channel_id=1, source_target_pairs={{0,64},{1,65},{2,66},{3,67},{4,68},{5,69},{6,70},{7,71},{8,72},{9,... | collective-permute-start | bytes 147464 | tf_op jit(solution)/shard_map/ppermute | solution.py:33
  26.7 10.8 %copy-start = (bf16[64,1536]{1,0:T(8,128)(2,1)S(1)}, bf16[64,1536]{1,0:T(8,128)(2,1)}, u32[]{:S(2)}) copy-start(bf16[64,1536]{1,0:T(8,128)(2,1)} %param.9) | copy-start | bytes 589828
  26.7 8.6 %collective-permute-start.5 = (bf16[64,1536]{1,0:T(8,128)(2,1)S(1)}, bf16[64,1536]{1,0:T(8,128)(2,1)S(1)}, u32[]{:S(2)}, u32[]{:S(2)}) collective-permute-start(bf16[64,1536]{1,0:T(8,128)(2,1)S(1)} %pad_maximum_fusion.refs_0_), channel_id=1, source_target_pairs={{0,48},{1,49},{2,50},{3,51},{4,52},{5,53},{6,54},{7,55},{8,56},{9,... | collective-permute-start | bytes 589832 | tf_op jit(solution)/shard_map/ppermute | solution.py:33
  29.8 7.2 %collective-permute-start.4 = (bf16[64,1536]{1,0:T(8,128)(2,1)S(1)}, bf16[64,1536]{1,0:T(8,128)(2,1)S(1)}, u32[]{:S(2)}, u32[]{:S(2)}) collective-permute-start(bf16[64,1536]{1,0:T(8,128)(2,1)S(1)} %pad_maximum_fusion.refs_0_), channel_id=1, source_target_pairs={{0,32},{1,33},{2,34},{3,35},{4,36},{5,37},{6,38},{7,39},{8,40},{9,... | collective-permute-start | bytes 589832 | tf_op jit(solution)/shard_map/ppermute | solution.py:33
  30.5 6.6 %collective-permute-start.3 = (bf16[64,1536]{1,0:T(8,128)(2,1)S(1)}, bf16[64,1536]{1,0:T(8,128)(2,1)S(1)}, u32[]{:S(2)}, u32[]{:S(2)}) collective-permute-start(bf16[64,1536]{1,0:T(8,128)(2,1)S(1)} %pad_maximum_fusion.refs_0_), channel_id=1, source_target_pairs={{0,16},{1,17},{2,18},{3,19},{4,20},{5,21},{6,22},{7,23},{8,24},{9,... | collective-permute-start | bytes 589832 | tf_op jit(solution)/shard_map/ppermute | solution.py:33
  30.9 6.6 %collective-permute-start.6 = (bf16[64,1536]{1,0:T(8,128)(2,1)S(1)}, bf16[64,1536]{1,0:T(8,128)(2,1)S(1)}, u32[]{:S(2)}, u32[]{:S(2)}) collective-permute-start(bf16[64,1536]{1,0:T(8,128)(2,1)S(1)} %pad_maximum_fusion.refs_0_), channel_id=1, source_target_pairs={{0,8},{1,9},{2,10},{3,11},{4,12},{5,13},{6,14},{7,15},{8,0},{9,1},... | collective-permute-start | bytes 589832 | tf_op jit(solution)/shard_map/ppermute | solution.py:33
  35.3 3.4 %collective-permute-start.9 = (bf16[64,1536]{1,0:T(8,128)(2,1)S(1)}, bf16[64,1536]{1,0:T(8,128)(2,1)S(1)}, u32[]{:S(2)}, u32[]{:S(2)}) collective-permute-start(bf16[64,1536]{1,0:T(8,128)(2,1)S(1)} %collective-permute-done.5.refs_3_), channel_id=1, source_target_pairs={{0,8},{1,9},{2,10},{3,11},{4,12},{5,13},{6,14},{7,15},{8,0},{9,1},... | collective-permute-start | bytes 589832 | tf_op jit(solution)/shard_map/ppermute | solution.py:33
  37.0 1.4 %collective-permute-start.8 = (bf16[64,1536]{1,0:T(8,128)(2,1)S(1)}, bf16[64,1536]{1,0:T(8,128)(2,1)S(1)}, u32[]{:S(2)}, u32[]{:S(2)}) collective-permute-start(bf16[64,1536]{1,0:T(8,128)(2,1)S(1)} %collective-permute-done.4.refs_2_), channel_id=1, source_target_pairs={{0,8},{1,9},{2,10},{3,11},{4,12},{5,13},{6,14},{7,15},{8,0},{9,1},... | collective-permute-start | bytes 589832 | tf_op jit(solution)/shard_map/ppermute | solution.py:33
  37.0 1.7 %collective-permute-start.7 = (bf16[64,1536]{1,0:T(8,128)(2,1)S(1)}, bf16[64,1536]{1,0:T(8,128)(2,1)S(1)}, u32[]{:S(2)}, u32[]{:S(2)}) collective-permute-start(bf16[64,1536]{1,0:T(8,128)(2,1)S(1)} %collective-permute-done.3.refs_1_), channel_id=1, source_target_pairs={{0,8},{1,9},{2,10},{3,11},{4,12},{5,13},{6,14},{7,15},{8,0},{9,1},... | collective-permute-start | bytes 589832 | tf_op jit(solution)/shard_map/ppermute | solution.py:33
  39.9 4.8 %collective-permute-start.10 = (bf16[64,768]{1,0:T(8,128)(2,1)S(1)}, bf16[64,768]{1,0:T(8,128)(2,1)S(1)}, u32[]{:S(2)}, u32[]{:S(2)}) collective-permute-start(bf16[64,768]{1,0:T(8,128)(2,1)S(1)} %get-tuple-element.52), channel_id=1, source_target_pairs={{0,1},{1,0},{2,3},{3,2},{4,5},{5,4},{6,7},{7,6},{8,15},{9,10},{10,... | collective-permute-start | bytes 294920 | tf_op jit(solution)/shard_map/ppermute | solution.py:33
  40.5 5.1 %collective-permute-start.17 = (bf16[64,768]{1,0:T(8,128)(2,1)S(1)}, bf16[64,768]{1,0:T(8,128)(2,1)S(1)}, u32[]{:S(2)}, u32[]{:S(2)}) collective-permute-start(bf16[64,768]{1,0:T(8,128)(2,1)S(1)} %get-tuple-element.62), channel_id=1, source_target_pairs={{0,1},{1,0},{2,3},{3,2},{4,5},{5,4},{6,7},{7,6},{8,15},{9,10},{10,... | collective-permute-start | bytes 294920 | tf_op jit(solution)/shard_map/ppermute | solution.py:33
  42.0 6.1 %collective-permute-start.12 = (bf16[64,1536]{1,0:T(8,128)(2,1)S(1)}, bf16[64,1536]{1,0:T(8,128)(2,1)S(1)}, u32[]{:S(2)}, u32[]{:S(2)}) collective-permute-start(bf16[64,1536]{1,0:T(8,128)(2,1)S(1)} %get-tuple-element.54), channel_id=1, source_target_pairs={{0,1},{1,0},{2,3},{3,2},{4,5},{5,4},{6,7},{7,6},{8,15},{9,10},{10,... | collective-permute-start | bytes 589832 | tf_op jit(solution)/shard_map/ppermute | solution.py:33
  44.7 5.9 %collective-permute-start.11 = (bf16[64,768]{1,0:T(8,128)(2,1)S(1)}, bf16[64,768]{1,0:T(8,128)(2,1)S(1)}, u32[]{:S(2)}, u32[]{:S(2)}) collective-permute-start(bf16[64,768]{1,0:T(8,128)(2,1)S(1)} %add_convert_fusion.10), channel_id=1, source_target_pairs={{0,7},{1,2},{2,1},{3,4},{4,3},{5,6},{6,5},{7,0},{8,9},{9,8},{10,11... | collective-permute-start | bytes 294920 | tf_op jit(solution)/shard_map/ppermute | solution.py:33
  45.7 6.0 %collective-permute-start.18 = (bf16[64,768]{1,0:T(8,128)(2,1)S(1)}, bf16[64,768]{1,0:T(8,128)(2,1)S(1)}, u32[]{:S(2)}, u32[]{:S(2)}) collective-permute-start(bf16[64,768]{1,0:T(8,128)(2,1)S(1)} %add_convert_fusion.7), channel_id=1, source_target_pairs={{0,7},{1,2},{2,1},{3,4},{4,3},{5,6},{6,5},{7,0},{8,9},{9,8},{10,11... | collective-permute-start | bytes 294920 | tf_op jit(solution)/shard_map/ppermute | solution.py:33
  48.2 8.7 %collective-permute-start.15 = (bf16[64,1536]{1,0:T(8,128)(2,1)S(1)}, bf16[64,1536]{1,0:T(8,128)(2,1)S(1)}, u32[]{:S(2)}, u32[]{:S(2)}) collective-permute-start(bf16[64,1536]{1,0:T(8,128)(2,1)S(1)} %add_convert_fusion.4), channel_id=1, source_target_pairs={{0,7},{1,2},{2,1},{3,4},{4,3},{5,6},{6,5},{7,0},{8,9},{9,8},{10,11... | collective-permute-start | bytes 589832 | tf_op jit(solution)/shard_map/ppermute | solution.py:33
  50.6 4.9 %collective-permute-start.13 = (bf16[64,768]{1,0:T(8,128)(2,1)S(1)}, bf16[64,768]{1,0:T(8,128)(2,1)S(1)}, u32[]{:S(2)}, u32[]{:S(2)}) collective-permute-start(bf16[64,768]{1,0:T(8,128)(2,1)S(1)} %add_convert_fusion.9), channel_id=1, source_target_pairs={{0,1},{1,0},{2,3},{3,2},{4,5},{5,4},{6,7},{7,6},{8,15},{9,10},{10,... | collective-permute-start | bytes 294920 | tf_op jit(solution)/shard_map/ppermute | solution.py:33
  51.7 5.4 %collective-permute-start.19 = (bf16[64,768]{1,0:T(8,128)(2,1)S(1)}, bf16[64,768]{1,0:T(8,128)(2,1)S(1)}, u32[]{:S(2)}, u32[]{:S(2)}) collective-permute-start(bf16[64,768]{1,0:T(8,128)(2,1)S(1)} %add_convert_fusion.6), channel_id=1, source_target_pairs={{0,1},{1,0},{2,3},{3,2},{4,5},{5,4},{6,7},{7,6},{8,15},{9,10},{10,... | collective-permute-start | bytes 294920 | tf_op jit(solution)/shard_map/ppermute | solution.py:33
  55.5 7.4 %collective-permute-start.14 = (bf16[64,768]{1,0:T(8,128)(2,1)S(1)}, bf16[64,768]{1,0:T(8,128)(2,1)S(1)}, u32[]{:S(2)}, u32[]{:S(2)}) collective-permute-start(bf16[64,768]{1,0:T(8,128)(2,1)S(1)} %add_convert_fusion.8), channel_id=1, source_target_pairs={{0,7},{1,2},{2,1},{3,4},{4,3},{5,6},{6,5},{7,0},{8,9},{9,8},{10,11... | collective-permute-start | bytes 294920 | tf_op jit(solution)/shard_map/ppermute | solution.py:33
  56.9 6.0 %collective-permute-start.16 = (bf16[64,1536]{1,0:T(8,128)(2,1)S(1)}, bf16[64,1536]{1,0:T(8,128)(2,1)S(1)}, u32[]{:S(2)}, u32[]{:S(2)}) collective-permute-start(bf16[64,1536]{1,0:T(8,128)(2,1)S(1)} %add_convert_fusion.3), channel_id=1, source_target_pairs={{0,1},{1,0},{2,3},{3,2},{4,5},{5,4},{6,7},{7,6},{8,15},{9,10},{10,... | collective-permute-start | bytes 589832 | tf_op jit(solution)/shard_map/ppermute | solution.py:33
  57.1 6.5 %collective-permute-start.20 = (bf16[64,768]{1,0:T(8,128)(2,1)S(1)}, bf16[64,768]{1,0:T(8,128)(2,1)S(1)}, u32[]{:S(2)}, u32[]{:S(2)}) collective-permute-start(bf16[64,768]{1,0:T(8,128)(2,1)S(1)} %add_convert_fusion.5), channel_id=1, source_target_pairs={{0,7},{1,2},{2,1},{3,4},{4,3},{5,6},{6,5},{7,0},{8,9},{9,8},{10,11... | collective-permute-start | bytes 294920 | tf_op jit(solution)/shard_map/ppermute | solution.py:33
  63.1 5.6 %collective-permute-start.21 = (bf16[64,768]{1,0:T(8,128)(2,1)S(1)}, bf16[64,768]{1,0:T(8,128)(2,1)S(1)}, u32[]{:S(2)}, u32[]{:S(2)}) collective-permute-start(bf16[64,768]{1,0:T(8,128)(2,1)S(1)} %get-tuple-element.85.refs_2_), channel_id=1, source_target_pairs={{0,1},{1,0},{2,3},{3,2},{4,5},{5,4},{6,7},{7,6},{8,15},{9,10},{10,... | collective-permute-start | bytes 294920 | tf_op jit(solution)/shard_map/ppermute | solution.py:33
  63.8 6.7 %collective-permute-start.25 = (bf16[64,768]{1,0:T(8,128)(2,1)S(1)}, bf16[64,768]{1,0:T(8,128)(2,1)S(1)}, u32[]{:S(2)}, u32[]{:S(2)}) collective-permute-start(bf16[64,768]{1,0:T(8,128)(2,1)S(1)} %get-tuple-element.83.refs_3_), channel_id=1, source_target_pairs={{0,1},{1,0},{2,3},{3,2},{4,5},{5,4},{6,7},{7,6},{8,15},{9,10},{10,... | collective-permute-start | bytes 294920 | tf_op jit(solution)/shard_map/ppermute | solution.py:33
  65.5 6.5 %collective-permute-start.32 = (bf16[64,768]{1,0:T(8,128)(2,1)S(1)}, bf16[64,768]{1,0:T(8,128)(2,1)S(1)}, u32[]{:S(2)}, u32[]{:S(2)}) collective-permute-start(bf16[64,768]{1,0:T(8,128)(2,1)S(1)} %get-tuple-element.83.refs_3_), channel_id=1, source_target_pairs={{0,7},{1,2},{2,1},{3,4},{4,3},{5,6},{6,5},{7,0},{8,9},{9,8},{10,11... | collective-permute-start | bytes 294920 | tf_op jit(solution)/shard_map/ppermute | solution.py:33
  67.3 5.8 %collective-permute-start.29 = (bf16[64,768]{1,0:T(8,128)(2,1)S(1)}, bf16[64,768]{1,0:T(8,128)(2,1)S(1)}, u32[]{:S(2)}, u32[]{:S(2)}) collective-permute-start(bf16[64,768]{1,0:T(8,128)(2,1)S(1)} %get-tuple-element.85.refs_2_), channel_id=1, source_target_pairs={{0,7},{1,2},{2,1},{3,4},{4,3},{5,6},{6,5},{7,0},{8,9},{9,8},{10,11... | collective-permute-start | bytes 294920 | tf_op jit(solution)/shard_map/ppermute | solution.py:33
  68.8 6.8 %collective-permute-start.22 = (bf16[64,768]{1,0:T(8,128)(2,1)S(1)}, bf16[64,768]{1,0:T(8,128)(2,1)S(1)}, u32[]{:S(2)}, u32[]{:S(2)}) collective-permute-start(bf16[64,768]{1,0:T(8,128)(2,1)S(1)} %collective-permute-done.21.refs_4_), channel_id=1, source_target_pairs={{0,7},{1,2},{2,1},{3,4},{4,3},{5,6},{6,5},{7,0},{8,9},{9,8},{10,11... | collective-permute-start | bytes 294920 | tf_op jit(solution)/shard_map/ppermute | solution.py:33
  70.5 7.2 %collective-permute-start.26 = (bf16[64,768]{1,0:T(8,128)(2,1)S(1)}, bf16[64,768]{1,0:T(8,128)(2,1)S(1)}, u32[]{:S(2)}, u32[]{:S(2)}) collective-permute-start(bf16[64,768]{1,0:T(8,128)(2,1)S(1)} %collective-permute-done.25.refs_5_), channel_id=1, source_target_pairs={{0,7},{1,2},{2,1},{3,4},{4,3},{5,6},{6,5},{7,0},{8,9},{9,8},{10,11... | collective-permute-start | bytes 294920 | tf_op jit(solution)/shard_map/ppermute | solution.py:33
  72.0 5.7 %collective-permute-start.33 = (bf16[64,768]{1,0:T(8,128)(2,1)S(1)}, bf16[64,768]{1,0:T(8,128)(2,1)S(1)}, u32[]{:S(2)}, u32[]{:S(2)}) collective-permute-start(bf16[64,768]{1,0:T(8,128)(2,1)S(1)} %collective-permute-done.32.refs_1_), channel_id=1, source_target_pairs={{0,1},{1,0},{2,3},{3,2},{4,5},{5,4},{6,7},{7,6},{8,15},{9,10},{10,... | collective-permute-start | bytes 294920 | tf_op jit(solution)/shard_map/ppermute | solution.py:33
  73.1 6.4 %collective-permute-start.30 = (bf16[64,768]{1,0:T(8,128)(2,1)S(1)}, bf16[64,768]{1,0:T(8,128)(2,1)S(1)}, u32[]{:S(2)}, u32[]{:S(2)}) collective-permute-start(bf16[64,768]{1,0:T(8,128)(2,1)S(1)} %collective-permute-done.29.refs_0_), channel_id=1, source_target_pairs={{0,1},{1,0},{2,3},{3,2},{4,5},{5,4},{6,7},{7,6},{8,15},{9,10},{10,... | collective-permute-start | bytes 294920 | tf_op jit(solution)/shard_map/ppermute | solution.py:33
  75.6 5.4 %collective-permute-start.23 = (bf16[64,768]{1,0:T(8,128)(2,1)S(1)}, bf16[64,768]{1,0:T(8,128)(2,1)S(1)}, u32[]{:S(2)}, u32[]{:S(2)}) collective-permute-start(bf16[64,768]{1,0:T(8,128)(2,1)S(1)} %collective-permute-done.22.refs_6_), channel_id=1, source_target_pairs={{0,1},{1,0},{2,3},{3,2},{4,5},{5,4},{6,7},{7,6},{8,15},{9,10},{10,... | collective-permute-start | bytes 294920 | tf_op jit(solution)/shard_map/ppermute | solution.py:33
  77.7 5.6 %collective-permute-start.27 = (bf16[64,768]{1,0:T(8,128)(2,1)S(1)}, bf16[64,768]{1,0:T(8,128)(2,1)S(1)}, u32[]{:S(2)}, u32[]{:S(2)}) collective-permute-start(bf16[64,768]{1,0:T(8,128)(2,1)S(1)} %collective-permute-done.26.refs_7_), channel_id=1, source_target_pairs={{0,1},{1,0},{2,3},{3,2},{4,5},{5,4},{6,7},{7,6},{8,15},{9,10},{10,... | collective-permute-start | bytes 294920 | tf_op jit(solution)/shard_map/ppermute | solution.py:33
  77.7 8.8 %collective-permute-start.34 = (bf16[64,768]{1,0:T(8,128)(2,1)S(1)}, bf16[64,768]{1,0:T(8,128)(2,1)S(1)}, u32[]{:S(2)}, u32[]{:S(2)}) collective-permute-start(bf16[64,768]{1,0:T(8,128)(2,1)S(1)} %collective-permute-done.33.refs_7_), channel_id=1, source_target_pairs={{0,7},{1,2},{2,1},{3,4},{4,3},{5,6},{6,5},{7,0},{8,9},{9,8},{10,11... | collective-permute-start | bytes 294920 | tf_op jit(solution)/shard_map/ppermute | solution.py:33
  79.5 7.1 %collective-permute-start.31 = (bf16[64,768]{1,0:T(8,128)(2,1)S(1)}, bf16[64,768]{1,0:T(8,128)(2,1)S(1)}, u32[]{:S(2)}, u32[]{:S(2)}) collective-permute-start(bf16[64,768]{1,0:T(8,128)(2,1)S(1)} %collective-permute-done.30.refs_6_), channel_id=1, source_target_pairs={{0,7},{1,2},{2,1},{3,4},{4,3},{5,6},{6,5},{7,0},{8,9},{9,8},{10,11... | collective-permute-start | bytes 294920 | tf_op jit(solution)/shard_map/ppermute | solution.py:33
  81.0 8.2 %collective-permute-start.24 = (bf16[64,768]{1,0:T(8,128)(2,1)S(1)}, bf16[64,768]{1,0:T(8,128)(2,1)S(1)}, u32[]{:S(2)}, u32[]{:S(2)}) collective-permute-start(bf16[64,768]{1,0:T(8,128)(2,1)S(1)} %collective-permute-done.23.refs_0_), channel_id=1, source_target_pairs={{0,7},{1,2},{2,1},{3,4},{4,3},{5,6},{6,5},{7,0},{8,9},{9,8},{10,11... | collective-permute-start | bytes 294920 | tf_op jit(solution)/shard_map/ppermute | solution.py:33
  83.4 5.8 %collective-permute-start.28 = (bf16[64,768]{1,0:T(8,128)(2,1)S(1)}, bf16[64,768]{1,0:T(8,128)(2,1)S(1)}, u32[]{:S(2)}, u32[]{:S(2)}) collective-permute-start(bf16[64,768]{1,0:T(8,128)(2,1)S(1)} %collective-permute-done.27.refs_1_), channel_id=1, source_target_pairs={{0,7},{1,2},{2,1},{3,4},{4,3},{5,6},{6,5},{7,0},{8,9},{9,8},{10,11... | collective-permute-start | bytes 294920 | tf_op jit(solution)/shard_map/ppermute | solution.py:33
  91.0 10.0 %collective-permute-start.35 = (bf16[64,1536]{1,0:T(8,128)(2,1)S(1)}, bf16[64,1536]{1,0:T(8,128)(2,1)S(1)}, u32[]{:S(2)}, u32[]{:S(2)}) collective-permute-start(bf16[64,1536]{1,0:T(8,128)(2,1)S(1)} %get-tuple-element.72), channel_id=1, source_target_pairs={{0,8},{1,9},{2,10},{3,11},{4,12},{5,13},{6,14},{7,15},{8,0},{9,1},... | collective-permute-start | bytes 589832 | tf_op jit(solution)/shard_map/ppermute | solution.py:33
  91.1 5.3 %collective-permute-start.36 = (bf16[64,1536]{1,0:T(8,128)(2,1)S(1)}, bf16[64,1536]{1,0:T(8,128)(2,1)S(1)}, u32[]{:S(2)}, u32[]{:S(2)}) collective-permute-start(bf16[64,1536]{1,0:T(8,128)(2,1)S(1)} %get-tuple-element.74), channel_id=1, source_target_pairs={{0,8},{1,9},{2,10},{3,11},{4,12},{5,13},{6,14},{7,15},{8,0},{9,1},... | collective-permute-start | bytes 589832 | tf_op jit(solution)/shard_map/ppermute | solution.py:33
  91.6 7.3 %collective-permute-start.38 = (bf16[64,1536]{1,0:T(8,128)(2,1)S(1)}, bf16[64,1536]{1,0:T(8,128)(2,1)S(1)}, u32[]{:S(2)}, u32[]{:S(2)}) collective-permute-start(bf16[64,1536]{1,0:T(8,128)(2,1)S(1)} %get-tuple-element.76), channel_id=1, source_target_pairs={{0,8},{1,9},{2,10},{3,11},{4,12},{5,13},{6,14},{7,15},{8,0},{9,1},... | collective-permute-start | bytes 589832 | tf_op jit(solution)/shard_map/ppermute | solution.py:33
  91.7 8.1 %collective-permute-start.40 = (bf16[64,1536]{1,0:T(8,128)(2,1)S(1)}, bf16[64,1536]{1,0:T(8,128)(2,1)S(1)}, u32[]{:S(2)}, u32[]{:S(2)}) collective-permute-start(bf16[64,1536]{1,0:T(8,128)(2,1)S(1)} %get-tuple-element.78), channel_id=1, source_target_pairs={{0,8},{1,9},{2,10},{3,11},{4,12},{5,13},{6,14},{7,15},{8,0},{9,1},... | collective-permute-start | bytes 589832 | tf_op jit(solution)/shard_map/ppermute | solution.py:33
  96.4 7.8 %collective-permute-start.37 = (bf16[64,1536]{1,0:T(8,128)(2,1)S(1)}, bf16[64,1536]{1,0:T(8,128)(2,1)S(1)}, u32[]{:S(2)}, u32[]{:S(2)}) collective-permute-start(bf16[64,1536]{1,0:T(8,128)(2,1)S(1)} %add_convert_fusion.2), channel_id=1, source_target_pairs={{0,48},{1,49},{2,50},{3,51},{4,52},{5,53},{6,54},{7,55},{8,200},{9... | collective-permute-start | bytes 589832 | tf_op jit(solution)/shard_map/ppermute | solution.py:33
  99.0 7.3 %collective-permute-start.39 = (bf16[64,1536]{1,0:T(8,128)(2,1)S(1)}, bf16[64,1536]{1,0:T(8,128)(2,1)S(1)}, u32[]{:S(2)}, u32[]{:S(2)}) collective-permute-start(bf16[64,1536]{1,0:T(8,128)(2,1)S(1)} %add_convert_fusion.1), channel_id=1, source_target_pairs={{0,32},{1,33},{2,34},{3,35},{4,36},{5,37},{6,38},{7,39},{8,136},{9... | collective-permute-start | bytes 589832 | tf_op jit(solution)/shard_map/ppermute | solution.py:33
  99.8 6.8 %collective-permute-start.41 = (bf16[64,1536]{1,0:T(8,128)(2,1)S(1)}, bf16[64,1536]{1,0:T(8,128)(2,1)S(1)}, u32[]{:S(2)}, u32[]{:S(2)}) collective-permute-start(bf16[64,1536]{1,0:T(8,128)(2,1)S(1)} %add_convert_fusion), channel_id=1, source_target_pairs={{0,16},{1,17},{2,18},{3,19},{4,20},{5,21},{6,22},{7,23},{8,72},{9,... | collective-permute-start | bytes 589832 | tf_op jit(solution)/shard_map/ppermute | solution.py:33
  106.7 5.4 %collective-permute-start.42 = (bf16[16,1536]{1,0:T(8,128)(2,1)S(1)}, bf16[16,1536]{1,0:T(8,128)(2,1)S(1)}, u32[]{:S(2)}, u32[]{:S(2)}) collective-permute-start(bf16[16,1536]{1,0:T(8,128)(2,1)S(1)} %get-tuple-element.87), channel_id=1, source_target_pairs={{0,192},{1,193},{2,194},{3,195},{4,196},{5,197},{6,198},{7,199},{8... | collective-permute-start | bytes 147464 | tf_op jit(solution)/shard_map/ppermute | solution.py:33
  108.4 5.6 %collective-permute-start.44 = (bf16[16,1536]{1,0:T(8,128)(2,1)S(1)}, bf16[16,1536]{1,0:T(8,128)(2,1)S(1)}, u32[]{:S(2)}, u32[]{:S(2)}) collective-permute-start(bf16[16,1536]{1,0:T(8,128)(2,1)S(1)} %get-tuple-element.88), channel_id=1, source_target_pairs={{0,128},{1,129},{2,130},{3,131},{4,132},{5,133},{6,134},{7,135},{8... | collective-permute-start | bytes 147464 | tf_op jit(solution)/shard_map/ppermute | solution.py:33
  111.5 4.1 %collective-permute-start.43 = (bf16[16,1536]{1,0:T(8,128)(2,1)S(1)}, bf16[16,1536]{1,0:T(8,128)(2,1)S(1)}, u32[]{:S(2)}, u32[]{:S(2)}) collective-permute-start(bf16[16,1536]{1,0:T(8,128)(2,1)S(1)} %get-tuple-element.89), channel_id=1, source_target_pairs={{0,64},{1,65},{2,66},{3,67},{4,68},{5,69},{6,70},{7,71},{8,24},{9,... | collective-permute-start | bytes 147464 | tf_op jit(solution)/shard_map/ppermute | solution.py:33
